TPU v7x, 32 devices: a whole 2x2x4 slice. The times are simulated.
32 devices in a mesh: span: 8 (over z, core), wall: 4 (over y, x).
Axes of the slice: x: 2, y: 2, z: 4, core: 2. Of those that a mesh axis runs over, the one named last changes fastest.
Arguments:
- noise: bfloat16 [3, 32, 256, 1024], P(None, None, 'wall', 'span'), may hold values from -6 to 6
- wall_scale: float32 [3], replicated, may hold values from 4 to 12
- span_scale: float32 [3], replicated, may hold values from 4 to 12
- lund_factor: float32 [6, 256], P(None, 'wall'), may hold values from 0.2 to 1
- mean_velocity: float32 [256], P('wall'), may hold values from 0.2 to 1
- owner_map: int32 [4, 8, 512, 1], P('wall', 'span'), may hold values from 0 to 31; in each aligned block of 512 rows (0 to 511, 512 to 1023, ..., all dimensions but the last counted through in order) at most 32 rows name the same one
Outputs:
- face_state: bfloat16 [32, 1024, 1536], P(('span', 'wall'))
Inputs may be any that keep to these rules, and one draw needn't show every extreme that they name: `owner_map`: within one tile no owner receives more than 32 elements, and in every draw some tile sends exactly 32 elements to some owner; every device owns some element.
All inputs are finite; a program needn't handle non-finite values.
Results may differ from a plain program's by a relative error of at most 0.001.
Values may be sent and summed in bfloat16 or wider, within the bound.
No kernel may reach another device: no remote copies, remote signals or barrier semaphores. Data moves between devices by JAX's collectives and lax.ppermute only.
A program may use at most 64 MiB of HBM per device.

v0:
```python
import math

import jax
import jax.numpy as jnp
from jax import lax
from jax.sharding import PartitionSpec as P

HALO = 24
EDGE = 4


def with_halo(block, sides, width, periodic):
    for axis, dim in sides:
        count = lax.axis_size(axis)
        forward = [(i, i + 1) for i in range(count - 1)]
        if periodic:
            forward.append((count - 1, 0))
        backward = [(target, source) for source, target in forward]
        low = lax.ppermute(
            lax.slice_in_dim(block, block.shape[dim] - width, None, axis=dim), axis, forward
        )
        high = lax.ppermute(lax.slice_in_dim(block, 0, width, axis=dim), axis, backward)
        block = jnp.concatenate([low, block, high], axis=dim)
    return block


def band_matrix(scale, rows):
    row_ids = jnp.arange(rows)[:, None]
    col_ids = jnp.arange(rows + 2 * HALO)[None, :]
    offset = (col_ids - row_ids).astype(jnp.float32)
    valid = (col_ids - row_ids >= 0) & (col_ids - row_ids <= 2 * HALO)
    taps_axis = jnp.arange(-HALO, HALO + 1).astype(jnp.float32)
    norms = jnp.sqrt(
        jnp.sum(jnp.exp(-math.pi * taps_axis[None, :] ** 2 / scale[:, None] ** 2), axis=1)
    )
    shifted = offset[None] - HALO
    values = jnp.exp(
        -math.pi * shifted * shifted / (2.0 * scale[:, None, None] * scale[:, None, None])
    )
    return jnp.where(valid[None], values, 0.0) / norms[:, None, None]


def wall_pass(extended, matrix):
    return jnp.einsum(
        "cij,ctjz->ctiz", matrix, extended.astype(jnp.float32), precision=lax.Precision.HIGHEST
    )


def span_pass(extended, matrix):
    return jnp.einsum("ctyk,czk->ctyz", extended, matrix, precision=lax.Precision.HIGHEST)


def per_device(noise, wall_scale, span_scale, lund_factor, mean_velocity, owner_map):
    trio, planes, rows, cols = noise.shape
    wall_matrix = band_matrix(wall_scale, rows)
    span_matrix = band_matrix(span_scale, cols)
    tall = with_halo(noise, (("wall", 2),), HALO, False)
    smooth = wall_pass(tall, wall_matrix)
    broad = with_halo(smooth, (("span", 3),), HALO, True)
    psi = span_pass(broad, span_matrix)
    factor = lund_factor[:, None, :, None]
    along = mean_velocity[None, :, None] + factor[0] * psi[0]
    normal = factor[1] * psi[0] + factor[2] * psi[1]
    spanwise = factor[3] * psi[0] + factor[4] * psi[1] + factor[5] * psi[2]
    velocity = jnp.stack([along, normal, spanwise]).astype(jnp.bfloat16)
    blocks = velocity.reshape(3, planes, rows // EDGE, EDGE, cols // EDGE, EDGE)
    payload = jnp.transpose(blocks, (2, 4, 0, 1, 3, 5)).reshape(-1, 3 * planes * EDGE * EDGE)
    elements = payload.shape[0]
    n_span = lax.axis_size("span")
    n_wall = lax.axis_size("wall")
    devices = n_span * n_wall
    slots = max(8, 2 * elements // devices)
    owners = owner_map.reshape(elements)
    onehot = (owners[:, None] == jnp.arange(devices, dtype=jnp.int32)[None, :]).astype(jnp.int32)
    rank = jnp.sum(onehot * (jnp.cumsum(onehot, axis=0) - 1), axis=1)
    target = owners * slots + rank
    outgoing = jnp.zeros((devices * slots, payload.shape[1]), jnp.bfloat16).at[target].set(payload)
    received = lax.all_to_all(
        outgoing.reshape(devices, slots, payload.shape[1]),
        ("span", "wall"),
        split_axis=0,
        concat_axis=0,
        tiled=True,
    )
    return received.reshape(1, devices * slots, payload.shape[1])


def solution(mesh):
    return jax.shard_map(
        per_device,
        mesh=mesh,
        in_specs=(
            P(None, None, "wall", "span"),
            P(),
            P(),
            P(None, "wall"),
            P("wall"),
            P("wall", "span", None, None),
        ),
        out_specs=P(("span", "wall"), None, None),
        check_vma=False,
    )
```

profile of v0, /device:TPU:0, one launch (start us, length us, event | category | flops | bytes accessed | tf_op | source)
XLA Modules:
  0.0 212.9 jit_solution(6563222286668957423)
XLA Ops:
  0.0 1.5 fusion.53
  1.5 4.9 %collective-permute-start = (bf16[3,32,24,128]{3,2,1,0:T(8,128)(2,1)S(1)}, bf16[3,32,24,128]{3,2,1,0:T(8,128)(2,1)S(1)}, u32[]{:S(2)}, u32[]{:S(2)}) collective-permute-start(bf16[3,32,24,128]{3,2,1,0:T(8,128)(2,1)S(1)} %get-tuple-element.12), channel_id=1, source_target_pairs={{0,1},{1,2},{2,3},{4,5},{5,6},{6,7},{8,9},{9,10},{10,11},{12,13},{... | collective-permute-start | bytes 1769480 | tf_op jit(solution)/shard_map/ppermute | solution.py:19
  6.4 1.3 collective-permute-start.1
  7.7 0.7 multiply_multiply_fusion.2
  8.3 0.2 fusion.47
  8.6 0.7 fusion.37
  9.3 1.2 reduce-window.6
  10.5 0.2 slice_reduce_fusion
  10.7 8.2 %collective-permute-done = bf16[3,32,24,128]{3,2,1,0:T(8,128)(2,1)S(1)} collective-permute-done((bf16[3,32,24,128]{3,2,1,0:T(8,128)(2,1)S(1)}, bf16[3,32,24,128]{3,2,1,0:T(8,128)(2,1)S(1)}, u32[]{:S(2)}, u32[]{:S(2)}) %collective-permute-start) | collective-permute-done | bytes 589856 | tf_op jit(solution)/shard_map/ppermute | solution.py:19
  18.9 0.0 copy-start.3
  18.9 14.6 %collective-permute-done.1 = bf16[3,32,24,128]{3,2,1,0:T(8,128)(2,1)S(1)} collective-permute-done((bf16[3,32,24,128]{3,2,1,0:T(8,128)(2,1)S(1)}, bf16[3,32,24,128]{3,2,1,0:T(8,128)(2,1)S(1)}, u32[]{:S(2)}, u32[]{:S(2)}) %collective-permute-start.1) | collective-permute-done | bytes 589856 | tf_op jit(solution)/shard_map/ppermute | solution.py:22
  33.5 0.0 copy-done.3
  33.5 0.0 copy-start.4
  33.5 0.8 copy-done.4
  34.3 3.2 %fusion.12 = f32[3,32,64,128]{3,2,1,0:T(8,128)S(1)} fusion(bf16[3,32,24,128]{3,2,1,0:T(8,128)(2,1)} %copy-done.4, bf16[3,32,64,128]{3,2,1,0:T(8,128)(2,1)} %param.6, bf16[3,32,24,128]{3,2,1,0:T(8,128)(2,1)} %copy-done.3, f32[3]{0:T(128)S(1)} %sqrt.14, f32[3]{0:T(128)S(1)} %get-tuple-element.25, f32[64,112]{1,0:T(8,128)S(1)} %multiply_multiply_fusion.1, ...), kind=kOutput, calls=%fused_computation.14 | convolution fusion | flops 1065286656 | bytes 5934104 | tf_op jit(solution)/shard_map/cij,ctjz->ctiz/dot_general | solution.py:44
  37.5 3.8 %fusion.52 = (f32[3,32,64,24]{3,2,1,0:T(8,128)}, f32[3,32,64,24]{3,2,1,0:T(8,128)}) fusion(f32[3,32,64,128]{3,2,1,0:T(8,128)S(1)} %fusion.12), kind=kLoop, calls=%fused_computation.77 | loop fusion | bytes 2359296 | tf_op jit(solution)/shard_map/slice | solution.py:20
  41.3 3.2 %copy.29 = f32[3,32,64,24]{2,3,1,0:T(8,128)} copy(f32[3,32,64,24]{3,2,1,0:T(8,128)} %get-tuple-element.10) | data formatting | bytes 1179648 | tf_op jit(solution)/shard_map/slice | solution.py:20
  44.4 0.0 copy-start
  44.5 0.0 copy-start.1
  44.5 0.0 collective-permute-start.2
  44.5 3.2 %copy.30 = f32[3,32,64,24]{2,3,1,0:T(8,128)} copy(f32[3,32,64,24]{3,2,1,0:T(8,128)} %get-tuple-element.11) | data formatting | bytes 1179648 | tf_op jit(solution)/shard_map/slice | solution.py:22
  47.6 3.5 %collective-permute-start.3 = (f32[3,32,64,24]{2,3,1,0:T(8,128)}, f32[3,32,64,24]{2,3,1,0:T(8,128)}, u32[]{:S(2)}, u32[]{:S(2)}) collective-permute-start(f32[3,32,64,24]{2,3,1,0:T(8,128)} %copy.30), channel_id=1, source_target_pairs={{4,0},{8,4},{12,8},{16,12},{20,16},{24,20},{28,24},{0,28},{5,1},{9... | collective-permute-start | bytes 1769480 | tf_op jit(solution)/shard_map/ppermute | solution.py:22
  51.2 0.0 copy-done
  51.2 0.1 fusion.36
  51.4 0.0 copy-done.1
  51.4 18.1 %collective-permute-done.2 = f32[3,32,64,24]{2,3,1,0:T(8,128)} collective-permute-done((f32[3,32,64,24]{2,3,1,0:T(8,128)}, f32[3,32,64,24]{2,3,1,0:T(8,128)}, u32[]{:S(2)}, u32[]{:S(2)}) %collective-permute-start.2) | collective-permute-done | bytes 589856 | tf_op jit(solution)/shard_map/ppermute | solution.py:19
  69.5 3.3 %copy.31 = f32[3,32,64,24]{3,2,1,0:T(8,128)} copy(f32[3,32,64,24]{2,3,1,0:T(8,128)} %collective-permute-done.2) | data formatting | bytes 1179648 | tf_op jit(solution)/shard_map/ppermute | solution.py:19
  72.8 0.0 collective-permute-done.3
  72.8 3.2 %copy.32 = f32[3,32,64,24]{3,2,1,0:T(8,128)} copy(f32[3,32,64,24]{2,3,1,0:T(8,128)} %collective-permute-done.3) | data formatting | bytes 1179648 | tf_op jit(solution)/shard_map/ppermute | solution.py:22
  76.0 0.0 copy-start.2
  76.0 9.4 %fusion = f32[3,32,64,128]{3,2,1,0:T(8,128)S(1)} fusion(f32[3,32,64,24]{3,2,1,0:T(8,128)} %copy.32, f32[3,32,64,128]{3,2,1,0:T(8,128)S(1)} %fusion.12, f32[3,32,64,24]{3,2,1,0:T(8,128)} %copy.31, f32[3]{0:T(128)S(1)} %sqrt.15, f32[3]{0:T(128)S(1)} %get-tuple-element.20, f32[128,176]{0,1:T(8,128)S(1)} %multiply_multiply_fusion, pred[128,176]{0,1:T(8,128)(4,1)S(1)} %fusion.34), kind=kOutput, calls=%fused_computation.1 | convolution fusion | flops 1663309824 | bytes 7583768 | tf_op jit(solution)/shard_map/ctyk,czk->ctyz/dot_general | solution.py:50
  85.4 0.0 copy-done.2
  85.5 1.4 add_convert_fusion.1
  86.8 2.0 copy.33
  88.9 1.9 copy.34
  90.8 1.9 copy.35
  92.6 9.5 %maximum_bitcast_fusion = bf16[16,32,3,32,4,4]{3,5,1,4,0,2:T(4,128)(2,1)} fusion(bf16[1,32,16,4,32,4]{1,5,4,3,2,0:T(4,128)(2,1)} %bitcast.62, bf16[1,32,16,4,32,4]{1,5,4,3,2,0:T(4,128)(2,1)} %bitcast.61, bf16[1,32,16,4,32,4]{1,5,4,3,2,0:T(4,128)(2,1)S(1)} %bitcast.60), kind=kLoop, calls=%fused_computation.7 | loop fusion | flops 1572864 | bytes 3145728 | tf_op jit(solution)/shard_map/transpose | solution.py:67
  102.1 14.5 %copy.36 = bf16[16,32,3,32,4,4]{1,0,5,4,3,2:T(8,128)(2,1)} copy(bf16[16,32,3,32,4,4]{3,5,1,4,0,2:T(4,128)(2,1)} %maximum_bitcast_fusion) | data formatting | bytes 3145728 | tf_op jit(solution)/shard_map/transpose | solution.py:67
  116.5 8.4 %reshape.178 = bf16[512,1536]{0,1:T(8,128)(2,1)S(1)} reshape(bf16[16,32,3,32,4,4]{1,0,5,4,3,2:T(8,128)(2,1)} %copy.36) | data formatting | bytes 3145728 | tf_op jit(solution)/shard_map/reshape | solution.py:67
  124.9 1.6 copy.37
  126.5 5.1 %scatter_custom_fusion = bf16[1024,1536]{1,0:T(8,128)(2,1)S(1)} fusion(s32[512]{0:T(512)S(1)} %bitcast.66, bf16[512,1536]{1,0:T(8,128)(2,1)} %copy.37, bf16[]{:T(256)} %constant.11.clone.1), kind=kCustom, calls=%fused_computation.15 | custom fusion | bytes 3146240 | tf_op jit(solution)/shard_map/scatter | solution.py:77
  131.6 79.6 %all_to_all.5 = bf16[32,32,1536]{2,1,0:T(8,128)(2,1)S(1)} all-to-all(bf16[32,32,1536]{2,1,0:T(8,128)(2,1)S(1)} %bitcast.58), channel_id=1, replica_groups=mesh['span'=8,'wall'=4] {'span','wall'}, dimensions={0} | all-to-all | bytes 6291456 | tf_op jit(solution)/shard_map/all_to_all | solution.py:78
  211.3 1.7 copy.43
  (11 shorter events, 0.2 us)
Async XLA Ops:
  1.5 17.4 %collective-permute-start = (bf16[3,32,24,128]{3,2,1,0:T(8,128)(2,1)S(1)}, bf16[3,32,24,128]{3,2,1,0:T(8,128)(2,1)S(1)}, u32[]{:S(2)}, u32[]{:S(2)}) collective-permute-start(bf16[3,32,24,128]{3,2,1,0:T(8,128)(2,1)S(1)} %get-tuple-element.12), channel_id=1, source_target_pairs={{0,1},{1,2},{2,3},{4,5},{5,6},{6,7},{8,9},{9,10},{10,11},{12,13},{... | collective-permute-start | bytes 1769480 | tf_op jit(solution)/shard_map/ppermute | solution.py:19
  6.4 27.1 %collective-permute-start.1 = (bf16[3,32,24,128]{3,2,1,0:T(8,128)(2,1)S(1)}, bf16[3,32,24,128]{3,2,1,0:T(8,128)(2,1)S(1)}, u32[]{:S(2)}, u32[]{:S(2)}) collective-permute-start(bf16[3,32,24,128]{3,2,1,0:T(8,128)(2,1)S(1)} %get-tuple-element.13), channel_id=1, source_target_pairs={{1,0},{2,1},{3,2},{5,4},{6,5},{7,6},{9,8},{10,9},{11,10},{13,12},{... | collective-permute-start | bytes 1769480 | tf_op jit(solution)/shard_map/ppermute | solution.py:22
  18.9 14.6 %copy-start.3 = (bf16[3,32,24,128]{3,2,1,0:T(8,128)(2,1)}, bf16[3,32,24,128]{3,2,1,0:T(8,128)(2,1)S(1)}, u32[]{:S(2)}) copy-start(bf16[3,32,24,128]{3,2,1,0:T(8,128)(2,1)S(1)} %collective-permute-done) | copy-start | bytes 1769476
  33.5 0.8 copy-start.4
  44.4 6.8 %copy-start = (s32[1,1,512,1]{2,3,1,0:T(1,128)S(1)}, s32[1,1,512,1]{2,3,1,0:T(1,128)}, u32[]{:S(2)}) copy-start(s32[1,1,512,1]{2,3,1,0:T(1,128)} %param.11) | copy-start | bytes 6148
  44.5 6.9 %copy-start.1 = (f32[6,64]{1,0:T(8,128)S(1)}, f32[6,64]{1,0:T(8,128)}, u32[]{:S(2)}) copy-start(f32[6,64]{1,0:T(8,128)} %param.9) | copy-start | bytes 4612
  44.5 25.1 %collective-permute-start.2 = (f32[3,32,64,24]{2,3,1,0:T(8,128)}, f32[3,32,64,24]{2,3,1,0:T(8,128)}, u32[]{:S(2)}, u32[]{:S(2)}) collective-permute-start(f32[3,32,64,24]{2,3,1,0:T(8,128)} %copy.29), channel_id=1, source_target_pairs={{0,4},{4,8},{8,12},{12,16},{16,20},{20,24},{24,28},{28,0},{1,5},{5... | collective-permute-start | bytes 1769480 | tf_op jit(solution)/shard_map/ppermute | solution.py:19
  47.6 25.2 %collective-permute-start.3 = (f32[3,32,64,24]{2,3,1,0:T(8,128)}, f32[3,32,64,24]{2,3,1,0:T(8,128)}, u32[]{:S(2)}, u32[]{:S(2)}) collective-permute-start(f32[3,32,64,24]{2,3,1,0:T(8,128)} %copy.30), channel_id=1, source_target_pairs={{4,0},{8,4},{12,8},{16,12},{20,16},{24,20},{28,24},{0,28},{5,1},{9... | collective-permute-start | bytes 1769480 | tf_op jit(solution)/shard_map/ppermute | solution.py:22
  76.0 9.4 %copy-start.2 = (f32[64]{0:T(128)S(1)}, f32[64]{0:T(128)}, u32[]{:S(2)}) copy-start(f32[64]{0:T(128)} %param.10) | copy-start | bytes 772
where the time goes:
time: 214 us; the launch traced here: 213 us
  blocking collectives  79.6 us (37%)
  local copies, waits for them, and re-layouts  56.1 us (26%)
  waiting for transfers between devices  40.9 us (19%)
  other arithmetic  13.8 us (6%)
  matrix products  12.6 us (6%)
  starting transfers between devices  9.69 us (5%)
    all_to_all x1, blocking collectives, per_device(): lax.all_to_all(outgoing.reshape(devices, slots, payload.shape[1]), ('span...  79.6 us
    ppermute x2, waiting for transfers between devices, with_halo(): lax.ppermute(lax.slice_in_dim(block, block.shape[dim] - width, None, axis...  26.3 us
    ppermute x2, waiting for transfers between devices, with_halo(): lax.ppermute(lax.slice_in_dim(block, 0, width, axis=dim), axis, backward)  14.6 us
    transpose x1, local copies, waits for them, and re-layouts, per_device(): jnp.transpose(blocks, (2, 4, 0, 1, 3, 5))  14.5 us
    reshape x2, local copies, waits for them, and re-layouts, per_device(): jnp.transpose(blocks, (2, 4, 0, 1, 3, 5))  9.94 us
    transpose x1, other arithmetic, per_device(): jnp.transpose(blocks, (2, 4, 0, 1, 3, 5))  9.46 us
    dot_general x1, matrix products, span_pass(): jnp.einsum('ctyk,czk->ctyz', extended, matrix, precision=lax.Precision.HI...  9.42 us
    slice x3, local copies, waits for them, and re-layouts, with_halo(): lax.slice_in_dim(block, block.shape[dim] - width, None, axis=dim)  8.45 us
  transfers between devices with their start and end apart: 4, of which 3 were waited for; matrix products, arithmetic and copies ran while one was open for 5% of the time, Pallas kernels for 0%

commit v1 on v0

v1 whole, which is shorter than its diff:
```python
import functools
import math

import jax
import jax.numpy as jnp
from jax import lax
from jax.experimental import pallas as pl
from jax.experimental.pallas import tpu as pltpu
from jax.sharding import PartitionSpec as P

HALO = 24
EDGE = 4
LANES = 128
F32 = jnp.float32
BF16 = jnp.bfloat16
VMEM = pl.BlockSpec(memory_space=pltpu.VMEM)
SMEM = pl.BlockSpec(memory_space=pltpu.SMEM)
ROWS_BY_ROWS = (((1,), (1,)), ((), ()))


def iota(shape, dim):
    return lax.broadcasted_iota(jnp.int32, shape, dim)


def tap_values(scale, distance, valid):
    scale = jnp.full((1, 1), scale, F32)
    k = iota((1, LANES), 1) - HALO
    squares = jnp.where(k <= HALO, jnp.exp(-math.pi * (k * k).astype(F32) / (scale * scale)), 0.0)
    norm = jnp.sqrt(jnp.sum(squares, axis=1, keepdims=True))
    d = distance.astype(F32)
    raw = jnp.exp(-math.pi * (d * d) / (2.0 * scale * scale))
    inside = valid & (distance >= -HALO) & (distance <= HALO)
    return jnp.where(inside, raw, 0.0) / norm


def split(x):
    high = x.astype(BF16)
    return high, (x - high.astype(F32)).astype(BF16)


def taps_kernel(wall_scale, span_scale, wall_ref, span_ref):
    trio, twice, rows = wall_ref.shape
    faces = rows // (EDGE * EDGE)
    cols = span_ref.shape[3] // 2
    i = iota((rows, rows), 0)
    y = (i % faces) * (EDGE * EDGE) + (i // (faces * EDGE)) * EDGE + (i // faces) % EDGE
    k = iota((2 * cols, cols), 0)
    q = k - cols
    side, odd, r = q // (2 * HALO), (q // HALO) % 2, q % HALO
    z = jnp.where(q < 0, k, jnp.where(side == 0, r - HALO, cols + r))
    n = iota((2 * cols, cols), 1)
    target = (n % (cols // EDGE)) * EDGE + n // (cols // EDGE)
    everywhere = i >= 0
    for c in range(trio):
        high, low = split(tap_values(wall_scale[c], iota((rows, rows), 1) - y, everywhere))
        wall_ref[c, :rows] = high
        wall_ref[c, rows:] = low
        for parity in range(2):
            valid = (q < 0) | ((q < 4 * HALO) & (odd == parity))
            high, low = split(tap_values(span_scale[c], z - target, valid))
            span_ref[c, parity] = jnp.concatenate([high, low], axis=1)


def edges_kernel(noise_ref, low_ref, high_ref):
    walls, trio, planes, rows, cols = noise_ref.shape
    wide = 2 * HALO
    row, col = iota((wide, cols), 0), iota((wide, cols), 1)
    pick = jnp.where(col == jnp.where(row < HALO, row, cols - wide + row), 1.0, 0.0).astype(BF16)
    for c in range(trio):
        for pair in range(planes // 2):
            edges = []
            for t in (2 * pair, 2 * pair + 1):
                plane = jnp.concatenate([noise_ref[w, c, t] for w in range(walls)], axis=0)
                edges.append(lax.dot_general(pick, plane, ROWS_BY_ROWS, preferred_element_type=F32))
            at = pl.ds((c * planes // 2 + pair) * wide, wide)
            low_ref[at] = jnp.concatenate([e[:HALO] for e in edges], axis=0).astype(BF16)
            high_ref[at] = jnp.concatenate([e[HALO:] for e in edges], axis=0).astype(BF16)


def swap_blocks(blocks, cols):
    part = cols // EDGE
    lane = iota(blocks[0].shape, 1)
    for step in (2, 1):
        first = (lane // (part * step)) % 2 == 0
        out = list(blocks)
        for a in range(EDGE):
            if a & step:
                continue
            one, two = blocks[a], blocks[a + step]
            out[a] = jnp.where(first, one, pltpu.roll(two, part * step, 1))
            out[a + step] = jnp.where(first, pltpu.roll(one, cols - part * step, 1), two)
        blocks = out
    return blocks


def main_kernel(noise_ref, low_ref, high_ref, wall_ref, span_ref, factor_ref, target_ref, out_ref, cells_ref):
    walls, trio, planes, rows, cols = noise_ref.shape
    full = walls * rows
    faces = full // (EDGE * EDGE)
    tile_faces = faces // walls
    devices, _, slots, _ = out_ref.shape
    values = planes * EDGE * EDGE
    wide = 2 * HALO

    def pair_step(pair, carry):
        psi = [[], []]
        for c in range(trio):
            at = pl.ds(pl.multiple_of((c * planes // 2 + pair) * wide, wide), wide)
            halo = jnp.concatenate(
                [low_ref[at], high_ref[at], jnp.zeros((cols - 2 * wide, full), BF16)], axis=0
            )
            both = jnp.concatenate(
                [
                    jnp.concatenate([noise_ref[w, c, 2 * pair + odd] for w in range(walls)], axis=0)
                    for odd in range(2)
                ],
                axis=1,
            )
            smooth = jnp.dot(wall_ref[c], both, preferred_element_type=F32)
            smooth = smooth[:full] + smooth[full:]
            beside = lax.dot_general(wall_ref[c], halo, ROWS_BY_ROWS, preferred_element_type=F32)
            beside = beside[:full] + beside[full:]
            for odd in range(2):
                high, low = split(
                    jnp.concatenate([smooth[:, odd * cols : (odd + 1) * cols], beside], axis=1)
                )
                matrix = span_ref[c, odd]
                broad = jnp.dot(high, matrix, preferred_element_type=F32)
                small = jnp.dot(low, matrix[:, :cols], preferred_element_type=F32)
                psi[odd].append(broad[:, :cols] + (broad[:, cols:] + small))
        for odd in range(2):
            p = psi[odd]
            velocity = (
                factor_ref[6] + factor_ref[0] * p[0],
                factor_ref[1] * p[0] + factor_ref[2] * p[1],
                factor_ref[3] * p[0] + factor_ref[4] * p[1] + factor_ref[5] * p[2],
            )
            quarter = full // EDGE
            for c in range(trio):
                blocks = [velocity[c][a * quarter : (a + 1) * quarter] for a in range(EDGE)]
                for dz, block in enumerate(swap_blocks(blocks, cols)):
                    for dy in range(EDGE):
                        j = (2 * pair + odd) * EDGE * EDGE + dy * EDGE + dz
                        cells_ref[c, pl.ds(j, faces, stride=values), :] = block[dy * faces : (dy + 1) * faces]
        return carry

    lax.fori_loop(0, planes // 2, pair_step, 0)

    for w in range(walls):
        payload = jnp.concatenate(
            [
                jnp.concatenate(
                    [
                        cells_ref[c, pl.ds((w * tile_faces + f) * values, values), :].astype(BF16)
                        for f in range(tile_faces)
                    ],
                    axis=1,
                )
                for c in range(trio)
            ],
            axis=0,
        )
        target = target_ref[pl.ds(w, 1), :]
        onehot = iota((devices * slots, target.shape[1]), 0) == target
        onehot = jnp.where(onehot, 1.0, 0.0).astype(BF16)
        sent = lax.dot_general(onehot, payload, ROWS_BY_ROWS, preferred_element_type=F32)
        out_ref[:, w] = sent.astype(BF16).reshape(devices, slots, trio * values)


def join_kernel(trio, in_ref, out_ref):
    walls, rows, width = in_ref.shape
    values = width // trio
    for c in range(trio):
        for w in range(walls):
            start = (c * walls + w) * values
            out_ref[0, :, start : start + values] = in_ref[w, :, c * values : (c + 1) * values]


def per_device(noise, wall_scale, span_scale, lund_factor, mean_velocity, owner_map):
    trio, all_planes, rows, cols = noise.shape
    n_span = lax.axis_size("span")
    n_wall = lax.axis_size("wall")
    devices = n_span * n_wall
    planes = all_planes // n_wall
    full = rows * n_wall
    faces = full // (EDGE * EDGE)
    values = planes * EDGE * EDGE
    big = pltpu.CompilerParams(vmem_limit_bytes=56 * 1024 * 1024)

    owners = owner_map.reshape(-1)
    elements = owners.shape[0]
    slots = max(8, 2 * elements // devices)
    same = (owners[:, None] == owners[None, :]) & (
        jnp.arange(elements)[None, :] < jnp.arange(elements)[:, None]
    )
    target = owners * slots + jnp.sum(same.astype(jnp.int32), axis=1)
    small = jnp.concatenate([lund_factor.reshape(-1), mean_velocity, target.astype(F32)])
    small = lax.all_gather(small, "wall")
    target = small[:, 7 * rows :].astype(jnp.int32)
    factor = small[:, : 7 * rows].reshape(n_wall, 7, rows).transpose(1, 0, 2)
    factor = factor.reshape(7, faces, EDGE, EDGE).transpose(0, 2, 3, 1).reshape(7, full)
    factor = jnp.broadcast_to(factor[:, :, None], (7, full, cols))

    wall_taps, span_taps = pl.pallas_call(
        taps_kernel,
        in_specs=[SMEM, SMEM],
        out_specs=[VMEM, VMEM],
        out_shape=[
            jax.ShapeDtypeStruct((trio, 2 * full, full), BF16),
            jax.ShapeDtypeStruct((trio, 2, 2 * cols, 2 * cols), BF16),
        ],
        compiler_params=big,
        name="taps",
    )(wall_scale, span_scale)

    swapped = noise.reshape(trio, n_wall, planes, rows, cols).transpose(1, 0, 2, 3, 4)
    swapped = lax.all_to_all(swapped, "wall", 0, 0, tiled=True)
    edge = jax.ShapeDtypeStruct((trio * planes * HALO, full), BF16)
    first, last = pl.pallas_call(
        edges_kernel,
        in_specs=[VMEM],
        out_specs=[VMEM, VMEM],
        out_shape=[edge, edge],
        compiler_params=big,
        name="edges",
    )(swapped)
    up = [(i, (i + 1) % n_span) for i in range(n_span)]
    low = lax.ppermute(last, "span", up)
    high = lax.ppermute(first, "span", [(b, a) for a, b in up])

    outgoing = pl.pallas_call(
        main_kernel,
        in_specs=[VMEM] * 7,
        out_specs=VMEM,
        out_shape=jax.ShapeDtypeStruct((devices, n_wall, slots, trio * values), BF16),
        scratch_shapes=[pltpu.VMEM((trio, faces * values, cols), F32)],
        compiler_params=big,
        name="filter",
    )(swapped, low, high, wall_taps, span_taps, factor, target)

    received = lax.all_to_all(outgoing, ("span", "wall"), 0, 0, tiled=True)
    return pl.pallas_call(
        functools.partial(join_kernel, trio),
        grid=(n_span,),
        in_specs=[pl.BlockSpec((n_wall, n_wall * slots, trio * values), lambda s: (s, 0, 0))],
        out_specs=pl.BlockSpec((1, n_wall * slots, trio * values * n_wall), lambda s: (0, s, 0)),
        out_shape=jax.ShapeDtypeStruct((1, devices * slots, trio * values * n_wall), BF16),
        compiler_params=big,
        name="join",
    )(received.reshape(devices, n_wall * slots, trio * values))


def solution(mesh):
    return jax.shard_map(
        per_device,
        mesh=mesh,
        in_specs=(
            P(None, None, "wall", "span"),
            P(),
            P(),
            P(None, "wall"),
            P("wall"),
            P("wall", "span", None, None),
        ),
        out_specs=P(("span", "wall"), None, None),
        check_vma=False,
    )
```

time: 214 us -> 150 us (0.70)
  local copies, waits for them, and re-layouts: 56.1 us -> 6.64 us
  Pallas kernels: 0 us -> 24.4 us
  waiting for transfers between devices: 40.9 us -> 17.7 us
  other arithmetic: 13.8 us -> 1.09 us
  matrix products: 12.6 us -> 0 us
  blocking collectives: 79.6 us -> 89.9 us
    ppermute x4 -> x2, waiting for transfers between devices: 40.9 us -> 0.01 us  [the longest x1 0.01 us: per_device(): low = lax.ppermute(last, 'span', up)]
    pallas_call x0 -> x4, Pallas kernels: none -> 24.4 us  [the longest x1 12.8 us: per_device(): pl.pallas_call(main_kernel, in_specs=[VMEM] * 7, out_specs=VMEM, out_shap...]
    all_to_all x0 -> x1, waiting for transfers between devices: none -> 17.7 us  [per_device(): swapped = lax.all_to_all(swapped, 'wall', 0, 0, tiled=True)]
    unnamed x0 -> x1, blocking collectives: none -> 15 us
    transpose x1 -> x2, local copies, waits for them, and re-layouts: 14.5 us -> 0.24 us  [the longest x1 0.23 us: per_device(): factor.reshape(7, faces, EDGE, EDGE).transpose(0, 2, 3, 1).reshape(7, full)]
    dot_general x2 -> x0, matrix products: 12.6 us -> none  [the longest x1 9.42 us: span_pass(): jnp.einsum('ctyk,czk->ctyz', extended, matrix, precision=lax.Precision.HI...]
    slice x5 -> x1, local copies, waits for them, and re-layouts: 11.8 us -> 0.01 us  [per_device(): factor = small[:, :7 * rows].reshape(n_wall, 7, rows).transpose(1, 0, 2)]
    transpose x1 -> x0, other arithmetic: 9.46 us -> none  [per_device(): jnp.transpose(blocks, (2, 4, 0, 1, 3, 5))]
  transfers between devices with their start and end apart: 4 -> 3, of which waited for: 3 -> 1; matrix products, arithmetic and copies ran while one was open for 5% -> 2% of each run, Pallas kernels for 0% -> 2%
where the time goes in v1:
time: 150 us; the launch traced here: 149 us
  blocking collectives  89.9 us (60%)
  Pallas kernels  24.4 us (16%)
  waiting for transfers between devices  17.7 us (12%)
  starting transfers between devices  8.84 us (6%)
  local copies, waits for them, and re-layouts  6.64 us (4%)
    all_to_all x1, blocking collectives, per_device(): received = lax.all_to_all(outgoing, ('span', 'wall'), 0, 0, tiled=True)  74.9 us
    all_to_all x1, waiting for transfers between devices, per_device(): swapped = lax.all_to_all(swapped, 'wall', 0, 0, tiled=True)  17.7 us
    unnamed x1, blocking collectives  15 us
    pallas_call x1, Pallas kernels, per_device(): pl.pallas_call(main_kernel, in_specs=[VMEM] * 7, out_specs=VMEM, out_shap...  12.8 us
    pallas_call x1, Pallas kernels, per_device(): pl.pallas_call(functools.partial(join_kernel, trio), grid=(n_span,), in_s...  6.26 us
    all_to_all x1, starting transfers between devices, per_device(): swapped = lax.all_to_all(swapped, 'wall', 0, 0, tiled=True)  5.29 us
    ppermute x1, starting transfers between devices, per_device(): high = lax.ppermute(first, 'span', [(b, a) for a, b in up])  3.54 us
  transfers between devices with their start and end apart: 3, of which 1 were waited for; matrix products, arithmetic and copies ran while one was open for 2% of the time, Pallas kernels for 2%

profile of v1, /device:TPU:0, one launch (start us, length us, event | category | flops | bytes accessed | tf_op | source)
XLA Modules:
  0.0 149.3 jit_solution(9190118312599477008)
XLA Ops:
  0.0 0.0 copy-start.4
  0.0 0.0 copy-start.6
  0.0 0.0 copy-start.3
  0.0 2.7 %copy.16 = bf16[3,4,8,64,128]{4,3,2,0,1:T(8,128)(2,1)} copy(bf16[3,4,8,64,128]{4,3,2,1,0:T(8,128)(2,1)} %bitcast.10) | data formatting | bytes 3145728 | tf_op jit(solution)/shard_map/reshape | solution.py:216
  2.7 0.0 copy-start.5
  2.7 5.3 %all-to-all-start = ((bf16[4,3,8,64,128]{4,3,2,1,0:T(8,128)(2,1)}), bf16[4,3,8,64,128]{4,3,2,1,0:T(8,128)(2,1)S(1)}, u32[]{:S(2)}, u32[]{:S(2)}) async-start(bf16[4,3,8,64,128]{4,3,2,1,0:T(8,128)(2,1)} %bitcast.8), calls=%async_computation | async-start | bytes 3145728 | tf_op jit(solution)/shard_map/all_to_all | solution.py:217
  8.0 0.0 copy-done.4
  8.0 0.1 reshape.22
  8.1 0.0 copy-done.6
  8.1 0.6 dynamic-slice
  9.3 0.0 copy-done.3
  9.3 0.2 convert_reduce_fusion
  9.6 17.7 %all-to-all-done.noise_ref = bf16[4,3,8,64,128]{4,3,2,1,0:T(8,128)(2,1)S(1)} async-done(((bf16[4,3,8,64,128]{4,3,2,1,0:T(8,128)(2,1)}), bf16[4,3,8,64,128]{4,3,2,1,0:T(8,128)(2,1)S(1)}, u32[]{:S(2)}, u32[]{:S(2)}) %all-to-all-start) | async-done | bytes 1572896 | tf_op jit(solution)/shard_map/all_to_all | solution.py:217
  27.3 0.0 copy-start
  27.3 1.1 copy-done
  28.4 2.9 %edges.1 = (bf16[576,256]{1,0:T(8,128)(2,1)}, bf16[576,256]{1,0:T(8,128)(2,1)}) custom-call(bf16[4,3,8,64,128]{4,3,2,1,0:T(8,128)(2,1)} %copy-done), custom_call_target="tpu_custom_call" | custom-call | tf_op jit(solution)/shard_map/edges/pallas_call | solution.py:219
  31.3 0.0 collective-permute-start
  31.3 3.5 %collective-permute-start.1 = (bf16[576,256]{1,0:T(8,128)(2,1)}, bf16[576,256]{1,0:T(8,128)(2,1)S(1)}, u32[]{:S(2)}, u32[]{:S(2)}) collective-permute-start(bf16[576,256]{1,0:T(8,128)(2,1)} %get-tuple-element.10), channel_id=1, source_target_pairs={{4,0},{8,4},{12,8},{16,12},{20,16},{24,20},{28,24},{0,28},{5,1},{9... | collective-permute-start | bytes 884744 | tf_op jit(solution)/shard_map/ppermute | solution.py:229
  34.8 0.0 copy-done.5
  34.8 0.2 maximum_dynamic-update-slice_fusion
  35.0 15.0 %all-reduce = f32[3840]{0:T(1024)S(1)} all-reduce(f32[3840]{0:T(1024)S(1)} %maximum_dynamic-update-slice_fusion), channel_id=2, replica_groups=mesh['span'=8,'wall'=4] {'wall'}, use_global_device_ids=true, to_apply=%add | all-reduce | flops 3840 | bytes 30720
  50.0 0.1 reshape.27
  50.1 0.1 reshape.24
  50.2 0.3 reshape.25
  50.5 0.2 copy.14
  50.7 0.1 broadcast_in_dim.4
  50.8 2.5 %taps.1 = (bf16[3,512,256]{2,1,0:T(8,128)(2,1)}, bf16[3,2,256,256]{3,2,1,0:T(8,128)(2,1)}) custom-call(f32[3]{0:T(128)} %wall_scale.1, f32[3]{0:T(128)} %span_scale.1), custom_call_target="tpu_custom_call" | custom-call | tf_op jit(solution)/shard_map/taps/pallas_call | solution.py:204
  53.4 0.7 slice_convert_fusion.target_ref
  54.1 0.0 collective-permute-done.low_ref
  54.1 0.0 copy-start.1
  54.1 0.0 collective-permute-done.1.high_ref
  54.1 0.0 copy-start.2
  54.1 1.2 broadcast_in_dim.10.factor_ref
  55.3 0.0 copy-done.1
  55.3 0.0 copy-done.2
  55.3 12.8 %filter.1 = bf16[32,4,32,384]{3,2,1,0:T(8,128)(2,1)} custom-call(bf16[4,3,8,64,128]{4,3,2,1,0:T(8,128)(2,1)} %copy-done, bf16[576,256]{1,0:T(8,128)(2,1)} %copy-done.1, bf16[576,256]{1,0:T(8,128)(2,1)} %copy-done.2, bf16[3,512,256]{2,1,0:T(8,128)(2,1)} %get-tuple-element.11.wall_ref, bf16[3,2,256,256]{3,2,1,0:T(8,128)(2,1)} %get-tuple-element.12.span_ref, ...), custom_call_target="tpu_custom_call" | custom-call | tf_op jit(solution)/shard_map/filter/pallas_call | solution.py:231
  68.1 74.9 %all_to_all.10 = bf16[32,4,32,384]{3,2,1,0:T(8,128)(2,1)} all-to-all(bf16[32,4,32,384]{3,2,1,0:T(8,128)(2,1)} %filter.1), channel_id=1, replica_groups=mesh['span'=8,'wall'=4] {'span','wall'}, dimensions={0} | all-to-all | bytes 6291456 | tf_op jit(solution)/shard_map/all_to_all | solution.py:241
  143.0 6.3 %join.1 = bf16[1,1024,1536]{2,1,0:T(8,128)(2,1)} custom-call(bf16[32,128,384]{2,1,0:T(8,128)(2,1)} %bitcast.9), custom_call_target="tpu_custom_call" | custom-call | tf_op jit(solution)/shard_map/join/pallas_call | solution.py:242
  (4 shorter events, 0.0 us)
Async XLA Ops:
  0.0 8.0 %copy-start.4 = (f32[6,64]{1,0:T(8,128)S(1)}, f32[6,64]{1,0:T(8,128)}, u32[]{:S(2)}) copy-start(f32[6,64]{1,0:T(8,128)} %param.9) | copy-start | bytes 4612
  0.0 8.1 %copy-start.6 = (u32[32]{0:T(128)S(1)}, u32[32]{0:T(128)}, u32[]{:S(2)}) copy-start(u32[32]{0:T(128)} %constant.7) | copy-start | bytes 388
  0.0 9.3 %copy-start.3 = (s32[1,1,512,1]{2,3,1,0:T(1,128)S(1)}, s32[1,1,512,1]{2,3,1,0:T(1,128)}, u32[]{:S(2)}) copy-start(s32[1,1,512,1]{2,3,1,0:T(1,128)} %param.11) | copy-start | bytes 6148
  2.7 32.1 %copy-start.5 = (f32[64]{0:T(128)S(1)}, f32[64]{0:T(128)}, u32[]{:S(2)}) copy-start(f32[64]{0:T(128)} %param.10) | copy-start | bytes 772
  2.7 24.5 %all-to-all-start = ((bf16[4,3,8,64,128]{4,3,2,1,0:T(8,128)(2,1)}), bf16[4,3,8,64,128]{4,3,2,1,0:T(8,128)(2,1)S(1)}, u32[]{:S(2)}, u32[]{:S(2)}) async-start(bf16[4,3,8,64,128]{4,3,2,1,0:T(8,128)(2,1)} %bitcast.8), calls=%async_computation | async-start | bytes 3145728 | tf_op jit(solution)/shard_map/all_to_all | solution.py:217
  27.3 1.1 copy-start
  31.3 22.8 %collective-permute-start = (bf16[576,256]{1,0:T(8,128)(2,1)}, bf16[576,256]{1,0:T(8,128)(2,1)S(1)}, u32[]{:S(2)}, u32[]{:S(2)}) collective-permute-start(bf16[576,256]{1,0:T(8,128)(2,1)} %get-tuple-element.9), channel_id=1, source_target_pairs={{0,4},{4,8},{8,12},{12,16},{16,20},{20,24},{24,28},{28,0},{1,5},{5... | collective-permute-start | bytes 884744 | tf_op jit(solution)/shard_map/ppermute | solution.py:228
  31.3 22.8 %collective-permute-start.1 = (bf16[576,256]{1,0:T(8,128)(2,1)}, bf16[576,256]{1,0:T(8,128)(2,1)S(1)}, u32[]{:S(2)}, u32[]{:S(2)}) collective-permute-start(bf16[576,256]{1,0:T(8,128)(2,1)} %get-tuple-element.10), channel_id=1, source_target_pairs={{4,0},{8,4},{12,8},{16,12},{20,16},{24,20},{28,24},{0,28},{5,1},{9... | collective-permute-start | bytes 884744 | tf_op jit(solution)/shard_map/ppermute | solution.py:229
  54.1 1.2 copy-start.1
  54.1 1.2 copy-start.2

commit v2 on v1

v2 whole, which is shorter than its diff:
```python
import functools
import math

import jax
import jax.numpy as jnp
from jax import lax
from jax.experimental import pallas as pl
from jax.experimental.pallas import tpu as pltpu
from jax.sharding import PartitionSpec as P

HALO = 24
EDGE = 4
LANES = 128
FACTORS = 7
F32 = jnp.float32
BF16 = jnp.bfloat16
VMEM = pl.BlockSpec(memory_space=pltpu.VMEM)
SMEM = pl.BlockSpec(memory_space=pltpu.SMEM)
ROWS_BY_ROWS = (((1,), (1,)), ((), ()))
LIMIT = pltpu.CompilerParams(vmem_limit_bytes=40 * 1024 * 1024)


def iota(shape, dim):
    return lax.broadcasted_iota(jnp.int32, shape, dim)


def split(x):
    high = x.astype(BF16)
    return high, (x - high.astype(F32)).astype(BF16)


def tap_values(scale, distance, valid):
    scale = jnp.full((1, 1), scale, F32)
    k = iota((1, LANES), 1) - HALO
    squares = jnp.where(k <= HALO, jnp.exp(-math.pi * (k * k).astype(F32) / (scale * scale)), 0.0)
    norm = jnp.sqrt(jnp.sum(squares, axis=1, keepdims=True))
    d = distance.astype(F32)
    raw = jnp.exp(-math.pi * (d * d) / (2.0 * scale * scale))
    inside = valid & (distance >= -HALO) & (distance <= HALO)
    return jnp.where(inside, raw, 0.0) / norm


def cell_row(i, faces):
    return (i % faces) * (EDGE * EDGE) + (i // (faces * EDGE)) * EDGE + (i // faces) % EDGE


def taps_kernel(wall_scale, span_scale, wall_first, wall_rest, span_first, span_rest):
    full = wall_first.shape[2]
    cols = span_first.shape[3] // 2
    i = iota((full, full), 0)
    y = cell_row(i, full // (EDGE * EDGE))
    k = iota((2 * cols, cols), 0)
    q = k - cols
    side, odd, r = q // (2 * HALO), (q // HALO) % 2, q % HALO
    z = jnp.where(q < 0, k, jnp.where(side == 0, r - HALO, cols + r))
    n = iota((2 * cols, cols), 1)
    target = (n % (cols // EDGE)) * EDGE + n // (cols // EDGE)
    for c in range(wall_first.shape[0] + wall_rest.shape[0]):
        wall_ref, span_ref, at = (wall_first, span_first, 0) if c == 0 else (wall_rest, span_rest, c - 1)
        high, low = split(tap_values(wall_scale[c], iota((full, full), 1) - y, i >= 0))
        wall_ref[at, :full] = high
        wall_ref[at, full:] = low
        for parity in range(2):
            valid = (q < 0) | ((q < 4 * HALO) & (odd == parity))
            high, low = split(tap_values(span_scale[c], z - target, valid))
            span_ref[at, parity] = jnp.concatenate([high, low], axis=1)


def pack_kernel(devices, noise_ref, lund_ref, mean_ref, owner_ref, out_ref):
    walls, height, cols = out_ref.shape
    planes = noise_ref.shape[1] // walls
    rows = noise_ref.shape[2]
    for w in range(walls):
        for t in range(planes):
            out_ref[w, t * rows : (t + 1) * rows] = noise_ref[0, w * planes + t]
    owner = owner_ref[...]
    elements = owner.shape[1]
    mine = jnp.where(iota((devices, elements), 0) == owner, 1.0, 0.0)
    before = jnp.where(iota((elements, elements), 0) < iota((elements, elements), 1), 1.0, 0.0)
    count = jnp.dot(mine.astype(BF16), before.astype(BF16), preferred_element_type=F32)
    rank = jnp.sum(mine * count, axis=0, keepdims=True)
    pieces = [owner.astype(F32), rank]
    pieces = [p[:, at : at + cols] for p in pieces for at in range(0, elements, cols)]
    factor = jnp.concatenate([lund_ref[...], mean_ref[...]], axis=0)
    factor = jnp.concatenate([factor, jnp.zeros((FACTORS, cols - rows), F32)], axis=1)
    for _ in range(3):
        part = factor.astype(BF16).astype(F32)
        pieces.append(part)
        factor = factor - part
    tail = height - planes * rows
    pieces.append(jnp.zeros((tail - sum(p.shape[0] for p in pieces), cols), F32))
    small = jnp.concatenate(pieces, axis=0).astype(BF16)
    for w in range(walls):
        out_ref[w, planes * rows :] = small


def small_kernel(slots, in_ref, factor_ref, target_ref):
    walls, tail, cols = in_ref.shape
    full = factor_ref.shape[1]
    rows = full // walls
    count = target_ref.shape[1]
    columns = jnp.zeros((full, tail), F32)
    y = cell_row(iota((full, cols), 0), full // (EDGE * EDGE))
    for w in range(walls):
        small = in_ref[w]
        pick = jnp.where(y == iota((full, cols), 1) + w * rows, 1.0, 0.0)
        pick = jnp.where(iota((full, cols), 1) < rows, pick, 0.0).astype(BF16)
        columns = columns + lax.dot_general(pick, small, ROWS_BY_ROWS, preferred_element_type=F32)
        numbers = small.astype(F32)
        target = numbers[:count] * slots + numbers[count : 2 * count]
        target_ref[w] = target.astype(jnp.int32)
    for f in range(FACTORS):
        at = 2 * count + f
        total = sum(columns[:, at + p * FACTORS : at + p * FACTORS + 1] for p in range(3))
        factor_ref[f] = jnp.broadcast_to(total, (full, cols))


def plane_of(noise_ref, c, t, rows):
    walls = noise_ref.shape[0]
    return jnp.concatenate(
        [noise_ref[w, c, t * rows : (t + 1) * rows] for w in range(walls)], axis=0
    )


def edges_kernel(planes, noise_ref, low_ref, high_ref):
    walls, some, _, cols = noise_ref.shape
    rows = low_ref.shape[1] // walls
    wide = 2 * HALO
    row, col = iota((wide, cols), 0), iota((wide, cols), 1)
    pick = jnp.where(col == jnp.where(row < HALO, row, cols - wide + row), 1.0, 0.0).astype(BF16)
    for c in range(some):
        for pair in range(planes // 2):
            edges = [
                lax.dot_general(
                    pick, plane_of(noise_ref, c, t, rows), ROWS_BY_ROWS, preferred_element_type=F32
                )
                for t in (2 * pair, 2 * pair + 1)
            ]
            at = pl.ds((c * planes // 2 + pair) * wide, wide)
            low_ref[at] = jnp.concatenate([e[:HALO] for e in edges], axis=0).astype(BF16)
            high_ref[at] = jnp.concatenate([e[HALO:] for e in edges], axis=0).astype(BF16)


def swap_blocks(blocks, cols):
    part = cols // EDGE
    lane = iota(blocks[0].shape, 1)
    for step in (2, 1):
        first = (lane // (part * step)) % 2 == 0
        out = list(blocks)
        for a in range(EDGE):
            if a & step:
                continue
            one, two = blocks[a], blocks[a + step]
            out[a] = jnp.where(first, one, pltpu.roll(two, part * step, 1))
            out[a + step] = jnp.where(first, pltpu.roll(one, cols - part * step, 1), two)
        blocks = out
    return blocks


def filter_kernel(first, planes, noise_ref, low_ref, high_ref, wall_ref, span_ref, factor_ref, target_ref, *rest):
    if first:
        out_ref, psi_ref, cells_ref = rest
    else:
        psi_ref, out_ref, cells_ref = rest
    walls, some, _, cols = noise_ref.shape
    full = wall_ref.shape[2]
    rows = full // walls
    faces = full // (EDGE * EDGE)
    tile_faces = faces // walls
    devices, _, slots, _ = out_ref.shape
    values = planes * EDGE * EDGE
    wide = 2 * HALO

    def pair_step(pair, carry):
        psi = [[], []]
        for c in range(some):
            at = pl.ds(pl.multiple_of((c * planes // 2 + pair) * wide, wide), wide)
            halo = jnp.concatenate(
                [low_ref[at], high_ref[at], jnp.zeros((cols - 2 * wide, full), BF16)], axis=0
            )
            both = []
            for odd in range(2):
                at = pl.ds(pl.multiple_of((2 * pair + odd) * rows, rows), rows)
                both.append(jnp.concatenate([noise_ref[w, c, at] for w in range(walls)], axis=0))
            both = jnp.concatenate(both, axis=1)
            smooth = jnp.dot(wall_ref[c], both, preferred_element_type=F32)
            smooth = smooth[:full] + smooth[full:]
            beside = lax.dot_general(wall_ref[c], halo, ROWS_BY_ROWS, preferred_element_type=F32)
            beside = beside[:full] + beside[full:]
            for odd in range(2):
                high, low = split(
                    jnp.concatenate([smooth[:, odd * cols : (odd + 1) * cols], beside], axis=1)
                )
                matrix = span_ref[c, odd]
                broad = jnp.dot(high, matrix, preferred_element_type=F32)
                small = jnp.dot(low, matrix[:, :cols], preferred_element_type=F32)
                psi[odd].append(broad[:, :cols] + (broad[:, cols:] + small))
        for odd in range(2):
            t = 2 * pair + odd
            if first:
                p = psi[odd][0]
                psi_ref[t] = p
                velocity = (factor_ref[6] + factor_ref[0] * p,)
            else:
                p, q, r = psi_ref[t], *psi[odd]
                velocity = (
                    factor_ref[1] * p + factor_ref[2] * q,
                    factor_ref[3] * p + factor_ref[4] * q + factor_ref[5] * r,
                )
            quarter = full // EDGE
            for c in range(some):
                blocks = [velocity[c][a * quarter : (a + 1) * quarter] for a in range(EDGE)]
                for dz, block in enumerate(swap_blocks(blocks, cols)):
                    for dy in range(EDGE):
                        j = t * EDGE * EDGE + dy * EDGE + dz
                        cells_ref[c, pl.ds(j, faces, stride=values), :] = block[dy * faces : (dy + 1) * faces]
        return carry

    lax.fori_loop(0, planes // 2, pair_step, 0)

    for w in range(walls):
        payload = [
            [
                cells_ref[c, pl.ds((w * tile_faces + f) * values, values), :].astype(BF16)
                for f in range(tile_faces)
            ]
            for c in range(some)
        ]
        payload = jnp.concatenate([jnp.concatenate(p, axis=1) for p in payload], axis=0)
        slot = iota((devices * slots, cols), 0)
        onehot = [
            jnp.where(slot == target_ref[w, f : f + 1], 1.0, 0.0).astype(BF16)
            for f in range(tile_faces)
        ]
        onehot = jnp.concatenate(onehot, axis=1)
        sent = lax.dot_general(onehot, payload, ROWS_BY_ROWS, preferred_element_type=F32)
        out_ref[:, w] = sent.astype(BF16).reshape(devices, slots, some * values)


def join_kernel(some, in_ref, *rest):
    out_ref = rest[-1]
    walls, _, width = in_ref.shape
    values = width // some
    for c in range(some):

        @pl.when(pl.program_id(1) == c)
        def _():
            for w in range(walls):
                out_ref[0, :, w * values : (w + 1) * values] = in_ref[w, :, c * values : (c + 1) * values]


def per_device(noise, wall_scale, span_scale, lund_factor, mean_velocity, owner_map):
    trio, all_planes, rows, cols = noise.shape
    n_span = lax.axis_size("span")
    n_wall = lax.axis_size("wall")
    devices = n_span * n_wall
    planes = all_planes // n_wall
    full = rows * n_wall
    faces = full // (EDGE * EDGE)
    values = planes * EDGE * EDGE
    owners = owner_map.reshape(1, -1)
    elements = owners.shape[1]
    slots = max(8, 2 * elements // devices)
    count = elements // cols
    tail = -(-(2 * count + 3 * FACTORS) // 16) * 16
    rest = trio - 1
    struct = jax.ShapeDtypeStruct

    def call(kernel, n_in, outs, name, scratch=(), grid=()):
        specs = [VMEM] * len(outs)
        return pl.pallas_call(
            kernel,
            grid=grid,
            in_specs=n_in if isinstance(n_in, list) else [VMEM] * n_in,
            out_specs=specs if len(outs) > 1 else specs[0],
            out_shape=outs if len(outs) > 1 else outs[0],
            scratch_shapes=scratch,
            compiler_params=LIMIT,
            name=name,
        )

    packed = call(
        functools.partial(pack_kernel, devices),
        [pl.BlockSpec((1, all_planes, rows, cols), lambda i: (0, 0, 0, 0)), VMEM, VMEM, VMEM],
        [struct((n_wall, planes * rows + tail, cols), BF16)],
        "pack",
        grid=(1,),
    )(noise, lund_factor, mean_velocity.reshape(1, rows), owners)
    packed = lax.all_to_all(packed, "wall", 0, 0, tiled=True)
    others = noise[1:].reshape(rest, n_wall, planes * rows, cols).transpose(1, 0, 2, 3)
    others = lax.all_to_all(others, "wall", 0, 0, tiled=True)

    wall_first, wall_rest, span_first, span_rest = call(
        taps_kernel,
        [SMEM, SMEM],
        [
            struct((1, 2 * full, full), BF16),
            struct((rest, 2 * full, full), BF16),
            struct((1, 2, 2 * cols, 2 * cols), BF16),
            struct((rest, 2, 2 * cols, 2 * cols), BF16),
        ],
        "taps",
    )(wall_scale, span_scale)
    factor, target = call(
        functools.partial(small_kernel, slots),
        1,
        [struct((FACTORS, full, cols), F32), struct((n_wall, count, cols), jnp.int32)],
        "small",
    )(packed[:, planes * rows :])

    up = [(i, (i + 1) % n_span) for i in range(n_span)]
    down = [(b, a) for a, b in up]

    def beside(swapped, some, name):
        edge = struct((some * planes * HALO, full), BF16)
        first, last = call(functools.partial(edges_kernel, planes), 1, [edge, edge], name)(swapped)
        return lax.ppermute(last, "span", up), lax.ppermute(first, "span", down)

    def send(x):
        return lax.all_to_all(x, ("span", "wall"), 0, 0, tiled=True).reshape(devices, n_wall * slots, -1)

    def out(some):
        return struct((devices, n_wall, slots, some * values), BF16)

    def cells(some):
        return [pltpu.VMEM((some, faces * values, cols), F32)]

    packed = packed[:, None]
    low, high = beside(packed, 1, "edges_first")
    sent, psi = call(
        functools.partial(filter_kernel, True, planes),
        7,
        [out(1), struct((planes, full, cols), F32)],
        "filter_first",
        cells(1),
    )(packed, low, high, wall_first, span_first, factor, target)
    got_first = send(sent)
    low, high = beside(others, rest, "edges_rest")
    sent = call(
        functools.partial(filter_kernel, False, planes), 8, [out(rest)], "filter_rest", cells(rest)
    )(others, low, high, wall_rest, span_rest, factor, target, psi)
    got_rest = send(sent)

    whole = struct((1, devices * slots, trio * values * n_wall), BF16)
    block = (1, n_wall * slots, values * n_wall)
    def join(received, some, before):
        keep = [] if before is None else [before]
        return pl.pallas_call(
            functools.partial(join_kernel, some),
            grid=(n_span, some),
            in_specs=[pl.BlockSpec((n_wall, n_wall * slots, some * values), lambda s, c: (s, 0, 0))]
            + [pl.BlockSpec(memory_space=pl.ANY)] * len(keep),
            out_specs=pl.BlockSpec(block, lambda s, c: (0, s, c + len(keep))),
            out_shape=whole,
            input_output_aliases={1: 0} if keep else {},
            compiler_params=LIMIT,
            name="join",
        )(received, *keep)

    return join(got_rest, rest, join(got_first, 1, None))


def solution(mesh):
    return jax.shard_map(
        per_device,
        mesh=mesh,
        in_specs=(
            P(None, None, "wall", "span"),
            P(),
            P(),
            P(None, "wall"),
            P("wall"),
            P("wall", "span", None, None),
        ),
        out_specs=P(("span", "wall"), None, None),
        check_vma=False,
    )
```

time: 150 us -> 140 us (0.933)
  blocking collectives: 89.9 us -> 0 us
  waiting for transfers between devices: 17.7 us -> 74.5 us
  starting transfers between devices: 8.84 us -> 28.8 us
  local copies, waits for them, and re-layouts: 6.64 us -> 12.2 us
    all_to_all x1 -> x0, blocking collectives: 74.9 us -> none  [per_device(): received = lax.all_to_all(outgoing, ('span', 'wall'), 0, 0, tiled=True)]
    all_to_all x1 -> x4, waiting for transfers between devices: 17.7 us -> 53.2 us  [the longest x2 45.9 us: send(): lax.all_to_all(x, ('span', 'wall'), 0, 0, tiled=True)]
    ppermute x2 -> x4, waiting for transfers between devices: 0.01 us -> 21.2 us  [beside(): return (lax.ppermute(last, 'span', up), lax.ppermute(first, 'span', down))]
    all_to_all x1 -> x4, starting transfers between devices: 5.29 us -> 21.6 us  [the longest x2 12.8 us: send(): lax.all_to_all(x, ('span', 'wall'), 0, 0, tiled=True)]
    unnamed x1 -> x0, blocking collectives: 15 us -> none
    unnamed x16 -> x30, local copies, waits for them, and re-layouts: 1.79 us -> 11.2 us
    ppermute x2 -> x4, starting transfers between devices: 3.54 us -> 7.18 us  [beside(): return (lax.ppermute(last, 'span', up), lax.ppermute(first, 'span', down))]
    reshape x4 -> x0, local copies, waits for them, and re-layouts: 3.17 us -> none  [the longest x1 2.71 us: per_device(): noise.reshape(trio, n_wall, planes, rows, cols).transpose(1, 0, 2, 3, 4)]
  transfers between devices with their start and end apart: 3 -> 8, of which waited for: 1 -> 3; matrix products, arithmetic and copies ran while one was open for 2% -> 1% of each run, Pallas kernels for 2% -> 12%
where the time goes in v2:
time: 140 us; the launch traced here: 139 us
  waiting for transfers between devices  74.5 us (53%)
  starting transfers between devices  28.8 us (21%)
  Pallas kernels  23.5 us (17%)
  local copies, waits for them, and re-layouts  12.2 us (9%)
    all_to_all x2, waiting for transfers between devices, send(): lax.all_to_all(x, ('span', 'wall'), 0, 0, tiled=True)  45.9 us
    ppermute x4, waiting for transfers between devices, beside(): return (lax.ppermute(last, 'span', up), lax.ppermute(first, 'span', down))  21.2 us
    all_to_all x2, starting transfers between devices, send(): lax.all_to_all(x, ('span', 'wall'), 0, 0, tiled=True)  12.8 us
    unnamed x30, local copies, waits for them, and re-layouts  11.2 us
    pallas_call x2, Pallas kernels, join(): pl.pallas_call(functools.partial(join_kernel, some), grid=(n_span, some),...  8.27 us
    all_to_all x1, waiting for transfers between devices, per_device(): packed = lax.all_to_all(packed, 'wall', 0, 0, tiled=True)  7.31 us
    pallas_call x1, Pallas kernels, per_device(): call(functools.partial(filter_kernel, False, planes), 8, [out(rest)], 'fi...  7.3 us
    ppermute x4, starting transfers between devices, beside(): return (lax.ppermute(last, 'span', up), lax.ppermute(first, 'span', down))  7.18 us
  transfers between devices with their start and end apart: 8, of which 3 were waited for; matrix products, arithmetic and copies ran while one was open for 1% of the time, Pallas kernels for 12%

profile of v2, /device:TPU:0, one launch (start us, length us, event | category | flops | bytes accessed | tf_op | source)
XLA Modules:
  0.0 139.1 jit_solution(17864757957609854484)
XLA Ops:
  0.0 0.0 copy-start
  0.0 1.4 %copy-done = bf16[3,32,64,128]{3,2,1,0:T(8,128)(2,1)S(1)} copy-done((bf16[3,32,64,128]{3,2,1,0:T(8,128)(2,1)S(1)}, bf16[3,32,64,128]{3,2,1,0:T(8,128)(2,1)}, u32[]{:S(2)}) %copy-start) | copy-done | bytes 1572888
  1.4 0.0 copy-start.10
  1.4 0.7 copy-done.10
  2.1 0.0 copy-start.11
  2.1 0.7 copy-done.11
  2.8 0.0 copy-start.12
  2.8 0.7 copy-done.12
  3.4 1.0 pack.1
  4.4 5.3 %all-to-all-start.1 = ((bf16[4,544,128]{2,1,0:T(8,128)(2,1)}), bf16[4,544,128]{2,1,0:T(8,128)(2,1)S(1)}, u32[]{:S(2)}, u32[]{:S(2)}) async-start(bf16[4,544,128]{2,1,0:T(8,128)(2,1)} %pack.1), calls=%async_computation.1 | async-start | bytes 1114112 | tf_op jit(solution)/shard_map/all_to_all | solution.py:289
  9.7 0.0 slice-done
  9.7 1.0 copy_bitcast_fusion
  10.8 7.3 %all-to-all-done.1 = bf16[4,544,128]{2,1,0:T(8,128)(2,1)S(1)} async-done(((bf16[4,544,128]{2,1,0:T(8,128)(2,1)}), bf16[4,544,128]{2,1,0:T(8,128)(2,1)S(1)}, u32[]{:S(2)}, u32[]{:S(2)}) %all-to-all-start.1) | async-done | bytes 557088 | tf_op jit(solution)/shard_map/all_to_all | solution.py:289
  18.1 3.5 %all-to-all-start = ((bf16[4,2,512,128]{3,2,1,0:T(8,128)(2,1)}), bf16[4,2,512,128]{3,2,1,0:T(8,128)(2,1)S(1)}, u32[]{:S(2)}, u32[]{:S(2)}) async-start(bf16[4,2,512,128]{3,2,1,0:T(8,128)(2,1)} %copy_bitcast_fusion), calls=%async_computation | async-start | bytes 2097152 | tf_op jit(solution)/shard_map/all_to_all | solution.py:291
  21.6 0.3 edges_first.1
  21.9 0.1 collective-permute-start.2
  22.0 3.5 %collective-permute-start.3 = (bf16[192,256]{1,0:T(8,128)(2,1)S(1)}, bf16[192,256]{1,0:T(8,128)(2,1)S(1)}, u32[]{:S(2)}, u32[]{:S(2)}) collective-permute-start(bf16[192,256]{1,0:T(8,128)(2,1)S(1)} %get-tuple-element.24), channel_id=1, source_target_pairs={{4,0},{8,4},{12,8},{16,12},{20,16},{24,20},{28,24},{0,28},{5,1},{9... | collective-permute-start | bytes 294920 | tf_op jit(solution)/shard_map/ppermute | solution.py:317
  25.5 0.0 copy-done.13
  25.5 0.0 copy-done.14
  25.5 1.3 taps.1
  26.9 0.0 copy-start.6
  26.9 0.8 copy-done.6
  27.7 0.8 copy-done.8
  28.5 0.6 small.1
  29.1 0.0 collective-permute-done.2.low_ref
  29.1 0.0 collective-permute-done.3.high_ref
  29.1 4.2 %filter_first.1 = (bf16[32,4,32,128]{3,2,1,0:T(8,128)(2,1)S(1)}, f32[8,256,128]{2,1,0:T(8,128)S(1)}) custom-call(bf16[4,1,544,128]{3,2,1,0:T(8,128)(2,1)S(1)} %bitcast.14, bf16[192,256]{1,0:T(8,128)(2,1)S(1)} %collective-permute-done.2.low_ref, bf16[192,256]{1,0:T(8,128)(2,1)S(1)} %collective-permute-done.3.high_ref, ...), custom_call_target="tpu_custom_call" | custom-call | tf_op jit(solution)/shard_map/filter_first/pallas_call | solution.py:330
  33.3 0.0 copy-start.1
  33.3 0.9 copy-done.1
  34.3 1.0 copy-done.3
  35.2 1.0 copy-done.5
  36.2 0.0 all-to-all-done.noise_ref
  36.2 4.9 %all-to-all-start.3 = ((bf16[32,4,32,128]{3,2,1,0:T(8,128)(2,1)}), bf16[32,4,32,128]{3,2,1,0:T(8,128)(2,1)S(1)}, u32[]{:S(2)}, u32[]{:S(2)}) async-start(bf16[32,4,32,128]{3,2,1,0:T(8,128)(2,1)} %copy-done.5), calls=%async_computation.3 | async-start | bytes 2097152 | tf_op jit(solution)/shard_map/all_to_all | solution.py:320
  41.2 0.5 edges_rest.1
  41.6 0.3 collective-permute-start
  41.9 3.3 %collective-permute-start.1 = (bf16[384,256]{1,0:T(8,128)(2,1)S(1)}, bf16[384,256]{1,0:T(8,128)(2,1)S(1)}, u32[]{:S(2)}, u32[]{:S(2)}) collective-permute-start(bf16[384,256]{1,0:T(8,128)(2,1)S(1)} %get-tuple-element.18), channel_id=1, source_target_pairs={{4,0},{8,4},{12,8},{16,12},{20,16},{24,20},{28,24},{0,28},{5,1},{9... | collective-permute-start | bytes 589832 | tf_op jit(solution)/shard_map/ppermute | solution.py:317
  45.2 21.2 %collective-permute-done.low_ref = bf16[384,256]{1,0:T(8,128)(2,1)S(1)} collective-permute-done((bf16[384,256]{1,0:T(8,128)(2,1)S(1)}, bf16[384,256]{1,0:T(8,128)(2,1)S(1)}, u32[]{:S(2)}, u32[]{:S(2)}) %collective-permute-start) | collective-permute-done | bytes 196640 | tf_op jit(solution)/shard_map/ppermute | solution.py:317
  66.5 0.0 collective-permute-done.1.high_ref
  66.5 0.0 copy-done.2
  66.5 1.2 copy-done.4
  67.7 1.0 copy-done.7
  68.7 1.0 copy-done.9
  69.8 7.3 %filter_rest.1 = bf16[32,4,32,256]{3,2,1,0:T(8,128)(2,1)} custom-call(bf16[4,2,512,128]{3,2,1,0:T(8,128)(2,1)S(1)} %all-to-all-done.noise_ref, bf16[384,256]{1,0:T(8,128)(2,1)S(1)} %collective-permute-done.low_ref, bf16[384,256]{1,0:T(8,128)(2,1)S(1)} %collective-permute-done.1.high_ref, bf16[2,512,256]{2,1,0:T(8,128)(2,1)S(1)} %copy-done.7, ...), custom_call_target="tpu_custom_call" | custom-call | tf_op jit(solution)/shard_map/filter_rest/pallas_call | solution.py:339
  77.1 0.0 all-to-all-done.3
  77.1 7.9 %all-to-all-start.2 = ((bf16[32,4,32,256]{3,2,1,0:T(8,128)(2,1)}), bf16[32,4,32,256]{3,2,1,0:T(8,128)(2,1)S(1)}, u32[]{:S(2)}, u32[]{:S(2)}) async-start(bf16[32,4,32,256]{3,2,1,0:T(8,128)(2,1)} %filter_rest.1), calls=%async_computation.2 | async-start | bytes 4194304 | tf_op jit(solution)/shard_map/all_to_all | solution.py:320
  85.0 2.8 %join.2.rest_0_ = bf16[1,1024,1536]{2,1,0:T(8,128)(2,1)} custom-call(bf16[32,128,128]{2,1,0:T(8,128)(2,1)S(1)} %bitcast.16), custom_call_target="tpu_custom_call" | custom-call | tf_op jit(solution)/shard_map/join/pallas_call | solution.py:348
  87.7 45.9 %all-to-all-done.2 = bf16[32,4,32,256]{3,2,1,0:T(8,128)(2,1)S(1)} async-done(((bf16[32,4,32,256]{3,2,1,0:T(8,128)(2,1)}), bf16[32,4,32,256]{3,2,1,0:T(8,128)(2,1)S(1)}, u32[]{:S(2)}, u32[]{:S(2)}) %all-to-all-start.2) | async-done | bytes 2097184 | tf_op jit(solution)/shard_map/all_to_all | solution.py:320
  133.7 5.5 %join.3 = bf16[1,1024,1536]{2,1,0:T(8,128)(2,1)} custom-call(bf16[32,128,256]{2,1,0:T(8,128)(2,1)S(1)} %bitcast.12, bf16[1,1024,1536]{2,1,0:T(8,128)(2,1)} %join.2.rest_0_), custom_call_target="tpu_custom_call", output_to_operand_aliasing={{}: (1, {})} | custom-call | tf_op jit(solution)/shard_map/join/pallas_call | solution.py:348
  (11 shorter events, 0.0 us)
Async XLA Ops:
  0.0 1.4 %copy-start = (bf16[3,32,64,128]{3,2,1,0:T(8,128)(2,1)S(1)}, bf16[3,32,64,128]{3,2,1,0:T(8,128)(2,1)}, u32[]{:S(2)}) copy-start(bf16[3,32,64,128]{3,2,1,0:T(8,128)(2,1)} %noise_ref.1) | copy-start | bytes 4718596
  1.4 0.7 copy-start.10
  2.1 0.7 copy-start.11
  2.8 0.7 copy-start.12
  4.4 5.3 %slice-start = ((bf16[3,32,64,128]{3,2,1,0:T(8,128)(2,1)}), bf16[2,32,64,128]{3,2,1,0:T(8,128)(2,1)S(1)}, s32[]{:S(2)}) async-start(bf16[3,32,64,128]{3,2,1,0:T(8,128)(2,1)} %noise_ref.1), calls=%async_computation.4 | async-start | bytes 2097152 | tf_op jit(solution)/shard_map/slice | solution.py:290
  4.4 13.7 %all-to-all-start.1 = ((bf16[4,544,128]{2,1,0:T(8,128)(2,1)}), bf16[4,544,128]{2,1,0:T(8,128)(2,1)S(1)}, u32[]{:S(2)}, u32[]{:S(2)}) async-start(bf16[4,544,128]{2,1,0:T(8,128)(2,1)} %pack.1), calls=%async_computation.1 | async-start | bytes 1114112 | tf_op jit(solution)/shard_map/all_to_all | solution.py:289
  9.7 15.8 %copy-start.13 = (f32[3]{0:T(128)S(1)}, f32[3]{0:T(128)}, u32[]{:S(2)}) copy-start(f32[3]{0:T(128)} %wall_scale.1) | copy-start | bytes 40
  9.7 15.8 %copy-start.14 = (f32[3]{0:T(128)S(1)}, f32[3]{0:T(128)}, u32[]{:S(2)}) copy-start(f32[3]{0:T(128)} %span_scale.1) | copy-start | bytes 40
  18.1 18.1 %all-to-all-start = ((bf16[4,2,512,128]{3,2,1,0:T(8,128)(2,1)}), bf16[4,2,512,128]{3,2,1,0:T(8,128)(2,1)S(1)}, u32[]{:S(2)}, u32[]{:S(2)}) async-start(bf16[4,2,512,128]{3,2,1,0:T(8,128)(2,1)} %copy_bitcast_fusion), calls=%async_computation | async-start | bytes 2097152 | tf_op jit(solution)/shard_map/all_to_all | solution.py:291
  21.9 7.2 %collective-permute-start.2 = (bf16[192,256]{1,0:T(8,128)(2,1)S(1)}, bf16[192,256]{1,0:T(8,128)(2,1)S(1)}, u32[]{:S(2)}, u32[]{:S(2)}) collective-permute-start(bf16[192,256]{1,0:T(8,128)(2,1)S(1)} %get-tuple-element.23), channel_id=1, source_target_pairs={{0,4},{4,8},{8,12},{12,16},{16,20},{20,24},{24,28},{28,0},{1,5},{5... | collective-permute-start | bytes 294920 | tf_op jit(solution)/shard_map/ppermute | solution.py:317
  22.0 7.1 %collective-permute-start.3 = (bf16[192,256]{1,0:T(8,128)(2,1)S(1)}, bf16[192,256]{1,0:T(8,128)(2,1)S(1)}, u32[]{:S(2)}, u32[]{:S(2)}) collective-permute-start(bf16[192,256]{1,0:T(8,128)(2,1)S(1)} %get-tuple-element.24), channel_id=1, source_target_pairs={{4,0},{8,4},{12,8},{16,12},{20,16},{24,20},{28,24},{0,28},{5,1},{9... | collective-permute-start | bytes 294920 | tf_op jit(solution)/shard_map/ppermute | solution.py:317
  26.9 0.8 copy-start.6
  27.7 0.8 copy-start.8
  33.3 0.9 copy-start.1
  34.3 1.0 copy-start.3
  35.2 1.0 copy-start.5
  36.2 30.3 %copy-start.2 = (f32[7,256,128]{2,1,0:T(8,128)S(1)}, f32[7,256,128]{2,1,0:T(8,128)}, u32[]{:S(2)}) copy-start(f32[7,256,128]{2,1,0:T(8,128)} %copy-done.1) | copy-start | bytes 2752516
  36.2 40.9 %all-to-all-start.3 = ((bf16[32,4,32,128]{3,2,1,0:T(8,128)(2,1)}), bf16[32,4,32,128]{3,2,1,0:T(8,128)(2,1)S(1)}, u32[]{:S(2)}, u32[]{:S(2)}) async-start(bf16[32,4,32,128]{3,2,1,0:T(8,128)(2,1)} %copy-done.5), calls=%async_computation.3 | async-start | bytes 2097152 | tf_op jit(solution)/shard_map/all_to_all | solution.py:320
  41.6 24.8 %collective-permute-start = (bf16[384,256]{1,0:T(8,128)(2,1)S(1)}, bf16[384,256]{1,0:T(8,128)(2,1)S(1)}, u32[]{:S(2)}, u32[]{:S(2)}) collective-permute-start(bf16[384,256]{1,0:T(8,128)(2,1)S(1)} %get-tuple-element.17), channel_id=1, source_target_pairs={{0,4},{4,8},{8,12},{12,16},{16,20},{20,24},{24,28},{28,0},{1,5},{5... | collective-permute-start | bytes 589832 | tf_op jit(solution)/shard_map/ppermute | solution.py:317
  41.9 24.5 %collective-permute-start.1 = (bf16[384,256]{1,0:T(8,128)(2,1)S(1)}, bf16[384,256]{1,0:T(8,128)(2,1)S(1)}, u32[]{:S(2)}, u32[]{:S(2)}) collective-permute-start(bf16[384,256]{1,0:T(8,128)(2,1)S(1)} %get-tuple-element.18), channel_id=1, source_target_pairs={{4,0},{8,4},{12,8},{16,12},{20,16},{24,20},{28,24},{0,28},{5,1},{9... | collective-permute-start | bytes 589832 | tf_op jit(solution)/shard_map/ppermute | solution.py:317
  66.5 1.2 copy-start.4
  67.7 1.0 copy-start.7
  68.7 1.0 copy-start.9
  77.1 56.6 %all-to-all-start.2 = ((bf16[32,4,32,256]{3,2,1,0:T(8,128)(2,1)}), bf16[32,4,32,256]{3,2,1,0:T(8,128)(2,1)S(1)}, u32[]{:S(2)}, u32[]{:S(2)}) async-start(bf16[32,4,32,256]{3,2,1,0:T(8,128)(2,1)} %filter_rest.1), calls=%async_computation.2 | async-start | bytes 4194304 | tf_op jit(solution)/shard_map/all_to_all | solution.py:320

commit v3 on v2

v3 whole, which is shorter than its diff:
```python
import functools
import math

import jax
import jax.numpy as jnp
from jax import lax
from jax.experimental import pallas as pl
from jax.experimental.pallas import tpu as pltpu
from jax.sharding import PartitionSpec as P

HALO = 24
EDGE = 4
LANES = 128
FACTORS = 7
F32 = jnp.float32
BF16 = jnp.bfloat16
VMEM = pl.BlockSpec(memory_space=pltpu.VMEM)
SMEM = pl.BlockSpec(memory_space=pltpu.SMEM)
ROWS_BY_ROWS = (((1,), (1,)), ((), ()))
LIMIT = pltpu.CompilerParams(vmem_limit_bytes=40 * 1024 * 1024)


def iota(shape, dim):
    return lax.broadcasted_iota(jnp.int32, shape, dim)


def split(x):
    high = x.astype(BF16)
    return high, (x - high.astype(F32)).astype(BF16)


def tap_values(scale, distance, valid):
    scale = jnp.full((1, 1), scale, F32)
    k = iota((1, LANES), 1) - HALO
    squares = jnp.where(k <= HALO, jnp.exp(-math.pi * (k * k).astype(F32) / (scale * scale)), 0.0)
    norm = jnp.sqrt(jnp.sum(squares, axis=1, keepdims=True))
    d = distance.astype(F32)
    raw = jnp.exp(-math.pi * (d * d) / (2.0 * scale * scale))
    inside = valid & (distance >= -HALO) & (distance <= HALO)
    return jnp.where(inside, raw, 0.0) / norm


def tail_rows(count):
    return -(-(2 * count + 3 * FACTORS) // 16) * 16


def cell_row(i, faces):
    return (i % faces) * (EDGE * EDGE) + (i // (faces * EDGE)) * EDGE + (i // faces) % EDGE


def taps_kernel(wall_scale, span_scale, wall_first, wall_rest, span_first, span_rest):
    full = wall_first.shape[2]
    cols = span_first.shape[3] // 2
    i = iota((full, full), 0)
    y = cell_row(i, full // (EDGE * EDGE))
    k = iota((2 * cols, cols), 0)
    q = k - cols
    side, odd, r = q // (2 * HALO), (q // HALO) % 2, q % HALO
    z = jnp.where(q < 0, k, jnp.where(side == 0, r - HALO, cols + r))
    n = iota((2 * cols, cols), 1)
    target = (n % (cols // EDGE)) * EDGE + n // (cols // EDGE)
    for c in range(wall_first.shape[0] + wall_rest.shape[0]):
        wall_ref, span_ref, at = (wall_first, span_first, 0) if c == 0 else (wall_rest, span_rest, c - 1)
        high, low = split(tap_values(wall_scale[c], iota((full, full), 1) - y, i >= 0))
        wall_ref[at, :full] = high
        wall_ref[at, full:] = low
        for parity in range(2):
            valid = (q < 0) | ((q < 4 * HALO) & (odd == parity))
            high, low = split(tap_values(span_scale[c], z - target, valid))
            span_ref[at, parity] = jnp.concatenate([high, low], axis=1)


def pack_kernel(devices, noise_ref, lund_ref, mean_ref, owner_ref, out_ref):
    walls, height, cols = out_ref.shape
    planes = noise_ref.shape[1] // walls
    rows = noise_ref.shape[2]
    for w in range(walls):
        for t in range(planes):
            out_ref[w, t * rows : (t + 1) * rows] = noise_ref[0, w * planes + t]
    owner = owner_ref[...]
    elements = owner.shape[1]
    mine = jnp.where(iota((devices, elements), 0) == owner, 1.0, 0.0)
    before = jnp.where(iota((elements, elements), 0) < iota((elements, elements), 1), 1.0, 0.0)
    count = jnp.dot(mine.astype(BF16), before.astype(BF16), preferred_element_type=F32)
    rank = jnp.sum(mine * count, axis=0, keepdims=True)
    pieces = [owner.astype(F32), rank]
    pieces = [p[:, at : at + cols] for p in pieces for at in range(0, elements, cols)]
    factor = jnp.concatenate([lund_ref[...], mean_ref[...]], axis=0)
    factor = jnp.concatenate([factor, jnp.zeros((FACTORS, cols - rows), F32)], axis=1)
    for _ in range(3):
        part = factor.astype(BF16).astype(F32)
        pieces.append(part)
        factor = factor - part
    tail = height - planes * rows
    pieces.append(jnp.zeros((tail - sum(p.shape[0] for p in pieces), cols), F32))
    small = jnp.concatenate(pieces, axis=0).astype(BF16)
    for w in range(walls):
        out_ref[w, planes * rows :] = small


def small_kernel(slots, in_ref, factor_ref, target_ref):
    walls, height, cols = in_ref.shape
    full = factor_ref.shape[0]
    rows = full // walls
    count = target_ref.shape[1]
    tail = tail_rows(count)
    columns = jnp.zeros((full, tail), F32)
    y = cell_row(iota((full, cols), 0), full // (EDGE * EDGE))
    for w in range(walls):
        small = in_ref[w, height - tail :]
        pick = jnp.where(y == iota((full, cols), 1) + w * rows, 1.0, 0.0)
        pick = jnp.where(iota((full, cols), 1) < rows, pick, 0.0).astype(BF16)
        columns = columns + lax.dot_general(pick, small, ROWS_BY_ROWS, preferred_element_type=F32)
        numbers = small.astype(F32)
        target = numbers[:count] * slots + numbers[count : 2 * count]
        target_ref[w] = target.astype(jnp.int32)
    at = 2 * count
    factor = sum(columns[:, at + p * FACTORS : at + (p + 1) * FACTORS] for p in range(3))
    factor_ref[...] = jnp.concatenate([factor, jnp.zeros((full, cols - FACTORS), F32)], axis=1)


def plane_of(noise_ref, c, t, rows):
    walls = noise_ref.shape[0]
    return jnp.concatenate(
        [noise_ref[w, c, t * rows : (t + 1) * rows] for w in range(walls)], axis=0
    )


def edge_picker(cols):
    wide = 2 * HALO
    row, col = iota((wide, cols), 0), iota((wide, cols), 1)
    return jnp.where(col == jnp.where(row < HALO, row, cols - wide + row), 1.0, 0.0).astype(BF16)


def edges_kernel(planes, noise_ref, low_ref, high_ref):
    walls, _, cols = noise_ref.shape
    rows = low_ref.shape[1] // walls
    wide = 2 * HALO
    pick = edge_picker(cols)
    for pair in range(planes // 2):
        edges = []
        for t in (2 * pair, 2 * pair + 1):
            plane = [noise_ref[w, t * rows : (t + 1) * rows] for w in range(walls)]
            plane = jnp.concatenate(plane, axis=0)
            edges.append(lax.dot_general(pick, plane, ROWS_BY_ROWS, preferred_element_type=F32))
        at = pl.ds(pair * wide, wide)
        low_ref[at] = jnp.concatenate([e[:HALO] for e in edges], axis=0).astype(BF16)
        high_ref[at] = jnp.concatenate([e[HALO:] for e in edges], axis=0).astype(BF16)


def raw_edges_kernel(noise_ref, low_ref, high_ref):
    _, all_planes, rows, cols = noise_ref.shape
    walls = low_ref.shape[0]
    pairs = all_planes // walls // 2
    pick = edge_picker(cols)
    for w in range(walls):
        edges = []
        for pair in range(pairs):
            t = 2 * (w * pairs + pair)
            plane = jnp.concatenate([noise_ref[0, t], noise_ref[0, t + 1]], axis=0)
            edges.append(lax.dot_general(pick, plane, ROWS_BY_ROWS, preferred_element_type=F32))
        low_ref[w] = jnp.concatenate([e[:HALO] for e in edges], axis=0).astype(BF16)
        high_ref[w] = jnp.concatenate([e[HALO:] for e in edges], axis=0).astype(BF16)


def swap_blocks(blocks, cols):
    part = cols // EDGE
    lane = iota(blocks[0].shape, 1)
    for step in (2, 1):
        first = (lane // (part * step)) % 2 == 0
        out = list(blocks)
        for a in range(EDGE):
            if a & step:
                continue
            one, two = blocks[a], blocks[a + step]
            out[a] = jnp.where(first, one, pltpu.roll(two, part * step, 1))
            out[a + step] = jnp.where(first, pltpu.roll(one, cols - part * step, 1), two)
        blocks = out
    return blocks


def halo_tiles(parts, cols):
    half = cols // 2
    sides = []
    for side in parts:
        planes = [[], []]
        for one, two in zip(side[::2], side[1::2]):
            lower = iota(one.shape, 1) < half
            planes[0].append(jnp.where(lower, one, pltpu.roll(two, half, 1)))
            planes[1].append(jnp.where(lower, pltpu.roll(one, half, 1), two))
        sides.append([jnp.concatenate(p, axis=1) for p in planes])
    pairs = sides[0][0].shape[0] // HALO
    zeros = jnp.zeros((cols - 4 * HALO, sides[0][0].shape[1]), F32)
    for pair in range(pairs):
        at = slice(pair * HALO, (pair + 1) * HALO)
        tile = [sides[s][odd][at] for s in range(2) for odd in range(2)]
        yield jnp.concatenate(tile + [zeros], axis=0).astype(BF16)


def filter_kernel(count, planes, noise_ref, low_ref, high_ref, factor_ref, target_ref, *rest):
    taps, (out_ref, cells_ref, halo_ref, wide_ref) = rest[:-4], rest[-4:]
    if count > 1:
        others_ref, taps = taps[0], taps[1:]
    wall_of = lambda c: taps[0][0] if c == 0 else taps[2][c - 1]
    span_of = lambda c, odd: taps[1][0, odd] if c == 0 else taps[3][c - 1, odd]
    kept = range(count) if count == 1 else range(1, count)
    walls, _, cols = noise_ref.shape
    full = low_ref.shape[1]
    rows = full // walls
    faces = full // (EDGE * EDGE)
    tile_faces = faces // walls
    devices, _, slots, _ = out_ref.shape
    values = planes * EDGE * EDGE
    wide = 2 * HALO
    pairs = planes // 2

    for f in range(FACTORS):
        wide_ref[f] = jnp.broadcast_to(factor_ref[:, f : f + 1], (full, cols))
    for pair in range(pairs):
        at = pl.ds(pair * wide, wide)
        halo_ref[pair, :wide] = low_ref[at]
        halo_ref[pair, wide : 2 * wide] = high_ref[at]
        halo_ref[pair, 2 * wide :] = jnp.zeros((cols - 2 * wide, full), BF16)
    for c in range(1, count):
        height = pairs * HALO
        start = (count - 1) * planes * rows
        parts = [
            [
                others_ref[w, pl.ds(start + (side * (count - 1) + c - 1) * height, height)].astype(F32)
                for w in range(walls)
            ]
            for side in range(2)
        ]
        for pair, tile in enumerate(halo_tiles(parts, cols)):
            halo_ref[c * pairs + pair] = tile

    def plane(c, t):
        ref, start = (noise_ref, 0) if c == 0 else (others_ref, (c - 1) * planes * rows)
        at = pl.ds(pl.multiple_of(start + t * rows, rows), rows)
        return jnp.concatenate([ref[w, at] for w in range(walls)], axis=0)

    def pair_step(pair, carry):
        psi = [[], []]
        for c in range(count):
            both = jnp.concatenate([plane(c, 2 * pair), plane(c, 2 * pair + 1)], axis=1)
            smooth = jnp.dot(wall_of(c), both, preferred_element_type=F32)
            smooth = smooth[:full] + smooth[full:]
            halo = halo_ref[c * pairs + pair]
            beside = lax.dot_general(wall_of(c), halo, ROWS_BY_ROWS, preferred_element_type=F32)
            beside = beside[:full] + beside[full:]
            for odd in range(2):
                high, low = split(
                    jnp.concatenate([smooth[:, odd * cols : (odd + 1) * cols], beside], axis=1)
                )
                matrix = span_of(c, odd)
                broad = jnp.dot(high, matrix, preferred_element_type=F32)
                small = jnp.dot(low, matrix[:, :cols], preferred_element_type=F32)
                psi[odd].append(broad[:, :cols] + (broad[:, cols:] + small))
        for odd in range(2):
            t = 2 * pair + odd
            p = psi[odd]
            if count == 1:
                velocity = (wide_ref[6] + wide_ref[0] * p[0],)
            else:
                velocity = (
                    wide_ref[1] * p[0] + wide_ref[2] * p[1],
                    wide_ref[3] * p[0] + wide_ref[4] * p[1] + wide_ref[5] * p[2],
                )
            quarter = full // EDGE
            for at, value in enumerate(velocity):
                blocks = [value[a * quarter : (a + 1) * quarter] for a in range(EDGE)]
                for dz, block in enumerate(swap_blocks(blocks, cols)):
                    for dy in range(EDGE):
                        j = t * EDGE * EDGE + dy * EDGE + dz
                        cells_ref[at, pl.ds(j, faces, stride=values), :] = block[dy * faces : (dy + 1) * faces]
        return carry

    lax.fori_loop(0, pairs, pair_step, 0)

    for w in range(walls):
        payload = [
            [
                cells_ref[at, pl.ds((w * tile_faces + f) * values, values), :].astype(BF16)
                for f in range(tile_faces)
            ]
            for at in range(len(kept))
        ]
        payload = jnp.concatenate([jnp.concatenate(p, axis=1) for p in payload], axis=0)
        slot = iota((devices * slots, cols), 0)
        onehot = [
            jnp.where(slot == target_ref[w, f : f + 1], 1.0, 0.0).astype(BF16)
            for f in range(tile_faces)
        ]
        onehot = jnp.concatenate(onehot, axis=1)
        sent = lax.dot_general(onehot, payload, ROWS_BY_ROWS, preferred_element_type=F32)
        out_ref[:, w] = sent.astype(BF16).reshape(devices, slots, len(kept) * values)


def join_kernel(first, some, walls, in_ref, *rest):
    out_ref, sems = rest[-2:]
    devices, height, width = in_ref.shape
    values = width // some
    copies = []
    for c in range(some):
        for s in range(devices // walls):
            for w in range(walls):
                copies.append(
                    pltpu.make_async_copy(
                        in_ref.at[s * walls + w, :, pl.ds(c * values, values)],
                        out_ref.at[0, pl.ds(s * height, height), pl.ds(((c + first) * walls + w) * values, values)],
                        sems.at[c, s * walls + w],
                    )
                )
    for copy in copies:
        copy.start()
    for copy in copies:
        copy.wait()


def join_narrow_kernel(some, in_ref, *rest):
    out_ref = rest[-1]
    walls, _, width = in_ref.shape
    values = width // some
    for c in range(some):

        @pl.when(pl.program_id(1) == c)
        def _():
            for w in range(walls):
                out_ref[0, :, w * values : (w + 1) * values] = in_ref[w, :, c * values : (c + 1) * values]


def per_device(noise, wall_scale, span_scale, lund_factor, mean_velocity, owner_map):
    trio, all_planes, rows, cols = noise.shape
    n_span = lax.axis_size("span")
    n_wall = lax.axis_size("wall")
    devices = n_span * n_wall
    planes = all_planes // n_wall
    pairs = planes // 2
    full = rows * n_wall
    faces = full // (EDGE * EDGE)
    values = planes * EDGE * EDGE
    owners = owner_map.reshape(1, -1)
    elements = owners.shape[1]
    slots = max(8, 2 * elements // devices)
    count = elements // cols
    rest = trio - 1
    struct = jax.ShapeDtypeStruct
    hbm = pltpu.MemorySpace.HBM

    def call(kernel, ins, outs, name, limit, scratch=(), grid=(), out_specs=None):
        specs = out_specs or [VMEM] * len(outs)
        return pl.pallas_call(
            kernel,
            grid=grid,
            in_specs=ins,
            out_specs=specs if len(outs) > 1 else specs[0],
            out_shape=outs if len(outs) > 1 else outs[0],
            scratch_shapes=scratch,
            compiler_params=pltpu.CompilerParams(vmem_limit_bytes=limit * 1024 * 1024),
            name=name,
        )

    up = [(i, (i + 1) % n_span) for i in range(n_span)]
    down = [(b, a) for a, b in up]

    def swap(x):
        return lax.all_to_all(x, "wall", 0, 0, tiled=True)

    def send(x):
        return lax.all_to_all(x, ("span", "wall"), 0, 0, tiled=True).reshape(devices, n_wall * slots, -1)

    packed = call(
        functools.partial(pack_kernel, devices),
        [pl.BlockSpec((1, all_planes, rows, cols), lambda i: (0, 0, 0, 0)), VMEM, VMEM, VMEM],
        [hbm((n_wall, planes * rows + tail_rows(count), cols), BF16)],
        "pack",
        56,
        grid=(1,),
    )(noise, lund_factor, mean_velocity.reshape(1, rows), owners)
    packed = swap(packed)

    height = pairs * HALO
    edge = hbm((n_wall, rest * height, cols), BF16)
    spec = pl.BlockSpec((n_wall, height, cols), lambda c: (0, c, 0))
    first, last = call(
        raw_edges_kernel,
        [pl.BlockSpec((1, all_planes, rows, cols), lambda c: (c + 1, 0, 0, 0))],
        [edge, edge],
        "edges_rest",
        56,
        grid=(rest,),
        out_specs=[spec, spec],
    )(noise)
    others = noise[1:].reshape(rest, n_wall, planes * rows, cols).transpose(1, 0, 2, 3)
    others = others.reshape(n_wall, rest * planes * rows, cols)
    low, high = lax.ppermute(last, "span", up), lax.ppermute(first, "span", down)
    others = swap(jnp.concatenate([others, low, high], axis=1))

    wall_first, wall_rest, span_first, span_rest = call(
        taps_kernel,
        [SMEM, SMEM],
        [
            struct((1, 2 * full, full), BF16),
            struct((rest, 2 * full, full), BF16),
            struct((1, 2, 2 * cols, 2 * cols), BF16),
            struct((rest, 2, 2 * cols, 2 * cols), BF16),
        ],
        "taps",
        16,
    )(wall_scale, span_scale)
    factor, target = call(
        functools.partial(small_kernel, slots),
        [VMEM],
        [struct((full, cols), F32), struct((n_wall, count, cols), jnp.int32)],
        "small",
        16,
    )(packed)

    edge = struct((planes * HALO, full), BF16)
    first, last = call(
        functools.partial(edges_kernel, planes), [VMEM], [edge, edge], "edges_first", 16
    )(packed)
    low, high = lax.ppermute(last, "span", up), lax.ppermute(first, "span", down)

    def filtered(n, some, extra, name):
        return call(
            functools.partial(filter_kernel, n, planes),
            [VMEM] * (5 + len(extra)),
            [hbm((devices, n_wall, slots, some * values), BF16)],
            name,
            32,
            [
                pltpu.VMEM((some, faces * values, cols), F32),
                pltpu.VMEM((n * pairs, cols, full), BF16),
                pltpu.VMEM((FACTORS, full, cols), F32),
            ],
        )(packed, low, high, factor, target, *extra)

    got_first = send(filtered(1, 1, (wall_first, span_first), "filter_first"))
    got_rest = send(
        filtered(trio, rest, (others, wall_first, span_first, wall_rest, span_rest), "filter_rest")
    )

    whole = hbm((1, devices * slots, trio * values * n_wall), BF16)
    block = (1, n_wall * slots, values * n_wall)

    def join(received, some, before):
        keep = [] if before is None else [before]
        anywhere = pl.BlockSpec(memory_space=pl.ANY)
        narrow = values % LANES != 0
        return pl.pallas_call(
            functools.partial(join_narrow_kernel, some)
            if narrow
            else functools.partial(join_kernel, len(keep), some, n_wall),
            grid=(n_span, some) if narrow else (),
            in_specs=[
                pl.BlockSpec((n_wall, n_wall * slots, some * values), lambda s, c: (s, 0, 0)) if narrow else anywhere
            ]
            + [anywhere] * len(keep),
            out_specs=pl.BlockSpec(block, lambda s, c: (0, s, c + len(keep))) if narrow else anywhere,
            out_shape=whole,
            scratch_shapes=[] if narrow else [pltpu.SemaphoreType.DMA((some, devices))],
            input_output_aliases={1: 0} if keep else {},
            compiler_params=pltpu.CompilerParams(vmem_limit_bytes=16 * 1024 * 1024),
            name="join",
        )(received, *keep)

    return join(got_rest, rest, join(got_first, 1, None))


def solution(mesh):
    return jax.shard_map(
        per_device,
        mesh=mesh,
        in_specs=(
            P(None, None, "wall", "span"),
            P(),
            P(),
            P(None, "wall"),
            P("wall"),
            P("wall", "span", None, None),
        ),
        out_specs=P(("span", "wall"), None, None),
        check_vma=False,
    )
```

time: 140 us -> 126 us (0.900)
  waiting for transfers between devices: 74.5 us -> 66.8 us
  local copies, waits for them, and re-layouts: 12.2 us -> 7.25 us
  starting transfers between devices: 28.8 us -> 25.3 us
    ppermute x4, waiting for transfers between devices: 21.2 us -> 0.01 us  [the longest x2 0.01 us: per_device(): lax.ppermute(last, 'span', up)]
    all_to_all x2, waiting for transfers between devices: 45.9 us -> 59.9 us  [send(): lax.all_to_all(x, ('span', 'wall'), 0, 0, tiled=True)]
    unnamed x30 -> x24, local copies, waits for them, and re-layouts: 11.2 us -> 7.18 us
    all_to_all x2, starting transfers between devices: 12.8 us -> 9.27 us  [send(): lax.all_to_all(x, ('span', 'wall'), 0, 0, tiled=True)]
  transfers between devices with their start and end apart: 8 -> 8, of which waited for: 3 -> 4; matrix products, arithmetic and copies ran while one was open for 1% -> 1% of each run, Pallas kernels for 12% -> 16%
where the time goes in v3:
time: 126 us; the launch traced here: 125 us
  waiting for transfers between devices  66.8 us (53%)
  starting transfers between devices  25.3 us (20%)
  Pallas kernels  24.6 us (20%)
  local copies, waits for them, and re-layouts  7.25 us (6%)
    all_to_all x2, waiting for transfers between devices, send(): lax.all_to_all(x, ('span', 'wall'), 0, 0, tiled=True)  59.9 us
    pallas_call x2, Pallas kernels, filtered(): call(functools.partial(filter_kernel, n, planes), [VMEM] * (5 + len(extra...  14.7 us
    all_to_all x2, starting transfers between devices, send(): lax.all_to_all(x, ('span', 'wall'), 0, 0, tiled=True)  9.27 us
    all_to_all x2, starting transfers between devices, swap(): return lax.all_to_all(x, 'wall', 0, 0, tiled=True)  7.9 us
    ppermute x2, starting transfers between devices, per_device(): lax.ppermute(first, 'span', down)  7.57 us
    unnamed x24, local copies, waits for them, and re-layouts  7.18 us
    all_to_all x2, waiting for transfers between devices, swap(): return lax.all_to_all(x, 'wall', 0, 0, tiled=True)  6.95 us
    pallas_call x2, Pallas kernels, join(): pl.pallas_call(functools.partial(join_narrow_kernel, some) if narrow else...  3.08 us
  transfers between devices with their start and end apart: 8, of which 4 were waited for; matrix products, arithmetic and copies ran while one was open for 1% of the time, Pallas kernels for 16%

profile of v3, /device:TPU:0, one launch (start us, length us, event | category | flops | bytes accessed | tf_op | source)
XLA Modules:
  0.0 125.2 jit_solution(14888016402079847901)
XLA Ops:
  0.0 2.7 %edges_rest.1 = (bf16[4,192,128]{2,1,0:T(8,128)(2,1)}, bf16[4,192,128]{2,1,0:T(8,128)(2,1)}) custom-call(bf16[3,32,64,128]{3,2,1,0:T(8,128)(2,1)} %noise_ref.3), custom_call_target="tpu_custom_call" | custom-call | tf_op jit(solution)/shard_map/edges_rest/pallas_call | solution.py:385
  2.7 0.5 collective-permute-start.2
  3.1 4.0 %collective-permute-start.3 = (bf16[4,192,128]{2,1,0:T(8,128)(2,1)}, bf16[4,192,128]{2,1,0:T(8,128)(2,1)S(1)}, u32[]{:S(2)}, u32[]{:S(2)}) collective-permute-start(bf16[4,192,128]{2,1,0:T(8,128)(2,1)} %get-tuple-element.20), channel_id=1, source_target_pairs={{4,0},{8,4},{12,8},{16,12},{20,16},{24,20},{28,24},{0,28},{5,1},{9... | collective-permute-start | bytes 589832 | tf_op jit(solution)/shard_map/ppermute | solution.py:396
  7.1 2.1 %pack.1 = bf16[4,544,128]{2,1,0:T(8,128)(2,1)} custom-call(bf16[3,32,64,128]{3,2,1,0:T(8,128)(2,1)} %noise_ref.3, f32[6,64]{1,0:T(8,128)} %lund_ref.1, f32[1,64]{1,0:T(1,128)} %bitcast.13, s32[1,512]{1,0:T(1,128)} %bitcast.12), custom_call_target="tpu_custom_call" | custom-call | tf_op jit(solution)/shard_map/pack/pallas_call | solution.py:372
  9.2 0.0 slice-start
  9.2 4.3 %all-to-all-start = ((bf16[4,544,128]{2,1,0:T(8,128)(2,1)}), bf16[4,544,128]{2,1,0:T(8,128)(2,1)S(1)}, u32[]{:S(2)}, u32[]{:S(2)}) async-start(bf16[4,544,128]{2,1,0:T(8,128)(2,1)} %pack.1), calls=%async_computation | async-start | bytes 1114112 | tf_op jit(solution)/shard_map/all_to_all | solution.py:367
  13.6 0.0 slice-done
  13.6 0.1 copy.8
  13.7 0.0 collective-permute-done.2
  13.7 0.0 collective-permute-done.3
  13.7 1.2 pad_maximum_fusion
  14.9 0.0 copy-start.10
  14.9 0.0 copy-start.11
  14.9 5.5 %all-to-all-done.noise_ref.in_ref = bf16[4,544,128]{2,1,0:T(8,128)(2,1)S(1)} async-done(((bf16[4,544,128]{2,1,0:T(8,128)(2,1)}), bf16[4,544,128]{2,1,0:T(8,128)(2,1)S(1)}, u32[]{:S(2)}, u32[]{:S(2)}) %all-to-all-start) | async-done | bytes 557088 | tf_op jit(solution)/shard_map/all_to_all | solution.py:367
  20.4 3.6 %all-to-all-start.1 = ((bf16[4,1408,128]{2,1,0:T(8,128)(2,1)}), bf16[4,1408,128]{2,1,0:T(8,128)(2,1)S(1)}, u32[]{:S(2)}, u32[]{:S(2)}) async-start(bf16[4,1408,128]{2,1,0:T(8,128)(2,1)} %pad_maximum_fusion), calls=%async_computation.1 | async-start | bytes 2883584 | tf_op jit(solution)/shard_map/all_to_all | solution.py:367
  24.0 0.3 edges_first.1
  24.3 0.1 collective-permute-start
  24.3 3.5 %collective-permute-start.1 = (bf16[192,256]{1,0:T(8,128)(2,1)S(1)}, bf16[192,256]{1,0:T(8,128)(2,1)S(1)}, u32[]{:S(2)}, u32[]{:S(2)}) collective-permute-start(bf16[192,256]{1,0:T(8,128)(2,1)S(1)} %get-tuple-element.16), channel_id=1, source_target_pairs={{4,0},{8,4},{12,8},{16,12},{20,16},{24,20},{28,24},{0,28},{5,1},{9... | collective-permute-start | bytes 294920 | tf_op jit(solution)/shard_map/ppermute | solution.py:423
  27.8 0.0 copy-done.10
  27.9 0.0 copy-done.11
  27.9 1.3 %taps.1 = (bf16[1,512,256]{2,1,0:T(8,128)(2,1)S(1)}, bf16[2,512,256]{2,1,0:T(8,128)(2,1)S(1)}, bf16[1,2,256,256]{3,2,1,0:T(8,128)(2,1)S(1)}, bf16[2,2,256,256]{3,2,1,0:T(8,128)(2,1)S(1)}) custom-call(f32[3]{0:T(128)S(1)} %copy-done.10, f32[3]{0:T(128)S(1)} %copy-done.11), custom_call_target="tpu_custom_call" | custom-call | tf_op jit(solution)/shard_map/taps/pallas_call | solution.py:399
  29.2 0.0 copy-start.2
  29.2 0.8 copy-done.2
  30.0 0.0 copy-start
  30.0 0.0 copy-start.4
  30.0 0.4 small.1
  30.4 0.0 collective-permute-done.low_ref
  30.4 0.0 collective-permute-done.1.high_ref
  30.4 0.3 copy-done
  30.7 5.5 %filter_first.1 = bf16[32,4,32,128]{3,2,1,0:T(8,128)(2,1)} custom-call(bf16[4,544,128]{2,1,0:T(8,128)(2,1)S(1)} %all-to-all-done.noise_ref.in_ref, bf16[192,256]{1,0:T(8,128)(2,1)S(1)} %collective-permute-done.low_ref, bf16[192,256]{1,0:T(8,128)(2,1)S(1)} %collective-permute-done.1.high_ref, f32[256,128]{1,0:T(8,128)S(1)} %get-tuple-element.17.factor_ref, ...), custom_call_target="tpu_custom_call" | custom-call | tf_op jit(solution)/shard_map/filter_first/pallas_call | solution.py:426
  36.2 0.0 copy-start.6
  36.2 0.6 copy-done.6
  36.9 0.6 copy-done.8
  37.5 1.4 %all-to-all-done.1.rest_0_ = bf16[4,1408,128]{2,1,0:T(8,128)(2,1)S(1)} async-done(((bf16[4,1408,128]{2,1,0:T(8,128)(2,1)}), bf16[4,1408,128]{2,1,0:T(8,128)(2,1)S(1)}, u32[]{:S(2)}, u32[]{:S(2)}) %all-to-all-start.1) | async-done | bytes 1441824 | tf_op jit(solution)/shard_map/all_to_all | solution.py:367
  38.9 0.0 copy-done.4
  38.9 5.8 %all-to-all-start.3 = ((bf16[32,4,32,128]{3,2,1,0:T(8,128)(2,1)}), bf16[32,4,32,128]{3,2,1,0:T(8,128)(2,1)S(1)}, u32[]{:S(2)}, u32[]{:S(2)}) async-start(bf16[32,4,32,128]{3,2,1,0:T(8,128)(2,1)} %filter_first.1), calls=%async_computation.3 | async-start | bytes 2097152 | tf_op jit(solution)/shard_map/all_to_all | solution.py:370
  44.8 0.0 copy-start.1
  44.8 0.9 copy-done.1
  45.8 1.0 copy-done.3
  46.8 1.0 copy-done.5
  47.8 0.9 copy-done.7
  48.7 0.9 copy-done.9
  49.6 9.2 %filter_rest.1 = bf16[32,4,32,256]{3,2,1,0:T(8,128)(2,1)} custom-call(bf16[4,544,128]{2,1,0:T(8,128)(2,1)S(1)} %all-to-all-done.noise_ref.in_ref, bf16[192,256]{1,0:T(8,128)(2,1)S(1)} %copy-done.7, bf16[192,256]{1,0:T(8,128)(2,1)S(1)} %copy-done.9, f32[256,128]{1,0:T(8,128)S(1)} %get-tuple-element.17.factor_ref, ...), custom_call_target="tpu_custom_call" | custom-call | tf_op jit(solution)/shard_map/filter_rest/pallas_call | solution.py:426
  58.8 12.4 %all-to-all-done.3 = bf16[32,4,32,128]{3,2,1,0:T(8,128)(2,1)S(1)} async-done(((bf16[32,4,32,128]{3,2,1,0:T(8,128)(2,1)}), bf16[32,4,32,128]{3,2,1,0:T(8,128)(2,1)S(1)}, u32[]{:S(2)}, u32[]{:S(2)}) %all-to-all-start.3) | async-done | bytes 1048608 | tf_op jit(solution)/shard_map/all_to_all | solution.py:370
  71.2 3.4 %all-to-all-start.2 = ((bf16[32,4,32,256]{3,2,1,0:T(8,128)(2,1)}), bf16[32,4,32,256]{3,2,1,0:T(8,128)(2,1)S(1)}, u32[]{:S(2)}, u32[]{:S(2)}) async-start(bf16[32,4,32,256]{3,2,1,0:T(8,128)(2,1)} %filter_rest.1), calls=%async_computation.2 | async-start | bytes 4194304 | tf_op jit(solution)/shard_map/all_to_all | solution.py:370
  74.7 1.2 join.2.rest_0_
  75.9 47.5 %all-to-all-done.2 = bf16[32,4,32,256]{3,2,1,0:T(8,128)(2,1)S(1)} async-done(((bf16[32,4,32,256]{3,2,1,0:T(8,128)(2,1)}), bf16[32,4,32,256]{3,2,1,0:T(8,128)(2,1)S(1)}, u32[]{:S(2)}, u32[]{:S(2)}) %all-to-all-start.2) | async-done | bytes 2097184 | tf_op jit(solution)/shard_map/all_to_all | solution.py:370
  123.4 1.8 %join.3 = bf16[1,1024,1536]{2,1,0:T(8,128)(2,1)} custom-call(bf16[32,128,256]{2,1,0:T(8,128)(2,1)S(1)} %bitcast.8, bf16[1,1024,1536]{2,1,0:T(8,128)(2,1)} %join.2.rest_0_), custom_call_target="tpu_custom_call", output_to_operand_aliasing={{}: (1, {})} | custom-call | tf_op jit(solution)/shard_map/join/pallas_call | solution.py:451
  (5 shorter events, 0.0 us)
Async XLA Ops:
  2.7 11.0 %collective-permute-start.2 = (bf16[4,192,128]{2,1,0:T(8,128)(2,1)}, bf16[4,192,128]{2,1,0:T(8,128)(2,1)S(1)}, u32[]{:S(2)}, u32[]{:S(2)}) collective-permute-start(bf16[4,192,128]{2,1,0:T(8,128)(2,1)} %get-tuple-element.19), channel_id=1, source_target_pairs={{0,4},{4,8},{8,12},{12,16},{16,20},{20,24},{24,28},{28,0},{1,5},{5... | collective-permute-start | bytes 589832 | tf_op jit(solution)/shard_map/ppermute | solution.py:396
  3.1 10.6 %collective-permute-start.3 = (bf16[4,192,128]{2,1,0:T(8,128)(2,1)}, bf16[4,192,128]{2,1,0:T(8,128)(2,1)S(1)}, u32[]{:S(2)}, u32[]{:S(2)}) collective-permute-start(bf16[4,192,128]{2,1,0:T(8,128)(2,1)} %get-tuple-element.20), channel_id=1, source_target_pairs={{4,0},{8,4},{12,8},{16,12},{20,16},{24,20},{28,24},{0,28},{5,1},{9... | collective-permute-start | bytes 589832 | tf_op jit(solution)/shard_map/ppermute | solution.py:396
  9.2 4.4 %slice-start = ((bf16[3,32,64,128]{3,2,1,0:T(8,128)(2,1)}), bf16[2,32,64,128]{3,2,1,0:T(8,128)(2,1)S(1)}, s32[]{:S(2)}) async-start(bf16[3,32,64,128]{3,2,1,0:T(8,128)(2,1)} %noise_ref.3), calls=%async_computation.4 | async-start | bytes 2097152 | tf_op jit(solution)/shard_map/slice | solution.py:394
  9.2 11.1 %all-to-all-start = ((bf16[4,544,128]{2,1,0:T(8,128)(2,1)}), bf16[4,544,128]{2,1,0:T(8,128)(2,1)S(1)}, u32[]{:S(2)}, u32[]{:S(2)}) async-start(bf16[4,544,128]{2,1,0:T(8,128)(2,1)} %pack.1), calls=%async_computation | async-start | bytes 1114112 | tf_op jit(solution)/shard_map/all_to_all | solution.py:367
  14.9 13.0 %copy-start.10 = (f32[3]{0:T(128)S(1)}, f32[3]{0:T(128)}, u32[]{:S(2)}) copy-start(f32[3]{0:T(128)} %wall_scale.1) | copy-start | bytes 40
  14.9 13.0 %copy-start.11 = (f32[3]{0:T(128)S(1)}, f32[3]{0:T(128)}, u32[]{:S(2)}) copy-start(f32[3]{0:T(128)} %span_scale.1) | copy-start | bytes 40
  20.4 18.6 %all-to-all-start.1 = ((bf16[4,1408,128]{2,1,0:T(8,128)(2,1)}), bf16[4,1408,128]{2,1,0:T(8,128)(2,1)S(1)}, u32[]{:S(2)}, u32[]{:S(2)}) async-start(bf16[4,1408,128]{2,1,0:T(8,128)(2,1)} %pad_maximum_fusion), calls=%async_computation.1 | async-start | bytes 2883584 | tf_op jit(solution)/shard_map/all_to_all | solution.py:367
  24.3 6.2 %collective-permute-start = (bf16[192,256]{1,0:T(8,128)(2,1)S(1)}, bf16[192,256]{1,0:T(8,128)(2,1)S(1)}, u32[]{:S(2)}, u32[]{:S(2)}) collective-permute-start(bf16[192,256]{1,0:T(8,128)(2,1)S(1)} %get-tuple-element.15), channel_id=1, source_target_pairs={{0,4},{4,8},{8,12},{12,16},{16,20},{20,24},{24,28},{28,0},{1,5},{5... | collective-permute-start | bytes 294920 | tf_op jit(solution)/shard_map/ppermute | solution.py:423
  24.3 6.1 %collective-permute-start.1 = (bf16[192,256]{1,0:T(8,128)(2,1)S(1)}, bf16[192,256]{1,0:T(8,128)(2,1)S(1)}, u32[]{:S(2)}, u32[]{:S(2)}) collective-permute-start(bf16[192,256]{1,0:T(8,128)(2,1)S(1)} %get-tuple-element.16), channel_id=1, source_target_pairs={{4,0},{8,4},{12,8},{16,12},{20,16},{24,20},{28,24},{0,28},{5,1},{9... | collective-permute-start | bytes 294920 | tf_op jit(solution)/shard_map/ppermute | solution.py:423
  29.2 0.8 copy-start.2
  30.0 0.7 copy-start
  30.0 8.9 %copy-start.4 = (bf16[2,2,256,256]{3,2,1,0:T(8,128)(2,1)}, bf16[2,2,256,256]{3,2,1,0:T(8,128)(2,1)S(1)}, u32[]{:S(2)}) copy-start(bf16[2,2,256,256]{3,2,1,0:T(8,128)(2,1)S(1)} %get-tuple-element.24.rest_4_) | copy-start | bytes 1572868
  36.2 0.6 copy-start.6
  36.9 0.6 copy-start.8
  38.9 32.3 %all-to-all-start.3 = ((bf16[32,4,32,128]{3,2,1,0:T(8,128)(2,1)}), bf16[32,4,32,128]{3,2,1,0:T(8,128)(2,1)S(1)}, u32[]{:S(2)}, u32[]{:S(2)}) async-start(bf16[32,4,32,128]{3,2,1,0:T(8,128)(2,1)} %filter_first.1), calls=%async_computation.3 | async-start | bytes 2097152 | tf_op jit(solution)/shard_map/all_to_all | solution.py:370
  44.8 1.0 copy-start.1
  45.8 1.0 copy-start.3
  46.8 1.0 copy-start.5
  47.8 0.9 copy-start.7
  48.7 0.9 copy-start.9
  71.2 52.1 %all-to-all-start.2 = ((bf16[32,4,32,256]{3,2,1,0:T(8,128)(2,1)}), bf16[32,4,32,256]{3,2,1,0:T(8,128)(2,1)S(1)}, u32[]{:S(2)}, u32[]{:S(2)}) async-start(bf16[32,4,32,256]{3,2,1,0:T(8,128)(2,1)} %filter_rest.1), calls=%async_computation.2 | async-start | bytes 4194304 | tf_op jit(solution)/shard_map/all_to_all | solution.py:370

commit v4 on v3

v4 whole, which is shorter than its diff:
```python
import functools
import math

import jax
import jax.numpy as jnp
from jax import lax
from jax.experimental import pallas as pl
from jax.experimental.pallas import tpu as pltpu
from jax.sharding import PartitionSpec as P

HALO = 24
EDGE = 4
LANES = 128
FACTORS = 7
F32 = jnp.float32
BF16 = jnp.bfloat16
VMEM = pl.BlockSpec(memory_space=pltpu.VMEM)
ANYWHERE = pl.BlockSpec(memory_space=pl.ANY)
SMEM = pl.BlockSpec(memory_space=pltpu.SMEM)
ROWS_BY_ROWS = (((1,), (1,)), ((), ()))


def iota(shape, dim):
    return lax.broadcasted_iota(jnp.int32, shape, dim)


def split(x):
    high = x.astype(BF16)
    return high, (x - high.astype(F32)).astype(BF16)


def tap_values(scale, distance, valid):
    scale = jnp.full((1, 1), scale, F32)
    k = iota((1, LANES), 1) - HALO
    squares = jnp.where(k <= HALO, jnp.exp(-math.pi * (k * k).astype(F32) / (scale * scale)), 0.0)
    norm = jnp.sqrt(jnp.sum(squares, axis=1, keepdims=True))
    d = distance.astype(F32)
    raw = jnp.exp(-math.pi * (d * d) / (2.0 * scale * scale))
    inside = valid & (distance >= -HALO) & (distance <= HALO)
    return jnp.where(inside, raw, 0.0) / norm


def tail_rows(count):
    return -(-(2 * count + 3 * FACTORS) // 16) * 16


def cell_row(i, faces):
    return (i % faces) * (EDGE * EDGE) + (i // (faces * EDGE)) * EDGE + (i // faces) % EDGE


def taps_kernel(first, wall_scale, span_scale, wall_ref, main_ref, halo_ref):
    some, full, _ = wall_ref.shape
    cols = main_ref.shape[1] // 2
    walls = lax.axis_size("wall")
    rows = full // walls
    i, j = iota((full, full), 0), iota((full, full), 1)
    y = cell_row(i, full // (EDGE * EDGE))
    source = lax.rem(lax.axis_index("wall") + walls - j // rows, walls)
    column = source * rows + j % rows if first else j
    n = iota((cols, cols), 1)
    target = (n % (cols // EDGE)) * EDGE + n // (cols // EDGE)
    k = iota((cols, cols), 0)
    side, odd, r = k // (2 * HALO), (k // HALO) % 2, k % HALO
    z = jnp.where(side == 0, r - HALO, cols + r)

    def span_matrix(scale, distance, valid):
        high, low = split(tap_values(scale, distance, valid))
        top = jnp.concatenate([high, low], axis=1)
        return jnp.concatenate([top, jnp.concatenate([high, jnp.zeros_like(high)], axis=1)], axis=0)

    for c in range(some):
        high, low = split(tap_values(wall_scale[first + c], column - y, i >= 0))
        wall_ref[c, :, :full] = high
        wall_ref[c, :, full:] = low
        scale = span_scale[first + c]
        main_ref[c] = span_matrix(scale, k - target, k >= 0)
        for parity in range(2):
            valid = (k < 4 * HALO) & (odd == parity)
            halo_ref[c, parity] = span_matrix(scale, z - target, valid)


def run(copies):
    for copy in copies:
        copy.start()
    for copy in copies:
        copy.wait()


def pack_kernel(devices, noise_ref, lund_ref, mean_ref, owner_ref, out_ref, small_ref, noise_sems, small_sems):
    walls, height, cols = out_ref.shape
    tail = small_ref.shape[0]
    block = height - tail
    rows = mean_ref.shape[1]
    copies = [
        pltpu.make_async_copy(
            noise_ref.at[0, pl.ds(w * block, block)], out_ref.at[w, pl.ds(0, block)], noise_sems.at[w]
        )
        for w in range(walls)
    ]
    for copy in copies:
        copy.start()
    owner = owner_ref[...]
    elements = owner.shape[1]
    mine = jnp.where(iota((devices, elements), 0) == owner, 1.0, 0.0)
    before = jnp.where(iota((elements, elements), 0) < iota((elements, elements), 1), 1.0, 0.0)
    count = jnp.dot(mine.astype(BF16), before.astype(BF16), preferred_element_type=F32)
    rank = jnp.sum(mine * count, axis=0, keepdims=True)
    pieces = [owner.astype(F32), rank]
    pieces = [p[:, at : at + cols] for p in pieces for at in range(0, elements, cols)]
    factor = jnp.concatenate([lund_ref[...], mean_ref[...]], axis=0)
    factor = jnp.concatenate([factor, jnp.zeros((FACTORS, cols - rows), F32)], axis=1)
    for _ in range(3):
        part = factor.astype(BF16).astype(F32)
        pieces.append(part)
        factor = factor - part
    pieces.append(jnp.zeros((tail - sum(p.shape[0] for p in pieces), cols), F32))
    small_ref[...] = jnp.concatenate(pieces, axis=0).astype(BF16)
    run(
        [
            pltpu.make_async_copy(small_ref, out_ref.at[w, pl.ds(block, tail)], small_sems.at[w])
            for w in range(walls)
        ]
    )
    for copy in copies:
        copy.wait()


def pack_planes_kernel(noise_ref, *rest):
    out_refs, sems = rest[:-1], rest[-1]
    walls = len(out_refs)
    block = noise_ref.shape[1] // walls
    me = lax.axis_index("wall")
    copies = []
    for step, out_ref in enumerate(out_refs):
        start = pl.multiple_of(lax.rem(me + step, walls) * block, block)
        copies.append(pltpu.make_async_copy(noise_ref.at[0, pl.ds(start, block)], out_ref, sems.at[step]))
    run(copies)


def pack_late_kernel(noise_ref, low_ref, high_ref, *rest):
    out_refs, sems = rest[:-1], rest[-1]
    walls, some, height, _ = low_ref.shape
    block = noise_ref.shape[1] // walls
    me = lax.axis_index("wall")
    copies = []
    for step, out_ref in enumerate(out_refs):
        to = lax.rem(me + step, walls)
        parts = [(noise_ref.at[0, pl.ds(pl.multiple_of(to * block, block), block)], 0, block)]
        for side, ref in enumerate((low_ref, high_ref)):
            for c in range(some):
                parts.append((ref.at[to, c], block + (side * some + c) * height, height))
        for part, (ref, start, size) in enumerate(parts):
            copies.append(
                pltpu.make_async_copy(ref, out_ref.at[pl.ds(start, size)], sems.at[step, part])
            )
    run(copies)


def small_kernel(slots, in_ref, factor_ref, target_ref):
    walls, height, cols = in_ref.shape
    full = factor_ref.shape[0]
    rows = full // walls
    count = target_ref.shape[1]
    tail = tail_rows(count)
    columns = jnp.zeros((full, tail), F32)
    y = cell_row(iota((full, cols), 0), full // (EDGE * EDGE))
    for w in range(walls):
        small = in_ref[w, height - tail :]
        pick = jnp.where(y == iota((full, cols), 1) + w * rows, 1.0, 0.0)
        pick = jnp.where(iota((full, cols), 1) < rows, pick, 0.0).astype(BF16)
        columns = columns + lax.dot_general(pick, small, ROWS_BY_ROWS, preferred_element_type=F32)
        numbers = small.astype(F32)
        target = numbers[:count] * slots + numbers[count : 2 * count]
        target_ref[w] = target.astype(jnp.int32)
    at = 2 * count
    factor = sum(columns[:, at + p * FACTORS : at + (p + 1) * FACTORS] for p in range(3))
    factor_ref[...] = jnp.concatenate([factor, jnp.zeros((full, cols - FACTORS), F32)], axis=1)


def edge_picker(cols):
    wide = 2 * HALO
    row, col = iota((wide, cols), 0), iota((wide, cols), 1)
    return jnp.where(col == jnp.where(row < HALO, row, cols - wide + row), 1.0, 0.0).astype(BF16)


def edges_kernel(planes, noise_ref, low_ref, high_ref):
    walls, _, cols = noise_ref.shape
    rows = low_ref.shape[1] // walls
    wide = 2 * HALO
    pick = edge_picker(cols)
    for pair in range(planes // 2):
        edges = []
        for t in (2 * pair, 2 * pair + 1):
            plane = [noise_ref[w, t * rows : (t + 1) * rows] for w in range(walls)]
            plane = jnp.concatenate(plane, axis=0)
            edges.append(lax.dot_general(pick, plane, ROWS_BY_ROWS, preferred_element_type=F32))
        at = pl.ds(pair * wide, wide)
        low_ref[at] = jnp.concatenate([e[:HALO] for e in edges], axis=0).astype(BF16)
        high_ref[at] = jnp.concatenate([e[HALO:] for e in edges], axis=0).astype(BF16)


def raw_edges_kernel(noise_ref, low_ref, high_ref):
    walls, _, height, cols = low_ref.shape
    pairs = height // HALO
    pick = edge_picker(cols)
    for w in range(walls):
        edges = []
        for pair in range(pairs):
            plane = noise_ref[0, (w * pairs + pair) * cols : (w * pairs + pair + 1) * cols]
            edges.append(lax.dot_general(pick, plane, ROWS_BY_ROWS, preferred_element_type=F32))
        low_ref[w, 0] = jnp.concatenate([e[:HALO] for e in edges], axis=0).astype(BF16)
        high_ref[w, 0] = jnp.concatenate([e[HALO:] for e in edges], axis=0).astype(BF16)


def swap_blocks(blocks, cols):
    part = cols // EDGE
    lane = iota(blocks[0].shape, 1)
    for step in (2, 1):
        first = (lane // (part * step)) % 2 == 0
        out = list(blocks)
        for a in range(EDGE):
            if a & step:
                continue
            one, two = blocks[a], blocks[a + step]
            out[a] = jnp.where(first, one, pltpu.roll(two, part * step, 1))
            out[a + step] = jnp.where(first, pltpu.roll(one, cols - part * step, 1), two)
        blocks = out
    return blocks


def halo_tiles(parts, cols):
    half = cols // 2
    sides = []
    for side in parts:
        planes = [[], []]
        for one, two in zip(side[::2], side[1::2]):
            lower = iota(one.shape, 1) < half
            planes[0].append(jnp.where(lower, one, pltpu.roll(two, half, 1)))
            planes[1].append(jnp.where(lower, pltpu.roll(one, half, 1), two))
        sides.append([jnp.concatenate(p, axis=1) for p in planes])
    pairs = sides[0][0].shape[0] // HALO
    zeros = jnp.zeros((cols - 4 * HALO, sides[0][0].shape[1]), F32)
    for pair in range(pairs):
        at = slice(pair * HALO, (pair + 1) * HALO)
        tile = [sides[s][odd][at] for s in range(2) for odd in range(2)]
        yield jnp.concatenate(tile + [zeros], axis=0).astype(BF16)


def span_product(x, matrix):
    cols = x.shape[1]
    both = jnp.dot(jnp.concatenate(split(x), axis=1), matrix, preferred_element_type=F32)
    return both[:, :cols] + both[:, cols:]


def main_part(planes, wall, matrix):
    both = jnp.concatenate(planes, axis=1)
    cols = planes[0].shape[1]
    smooth = jnp.dot(wall, jnp.concatenate([both, both], axis=0), preferred_element_type=F32)
    return [span_product(smooth[:, odd * cols : (odd + 1) * cols], matrix) for odd in range(2)]


def halo_part(tile, wall, halo_ref):
    smooth = lax.dot_general(
        wall, jnp.concatenate([tile, tile], axis=1), ROWS_BY_ROWS, preferred_element_type=F32
    )
    return [span_product(smooth, halo_ref[odd]) for odd in range(2)]


def main_kernel(planes, noise_ref, wall_ref, main_ref, psi_ref):
    walls = noise_ref.shape[0]
    rows = psi_ref.shape[1] // walls

    def pair_step(pair, carry):
        pair_planes = []
        for odd in range(2):
            at = pl.ds(pl.multiple_of((2 * pair + odd) * rows, rows), rows)
            pair_planes.append(jnp.concatenate([noise_ref[w, at] for w in range(walls)], axis=0))
        for odd, psi in enumerate(main_part(pair_planes, wall_ref[0], main_ref[0])):
            psi_ref[2 * pair + odd] = psi
        return carry

    lax.fori_loop(0, planes // 2, pair_step, 0, unroll=True)


def widen(factor_ref, wide_ref, which):
    for f in which:
        wide_ref[f] = jnp.broadcast_to(factor_ref[:, f : f + 1], wide_ref.shape[1:])


def place_cells(velocity, t, cells_ref, at):
    full, cols = velocity.shape
    quarter, faces = full // EDGE, full // (EDGE * EDGE)
    values = cells_ref.shape[1] // faces
    blocks = [velocity[a * quarter : (a + 1) * quarter] for a in range(EDGE)]
    for dz, block in enumerate(swap_blocks(blocks, cols)):
        for dy in range(EDGE):
            j = t * EDGE * EDGE + dy * EDGE + dz
            cells_ref[at, pl.ds(j, faces, stride=values), :] = block[dy * faces : (dy + 1) * faces]


def scatter_cells(cells_ref, target_ref, sent_ref, out_ref, sems):
    walls, tile_faces, cols = target_ref.shape
    some = cells_ref.shape[0]
    values = cells_ref.shape[1] // (walls * tile_faces)
    _, devices, slots, width = sent_ref.shape
    copies = []
    for w in range(walls):
        payload = [
            [
                cells_ref[at, pl.ds((w * tile_faces + f) * values, values), :].astype(BF16)
                for f in range(tile_faces)
            ]
            for at in range(some)
        ]
        payload = jnp.concatenate([jnp.concatenate(p, axis=1) for p in payload], axis=0)
        slot = iota((devices * slots, cols), 0)
        onehot = [
            jnp.where(slot == target_ref[w, f : f + 1], 1.0, 0.0).astype(BF16)
            for f in range(tile_faces)
        ]
        onehot = jnp.concatenate(onehot, axis=1)
        sent = lax.dot_general(onehot, payload, ROWS_BY_ROWS, preferred_element_type=F32)
        sent_ref[w] = sent.astype(BF16).reshape(devices, slots, width)
        copies.append(pltpu.make_async_copy(sent_ref.at[w], out_ref.at[:, w], sems.at[w]))
        copies[-1].start()
    for copy in copies:
        copy.wait()


def first_kernel(
    planes, psi_in, low_ref, high_ref, factor_ref, target_ref, wall_ref, halo_ref,
    out_ref, psi_out, psi_ref, cells_ref, wide_ref, sent_ref, sems, psi_sem,
):
    full, cols = psi_ref.shape[1:]
    wide = 2 * HALO
    widen(factor_ref, wide_ref, (0, 6))

    def pair_step(pair, carry):
        at = pl.ds(pl.multiple_of(pair * wide, wide), wide)
        tile = [low_ref[at], high_ref[at], jnp.zeros((cols - 2 * wide, full), BF16)]
        beside = halo_part(jnp.concatenate(tile, axis=0), wall_ref[0], halo_ref.at[0])
        for odd in range(2):
            t = 2 * pair + odd
            psi = psi_in[t] + beside[odd]
            psi_ref[t] = psi
            place_cells(wide_ref[6] + wide_ref[0] * psi, t, cells_ref, 0)
        return carry

    lax.fori_loop(0, planes // 2, pair_step, 0, unroll=True)
    copy = pltpu.make_async_copy(psi_ref, psi_out, psi_sem.at[0])
    copy.start()
    scatter_cells(cells_ref, target_ref, sent_ref, out_ref, sems)
    copy.wait()


def rest_kernel(
    planes, psi_ref, factor_ref, target_ref, wall_ref, main_ref, halo_ref, *rest,
):
    *in_refs, out_ref, cells_ref, tile_ref, wide_ref, sent_ref, sems = rest
    early_refs, late_refs = in_refs[: len(in_refs) // 2], in_refs[len(in_refs) // 2 :]
    full, cols = psi_ref.shape[1:]
    some = wall_ref.shape[0]
    rows = full // len(early_refs)
    pairs = planes // 2
    height = pairs * HALO
    widen(factor_ref, wide_ref, range(1, 6))
    for c in range(some):
        starts = [planes * rows + (side * some + c) * height for side in range(2)]
        parts = [[ref[pl.ds(at, height)].astype(F32) for ref in late_refs] for at in starts]
        for pair, tile in enumerate(halo_tiles(parts, cols)):
            tile_ref[c * pairs + pair] = tile

    def pair_step(pair, carry):
        psi = []
        for c in range(some):
            pair_planes = []
            for odd in range(2):
                at = pl.ds(pl.multiple_of((2 * pair + odd) * rows, rows), rows)
                pair_planes.append(jnp.concatenate([ref[at] for ref in (early_refs, late_refs)[c]], axis=0))
            main = main_part(pair_planes, wall_ref[c], main_ref[c])
            beside = halo_part(tile_ref[c * pairs + pair], wall_ref[c], halo_ref.at[c])
            psi.append([m + b for m, b in zip(main, beside)])
        for odd in range(2):
            t = 2 * pair + odd
            p, q, r = psi_ref[t], psi[0][odd], psi[1][odd]
            place_cells(wide_ref[1] * p + wide_ref[2] * q, t, cells_ref, 0)
            place_cells(wide_ref[3] * p + wide_ref[4] * q + wide_ref[5] * r, t, cells_ref, 1)
        return carry

    lax.fori_loop(0, pairs, pair_step, 0, unroll=True)
    scatter_cells(cells_ref, target_ref, sent_ref, out_ref, sems)


def join_kernel(first, some, walls, in_ref, *rest):
    out_ref, sems = rest[-2:]
    devices, height, width = in_ref.shape
    values = width // some
    copies = []
    for c in range(some):
        for s in range(devices // walls):
            for w in range(walls):
                copies.append(
                    pltpu.make_async_copy(
                        in_ref.at[s * walls + w, :, pl.ds(c * values, values)],
                        out_ref.at[0, pl.ds(s * height, height), pl.ds(((c + first) * walls + w) * values, values)],
                        sems.at[c, s * walls + w],
                    )
                )
    run(copies)


def join_narrow_kernel(some, in_ref, *rest):
    out_ref = rest[-1]
    walls, _, width = in_ref.shape
    values = width // some
    for c in range(some):

        @pl.when(pl.program_id(1) == c)
        def _():
            for w in range(walls):
                out_ref[0, :, w * values : (w + 1) * values] = in_ref[w, :, c * values : (c + 1) * values]


def per_device(noise, wall_scale, span_scale, lund_factor, mean_velocity, owner_map):
    trio, all_planes, rows, cols = noise.shape
    n_span = lax.axis_size("span")
    n_wall = lax.axis_size("wall")
    devices = n_span * n_wall
    planes = all_planes // n_wall
    pairs = planes // 2
    full = rows * n_wall
    faces = full // (EDGE * EDGE)
    values = planes * EDGE * EDGE
    owners = owner_map.reshape(1, -1)
    elements = owners.shape[1]
    slots = max(8, 2 * elements // devices)
    count = elements // cols
    rest = trio - 1
    struct = jax.ShapeDtypeStruct
    hbm = pltpu.MemorySpace.HBM

    def call(kernel, ins, outs, name, limit, scratch=(), grid=(), out_specs=None):
        specs = out_specs or [VMEM] * len(outs)
        return pl.pallas_call(
            kernel,
            grid=grid,
            in_specs=ins,
            out_specs=specs if len(outs) > 1 else specs[0],
            out_shape=outs if len(outs) > 1 else outs[0],
            scratch_shapes=scratch,
            compiler_params=pltpu.CompilerParams(vmem_limit_bytes=limit * 1024 * 1024),
            cost_estimate=pl.CostEstimate(flops=1024, bytes_accessed=1024, transcendentals=0),
            name=name,
        )

    up = [(i, (i + 1) % n_span) for i in range(n_span)]
    down = [(b, a) for a, b in up]

    def swap(x):
        return lax.all_to_all(x, "wall", 0, 0, tiled=True)

    def send(x):
        return lax.all_to_all(x, ("span", "wall"), 0, 0, tiled=True).reshape(devices, n_wall * slots, -1)

    dma = pltpu.SemaphoreType.DMA
    noise = noise.reshape(trio, all_planes * rows, cols)
    packed = call(
        functools.partial(pack_kernel, devices),
        [pl.BlockSpec((1, all_planes * rows, cols), lambda i: (0, 0, 0)), VMEM, VMEM, VMEM],
        [hbm((n_wall, planes * rows + tail_rows(count), cols), BF16)],
        "pack",
        56,
        [pltpu.VMEM((tail_rows(count), cols), BF16), dma((n_wall,)), dma((n_wall,))],
        grid=(1,),
        out_specs=[ANYWHERE],
    )(noise, lund_factor, mean_velocity.reshape(1, rows), owners)
    noise, packed = lax.optimization_barrier((noise, packed))
    packed = swap(packed)

    height = pairs * HALO
    edge = hbm((n_wall, rest, height, cols), BF16)
    spec = pl.BlockSpec((n_wall, 1, height, cols), lambda c: (0, c, 0, 0))
    first, last = call(
        raw_edges_kernel,
        [pl.BlockSpec((1, all_planes * rows, cols), lambda c: (c + 1, 0, 0))],
        [edge, edge],
        "edges_rest",
        56,
        grid=(rest,),
        out_specs=[spec, spec],
    )(noise)
    rest_low, rest_high = lax.ppermute(last, "span", up), lax.ppermute(first, "span", down)
    early = call(
        pack_planes_kernel,
        [pl.BlockSpec((1, all_planes * rows, cols), lambda i: (1, 0, 0))],
        [hbm((planes * rows, cols), BF16)] * n_wall,
        "pack_early",
        56,
        [dma((n_wall,))],
        grid=(1,),
        out_specs=[ANYWHERE] * n_wall,
    )(noise)
    packed, _ = lax.optimization_barrier((packed, (first, last, early)))

    def spread(blocks):
        return [blocks[0]] + [
            lax.ppermute(x, "wall", [(i, (i + step) % n_wall) for i in range(n_wall)])
            for step, x in enumerate(blocks[1:], 1)
        ]

    def taps(first, some, make, name):
        return call(
            functools.partial(taps_kernel, first),
            [SMEM, SMEM],
            [
                make((some, full, 2 * full), BF16),
                make((some, 2 * cols, 2 * cols), BF16),
                make((some, 2, 2 * cols, 2 * cols), BF16),
            ],
            name,
            16,
        )(wall_scale, span_scale)

    wall_first, main_first, halo_first = taps(0, 1, struct, "taps_first")
    factor, target = call(
        functools.partial(small_kernel, slots),
        [VMEM],
        [struct((full, cols), F32), struct((n_wall, count, cols), jnp.int32)],
        "small",
        16,
    )(packed)

    edge = struct((planes * HALO, full), BF16)
    first, last = call(
        functools.partial(edges_kernel, planes), [VMEM], [edge, edge], "edges_first", 16
    )(packed)
    low, high = lax.ppermute(last, "span", up), lax.ppermute(first, "span", down)
    early = spread(early)
    low, early = lax.optimization_barrier((low, early))

    psi = struct((planes, full, cols), F32)
    psi_main = call(functools.partial(main_kernel, planes), [VMEM] * 3, [psi], "main_first", 16)(
        packed, wall_first, main_first
    )

    def scratch(some):
        return [
            pltpu.VMEM((some, faces * values, cols), F32),
            pltpu.VMEM((rest * pairs, cols, full), BF16),
            pltpu.VMEM((FACTORS, full, cols), F32),
            pltpu.VMEM((n_wall, devices, slots, some * values), BF16),
            dma((n_wall,)),
        ]

    def out(some):
        return hbm((devices, n_wall, slots, some * values), BF16)

    cells, _, *more = scratch(1)
    sent, psi = call(
        functools.partial(first_kernel, planes),
        [VMEM] * 7,
        [out(1), hbm(psi.shape, F32)],
        "filter_first",
        24,
        [pltpu.VMEM(psi.shape, F32), cells, *more, dma((1,))],
        out_specs=[ANYWHERE, ANYWHERE],
    )(psi_main, low, high, factor, target, wall_first, halo_first)
    (noise, rest_low, rest_high, wall_scale, span_scale), sent = lax.optimization_barrier(
        ((noise, rest_low, rest_high, wall_scale, span_scale), sent)
    )
    got_first = send(sent)
    late = call(
        pack_late_kernel,
        [pl.BlockSpec((1, all_planes * rows, cols), lambda i: (trio - 1, 0, 0)), VMEM, VMEM],
        [hbm((planes * rows + 2 * rest * height, cols), BF16)] * n_wall,
        "pack_late",
        56,
        [dma((n_wall, 1 + 2 * rest))],
        grid=(1,),
        out_specs=[ANYWHERE] * n_wall,
    )(noise, rest_low, rest_high)
    late = spread(late)
    wall_rest, main_rest, halo_rest = taps(1, rest, struct, "taps_rest")
    sent = call(
        functools.partial(rest_kernel, planes),
        [VMEM] * (6 + 2 * n_wall),
        [out(rest)],
        "filter_rest",
        32,
        scratch(rest),
        out_specs=[ANYWHERE],
    )(psi, factor, target, wall_rest, main_rest, halo_rest, *early, *late)
    got_rest = send(sent)

    whole = hbm((1, devices * slots, trio * values * n_wall), BF16)
    block = (1, n_wall * slots, values * n_wall)

    def join(received, some, before):
        keep = [] if before is None else [before]
        narrow = values % LANES != 0
        return pl.pallas_call(
            functools.partial(join_narrow_kernel, some)
            if narrow
            else functools.partial(join_kernel, len(keep), some, n_wall),
            grid=(n_span, some) if narrow else (),
            in_specs=[
                pl.BlockSpec((n_wall, n_wall * slots, some * values), lambda s, c: (s, 0, 0)) if narrow else ANYWHERE
            ]
            + [ANYWHERE] * len(keep),
            out_specs=pl.BlockSpec(block, lambda s, c: (0, s, c + len(keep))) if narrow else ANYWHERE,
            out_shape=whole,
            scratch_shapes=[] if narrow else [pltpu.SemaphoreType.DMA((some, devices))],
            input_output_aliases={1: 0} if keep else {},
            compiler_params=pltpu.CompilerParams(vmem_limit_bytes=16 * 1024 * 1024),
            name="join",
        )(received, *keep)

    return join(got_rest, rest, join(got_first, 1, None))


def solution(mesh):
    return jax.shard_map(
        per_device,
        mesh=mesh,
        in_specs=(
            P(None, None, "wall", "span"),
            P(),
            P(),
            P(None, "wall"),
            P("wall"),
            P("wall", "span", None, None),
        ),
        out_specs=P(("span", "wall"), None, None),
        check_vma=False,
    )
```

time: 126 us -> 120 us (0.952)
  local copies, waits for them, and re-layouts: 7.25 us -> 0.96 us
  starting transfers between devices: 25.3 us -> 28.2 us
  waiting for transfers between devices: 66.8 us -> 65.3 us
    ppermute x0 -> x6, waiting for transfers between devices: none -> 16.7 us  [spread(): lax.ppermute(x, 'wall', [(i, (i + step) % n_wall) for i in range(n_wall)])]
    all_to_all x2, waiting for transfers between devices: 59.9 us -> 47.5 us  [send(): lax.all_to_all(x, ('span', 'wall'), 0, 0, tiled=True)]
    ppermute x0 -> x6, starting transfers between devices: none -> 9.74 us  [spread(): lax.ppermute(x, 'wall', [(i, (i + step) % n_wall) for i in range(n_wall)])]
    all_to_all x2 -> x1, waiting for transfers between devices: 6.95 us -> 0.68 us  [swap(): return lax.all_to_all(x, 'wall', 0, 0, tiled=True)]
    unnamed x24 -> x14, local copies, waits for them, and re-layouts: 7.18 us -> 0.96 us
    ppermute x2, starting transfers between devices: 7.57 us -> 4.21 us  [per_device(): lax.ppermute(first, 'span', down)]
    all_to_all x2 -> x1, starting transfers between devices: 7.9 us -> 5.18 us  [swap(): return lax.all_to_all(x, 'wall', 0, 0, tiled=True)]
    pallas_call x4 -> x8, Pallas kernels: 18.7 us -> 19.4 us  [the longest x1 5.99 us: per_device(): call(functools.partial(rest_kernel, planes), [VMEM] * (6 + 2 * n_wall), [...]
  transfers between devices with their start and end apart: 8 -> 13, of which waited for: 4 -> 6; matrix products, arithmetic and copies ran while one was open for 1% -> 0% of each run, Pallas kernels for 16% -> 18%
where the time goes in v4:
time: 120 us
  waiting for transfers between devices  65.3 us (54%)
  starting transfers between devices  28.2 us (24%)
  Pallas kernels  25.1 us (21%)
    all_to_all x2, waiting for transfers between devices, send(): lax.all_to_all(x, ('span', 'wall'), 0, 0, tiled=True)  47.5 us
    ppermute x6, waiting for transfers between devices, spread(): lax.ppermute(x, 'wall', [(i, (i + step) % n_wall) for i in range(n_wall)])  16.7 us
    ppermute x6, starting transfers between devices, spread(): lax.ppermute(x, 'wall', [(i, (i + step) % n_wall) for i in range(n_wall)])  9.74 us
    all_to_all x2, starting transfers between devices, send(): lax.all_to_all(x, ('span', 'wall'), 0, 0, tiled=True)  9.04 us
    pallas_call x1, Pallas kernels, per_device(): call(functools.partial(rest_kernel, planes), [VMEM] * (6 + 2 * n_wall), [...  5.99 us
    all_to_all x1, starting transfers between devices, swap(): return lax.all_to_all(x, 'wall', 0, 0, tiled=True)  5.18 us
    ppermute x2, starting transfers between devices, per_device(): lax.ppermute(first, 'span', down)  4.21 us
    pallas_call x1, Pallas kernels, per_device(): call(functools.partial(first_kernel, planes), [VMEM] * 7, [out(1), hbm(ps...  3.67 us
  transfers between devices with their start and end apart: 13, of which 6 were waited for; matrix products, arithmetic and copies ran while one was open for 0% of the time, Pallas kernels for 18%

profile of v4, /device:TPU:0, one launch (start us, length us, event | category | flops | bytes accessed | tf_op | source)
XLA Modules:
  0.0 119.8 jit_solution(17060945625696792314)
XLA Ops:
  0.0 2.0 %pack.1 = bf16[4,544,128]{2,1,0:T(8,128)(2,1)} custom-call(bf16[3,2048,128]{2,1,0:T(8,128)(2,1)} %bitcast.7, f32[6,64]{1,0:T(8,128)} %lund_ref.1, f32[1,64]{1,0:T(1,128)} %bitcast.12, s32[1,512]{1,0:T(1,128)} %bitcast.11), custom_call_target="tpu_custom_call" | custom-call | flops 1024 | bytes 1024 | tf_op jit(solution)/shard_map/pack/pallas_call | solution.py:467
  2.0 5.2 %all-to-all-start = ((bf16[4,544,128]{2,1,0:T(8,128)(2,1)}), bf16[4,544,128]{2,1,0:T(8,128)(2,1)S(1)}, u32[]{:S(2)}, u32[]{:S(2)}) async-start(bf16[4,544,128]{2,1,0:T(8,128)(2,1)} %pack.1), calls=%async_computation | async-start | bytes 1114112 | tf_op jit(solution)/shard_map/all_to_all | solution.py:460
  7.1 1.9 %pack_early.1 = (bf16[512,128]{1,0:T(8,128)(2,1)}, bf16[512,128]{1,0:T(8,128)(2,1)}, bf16[512,128]{1,0:T(8,128)(2,1)}, bf16[512,128]{1,0:T(8,128)(2,1)}) custom-call(bf16[3,2048,128]{2,1,0:T(8,128)(2,1)} %bitcast.8), custom_call_target="tpu_custom_call" | custom-call | flops 1024 | bytes 1024 | tf_op jit(solution)/shard_map/pack_early/pallas_call | solution.py:493
  9.1 2.1 %collective-permute-start.1 = (bf16[512,128]{1,0:T(8,128)(2,1)}, bf16[512,128]{1,0:T(8,128)(2,1)S(1)}, u32[]{:S(2)}, u32[]{:S(2)}) collective-permute-start(bf16[512,128]{1,0:T(8,128)(2,1)} %get-tuple-element.46), channel_id=1, source_target_pairs={{0,1},{1,2},{2,3},{3,0},{4,5},{5,6},{6,7},{7,4},{8,9},{9,10},{10,1... | collective-permute-start | bytes 393224 | tf_op jit(solution)/shard_map/ppermute | solution.py:507
  11.1 1.5 %collective-permute-start.2 = (bf16[512,128]{1,0:T(8,128)(2,1)}, bf16[512,128]{1,0:T(8,128)(2,1)S(1)}, u32[]{:S(2)}, u32[]{:S(2)}) collective-permute-start(bf16[512,128]{1,0:T(8,128)(2,1)} %get-tuple-element.47), channel_id=1, source_target_pairs={{0,2},{1,3},{2,0},{3,1},{4,6},{5,7},{6,4},{7,5},{8,10},{9,11},{10,... | collective-permute-start | bytes 393224 | tf_op jit(solution)/shard_map/ppermute | solution.py:507
  12.6 2.6 %edges_rest.1 = (bf16[4,2,96,128]{3,2,1,0:T(8,128)(2,1)}, bf16[4,2,96,128]{3,2,1,0:T(8,128)(2,1)}) custom-call(bf16[3,2048,128]{2,1,0:T(8,128)(2,1)} %bitcast.9), custom_call_target="tpu_custom_call" | custom-call | flops 1024 | bytes 1024 | tf_op jit(solution)/shard_map/edges_rest/pallas_call | solution.py:483
  15.2 1.9 %collective-permute-start.6 = (bf16[4,2,96,128]{3,2,1,0:T(8,128)(2,1)}, bf16[4,2,96,128]{3,2,1,0:T(8,128)(2,1)S(1)}, u32[]{:S(2)}, u32[]{:S(2)}) collective-permute-start(bf16[4,2,96,128]{3,2,1,0:T(8,128)(2,1)} %get-tuple-element.43), channel_id=1, source_target_pairs={{4,0},{8,4},{12,8},{16,12},{20,16},{24,20},{28,24},{0,28},{5,1},{9... | collective-permute-start | bytes 589832 | tf_op jit(solution)/shard_map/ppermute | solution.py:492
  17.2 0.0 collective-permute-start.5
  17.2 1.5 %collective-permute-start.3 = (bf16[512,128]{1,0:T(8,128)(2,1)}, bf16[512,128]{1,0:T(8,128)(2,1)S(1)}, u32[]{:S(2)}, u32[]{:S(2)}) collective-permute-start(bf16[512,128]{1,0:T(8,128)(2,1)} %get-tuple-element.48), channel_id=1, source_target_pairs={{0,3},{1,0},{2,1},{3,2},{4,7},{5,4},{6,5},{7,6},{8,11},{9,8},{10,9... | collective-permute-start | bytes 393224 | tf_op jit(solution)/shard_map/ppermute | solution.py:507
  18.6 0.7 all-to-all-done.noise_ref.in_ref
  19.3 0.3 edges_first.1
  19.6 0.0 collective-permute-done.1.rest_1_
  19.6 0.1 collective-permute-start
  19.7 1.4 %collective-permute-done.2.rest_2_ = bf16[512,128]{1,0:T(8,128)(2,1)S(1)} collective-permute-done((bf16[512,128]{1,0:T(8,128)(2,1)}, bf16[512,128]{1,0:T(8,128)(2,1)S(1)}, u32[]{:S(2)}, u32[]{:S(2)}) %collective-permute-start.2) | collective-permute-done | bytes 131104 | tf_op jit(solution)/shard_map/ppermute | solution.py:507
  21.1 2.3 %collective-permute-start.4 = (bf16[192,256]{1,0:T(8,128)(2,1)S(1)}, bf16[192,256]{1,0:T(8,128)(2,1)S(1)}, u32[]{:S(2)}, u32[]{:S(2)}) collective-permute-start(bf16[192,256]{1,0:T(8,128)(2,1)S(1)} %get-tuple-element.54), channel_id=1, source_target_pairs={{4,0},{8,4},{12,8},{16,12},{20,16},{24,20},{28,24},{0,28},{5,1},{9... | collective-permute-start | bytes 294920 | tf_op jit(solution)/shard_map/ppermute | solution.py:537
  23.4 0.0 copy-done.3
  23.4 0.0 copy-done.4
  23.4 0.9 taps_first.1
  24.3 0.4 small.1
  24.7 0.9 main_first.1.psi_in
  25.6 0.0 collective-permute-done.3.rest_3_
  25.6 0.4 collective-permute-done.low_ref
  26.0 0.0 collective-permute-done.4.high_ref
  26.0 3.7 %filter_first.1 = (bf16[32,4,32,128]{3,2,1,0:T(8,128)(2,1)}, f32[8,256,128]{2,1,0:T(8,128)}) custom-call(f32[8,256,128]{2,1,0:T(8,128)S(1)} %main_first.1.psi_in, bf16[192,256]{1,0:T(8,128)(2,1)S(1)} %collective-permute-done.low_ref, bf16[192,256]{1,0:T(8,128)(2,1)S(1)} %collective-permute-done.4.high_ref, f32[256,128]{1,0:T(8,128)S(1)} %get-tuple-element.55.factor_ref, ...), custom_call_target="tpu_custom_call" | custom-call | flops 1024 | bytes 1024 | tf_op jit(solution)/shard_map/filter_first/pallas_call | solution.py:559
  29.6 0.0 copy-start
  29.7 0.0 copy-start.2
  29.7 0.0 collective-permute-done.6.high_ref
  29.7 0.0 copy-start.5
  29.7 0.0 collective-permute-done.5.low_ref
  29.7 0.0 copy-start.6
  29.7 3.7 %all-to-all-start.2 = ((bf16[32,4,32,128]{3,2,1,0:T(8,128)(2,1)}), bf16[32,4,32,128]{3,2,1,0:T(8,128)(2,1)S(1)}, u32[]{:S(2)}, u32[]{:S(2)}) async-start(bf16[32,4,32,128]{3,2,1,0:T(8,128)(2,1)} %get-tuple-element.76), calls=%async_computation.2 | async-start | bytes 2097152 | tf_op jit(solution)/shard_map/all_to_all | solution.py:463
  33.4 0.0 copy-done.5
  33.4 2.3 %pack_late.1 = (bf16[896,128]{1,0:T(8,128)(2,1)}, bf16[896,128]{1,0:T(8,128)(2,1)}, bf16[896,128]{1,0:T(8,128)(2,1)}, bf16[896,128]{1,0:T(8,128)(2,1)}) custom-call(bf16[3,2048,128]{2,1,0:T(8,128)(2,1)} %bitcast.10, bf16[4,2,96,128]{3,2,1,0:T(8,128)(2,1)} %copy-done.6, bf16[4,2,96,128]{3,2,1,0:T(8,128)(2,1)} %copy-done.5), custom_call_target="tpu_custom_call" | custom-call | flops 1024 | bytes 1024 | tf_op jit(solution)/shard_map/pack_late/pallas_call | solution.py:572
  35.7 1.8 %collective-permute-start.7 = (bf16[896,128]{1,0:T(8,128)(2,1)}, bf16[896,128]{1,0:T(8,128)(2,1)S(1)}, u32[]{:S(2)}, u32[]{:S(2)}) collective-permute-start(bf16[896,128]{1,0:T(8,128)(2,1)} %get-tuple-element.73), channel_id=1, source_target_pairs={{0,1},{1,2},{2,3},{3,0},{4,5},{5,6},{6,7},{7,4},{8,9},{9,10},{10,1... | collective-permute-start | bytes 688136 | tf_op jit(solution)/shard_map/ppermute | solution.py:507
  37.5 1.5 %collective-permute-start.8 = (bf16[896,128]{1,0:T(8,128)(2,1)}, bf16[896,128]{1,0:T(8,128)(2,1)S(1)}, u32[]{:S(2)}, u32[]{:S(2)}) collective-permute-start(bf16[896,128]{1,0:T(8,128)(2,1)} %get-tuple-element.74), channel_id=1, source_target_pairs={{0,2},{1,3},{2,0},{3,1},{4,6},{5,7},{6,4},{7,5},{8,10},{9,11},{10,... | collective-permute-start | bytes 688136 | tf_op jit(solution)/shard_map/ppermute | solution.py:507
  39.0 1.5 %collective-permute-start.9 = (bf16[896,128]{1,0:T(8,128)(2,1)}, bf16[896,128]{1,0:T(8,128)(2,1)S(1)}, u32[]{:S(2)}, u32[]{:S(2)}) collective-permute-start(bf16[896,128]{1,0:T(8,128)(2,1)} %get-tuple-element.75), channel_id=1, source_target_pairs={{0,3},{1,0},{2,1},{3,2},{4,7},{5,4},{6,5},{7,6},{8,11},{9,8},{10,9... | collective-permute-start | bytes 688136 | tf_op jit(solution)/shard_map/ppermute | solution.py:507
  40.5 1.1 taps_rest.1
  41.6 10.3 %collective-permute-done.7.rest_5_ = bf16[896,128]{1,0:T(8,128)(2,1)S(1)} collective-permute-done((bf16[896,128]{1,0:T(8,128)(2,1)}, bf16[896,128]{1,0:T(8,128)(2,1)S(1)}, u32[]{:S(2)}, u32[]{:S(2)}) %collective-permute-start.7) | collective-permute-done | bytes 229408 | tf_op jit(solution)/shard_map/ppermute | solution.py:507
  51.8 5.0 %collective-permute-done.8.rest_6_ = bf16[896,128]{1,0:T(8,128)(2,1)S(1)} collective-permute-done((bf16[896,128]{1,0:T(8,128)(2,1)}, bf16[896,128]{1,0:T(8,128)(2,1)S(1)}, u32[]{:S(2)}, u32[]{:S(2)}) %collective-permute-start.8) | collective-permute-done | bytes 229408 | tf_op jit(solution)/shard_map/ppermute | solution.py:507
  56.9 0.0 collective-permute-done.9.rest_7_
  56.9 0.0 copy-done.2
  56.9 0.9 copy-done.1
  57.8 6.0 %filter_rest.1 = bf16[32,4,32,256]{3,2,1,0:T(8,128)(2,1)} custom-call(f32[8,256,128]{2,1,0:T(8,128)S(1)} %copy-done, f32[256,128]{1,0:T(8,128)S(1)} %get-tuple-element.55.factor_ref, s32[4,4,128]{2,1,0:T(4,128)S(1)} %get-tuple-element.56.target_ref, bf16[2,256,512]{2,1,0:T(8,128)(2,1)S(1)} %get-tuple-element.62.wall_ref, ...), custom_call_target="tpu_custom_call" | custom-call | flops 1024 | bytes 1024 | tf_op jit(solution)/shard_map/filter_rest/pallas_call | solution.py:584
  63.8 0.0 all-to-all-done.2
  63.8 5.4 %all-to-all-start.1 = ((bf16[32,4,32,256]{3,2,1,0:T(8,128)(2,1)}), bf16[32,4,32,256]{3,2,1,0:T(8,128)(2,1)S(1)}, u32[]{:S(2)}, u32[]{:S(2)}) async-start(bf16[32,4,32,256]{3,2,1,0:T(8,128)(2,1)} %filter_rest.1), calls=%async_computation.1 | async-start | bytes 4194304 | tf_op jit(solution)/shard_map/all_to_all | solution.py:463
  69.2 1.2 %join.2.rest_0_ = bf16[1,1024,1536]{2,1,0:T(8,128)(2,1)} custom-call(bf16[32,128,128]{2,1,0:T(8,128)(2,1)S(1)} %bitcast.6), custom_call_target="tpu_custom_call" | custom-call | tf_op jit(solution)/shard_map/join/pallas_call | solution.py:601
  70.5 47.5 %all-to-all-done.1 = bf16[32,4,32,256]{3,2,1,0:T(8,128)(2,1)S(1)} async-done(((bf16[32,4,32,256]{3,2,1,0:T(8,128)(2,1)}), bf16[32,4,32,256]{3,2,1,0:T(8,128)(2,1)S(1)}, u32[]{:S(2)}, u32[]{:S(2)}) %all-to-all-start.1) | async-done | bytes 2097184 | tf_op jit(solution)/shard_map/all_to_all | solution.py:463
  117.9 1.8 %join.3 = bf16[1,1024,1536]{2,1,0:T(8,128)(2,1)} custom-call(bf16[32,128,256]{2,1,0:T(8,128)(2,1)S(1)} %bitcast.5, bf16[1,1024,1536]{2,1,0:T(8,128)(2,1)} %join.2.rest_0_), custom_call_target="tpu_custom_call", output_to_operand_aliasing={{}: (1, {})} | custom-call | tf_op jit(solution)/shard_map/join/pallas_call | solution.py:601
  (5 shorter events, 0.0 us)
Async XLA Ops:
  2.0 17.4 %all-to-all-start = ((bf16[4,544,128]{2,1,0:T(8,128)(2,1)}), bf16[4,544,128]{2,1,0:T(8,128)(2,1)S(1)}, u32[]{:S(2)}, u32[]{:S(2)}) async-start(bf16[4,544,128]{2,1,0:T(8,128)(2,1)} %pack.1), calls=%async_computation | async-start | bytes 1114112 | tf_op jit(solution)/shard_map/all_to_all | solution.py:460
  7.1 16.2 %copy-start.3 = (f32[3]{0:T(128)S(1)}, f32[3]{0:T(128)}, u32[]{:S(2)}) copy-start(f32[3]{0:T(128)} %wall_scale.2) | copy-start | bytes 40
  7.1 16.2 %copy-start.4 = (f32[3]{0:T(128)S(1)}, f32[3]{0:T(128)}, u32[]{:S(2)}) copy-start(f32[3]{0:T(128)} %span_scale.2) | copy-start | bytes 40
  9.1 10.6 %collective-permute-start.1 = (bf16[512,128]{1,0:T(8,128)(2,1)}, bf16[512,128]{1,0:T(8,128)(2,1)S(1)}, u32[]{:S(2)}, u32[]{:S(2)}) collective-permute-start(bf16[512,128]{1,0:T(8,128)(2,1)} %get-tuple-element.46), channel_id=1, source_target_pairs={{0,1},{1,2},{2,3},{3,0},{4,5},{5,6},{6,7},{7,4},{8,9},{9,10},{10,1... | collective-permute-start | bytes 393224 | tf_op jit(solution)/shard_map/ppermute | solution.py:507
  11.1 9.9 %collective-permute-start.2 = (bf16[512,128]{1,0:T(8,128)(2,1)}, bf16[512,128]{1,0:T(8,128)(2,1)S(1)}, u32[]{:S(2)}, u32[]{:S(2)}) collective-permute-start(bf16[512,128]{1,0:T(8,128)(2,1)} %get-tuple-element.47), channel_id=1, source_target_pairs={{0,2},{1,3},{2,0},{3,1},{4,6},{5,7},{6,4},{7,5},{8,10},{9,11},{10,... | collective-permute-start | bytes 393224 | tf_op jit(solution)/shard_map/ppermute | solution.py:507
  15.2 14.4 %collective-permute-start.6 = (bf16[4,2,96,128]{3,2,1,0:T(8,128)(2,1)}, bf16[4,2,96,128]{3,2,1,0:T(8,128)(2,1)S(1)}, u32[]{:S(2)}, u32[]{:S(2)}) collective-permute-start(bf16[4,2,96,128]{3,2,1,0:T(8,128)(2,1)} %get-tuple-element.43), channel_id=1, source_target_pairs={{4,0},{8,4},{12,8},{16,12},{20,16},{24,20},{28,24},{0,28},{5,1},{9... | collective-permute-start | bytes 589832 | tf_op jit(solution)/shard_map/ppermute | solution.py:492
  17.2 12.5 %collective-permute-start.5 = (bf16[4,2,96,128]{3,2,1,0:T(8,128)(2,1)}, bf16[4,2,96,128]{3,2,1,0:T(8,128)(2,1)S(1)}, u32[]{:S(2)}, u32[]{:S(2)}) collective-permute-start(bf16[4,2,96,128]{3,2,1,0:T(8,128)(2,1)} %get-tuple-element.44), channel_id=1, source_target_pairs={{0,4},{4,8},{8,12},{12,16},{16,20},{20,24},{24,28},{28,0},{1,5},{5... | collective-permute-start | bytes 589832 | tf_op jit(solution)/shard_map/ppermute | solution.py:492
  17.2 8.4 %collective-permute-start.3 = (bf16[512,128]{1,0:T(8,128)(2,1)}, bf16[512,128]{1,0:T(8,128)(2,1)S(1)}, u32[]{:S(2)}, u32[]{:S(2)}) collective-permute-start(bf16[512,128]{1,0:T(8,128)(2,1)} %get-tuple-element.48), channel_id=1, source_target_pairs={{0,3},{1,0},{2,1},{3,2},{4,7},{5,4},{6,5},{7,6},{8,11},{9,8},{10,9... | collective-permute-start | bytes 393224 | tf_op jit(solution)/shard_map/ppermute | solution.py:507
  19.6 6.3 %collective-permute-start = (bf16[192,256]{1,0:T(8,128)(2,1)S(1)}, bf16[192,256]{1,0:T(8,128)(2,1)S(1)}, u32[]{:S(2)}, u32[]{:S(2)}) collective-permute-start(bf16[192,256]{1,0:T(8,128)(2,1)S(1)} %get-tuple-element.52), channel_id=1, source_target_pairs={{0,4},{4,8},{8,12},{12,16},{16,20},{20,24},{24,28},{28,0},{1,5},{5... | collective-permute-start | bytes 294920 | tf_op jit(solution)/shard_map/ppermute | solution.py:537
  21.1 4.9 %collective-permute-start.4 = (bf16[192,256]{1,0:T(8,128)(2,1)S(1)}, bf16[192,256]{1,0:T(8,128)(2,1)S(1)}, u32[]{:S(2)}, u32[]{:S(2)}) collective-permute-start(bf16[192,256]{1,0:T(8,128)(2,1)S(1)} %get-tuple-element.54), channel_id=1, source_target_pairs={{4,0},{8,4},{12,8},{16,12},{20,16},{24,20},{28,24},{0,28},{5,1},{9... | collective-permute-start | bytes 294920 | tf_op jit(solution)/shard_map/ppermute | solution.py:537
  29.6 27.2 %copy-start = (f32[8,256,128]{2,1,0:T(8,128)S(1)}, f32[8,256,128]{2,1,0:T(8,128)}, u32[]{:S(2)}) copy-start(f32[8,256,128]{2,1,0:T(8,128)} %get-tuple-element.58.psi_ref) | copy-start | bytes 3145732
  29.7 27.2 %copy-start.2 = (bf16[512,128]{1,0:T(8,128)(2,1)S(1)}, bf16[512,128]{1,0:T(8,128)(2,1)}, u32[]{:S(2)}) copy-start(bf16[512,128]{1,0:T(8,128)(2,1)} %get-tuple-element.65.rest_0_) | copy-start | bytes 393220
  29.7 3.7 %copy-start.5 = (bf16[4,2,96,128]{3,2,1,0:T(8,128)(2,1)}, bf16[4,2,96,128]{3,2,1,0:T(8,128)(2,1)S(1)}, u32[]{:S(2)}) copy-start(bf16[4,2,96,128]{3,2,1,0:T(8,128)(2,1)S(1)} %collective-permute-done.6.high_ref) | copy-start | bytes 589828
  29.7 3.7 %copy-start.6 = (bf16[4,2,96,128]{3,2,1,0:T(8,128)(2,1)}, bf16[4,2,96,128]{3,2,1,0:T(8,128)(2,1)S(1)}, u32[]{:S(2)}) copy-start(bf16[4,2,96,128]{3,2,1,0:T(8,128)(2,1)S(1)} %collective-permute-done.5.low_ref) | copy-start | bytes 589828
  29.7 34.1 %all-to-all-start.2 = ((bf16[32,4,32,128]{3,2,1,0:T(8,128)(2,1)}), bf16[32,4,32,128]{3,2,1,0:T(8,128)(2,1)S(1)}, u32[]{:S(2)}, u32[]{:S(2)}) async-start(bf16[32,4,32,128]{3,2,1,0:T(8,128)(2,1)} %get-tuple-element.76), calls=%async_computation.2 | async-start | bytes 2097152 | tf_op jit(solution)/shard_map/all_to_all | solution.py:463
  35.7 16.1 %collective-permute-start.7 = (bf16[896,128]{1,0:T(8,128)(2,1)}, bf16[896,128]{1,0:T(8,128)(2,1)S(1)}, u32[]{:S(2)}, u32[]{:S(2)}) collective-permute-start(bf16[896,128]{1,0:T(8,128)(2,1)} %get-tuple-element.73), channel_id=1, source_target_pairs={{0,1},{1,2},{2,3},{3,0},{4,5},{5,6},{6,7},{7,4},{8,9},{9,10},{10,1... | collective-permute-start | bytes 688136 | tf_op jit(solution)/shard_map/ppermute | solution.py:507
  37.5 19.3 %collective-permute-start.8 = (bf16[896,128]{1,0:T(8,128)(2,1)}, bf16[896,128]{1,0:T(8,128)(2,1)S(1)}, u32[]{:S(2)}, u32[]{:S(2)}) collective-permute-start(bf16[896,128]{1,0:T(8,128)(2,1)} %get-tuple-element.74), channel_id=1, source_target_pairs={{0,2},{1,3},{2,0},{3,1},{4,6},{5,7},{6,4},{7,5},{8,10},{9,11},{10,... | collective-permute-start | bytes 688136 | tf_op jit(solution)/shard_map/ppermute | solution.py:507
  39.0 17.9 %collective-permute-start.9 = (bf16[896,128]{1,0:T(8,128)(2,1)}, bf16[896,128]{1,0:T(8,128)(2,1)S(1)}, u32[]{:S(2)}, u32[]{:S(2)}) collective-permute-start(bf16[896,128]{1,0:T(8,128)(2,1)} %get-tuple-element.75), channel_id=1, source_target_pairs={{0,3},{1,0},{2,1},{3,2},{4,7},{5,4},{6,5},{7,6},{8,11},{9,8},{10,9... | collective-permute-start | bytes 688136 | tf_op jit(solution)/shard_map/ppermute | solution.py:507
  56.9 0.9 copy-start.1
  63.8 54.1 %all-to-all-start.1 = ((bf16[32,4,32,256]{3,2,1,0:T(8,128)(2,1)}), bf16[32,4,32,256]{3,2,1,0:T(8,128)(2,1)S(1)}, u32[]{:S(2)}, u32[]{:S(2)}) async-start(bf16[32,4,32,256]{3,2,1,0:T(8,128)(2,1)} %filter_rest.1), calls=%async_computation.1 | async-start | bytes 4194304 | tf_op jit(solution)/shard_map/all_to_all | solution.py:463

commit v5 on v4

--- a/solution.py
+++ b/solution.py
@@ -125,18 +125,6 @@
         copy.wait()
 
 
-def pack_planes_kernel(noise_ref, *rest):
-    out_refs, sems = rest[:-1], rest[-1]
-    walls = len(out_refs)
-    block = noise_ref.shape[1] // walls
-    me = lax.axis_index("wall")
-    copies = []
-    for step, out_ref in enumerate(out_refs):
-        start = pl.multiple_of(lax.rem(me + step, walls) * block, block)
-        copies.append(pltpu.make_async_copy(noise_ref.at[0, pl.ds(start, block)], out_ref, sems.at[step]))
-    run(copies)
-
-
 def pack_late_kernel(noise_ref, low_ref, high_ref, *rest):
     out_refs, sems = rest[:-1], rest[-1]
     walls, some, height, _ = low_ref.shape
@@ -145,10 +133,12 @@
     copies = []
     for step, out_ref in enumerate(out_refs):
         to = lax.rem(me + step, walls)
-        parts = [(noise_ref.at[0, pl.ds(pl.multiple_of(to * block, block), block)], 0, block)]
+        half = block // 2
+        source = pl.multiple_of(to * block + half, half)
+        parts = [(noise_ref.at[0, pl.ds(source, half)], 0, half)]
         for side, ref in enumerate((low_ref, high_ref)):
             for c in range(some):
-                parts.append((ref.at[to, c], block + (side * some + c) * height, height))
+                parts.append((ref.at[to, c], half + (side * some + c) * height, height))
         for part, (ref, start, size) in enumerate(parts):
             copies.append(
                 pltpu.make_async_copy(ref, out_ref.at[pl.ds(start, size)], sems.at[step, part])
@@ -199,8 +189,38 @@
         high_ref[at] = jnp.concatenate([e[HALO:] for e in edges], axis=0).astype(BF16)
 
 
-def raw_edges_kernel(noise_ref, low_ref, high_ref):
+def prepare_rest_kernel(noise_ref, low_ref, high_ref, *rest):
+    out_refs, sems = rest[:-1], rest[-1]
     walls, _, height, cols = low_ref.shape
+    block = noise_ref.shape[1] // walls
+    me = lax.axis_index("wall")
+    c = pl.program_id(0)
+    last = pl.num_programs(0) - 1
+
+    def copies(size):
+        out = []
+        for step, out_ref in enumerate(out_refs):
+            source = pl.multiple_of(lax.rem(me + step, walls) * block, block)
+            target = pl.multiple_of(c * block, block)
+            out.append(
+                pltpu.make_async_copy(
+                    noise_ref.at[0, pl.ds(source, size)], out_ref.at[pl.ds(target, size)], sems.at[step]
+                )
+            )
+        return out
+
+    def each(do):
+        @pl.when(c < last)
+        def _():
+            for copy in copies(block):
+                do(copy)
+
+        @pl.when(c == last)
+        def _():
+            for copy in copies(block // 2):
+                do(copy)
+
+    each(lambda copy: copy.start())
     pairs = height // HALO
     pick = edge_picker(cols)
     for w in range(walls):
@@ -210,6 +230,8 @@
             edges.append(lax.dot_general(pick, plane, ROWS_BY_ROWS, preferred_element_type=F32))
         low_ref[w, 0] = jnp.concatenate([e[:HALO] for e in edges], axis=0).astype(BF16)
         high_ref[w, 0] = jnp.concatenate([e[HALO:] for e in edges], axis=0).astype(BF16)
+
+    each(lambda copy: copy.wait())
 
 
 def swap_blocks(blocks, cols):
@@ -266,20 +288,25 @@
     return [span_product(smooth, halo_ref[odd]) for odd in range(2)]
 
 
-def main_kernel(planes, noise_ref, wall_ref, main_ref, psi_ref):
-    walls = noise_ref.shape[0]
-    rows = psi_ref.shape[1] // walls
-
-    def pair_step(pair, carry):
-        pair_planes = []
-        for odd in range(2):
-            at = pl.ds(pl.multiple_of((2 * pair + odd) * rows, rows), rows)
-            pair_planes.append(jnp.concatenate([noise_ref[w, at] for w in range(walls)], axis=0))
-        for odd, psi in enumerate(main_part(pair_planes, wall_ref[0], main_ref[0])):
-            psi_ref[2 * pair + odd] = psi
-        return carry
-
-    lax.fori_loop(0, planes // 2, pair_step, 0, unroll=True)
+def planes_of(refs, t, rows):
+    return [
+        jnp.concatenate([ref[at * rows : (at + 1) * rows] for ref in refs], axis=0) for at in (t, t + 1)
+    ]
+
+
+def main_first_kernel(planes, wall_ref, main_ref, noise_ref, psi_ref):
+    refs = [noise_ref.at[w] for w in range(noise_ref.shape[0])]
+    rows = psi_ref.shape[1] // len(refs)
+    for t in range(0, planes, 2):
+        psi_ref[t], psi_ref[t + 1] = main_part(planes_of(refs, t, rows), wall_ref[0], main_ref[0])
+
+
+def main_next_kernel(planes, wall_ref, main_ref, *rest):
+    *refs, psi_ref = rest
+    rows = psi_ref.shape[1] // len(refs)
+    for t in range(0, psi_ref.shape[0], 2):
+        c = t // planes
+        psi_ref[t], psi_ref[t + 1] = main_part(planes_of(refs, t, rows), wall_ref[c], main_ref[c])
 
 
 def widen(factor_ref, wide_ref, which):
@@ -354,30 +381,30 @@
 
 
 def rest_kernel(
-    planes, psi_ref, factor_ref, target_ref, wall_ref, main_ref, halo_ref, *rest,
+    planes, psi_ref, next_ref, factor_ref, target_ref, wall_ref, main_ref, halo_ref, *rest,
 ):
-    *in_refs, out_ref, cells_ref, tile_ref, wide_ref, sent_ref, sems = rest
-    early_refs, late_refs = in_refs[: len(in_refs) // 2], in_refs[len(in_refs) // 2 :]
+    *late_refs, out_ref, cells_ref, tile_ref, wide_ref, sent_ref, sems = rest
     full, cols = psi_ref.shape[1:]
     some = wall_ref.shape[0]
-    rows = full // len(early_refs)
+    rows = full // len(late_refs)
     pairs = planes // 2
     height = pairs * HALO
     widen(factor_ref, wide_ref, range(1, 6))
     for c in range(some):
-        starts = [planes * rows + (side * some + c) * height for side in range(2)]
+        starts = [planes * rows // 2 + (side * some + c) * height for side in range(2)]
         parts = [[ref[pl.ds(at, height)].astype(F32) for ref in late_refs] for at in starts]
         for pair, tile in enumerate(halo_tiles(parts, cols)):
             tile_ref[c * pairs + pair] = tile
 
-    def pair_step(pair, carry):
+    for pair in range(pairs):
         psi = []
         for c in range(some):
-            pair_planes = []
-            for odd in range(2):
-                at = pl.ds(pl.multiple_of((2 * pair + odd) * rows, rows), rows)
-                pair_planes.append(jnp.concatenate([ref[at] for ref in (early_refs, late_refs)[c]], axis=0))
-            main = main_part(pair_planes, wall_ref[c], main_ref[c])
+            at = c * planes + 2 * pair
+            if at < next_ref.shape[0]:
+                main = [next_ref[at], next_ref[at + 1]]
+            else:
+                at = at - next_ref.shape[0]
+                main = main_part(planes_of(late_refs, at, rows), wall_ref[c], main_ref[c])
             beside = halo_part(tile_ref[c * pairs + pair], wall_ref[c], halo_ref.at[c])
             psi.append([m + b for m, b in zip(main, beside)])
         for odd in range(2):
@@ -385,9 +412,6 @@
             p, q, r = psi_ref[t], psi[0][odd], psi[1][odd]
             place_cells(wide_ref[1] * p + wide_ref[2] * q, t, cells_ref, 0)
             place_cells(wide_ref[3] * p + wide_ref[4] * q + wide_ref[5] * r, t, cells_ref, 1)
-        return carry
-
-    lax.fori_loop(0, pairs, pair_step, 0, unroll=True)
     scatter_cells(cells_ref, target_ref, sent_ref, out_ref, sems)
 
 
@@ -480,26 +504,17 @@
     height = pairs * HALO
     edge = hbm((n_wall, rest, height, cols), BF16)
     spec = pl.BlockSpec((n_wall, 1, height, cols), lambda c: (0, c, 0, 0))
-    first, last = call(
-        raw_edges_kernel,
+    first, last, *early = call(
+        prepare_rest_kernel,
         [pl.BlockSpec((1, all_planes * rows, cols), lambda c: (c + 1, 0, 0))],
-        [edge, edge],
-        "edges_rest",
-        56,
+        [edge, edge] + [hbm((rest * planes * rows - planes * rows // 2, cols), BF16)] * n_wall,
+        "prepare_rest",
+        16,
+        [dma((n_wall,))],
         grid=(rest,),
-        out_specs=[spec, spec],
+        out_specs=[spec, spec] + [ANYWHERE] * n_wall,
     )(noise)
     rest_low, rest_high = lax.ppermute(last, "span", up), lax.ppermute(first, "span", down)
-    early = call(
-        pack_planes_kernel,
-        [pl.BlockSpec((1, all_planes * rows, cols), lambda i: (1, 0, 0))],
-        [hbm((planes * rows, cols), BF16)] * n_wall,
-        "pack_early",
-        56,
-        [dma((n_wall,))],
-        grid=(1,),
-        out_specs=[ANYWHERE] * n_wall,
-    )(noise)
     packed, _ = lax.optimization_barrier((packed, (first, last, early)))
 
     def spread(blocks):
@@ -536,12 +551,22 @@
     )(packed)
     low, high = lax.ppermute(last, "span", up), lax.ppermute(first, "span", down)
     early = spread(early)
-    low, early = lax.optimization_barrier((low, early))
+    late = call(
+        pack_late_kernel,
+        [pl.BlockSpec((1, all_planes * rows, cols), lambda i: (trio - 1, 0, 0)), VMEM, VMEM],
+        [hbm((planes * rows // 2 + 2 * rest * height, cols), BF16)] * n_wall,
+        "pack_late",
+        16,
+        [dma((n_wall, 1 + 2 * rest))],
+        grid=(1,),
+        out_specs=[ANYWHERE] * n_wall,
+    )(noise, rest_low, rest_high)
+    low, early, late = lax.optimization_barrier((low, early, late))
 
     psi = struct((planes, full, cols), F32)
-    psi_main = call(functools.partial(main_kernel, planes), [VMEM] * 3, [psi], "main_first", 16)(
-        packed, wall_first, main_first
-    )
+    psi_main = call(
+        functools.partial(main_first_kernel, planes), [VMEM] * 3, [psi], "main_first", 16
+    )(wall_first, main_first, packed)
 
     def scratch(some):
         return [
@@ -565,31 +590,26 @@
         [pltpu.VMEM(psi.shape, F32), cells, *more, dma((1,))],
         out_specs=[ANYWHERE, ANYWHERE],
     )(psi_main, low, high, factor, target, wall_first, halo_first)
-    (noise, rest_low, rest_high, wall_scale, span_scale), sent = lax.optimization_barrier(
-        ((noise, rest_low, rest_high, wall_scale, span_scale), sent)
-    )
+    (wall_scale, span_scale), sent = lax.optimization_barrier(((wall_scale, span_scale), sent))
     got_first = send(sent)
-    late = call(
-        pack_late_kernel,
-        [pl.BlockSpec((1, all_planes * rows, cols), lambda i: (trio - 1, 0, 0)), VMEM, VMEM],
-        [hbm((planes * rows + 2 * rest * height, cols), BF16)] * n_wall,
-        "pack_late",
-        56,
-        [dma((n_wall, 1 + 2 * rest))],
-        grid=(1,),
-        out_specs=[ANYWHERE] * n_wall,
-    )(noise, rest_low, rest_high)
     late = spread(late)
     wall_rest, main_rest, halo_rest = taps(1, rest, struct, "taps_rest")
+    psi_next = call(
+        functools.partial(main_next_kernel, planes),
+        [VMEM] * (2 + n_wall),
+        [struct((rest * planes - planes // 2, full, cols), F32)],
+        "main_next",
+        16,
+    )(wall_rest, main_rest, *early)
     sent = call(
         functools.partial(rest_kernel, planes),
-        [VMEM] * (6 + 2 * n_wall),
+        [VMEM] * (7 + n_wall),
         [out(rest)],
         "filter_rest",
         32,
         scratch(rest),
         out_specs=[ANYWHERE],
-    )(psi, factor, target, wall_rest, main_rest, halo_rest, *early, *late)
+    )(psi, psi_next, factor, target, wall_rest, main_rest, halo_rest, *late)
     got_rest = send(sent)
 
     whole = hbm((1, devices * slots, trio * values * n_wall), BF16)

time: 120 us -> 114 us (0.950)
  Pallas kernels: 25.1 us -> 22.3 us
  waiting for transfers between devices: 65.3 us -> 62.7 us
    ppermute x6, waiting for transfers between devices: 16.7 us -> 11.8 us  [spread(): lax.ppermute(x, 'wall', [(i, (i + step) % n_wall) for i in range(n_wall)])]
    ppermute x2, waiting for transfers between devices: 0.39 us -> 2.14 us  [per_device(): lax.ppermute(last, 'span', up)]
    pallas_call x4, Pallas kernels: 11.4 us -> 9.72 us  [the longest x1 5.34 us: per_device(): call(functools.partial(rest_kernel, planes), [VMEM] * (7 + n_wall), [out(...]
    all_to_all x2, waiting for transfers between devices: 47.5 us -> 48.8 us  [send(): lax.all_to_all(x, ('span', 'wall'), 0, 0, tiled=True)]
    pallas_call x1, Pallas kernels: 2.3 us -> 1.03 us  [per_device(): call(pack_late_kernel, [pl.BlockSpec((1, all_planes * rows, cols), lambda...]
  transfers between devices with their start and end apart: 13 -> 13, of which waited for: 6 -> 5; matrix products, arithmetic and copies ran while one was open for 0% -> 0% of each run, Pallas kernels for 18% -> 13%
where the time goes in v5:
time: 114 us; the launch traced here: 113 us
  waiting for transfers between devices  62.7 us (55%)
  starting transfers between devices  27.2 us (24%)
  Pallas kernels  22.3 us (20%)
    all_to_all x2, waiting for transfers between devices, send(): lax.all_to_all(x, ('span', 'wall'), 0, 0, tiled=True)  48.8 us
    ppermute x6, waiting for transfers between devices, spread(): lax.ppermute(x, 'wall', [(i, (i + step) % n_wall) for i in range(n_wall)])  11.8 us
    ppermute x6, starting transfers between devices, spread(): lax.ppermute(x, 'wall', [(i, (i + step) % n_wall) for i in range(n_wall)])  9.33 us
    all_to_all x2, starting transfers between devices, send(): lax.all_to_all(x, ('span', 'wall'), 0, 0, tiled=True)  8.31 us
    pallas_call x1, Pallas kernels, per_device(): call(functools.partial(rest_kernel, planes), [VMEM] * (7 + n_wall), [out(...  5.34 us
    all_to_all x1, starting transfers between devices, swap(): return lax.all_to_all(x, 'wall', 0, 0, tiled=True)  5.17 us
    ppermute x2, starting transfers between devices, per_device(): lax.ppermute(first, 'span', down)  4.3 us
    pallas_call x1, Pallas kernels, per_device(): call(functools.partial(first_kernel, planes), [VMEM] * 7, [out(1), hbm(ps...  3.68 us
  transfers between devices with their start and end apart: 13, of which 5 were waited for; matrix products, arithmetic and copies ran while one was open for 0% of the time, Pallas kernels for 13%

profile of v5, /device:TPU:0, one launch (start us, length us, event | category | flops | bytes accessed | tf_op | source)
XLA Modules:
  0.0 113.4 jit_solution(554403000251238691)
XLA Ops:
  0.0 2.1 %pack.1 = bf16[4,544,128]{2,1,0:T(8,128)(2,1)} custom-call(bf16[3,2048,128]{2,1,0:T(8,128)(2,1)} %bitcast.5, f32[6,64]{1,0:T(8,128)} %lund_ref.1, f32[1,64]{1,0:T(1,128)} %bitcast.11, s32[1,512]{1,0:T(1,128)} %bitcast.10), custom_call_target="tpu_custom_call" | custom-call | flops 1024 | bytes 1024 | tf_op jit(solution)/shard_map/pack/pallas_call | solution.py:491
  2.1 0.0 copy-start.6
  2.1 0.0 copy-start.7
  2.1 5.2 %all-to-all-start = ((bf16[4,544,128]{2,1,0:T(8,128)(2,1)}), bf16[4,544,128]{2,1,0:T(8,128)(2,1)S(1)}, u32[]{:S(2)}, u32[]{:S(2)}) async-start(bf16[4,544,128]{2,1,0:T(8,128)(2,1)} %pack.1), calls=%async_computation | async-start | bytes 1114112 | tf_op jit(solution)/shard_map/all_to_all | solution.py:484
  7.3 0.0 copy-done
  7.3 2.3 %prepare_rest.1 = (bf16[4,2,96,128]{3,2,1,0:T(8,128)(2,1)}, bf16[4,2,96,128]{3,2,1,0:T(8,128)(2,1)}, bf16[768,128]{1,0:T(8,128)(2,1)}, bf16[768,128]{1,0:T(8,128...) custom-call(bf16[3,2048,128]{2,1,0:T(8,128)(2,1)S(1)} %bitcast.6), custom_call_target="tpu_custom_call" | custom-call | flops 1024 | bytes 1024 | tf_op jit(solution)/shard_map/prepare_rest/pallas_call | solution.py:507
  9.6 2.9 %collective-permute-start.5 = (bf16[4,2,96,128]{3,2,1,0:T(8,128)(2,1)}, bf16[4,2,96,128]{3,2,1,0:T(8,128)(2,1)S(1)}, u32[]{:S(2)}, u32[]{:S(2)}) collective-permute-start(bf16[4,2,96,128]{3,2,1,0:T(8,128)(2,1)} %get-tuple-element.46), channel_id=1, source_target_pairs={{4,0},{8,4},{12,8},{16,12},{20,16},{24,20},{28,24},{0,28},{5,1},{9... | collective-permute-start | bytes 589832 | tf_op jit(solution)/shard_map/ppermute | solution.py:517
  12.5 0.0 collective-permute-start.4
  12.5 1.7 %collective-permute-start.1 = (bf16[768,128]{1,0:T(8,128)(2,1)}, bf16[768,128]{1,0:T(8,128)(2,1)S(1)}, u32[]{:S(2)}, u32[]{:S(2)}) collective-permute-start(bf16[768,128]{1,0:T(8,128)(2,1)} %get-tuple-element.49), channel_id=1, source_target_pairs={{0,1},{1,2},{2,3},{3,0},{4,5},{5,6},{6,7},{7,4},{8,9},{9,10},{10,1... | collective-permute-start | bytes 589832 | tf_op jit(solution)/shard_map/ppermute | solution.py:522
  14.2 1.5 %collective-permute-start.2 = (bf16[768,128]{1,0:T(8,128)(2,1)}, bf16[768,128]{1,0:T(8,128)(2,1)S(1)}, u32[]{:S(2)}, u32[]{:S(2)}) collective-permute-start(bf16[768,128]{1,0:T(8,128)(2,1)} %get-tuple-element.50), channel_id=1, source_target_pairs={{0,2},{1,3},{2,0},{3,1},{4,6},{5,7},{6,4},{7,5},{8,10},{9,11},{10,... | collective-permute-start | bytes 589832 | tf_op jit(solution)/shard_map/ppermute | solution.py:522
  15.7 1.5 %collective-permute-start.3 = (bf16[768,128]{1,0:T(8,128)(2,1)}, bf16[768,128]{1,0:T(8,128)(2,1)S(1)}, u32[]{:S(2)}, u32[]{:S(2)}) collective-permute-start(bf16[768,128]{1,0:T(8,128)(2,1)} %get-tuple-element.51), channel_id=1, source_target_pairs={{0,3},{1,0},{2,1},{3,2},{4,7},{5,4},{6,5},{7,6},{8,11},{9,8},{10,9... | collective-permute-start | bytes 589832 | tf_op jit(solution)/shard_map/ppermute | solution.py:522
  17.1 0.0 all-to-all-done.noise_ref.in_ref
  17.1 0.3 edges_first.1
  17.4 0.0 collective-permute-done.5.high_ref
  17.4 0.1 collective-permute-start
  17.5 2.1 %collective-permute-done.4.low_ref = bf16[4,2,96,128]{3,2,1,0:T(8,128)(2,1)S(1)} collective-permute-done((bf16[4,2,96,128]{3,2,1,0:T(8,128)(2,1)}, bf16[4,2,96,128]{3,2,1,0:T(8,128)(2,1)S(1)}, u32[]{:S(2)}, u32[]{:S(2)}) %collective-permute-start.4) | collective-permute-done | bytes 196640 | tf_op jit(solution)/shard_map/ppermute | solution.py:517
  19.6 1.4 %collective-permute-start.6 = (bf16[192,256]{1,0:T(8,128)(2,1)S(1)}, bf16[192,256]{1,0:T(8,128)(2,1)S(1)}, u32[]{:S(2)}, u32[]{:S(2)}) collective-permute-start(bf16[192,256]{1,0:T(8,128)(2,1)S(1)} %get-tuple-element.59), channel_id=1, source_target_pairs={{4,0},{8,4},{12,8},{16,12},{20,16},{24,20},{28,24},{0,28},{5,1},{9... | collective-permute-start | bytes 294920 | tf_op jit(solution)/shard_map/ppermute | solution.py:552
  21.0 0.9 taps_first.1
  22.0 1.0 pack_late.1
  23.0 0.4 small.1
  23.4 0.9 main_first.1.psi_in
  24.3 0.0 copy-start.10
  24.3 0.0 copy-start.9
  24.3 0.0 copy-start.8
  24.3 0.0 copy-start.2
  24.3 0.0 collective-permute-done.1.rest_1_
  24.3 0.0 collective-permute-done.2.rest_2_
  24.3 0.0 collective-permute-done.3.rest_3_
  24.4 0.0 copy-start.3
  24.4 0.0 collective-permute-done.low_ref
  24.4 0.0 collective-permute-done.6.high_ref
  24.4 3.7 %filter_first.1 = (bf16[32,4,32,128]{3,2,1,0:T(8,128)(2,1)}, f32[8,256,128]{2,1,0:T(8,128)}) custom-call(f32[8,256,128]{2,1,0:T(8,128)S(1)} %main_first.1.psi_in, bf16[192,256]{1,0:T(8,128)(2,1)S(1)} %collective-permute-done.low_ref, bf16[192,256]{1,0:T(8,128)(2,1)S(1)} %collective-permute-done.6.high_ref, f32[256,128]{1,0:T(8,128)S(1)} %get-tuple-element.60.factor_ref, ...), custom_call_target="tpu_custom_call" | custom-call | flops 1024 | bytes 1024 | tf_op jit(solution)/shard_map/filter_first/pallas_call | solution.py:584
  28.1 4.6 %all-to-all-start.2 = ((bf16[32,4,32,128]{3,2,1,0:T(8,128)(2,1)}), bf16[32,4,32,128]{3,2,1,0:T(8,128)(2,1)S(1)}, u32[]{:S(2)}, u32[]{:S(2)}) async-start(bf16[32,4,32,128]{3,2,1,0:T(8,128)(2,1)} %get-tuple-element.78), calls=%async_computation.2 | async-start | bytes 2097152 | tf_op jit(solution)/shard_map/all_to_all | solution.py:487
  32.7 1.8 %collective-permute-start.7 = (bf16[640,128]{1,0:T(8,128)(2,1)S(1)}, bf16[640,128]{1,0:T(8,128)(2,1)S(1)}, u32[]{:S(2)}, u32[]{:S(2)}) collective-permute-start(bf16[640,128]{1,0:T(8,128)(2,1)S(1)} %copy-done.10), channel_id=1, source_target_pairs={{0,1},{1,2},{2,3},{3,0},{4,5},{5,6},{6,7},{7,4},{8,9},{9,10},{10,1... | collective-permute-start | bytes 491528 | tf_op jit(solution)/shard_map/ppermute | solution.py:522
  34.5 1.5 %collective-permute-start.8 = (bf16[640,128]{1,0:T(8,128)(2,1)S(1)}, bf16[640,128]{1,0:T(8,128)(2,1)S(1)}, u32[]{:S(2)}, u32[]{:S(2)}) collective-permute-start(bf16[640,128]{1,0:T(8,128)(2,1)S(1)} %copy-done.9), channel_id=1, source_target_pairs={{0,2},{1,3},{2,0},{3,1},{4,6},{5,7},{6,4},{7,5},{8,10},{9,11},{10,... | collective-permute-start | bytes 491528 | tf_op jit(solution)/shard_map/ppermute | solution.py:522
  36.0 1.5 %collective-permute-start.9 = (bf16[640,128]{1,0:T(8,128)(2,1)S(1)}, bf16[640,128]{1,0:T(8,128)(2,1)S(1)}, u32[]{:S(2)}, u32[]{:S(2)}) collective-permute-start(bf16[640,128]{1,0:T(8,128)(2,1)S(1)} %copy-done.8), channel_id=1, source_target_pairs={{0,3},{1,0},{2,1},{3,2},{4,7},{5,4},{6,5},{7,6},{8,11},{9,8},{10,9... | collective-permute-start | bytes 491528 | tf_op jit(solution)/shard_map/ppermute | solution.py:522
  37.4 1.1 taps_rest.1
  38.6 0.9 copy-done.4
  39.5 1.2 %main_next.1.next_ref = f32[12,256,128]{2,1,0:T(8,128)S(1)} custom-call(bf16[2,256,512]{2,1,0:T(8,128)(2,1)S(1)} %get-tuple-element.67.wall_ref, bf16[2,256,256]{2,1,0:T(8,128)(2,1)S(1)} %get-tuple-element.68.main_ref, bf16[768,128]{1,0:T(8,128)(2,1)S(1)} %copy-done.2, bf16[768,128]{1,0:T(8,128)(2,1)S(1)} %collective-permute-done.1.rest_1_, ...), custom_call_target="tpu_custom_call" | custom-call | flops 1024 | bytes 1024 | tf_op jit(solution)/shard_map/main_next/pallas_call | solution.py:597
  40.6 8.5 %collective-permute-done.7.rest_1_ = bf16[640,128]{1,0:T(8,128)(2,1)S(1)} collective-permute-done((bf16[640,128]{1,0:T(8,128)(2,1)S(1)}, bf16[640,128]{1,0:T(8,128)(2,1)S(1)}, u32[]{:S(2)}, u32[]{:S(2)}) %collective-permute-start.7) | collective-permute-done | bytes 163872 | tf_op jit(solution)/shard_map/ppermute | solution.py:522
  49.2 3.2 %collective-permute-done.8.rest_2_ = bf16[640,128]{1,0:T(8,128)(2,1)S(1)} collective-permute-done((bf16[640,128]{1,0:T(8,128)(2,1)S(1)}, bf16[640,128]{1,0:T(8,128)(2,1)S(1)}, u32[]{:S(2)}, u32[]{:S(2)}) %collective-permute-start.8) | collective-permute-done | bytes 163872 | tf_op jit(solution)/shard_map/ppermute | solution.py:522
  52.4 0.0 collective-permute-done.9.rest_3_
  52.4 5.3 %filter_rest.1 = bf16[32,4,32,256]{3,2,1,0:T(8,128)(2,1)} custom-call(f32[8,256,128]{2,1,0:T(8,128)S(1)} %copy-done.1, f32[12,256,128]{2,1,0:T(8,128)S(1)} %main_next.1.next_ref, f32[256,128]{1,0:T(8,128)S(1)} %get-tuple-element.60.factor_ref, s32[4,4,128]{2,1,0:T(4,128)S(1)} %get-tuple-element.61.target_ref, ...), custom_call_target="tpu_custom_call" | custom-call | flops 1024 | bytes 1024 | tf_op jit(solution)/shard_map/filter_rest/pallas_call | solution.py:604
  57.7 1.4 %all-to-all-done.2 = bf16[32,4,32,128]{3,2,1,0:T(8,128)(2,1)S(1)} async-done(((bf16[32,4,32,128]{3,2,1,0:T(8,128)(2,1)}), bf16[32,4,32,128]{3,2,1,0:T(8,128)(2,1)S(1)}, u32[]{:S(2)}, u32[]{:S(2)}) %all-to-all-start.2) | async-done | bytes 1048608 | tf_op jit(solution)/shard_map/all_to_all | solution.py:487
  59.1 3.7 %all-to-all-start.1 = ((bf16[32,4,32,256]{3,2,1,0:T(8,128)(2,1)}), bf16[32,4,32,256]{3,2,1,0:T(8,128)(2,1)S(1)}, u32[]{:S(2)}, u32[]{:S(2)}) async-start(bf16[32,4,32,256]{3,2,1,0:T(8,128)(2,1)} %filter_rest.1), calls=%async_computation.1 | async-start | bytes 4194304 | tf_op jit(solution)/shard_map/all_to_all | solution.py:487
  62.8 1.2 %join.2.rest_0_ = bf16[1,1024,1536]{2,1,0:T(8,128)(2,1)} custom-call(bf16[32,128,128]{2,1,0:T(8,128)(2,1)S(1)} %bitcast.9), custom_call_target="tpu_custom_call" | custom-call | tf_op jit(solution)/shard_map/join/pallas_call | solution.py:621
  64.1 47.5 %all-to-all-done.1 = bf16[32,4,32,256]{3,2,1,0:T(8,128)(2,1)S(1)} async-done(((bf16[32,4,32,256]{3,2,1,0:T(8,128)(2,1)}), bf16[32,4,32,256]{3,2,1,0:T(8,128)(2,1)S(1)}, u32[]{:S(2)}, u32[]{:S(2)}) %all-to-all-start.1) | async-done | bytes 2097184 | tf_op jit(solution)/shard_map/all_to_all | solution.py:487
  111.6 1.8 %join.3 = bf16[1,1024,1536]{2,1,0:T(8,128)(2,1)} custom-call(bf16[32,128,256]{2,1,0:T(8,128)(2,1)S(1)} %bitcast.8, bf16[1,1024,1536]{2,1,0:T(8,128)(2,1)} %join.2.rest_0_), custom_call_target="tpu_custom_call", output_to_operand_aliasing={{}: (1, {})} | custom-call | tf_op jit(solution)/shard_map/join/pallas_call | solution.py:621
  (13 shorter events, 0.0 us)
Async XLA Ops:
  0.0 7.3 %copy-start = (bf16[3,32,64,128]{3,2,1,0:T(8,128)(2,1)S(1)}, bf16[3,32,64,128]{3,2,1,0:T(8,128)(2,1)}, u32[]{:S(2)}) copy-start(bf16[3,32,64,128]{3,2,1,0:T(8,128)(2,1)} %param.6) | copy-start | bytes 4718596
  2.1 19.0 %copy-start.6 = (f32[3]{0:T(128)S(1)}, f32[3]{0:T(128)}, u32[]{:S(2)}) copy-start(f32[3]{0:T(128)} %wall_scale.2) | copy-start | bytes 40
  2.1 18.9 %copy-start.7 = (f32[3]{0:T(128)S(1)}, f32[3]{0:T(128)}, u32[]{:S(2)}) copy-start(f32[3]{0:T(128)} %span_scale.2) | copy-start | bytes 40
  2.1 15.0 %all-to-all-start = ((bf16[4,544,128]{2,1,0:T(8,128)(2,1)}), bf16[4,544,128]{2,1,0:T(8,128)(2,1)S(1)}, u32[]{:S(2)}, u32[]{:S(2)}) async-start(bf16[4,544,128]{2,1,0:T(8,128)(2,1)} %pack.1), calls=%async_computation | async-start | bytes 1114112 | tf_op jit(solution)/shard_map/all_to_all | solution.py:484
  9.6 7.8 %collective-permute-start.5 = (bf16[4,2,96,128]{3,2,1,0:T(8,128)(2,1)}, bf16[4,2,96,128]{3,2,1,0:T(8,128)(2,1)S(1)}, u32[]{:S(2)}, u32[]{:S(2)}) collective-permute-start(bf16[4,2,96,128]{3,2,1,0:T(8,128)(2,1)} %get-tuple-element.46), channel_id=1, source_target_pairs={{4,0},{8,4},{12,8},{16,12},{20,16},{24,20},{28,24},{0,28},{5,1},{9... | collective-permute-start | bytes 589832 | tf_op jit(solution)/shard_map/ppermute | solution.py:517
  12.5 7.1 %collective-permute-start.4 = (bf16[4,2,96,128]{3,2,1,0:T(8,128)(2,1)}, bf16[4,2,96,128]{3,2,1,0:T(8,128)(2,1)S(1)}, u32[]{:S(2)}, u32[]{:S(2)}) collective-permute-start(bf16[4,2,96,128]{3,2,1,0:T(8,128)(2,1)} %get-tuple-element.47), channel_id=1, source_target_pairs={{0,4},{4,8},{8,12},{12,16},{16,20},{20,24},{24,28},{28,0},{1,5},{5... | collective-permute-start | bytes 589832 | tf_op jit(solution)/shard_map/ppermute | solution.py:517
  12.5 11.8 %collective-permute-start.1 = (bf16[768,128]{1,0:T(8,128)(2,1)}, bf16[768,128]{1,0:T(8,128)(2,1)S(1)}, u32[]{:S(2)}, u32[]{:S(2)}) collective-permute-start(bf16[768,128]{1,0:T(8,128)(2,1)} %get-tuple-element.49), channel_id=1, source_target_pairs={{0,1},{1,2},{2,3},{3,0},{4,5},{5,6},{6,7},{7,4},{8,9},{9,10},{10,1... | collective-permute-start | bytes 589832 | tf_op jit(solution)/shard_map/ppermute | solution.py:522
  14.2 10.1 %collective-permute-start.2 = (bf16[768,128]{1,0:T(8,128)(2,1)}, bf16[768,128]{1,0:T(8,128)(2,1)S(1)}, u32[]{:S(2)}, u32[]{:S(2)}) collective-permute-start(bf16[768,128]{1,0:T(8,128)(2,1)} %get-tuple-element.50), channel_id=1, source_target_pairs={{0,2},{1,3},{2,0},{3,1},{4,6},{5,7},{6,4},{7,5},{8,10},{9,11},{10,... | collective-permute-start | bytes 589832 | tf_op jit(solution)/shard_map/ppermute | solution.py:522
  15.7 8.7 %collective-permute-start.3 = (bf16[768,128]{1,0:T(8,128)(2,1)}, bf16[768,128]{1,0:T(8,128)(2,1)S(1)}, u32[]{:S(2)}, u32[]{:S(2)}) collective-permute-start(bf16[768,128]{1,0:T(8,128)(2,1)} %get-tuple-element.51), channel_id=1, source_target_pairs={{0,3},{1,0},{2,1},{3,2},{4,7},{5,4},{6,5},{7,6},{8,11},{9,8},{10,9... | collective-permute-start | bytes 589832 | tf_op jit(solution)/shard_map/ppermute | solution.py:522
  17.4 6.9 %collective-permute-start = (bf16[192,256]{1,0:T(8,128)(2,1)S(1)}, bf16[192,256]{1,0:T(8,128)(2,1)S(1)}, u32[]{:S(2)}, u32[]{:S(2)}) collective-permute-start(bf16[192,256]{1,0:T(8,128)(2,1)S(1)} %get-tuple-element.53), channel_id=1, source_target_pairs={{0,4},{4,8},{8,12},{12,16},{16,20},{20,24},{24,28},{28,0},{1,5},{5... | collective-permute-start | bytes 294920 | tf_op jit(solution)/shard_map/ppermute | solution.py:552
  19.6 4.7 %collective-permute-start.6 = (bf16[192,256]{1,0:T(8,128)(2,1)S(1)}, bf16[192,256]{1,0:T(8,128)(2,1)S(1)}, u32[]{:S(2)}, u32[]{:S(2)}) collective-permute-start(bf16[192,256]{1,0:T(8,128)(2,1)S(1)} %get-tuple-element.59), channel_id=1, source_target_pairs={{4,0},{8,4},{12,8},{16,12},{20,16},{24,20},{28,24},{0,28},{5,1},{9... | collective-permute-start | bytes 294920 | tf_op jit(solution)/shard_map/ppermute | solution.py:552
  24.3 8.4 %copy-start.10 = (bf16[640,128]{1,0:T(8,128)(2,1)S(1)}, bf16[640,128]{1,0:T(8,128)(2,1)}, u32[]{:S(2)}) copy-start(bf16[640,128]{1,0:T(8,128)(2,1)} %get-tuple-element.75) | copy-start | bytes 491524
  24.3 10.2 %copy-start.9 = (bf16[640,128]{1,0:T(8,128)(2,1)S(1)}, bf16[640,128]{1,0:T(8,128)(2,1)}, u32[]{:S(2)}) copy-start(bf16[640,128]{1,0:T(8,128)(2,1)} %get-tuple-element.76) | copy-start | bytes 491524
  24.3 11.7 %copy-start.8 = (bf16[640,128]{1,0:T(8,128)(2,1)S(1)}, bf16[640,128]{1,0:T(8,128)(2,1)}, u32[]{:S(2)}) copy-start(bf16[640,128]{1,0:T(8,128)(2,1)} %get-tuple-element.77) | copy-start | bytes 491524
  24.3 14.2 %copy-start.2 = (bf16[768,128]{1,0:T(8,128)(2,1)S(1)}, bf16[768,128]{1,0:T(8,128)(2,1)}, u32[]{:S(2)}) copy-start(bf16[768,128]{1,0:T(8,128)(2,1)} %get-tuple-element.69.rest_0_) | copy-start | bytes 589828
  24.4 3.7 %copy-start.3 = (bf16[768,128]{1,0:T(8,128)(2,1)}, bf16[768,128]{1,0:T(8,128)(2,1)S(1)}, u32[]{:S(2)}) copy-start(bf16[768,128]{1,0:T(8,128)(2,1)S(1)} %collective-permute-done.3.rest_3_) | copy-start | bytes 589828
  28.1 24.3 %copy-start.5 = (bf16[640,128]{1,0:T(8,128)(2,1)S(1)}, bf16[640,128]{1,0:T(8,128)(2,1)}, u32[]{:S(2)}) copy-start(bf16[640,128]{1,0:T(8,128)(2,1)} %get-tuple-element.74.rest_0_) | copy-start | bytes 491524
  28.1 31.0 %all-to-all-start.2 = ((bf16[32,4,32,128]{3,2,1,0:T(8,128)(2,1)}), bf16[32,4,32,128]{3,2,1,0:T(8,128)(2,1)S(1)}, u32[]{:S(2)}, u32[]{:S(2)}) async-start(bf16[32,4,32,128]{3,2,1,0:T(8,128)(2,1)} %get-tuple-element.78), calls=%async_computation.2 | async-start | bytes 2097152 | tf_op jit(solution)/shard_map/all_to_all | solution.py:487
  32.7 19.7 %copy-start.1 = (f32[8,256,128]{2,1,0:T(8,128)S(1)}, f32[8,256,128]{2,1,0:T(8,128)}, u32[]{:S(2)}) copy-start(f32[8,256,128]{2,1,0:T(8,128)} %get-tuple-element.63.psi_ref) | copy-start | bytes 3145732
  32.7 16.5 %collective-permute-start.7 = (bf16[640,128]{1,0:T(8,128)(2,1)S(1)}, bf16[640,128]{1,0:T(8,128)(2,1)S(1)}, u32[]{:S(2)}, u32[]{:S(2)}) collective-permute-start(bf16[640,128]{1,0:T(8,128)(2,1)S(1)} %copy-done.10), channel_id=1, source_target_pairs={{0,1},{1,2},{2,3},{3,0},{4,5},{5,6},{6,7},{7,4},{8,9},{9,10},{10,1... | collective-permute-start | bytes 491528 | tf_op jit(solution)/shard_map/ppermute | solution.py:522
  34.5 17.9 %collective-permute-start.8 = (bf16[640,128]{1,0:T(8,128)(2,1)S(1)}, bf16[640,128]{1,0:T(8,128)(2,1)S(1)}, u32[]{:S(2)}, u32[]{:S(2)}) collective-permute-start(bf16[640,128]{1,0:T(8,128)(2,1)S(1)} %copy-done.9), channel_id=1, source_target_pairs={{0,2},{1,3},{2,0},{3,1},{4,6},{5,7},{6,4},{7,5},{8,10},{9,11},{10,... | collective-permute-start | bytes 491528 | tf_op jit(solution)/shard_map/ppermute | solution.py:522
  36.0 16.4 %collective-permute-start.9 = (bf16[640,128]{1,0:T(8,128)(2,1)S(1)}, bf16[640,128]{1,0:T(8,128)(2,1)S(1)}, u32[]{:S(2)}, u32[]{:S(2)}) collective-permute-start(bf16[640,128]{1,0:T(8,128)(2,1)S(1)} %copy-done.8), channel_id=1, source_target_pairs={{0,3},{1,0},{2,1},{3,2},{4,7},{5,4},{6,5},{7,6},{8,11},{9,8},{10,9... | collective-permute-start | bytes 491528 | tf_op jit(solution)/shard_map/ppermute | solution.py:522
  38.5 0.9 copy-start.4
  59.1 52.5 %all-to-all-start.1 = ((bf16[32,4,32,256]{3,2,1,0:T(8,128)(2,1)}), bf16[32,4,32,256]{3,2,1,0:T(8,128)(2,1)S(1)}, u32[]{:S(2)}, u32[]{:S(2)}) async-start(bf16[32,4,32,256]{3,2,1,0:T(8,128)(2,1)} %filter_rest.1), calls=%async_computation.1 | async-start | bytes 4194304 | tf_op jit(solution)/shard_map/all_to_all | solution.py:487

commit v6 on v5

--- a/solution.py
+++ b/solution.py
@@ -12,6 +12,7 @@
 EDGE = 4
 LANES = 128
 FACTORS = 7
+CORES = 2
 F32 = jnp.float32
 BF16 = jnp.bfloat16
 VMEM = pl.BlockSpec(memory_space=pltpu.VMEM)
@@ -61,7 +62,8 @@
     target = (n % (cols // EDGE)) * EDGE + n // (cols // EDGE)
     k = iota((cols, cols), 0)
     side, odd, r = k // (2 * HALO), (k // HALO) % 2, k % HALO
-    z = jnp.where(side == 0, r - HALO, cols + r)
+    core = lax.rem(lax.axis_index("span"), CORES)
+    z = jnp.where(side + core == 1, r - HALO, cols + r)
 
     def span_matrix(scale, distance, valid):
         high, low = split(tap_values(scale, distance, valid))
@@ -125,20 +127,20 @@
         copy.wait()
 
 
-def pack_late_kernel(noise_ref, low_ref, high_ref, *rest):
+def pack_late_kernel(noise_ref, near_ref, far_ref, *rest):
     out_refs, sems = rest[:-1], rest[-1]
-    walls, some, height, _ = low_ref.shape
+    walls, some, height, _ = near_ref.shape
     block = noise_ref.shape[1] // walls
     me = lax.axis_index("wall")
     copies = []
     for step, out_ref in enumerate(out_refs):
         to = lax.rem(me + step, walls)
-        half = block // 2
-        source = pl.multiple_of(to * block + half, half)
-        parts = [(noise_ref.at[0, pl.ds(source, half)], 0, half)]
-        for side, ref in enumerate((low_ref, high_ref)):
+        left = out_ref.shape[0] - 2 * some * height
+        source = pl.multiple_of(to * block + block - left, math.gcd(block, left))
+        parts = [(noise_ref.at[0, pl.ds(source, left)], 0, left)]
+        for side, ref in enumerate((near_ref, far_ref)):
             for c in range(some):
-                parts.append((ref.at[to, c], half + (side * some + c) * height, height))
+                parts.append((ref.at[to, c], left + (side * some + c) * height, height))
         for part, (ref, start, size) in enumerate(parts):
             copies.append(
                 pltpu.make_async_copy(ref, out_ref.at[pl.ds(start, size)], sems.at[step, part])
@@ -168,14 +170,15 @@
 
 
 def edge_picker(cols):
-    wide = 2 * HALO
-    row, col = iota((wide, cols), 0), iota((wide, cols), 1)
-    return jnp.where(col == jnp.where(row < HALO, row, cols - wide + row), 1.0, 0.0).astype(BF16)
-
-
-def edges_kernel(planes, noise_ref, low_ref, high_ref):
+    core = lax.rem(lax.axis_index("span"), CORES)
+    row, col = iota((2 * HALO, cols), 0), iota((2 * HALO, cols), 1)
+    start = jnp.where(row // HALO == core, cols - HALO, 0)
+    return jnp.where(col == start + row % HALO, 1.0, 0.0).astype(BF16)
+
+
+def edges_kernel(planes, noise_ref, near_ref, far_ref):
     walls, _, cols = noise_ref.shape
-    rows = low_ref.shape[1] // walls
+    rows = near_ref.shape[1] // walls
     wide = 2 * HALO
     pick = edge_picker(cols)
     for pair in range(planes // 2):
@@ -185,13 +188,13 @@
             plane = jnp.concatenate(plane, axis=0)
             edges.append(lax.dot_general(pick, plane, ROWS_BY_ROWS, preferred_element_type=F32))
         at = pl.ds(pair * wide, wide)
-        low_ref[at] = jnp.concatenate([e[:HALO] for e in edges], axis=0).astype(BF16)
-        high_ref[at] = jnp.concatenate([e[HALO:] for e in edges], axis=0).astype(BF16)
-
-
-def prepare_rest_kernel(noise_ref, low_ref, high_ref, *rest):
+        near_ref[at] = jnp.concatenate([e[:HALO] for e in edges], axis=0).astype(BF16)
+        far_ref[at] = jnp.concatenate([e[HALO:] for e in edges], axis=0).astype(BF16)
+
+
+def prepare_rest_kernel(noise_ref, near_ref, far_ref, *rest):
     out_refs, sems = rest[:-1], rest[-1]
-    walls, _, height, cols = low_ref.shape
+    walls, _, height, cols = near_ref.shape
     block = noise_ref.shape[1] // walls
     me = lax.axis_index("wall")
     c = pl.program_id(0)
@@ -217,7 +220,7 @@
 
         @pl.when(c == last)
         def _():
-            for copy in copies(block // 2):
+            for copy in copies(out_refs[0].shape[0] - last * block):
                 do(copy)
 
     each(lambda copy: copy.start())
@@ -228,8 +231,8 @@
         for pair in range(pairs):
             plane = noise_ref[0, (w * pairs + pair) * cols : (w * pairs + pair + 1) * cols]
             edges.append(lax.dot_general(pick, plane, ROWS_BY_ROWS, preferred_element_type=F32))
-        low_ref[w, 0] = jnp.concatenate([e[:HALO] for e in edges], axis=0).astype(BF16)
-        high_ref[w, 0] = jnp.concatenate([e[HALO:] for e in edges], axis=0).astype(BF16)
+        near_ref[w, 0] = jnp.concatenate([e[:HALO] for e in edges], axis=0).astype(BF16)
+        far_ref[w, 0] = jnp.concatenate([e[HALO:] for e in edges], axis=0).astype(BF16)
 
     each(lambda copy: copy.wait())
 
@@ -355,7 +358,7 @@
 
 
 def first_kernel(
-    planes, psi_in, low_ref, high_ref, factor_ref, target_ref, wall_ref, halo_ref,
+    planes, psi_in, near_ref, far_ref, factor_ref, target_ref, wall_ref, halo_ref,
     out_ref, psi_out, psi_ref, cells_ref, wide_ref, sent_ref, sems, psi_sem,
 ):
     full, cols = psi_ref.shape[1:]
@@ -364,7 +367,7 @@
 
     def pair_step(pair, carry):
         at = pl.ds(pl.multiple_of(pair * wide, wide), wide)
-        tile = [low_ref[at], high_ref[at], jnp.zeros((cols - 2 * wide, full), BF16)]
+        tile = [near_ref[at], far_ref[at], jnp.zeros((cols - 2 * wide, full), BF16)]
         beside = halo_part(jnp.concatenate(tile, axis=0), wall_ref[0], halo_ref.at[0])
         for odd in range(2):
             t = 2 * pair + odd
@@ -391,7 +394,8 @@
     height = pairs * HALO
     widen(factor_ref, wide_ref, range(1, 6))
     for c in range(some):
-        starts = [planes * rows // 2 + (side * some + c) * height for side in range(2)]
+        left = (some * planes - next_ref.shape[0]) * rows
+        starts = [left + (side * some + c) * height for side in range(2)]
         parts = [[ref[pl.ds(at, height)].astype(F32) for ref in late_refs] for at in starts]
         for pair, tile in enumerate(halo_tiles(parts, cols)):
             tile_ref[c * pairs + pair] = tile
@@ -415,34 +419,33 @@
     scatter_cells(cells_ref, target_ref, sent_ref, out_ref, sems)
 
 
-def join_kernel(first, some, walls, in_ref, *rest):
+def join_kernel(first, some, in_ref, *rest):
     out_ref, sems = rest[-2:]
-    devices, height, width = in_ref.shape
+    _, walls, _, width = in_ref.shape
     values = width // some
-    copies = []
-    for c in range(some):
-        for s in range(devices // walls):
-            for w in range(walls):
-                copies.append(
-                    pltpu.make_async_copy(
-                        in_ref.at[s * walls + w, :, pl.ds(c * values, values)],
-                        out_ref.at[0, pl.ds(s * height, height), pl.ds(((c + first) * walls + w) * values, values)],
-                        sems.at[c, s * walls + w],
-                    )
-                )
-    run(copies)
+    run(
+        [
+            pltpu.make_async_copy(
+                in_ref.at[:, w, :, pl.ds(c * values, values)],
+                out_ref.at[:, :, pl.ds(((c + first) * walls + w) * values, values)],
+                sems.at[c, w],
+            )
+            for c in range(some)
+            for w in range(walls)
+        ]
+    )
 
 
 def join_narrow_kernel(some, in_ref, *rest):
     out_ref = rest[-1]
-    walls, _, width = in_ref.shape
+    _, walls, _, width = in_ref.shape
     values = width // some
     for c in range(some):
 
         @pl.when(pl.program_id(1) == c)
         def _():
             for w in range(walls):
-                out_ref[0, :, w * values : (w + 1) * values] = in_ref[w, :, c * values : (c + 1) * values]
+                out_ref[0, :, w * values : (w + 1) * values] = in_ref[0, w, :, c * values : (c + 1) * values]
 
 
 def per_device(noise, wall_scale, span_scale, lund_factor, mean_velocity, owner_map):
@@ -460,6 +463,7 @@
     slots = max(8, 2 * elements // devices)
     count = elements // cols
     rest = trio - 1
+    ahead = rest * planes - planes // 2
     struct = jax.ShapeDtypeStruct
     hbm = pltpu.MemorySpace.HBM
 
@@ -477,8 +481,11 @@
             name=name,
         )
 
-    up = [(i, (i + 1) % n_span) for i in range(n_span)]
-    down = [(b, a) for a, b in up]
+    core_pairs = [(i, i ^ 1) for i in range(n_span)]
+    chip_pairs = [(i, (i + 2 * (i % CORES) - 1) % n_span) for i in range(n_span)]
+
+    def exchange(near, far):
+        return lax.ppermute(near, "span", core_pairs), lax.ppermute(far, "span", chip_pairs)
 
     def swap(x):
         return lax.all_to_all(x, "wall", 0, 0, tiled=True)
@@ -504,18 +511,18 @@
     height = pairs * HALO
     edge = hbm((n_wall, rest, height, cols), BF16)
     spec = pl.BlockSpec((n_wall, 1, height, cols), lambda c: (0, c, 0, 0))
-    first, last, *early = call(
+    near, far, *early = call(
         prepare_rest_kernel,
         [pl.BlockSpec((1, all_planes * rows, cols), lambda c: (c + 1, 0, 0))],
-        [edge, edge] + [hbm((rest * planes * rows - planes * rows // 2, cols), BF16)] * n_wall,
+        [edge, edge] + [hbm((ahead * rows, cols), BF16)] * n_wall,
         "prepare_rest",
         16,
         [dma((n_wall,))],
         grid=(rest,),
         out_specs=[spec, spec] + [ANYWHERE] * n_wall,
     )(noise)
-    rest_low, rest_high = lax.ppermute(last, "span", up), lax.ppermute(first, "span", down)
-    packed, _ = lax.optimization_barrier((packed, (first, last, early)))
+    rest_near, rest_far = exchange(near, far)
+    packed, _ = lax.optimization_barrier((packed, (near, far, early)))
 
     def spread(blocks):
         return [blocks[0]] + [
@@ -546,22 +553,22 @@
     )(packed)
 
     edge = struct((planes * HALO, full), BF16)
-    first, last = call(
+    near, far = call(
         functools.partial(edges_kernel, planes), [VMEM], [edge, edge], "edges_first", 16
     )(packed)
-    low, high = lax.ppermute(last, "span", up), lax.ppermute(first, "span", down)
+    near, far = exchange(near, far)
     early = spread(early)
     late = call(
         pack_late_kernel,
         [pl.BlockSpec((1, all_planes * rows, cols), lambda i: (trio - 1, 0, 0)), VMEM, VMEM],
-        [hbm((planes * rows // 2 + 2 * rest * height, cols), BF16)] * n_wall,
+        [hbm(((rest * planes - ahead) * rows + 2 * rest * height, cols), BF16)] * n_wall,
         "pack_late",
         16,
         [dma((n_wall, 1 + 2 * rest))],
         grid=(1,),
         out_specs=[ANYWHERE] * n_wall,
-    )(noise, rest_low, rest_high)
-    low, early, late = lax.optimization_barrier((low, early, late))
+    )(noise, rest_near, rest_far)
+    near, early, late = lax.optimization_barrier((near, early, late))
 
     psi = struct((planes, full, cols), F32)
     psi_main = call(
@@ -589,7 +596,7 @@
         24,
         [pltpu.VMEM(psi.shape, F32), cells, *more, dma((1,))],
         out_specs=[ANYWHERE, ANYWHERE],
-    )(psi_main, low, high, factor, target, wall_first, halo_first)
+    )(psi_main, near, far, factor, target, wall_first, halo_first)
     (wall_scale, span_scale), sent = lax.optimization_barrier(((wall_scale, span_scale), sent))
     got_first = send(sent)
     late = spread(late)
@@ -597,7 +604,7 @@
     psi_next = call(
         functools.partial(main_next_kernel, planes),
         [VMEM] * (2 + n_wall),
-        [struct((rest * planes - planes // 2, full, cols), F32)],
+        [struct((ahead, full, cols), F32)],
         "main_next",
         16,
     )(wall_rest, main_rest, *early)
@@ -612,30 +619,30 @@
     )(psi, psi_next, factor, target, wall_rest, main_rest, halo_rest, *late)
     got_rest = send(sent)
 
-    whole = hbm((1, devices * slots, trio * values * n_wall), BF16)
-    block = (1, n_wall * slots, values * n_wall)
+    whole = hbm((n_span, n_wall * slots, trio * values * n_wall), BF16)
+    narrow = values % LANES != 0
 
     def join(received, some, before):
         keep = [] if before is None else [before]
-        narrow = values % LANES != 0
+        shape = (n_span, n_wall, n_wall * slots, some * values)
         return pl.pallas_call(
             functools.partial(join_narrow_kernel, some)
             if narrow
-            else functools.partial(join_kernel, len(keep), some, n_wall),
+            else functools.partial(join_kernel, len(keep), some),
             grid=(n_span, some) if narrow else (),
-            in_specs=[
-                pl.BlockSpec((n_wall, n_wall * slots, some * values), lambda s, c: (s, 0, 0)) if narrow else ANYWHERE
-            ]
+            in_specs=[pl.BlockSpec((1, *shape[1:]), lambda s, c: (s, 0, 0, 0)) if narrow else VMEM]
             + [ANYWHERE] * len(keep),
-            out_specs=pl.BlockSpec(block, lambda s, c: (0, s, c + len(keep))) if narrow else ANYWHERE,
+            out_specs=pl.BlockSpec((1, n_wall * slots, values * n_wall), lambda s, c: (s, 0, c + len(keep)))
+            if narrow
+            else ANYWHERE,
             out_shape=whole,
-            scratch_shapes=[] if narrow else [pltpu.SemaphoreType.DMA((some, devices))],
+            scratch_shapes=[] if narrow else [dma((some, n_wall))],
             input_output_aliases={1: 0} if keep else {},
             compiler_params=pltpu.CompilerParams(vmem_limit_bytes=16 * 1024 * 1024),
             name="join",
-        )(received, *keep)
-
-    return join(got_rest, rest, join(got_first, 1, None))
+        )(received.reshape(shape), *keep)
+
+    return join(got_rest, rest, join(got_first, 1, None)).reshape(1, devices * slots, -1)
 
 
 def solution(mesh):

time: 114 us -> 113 us (level)
  starting transfers between devices: 27.2 us -> 29.2 us
  waiting for transfers between devices: 62.7 us -> 61.1 us
    ppermute x4, starting transfers between devices: 4.36 us -> 6.6 us  [the longest x2 6.46 us: exchange(): lax.ppermute(far, 'span', chip_pairs)]
    ppermute x4, waiting for transfers between devices: 2.14 us -> 0.29 us  [the longest x2 0.28 us: exchange(): lax.ppermute(far, 'span', chip_pairs)]
where the time goes in v6:
time: 113 us
  waiting for transfers between devices  61.1 us (54%)
  starting transfers between devices  29.2 us (26%)
  Pallas kernels  21.6 us (19%)
    all_to_all x2, waiting for transfers between devices, send(): lax.all_to_all(x, ('span', 'wall'), 0, 0, tiled=True)  49.1 us
    ppermute x6, waiting for transfers between devices, spread(): lax.ppermute(x, 'wall', [(i, (i + step) % n_wall) for i in range(n_wall)])  11.7 us
    ppermute x6, starting transfers between devices, spread(): lax.ppermute(x, 'wall', [(i, (i + step) % n_wall) for i in range(n_wall)])  9.69 us
    all_to_all x2, starting transfers between devices, send(): lax.all_to_all(x, ('span', 'wall'), 0, 0, tiled=True)  7.7 us
    ppermute x2, starting transfers between devices, exchange(): lax.ppermute(far, 'span', chip_pairs)  6.46 us
    pallas_call x1, Pallas kernels, per_device(): call(functools.partial(rest_kernel, planes), [VMEM] * (7 + n_wall), [out(...  5.34 us
    all_to_all x1, starting transfers between devices, swap(): return lax.all_to_all(x, 'wall', 0, 0, tiled=True)  5.17 us
    pallas_call x1, Pallas kernels, per_device(): call(functools.partial(first_kernel, planes), [VMEM] * 7, [out(1), hbm(ps...  3.67 us
  transfers between devices with their start and end apart: 13, of which 5 were waited for; matrix products, arithmetic and copies ran while one was open for 0% of the time, Pallas kernels for 13%

profile of v6, /device:TPU:0, one launch (start us, length us, event | category | flops | bytes accessed | tf_op | source)
XLA Modules:
  0.0 113.1 jit_solution(15704879383502052113)
XLA Ops:
  0.0 2.1 %pack.1 = bf16[4,544,128]{2,1,0:T(8,128)(2,1)} custom-call(bf16[3,2048,128]{2,1,0:T(8,128)(2,1)} %bitcast.6, f32[6,64]{1,0:T(8,128)} %lund_ref.1, f32[1,64]{1,0:T(1,128)} %bitcast.12, s32[1,512]{1,0:T(1,128)} %bitcast.11), custom_call_target="tpu_custom_call" | custom-call | flops 1024 | bytes 1024 | tf_op jit(solution)/shard_map/pack/pallas_call | solution.py:498
  2.1 0.0 copy-start.6
  2.1 0.0 copy-start.7
  2.1 5.2 %all-to-all-start = ((bf16[4,544,128]{2,1,0:T(8,128)(2,1)}), bf16[4,544,128]{2,1,0:T(8,128)(2,1)S(1)}, u32[]{:S(2)}, u32[]{:S(2)}) async-start(bf16[4,544,128]{2,1,0:T(8,128)(2,1)} %pack.1), calls=%async_computation | async-start | bytes 1114112 | tf_op jit(solution)/shard_map/all_to_all | solution.py:491
  7.3 0.0 copy-done
  7.3 2.3 %prepare_rest.1 = (bf16[4,2,96,128]{3,2,1,0:T(8,128)(2,1)}, bf16[4,2,96,128]{3,2,1,0:T(8,128)(2,1)}, bf16[768,128]{1,0:T(8,128)(2,1)}, bf16[768,128]{1,0:T(8,128...) custom-call(bf16[3,2048,128]{2,1,0:T(8,128)(2,1)S(1)} %bitcast.7), custom_call_target="tpu_custom_call" | custom-call | flops 1024 | bytes 1024 | tf_op jit(solution)/shard_map/prepare_rest/pallas_call | solution.py:514
  9.6 0.1 collective-permute-start.4
  9.7 3.7 %collective-permute-start.5 = (bf16[4,2,96,128]{3,2,1,0:T(8,128)(2,1)}, bf16[4,2,96,128]{3,2,1,0:T(8,128)(2,1)S(1)}, u32[]{:S(2)}, u32[]{:S(2)}) collective-permute-start(bf16[4,2,96,128]{3,2,1,0:T(8,128)(2,1)} %get-tuple-element.47), channel_id=1, source_target_pairs={{0,28},{4,8},{8,4},{12,16},{16,12},{20,24},{24,20},{28,0},{1,29},{... | collective-permute-start | bytes 589832 | tf_op jit(solution)/shard_map/ppermute | solution.py:488
  13.4 2.0 %collective-permute-start.1 = (bf16[768,128]{1,0:T(8,128)(2,1)}, bf16[768,128]{1,0:T(8,128)(2,1)S(1)}, u32[]{:S(2)}, u32[]{:S(2)}) collective-permute-start(bf16[768,128]{1,0:T(8,128)(2,1)} %get-tuple-element.49), channel_id=1, source_target_pairs={{0,1},{1,2},{2,3},{3,0},{4,5},{5,6},{6,7},{7,4},{8,9},{9,10},{10,1... | collective-permute-start | bytes 589832 | tf_op jit(solution)/shard_map/ppermute | solution.py:529
  15.4 1.5 %collective-permute-start.2 = (bf16[768,128]{1,0:T(8,128)(2,1)}, bf16[768,128]{1,0:T(8,128)(2,1)S(1)}, u32[]{:S(2)}, u32[]{:S(2)}) collective-permute-start(bf16[768,128]{1,0:T(8,128)(2,1)} %get-tuple-element.50), channel_id=1, source_target_pairs={{0,2},{1,3},{2,0},{3,1},{4,6},{5,7},{6,4},{7,5},{8,10},{9,11},{10,... | collective-permute-start | bytes 589832 | tf_op jit(solution)/shard_map/ppermute | solution.py:529
  16.9 1.5 %collective-permute-start.3 = (bf16[768,128]{1,0:T(8,128)(2,1)}, bf16[768,128]{1,0:T(8,128)(2,1)S(1)}, u32[]{:S(2)}, u32[]{:S(2)}) collective-permute-start(bf16[768,128]{1,0:T(8,128)(2,1)} %get-tuple-element.51), channel_id=1, source_target_pairs={{0,3},{1,0},{2,1},{3,2},{4,7},{5,4},{6,5},{7,6},{8,11},{9,8},{10,9... | collective-permute-start | bytes 589832 | tf_op jit(solution)/shard_map/ppermute | solution.py:529
  18.4 0.0 all-to-all-done.noise_ref.in_ref
  18.4 0.3 edges_first.1
  18.7 0.0 collective-permute-done.4.near_ref
  18.7 0.1 collective-permute-start
  18.8 0.0 collective-permute-done.5.far_ref
  18.8 2.8 %collective-permute-start.6 = (bf16[192,256]{1,0:T(8,128)(2,1)S(1)}, bf16[192,256]{1,0:T(8,128)(2,1)S(1)}, u32[]{:S(2)}, u32[]{:S(2)}) collective-permute-start(bf16[192,256]{1,0:T(8,128)(2,1)S(1)} %get-tuple-element.59), channel_id=1, source_target_pairs={{0,28},{4,8},{8,4},{12,16},{16,12},{20,24},{24,20},{28,0},{1,29},{... | collective-permute-start | bytes 294920 | tf_op jit(solution)/shard_map/ppermute | solution.py:488
  21.5 0.9 taps_first.1
  22.4 1.0 pack_late.1
  23.5 0.4 small.1
  23.9 0.9 main_first.1.psi_in
  24.8 0.0 copy-start.10
  24.8 0.0 copy-start.9
  24.8 0.0 copy-start.8
  24.8 0.0 copy-start.2
  24.8 0.0 collective-permute-done.1.rest_1_
  24.8 0.0 collective-permute-done.2.rest_2_
  24.8 0.0 collective-permute-done.3.rest_3_
  24.8 0.0 copy-start.3
  24.8 0.0 collective-permute-done.near_ref
  24.9 0.3 collective-permute-done.6.far_ref
  25.1 3.7 %filter_first.1 = (bf16[32,4,32,128]{3,2,1,0:T(8,128)(2,1)}, f32[8,256,128]{2,1,0:T(8,128)}) custom-call(f32[8,256,128]{2,1,0:T(8,128)S(1)} %main_first.1.psi_in, bf16[192,256]{1,0:T(8,128)(2,1)S(1)} %collective-permute-done.near_ref, bf16[192,256]{1,0:T(8,128)(2,1)S(1)} %collective-permute-done.6.far_ref, f32[256,128]{1,0:T(8,128)S(1)} %get-tuple-element.60.factor_ref, ...), custom_call_target="tpu_custom_call" | custom-call | flops 1024 | bytes 1024 | tf_op jit(solution)/shard_map/filter_first/pallas_call | solution.py:591
  28.8 3.9 %all-to-all-start.2 = ((bf16[32,4,32,128]{3,2,1,0:T(8,128)(2,1)}), bf16[32,4,32,128]{3,2,1,0:T(8,128)(2,1)S(1)}, u32[]{:S(2)}, u32[]{:S(2)}) async-start(bf16[32,4,32,128]{3,2,1,0:T(8,128)(2,1)} %get-tuple-element.78), calls=%async_computation.2 | async-start | bytes 2097152 | tf_op jit(solution)/shard_map/all_to_all | solution.py:494
  32.8 1.8 %collective-permute-start.7 = (bf16[640,128]{1,0:T(8,128)(2,1)S(1)}, bf16[640,128]{1,0:T(8,128)(2,1)S(1)}, u32[]{:S(2)}, u32[]{:S(2)}) collective-permute-start(bf16[640,128]{1,0:T(8,128)(2,1)S(1)} %copy-done.10), channel_id=1, source_target_pairs={{0,1},{1,2},{2,3},{3,0},{4,5},{5,6},{6,7},{7,4},{8,9},{9,10},{10,1... | collective-permute-start | bytes 491528 | tf_op jit(solution)/shard_map/ppermute | solution.py:529
  34.6 1.5 %collective-permute-start.8 = (bf16[640,128]{1,0:T(8,128)(2,1)S(1)}, bf16[640,128]{1,0:T(8,128)(2,1)S(1)}, u32[]{:S(2)}, u32[]{:S(2)}) collective-permute-start(bf16[640,128]{1,0:T(8,128)(2,1)S(1)} %copy-done.9), channel_id=1, source_target_pairs={{0,2},{1,3},{2,0},{3,1},{4,6},{5,7},{6,4},{7,5},{8,10},{9,11},{10,... | collective-permute-start | bytes 491528 | tf_op jit(solution)/shard_map/ppermute | solution.py:529
  36.1 1.5 %collective-permute-start.9 = (bf16[640,128]{1,0:T(8,128)(2,1)S(1)}, bf16[640,128]{1,0:T(8,128)(2,1)S(1)}, u32[]{:S(2)}, u32[]{:S(2)}) collective-permute-start(bf16[640,128]{1,0:T(8,128)(2,1)S(1)} %copy-done.8), channel_id=1, source_target_pairs={{0,3},{1,0},{2,1},{3,2},{4,7},{5,4},{6,5},{7,6},{8,11},{9,8},{10,9... | collective-permute-start | bytes 491528 | tf_op jit(solution)/shard_map/ppermute | solution.py:529
  37.6 1.1 taps_rest.1
  38.7 0.9 copy-done.4
  39.6 1.2 %main_next.1.next_ref = f32[12,256,128]{2,1,0:T(8,128)S(1)} custom-call(bf16[2,256,512]{2,1,0:T(8,128)(2,1)S(1)} %get-tuple-element.67.wall_ref, bf16[2,256,256]{2,1,0:T(8,128)(2,1)S(1)} %get-tuple-element.68.main_ref, bf16[768,128]{1,0:T(8,128)(2,1)S(1)} %copy-done.2, bf16[768,128]{1,0:T(8,128)(2,1)S(1)} %collective-permute-done.1.rest_1_, ...), custom_call_target="tpu_custom_call" | custom-call | flops 1024 | bytes 1024 | tf_op jit(solution)/shard_map/main_next/pallas_call | solution.py:604
  40.8 8.5 %collective-permute-done.7.rest_1_ = bf16[640,128]{1,0:T(8,128)(2,1)S(1)} collective-permute-done((bf16[640,128]{1,0:T(8,128)(2,1)S(1)}, bf16[640,128]{1,0:T(8,128)(2,1)S(1)}, u32[]{:S(2)}, u32[]{:S(2)}) %collective-permute-start.7) | collective-permute-done | bytes 163872 | tf_op jit(solution)/shard_map/ppermute | solution.py:529
  49.3 3.2 %collective-permute-done.8.rest_2_ = bf16[640,128]{1,0:T(8,128)(2,1)S(1)} collective-permute-done((bf16[640,128]{1,0:T(8,128)(2,1)S(1)}, bf16[640,128]{1,0:T(8,128)(2,1)S(1)}, u32[]{:S(2)}, u32[]{:S(2)}) %collective-permute-start.8) | collective-permute-done | bytes 163872 | tf_op jit(solution)/shard_map/ppermute | solution.py:529
  52.5 0.0 collective-permute-done.9.rest_3_
  52.5 5.3 %filter_rest.1 = bf16[32,4,32,256]{3,2,1,0:T(8,128)(2,1)} custom-call(f32[8,256,128]{2,1,0:T(8,128)S(1)} %copy-done.1, f32[12,256,128]{2,1,0:T(8,128)S(1)} %main_next.1.next_ref, f32[256,128]{1,0:T(8,128)S(1)} %get-tuple-element.60.factor_ref, s32[4,4,128]{2,1,0:T(4,128)S(1)} %get-tuple-element.61.target_ref, ...), custom_call_target="tpu_custom_call" | custom-call | flops 1024 | bytes 1024 | tf_op jit(solution)/shard_map/filter_rest/pallas_call | solution.py:611
  57.9 1.4 %all-to-all-done.2 = bf16[32,4,32,128]{3,2,1,0:T(8,128)(2,1)S(1)} async-done(((bf16[32,4,32,128]{3,2,1,0:T(8,128)(2,1)}), bf16[32,4,32,128]{3,2,1,0:T(8,128)(2,1)S(1)}, u32[]{:S(2)}, u32[]{:S(2)}) %all-to-all-start.2) | async-done | bytes 1048608 | tf_op jit(solution)/shard_map/all_to_all | solution.py:494
  59.2 3.7 %all-to-all-start.1 = ((bf16[32,4,32,256]{3,2,1,0:T(8,128)(2,1)}), bf16[32,4,32,256]{3,2,1,0:T(8,128)(2,1)S(1)}, u32[]{:S(2)}, u32[]{:S(2)}) async-start(bf16[32,4,32,256]{3,2,1,0:T(8,128)(2,1)} %filter_rest.1), calls=%async_computation.1 | async-start | bytes 4194304 | tf_op jit(solution)/shard_map/all_to_all | solution.py:494
  63.0 1.0 join.2.rest_0_
  64.0 47.7 %all-to-all-done.1 = bf16[32,4,32,256]{3,2,1,0:T(8,128)(2,1)S(1)} async-done(((bf16[32,4,32,256]{3,2,1,0:T(8,128)(2,1)}), bf16[32,4,32,256]{3,2,1,0:T(8,128)(2,1)S(1)}, u32[]{:S(2)}, u32[]{:S(2)}) %all-to-all-start.1) | async-done | bytes 2097184 | tf_op jit(solution)/shard_map/all_to_all | solution.py:494
  111.7 1.4 %join.3 = bf16[8,128,1536]{2,1,0:T(8,128)(2,1)} custom-call(bf16[8,4,128,256]{3,2,1,0:T(8,128)(2,1)S(1)} %bitcast.9, bf16[8,128,1536]{2,1,0:T(8,128)(2,1)} %join.2.rest_0_), custom_call_target="tpu_custom_call", output_to_operand_aliasing={{}: (1, {})} | custom-call | tf_op jit(solution)/shard_map/join/pallas_call | solution.py:628
  (13 shorter events, 0.0 us)
Async XLA Ops:
  0.0 7.3 %copy-start = (bf16[3,32,64,128]{3,2,1,0:T(8,128)(2,1)S(1)}, bf16[3,32,64,128]{3,2,1,0:T(8,128)(2,1)}, u32[]{:S(2)}) copy-start(bf16[3,32,64,128]{3,2,1,0:T(8,128)(2,1)} %param.6) | copy-start | bytes 4718596
  2.1 19.4 %copy-start.6 = (f32[3]{0:T(128)S(1)}, f32[3]{0:T(128)}, u32[]{:S(2)}) copy-start(f32[3]{0:T(128)} %wall_scale.2) | copy-start | bytes 40
  2.1 19.4 %copy-start.7 = (f32[3]{0:T(128)S(1)}, f32[3]{0:T(128)}, u32[]{:S(2)}) copy-start(f32[3]{0:T(128)} %span_scale.2) | copy-start | bytes 40
  2.1 16.3 %all-to-all-start = ((bf16[4,544,128]{2,1,0:T(8,128)(2,1)}), bf16[4,544,128]{2,1,0:T(8,128)(2,1)S(1)}, u32[]{:S(2)}, u32[]{:S(2)}) async-start(bf16[4,544,128]{2,1,0:T(8,128)(2,1)} %pack.1), calls=%async_computation | async-start | bytes 1114112 | tf_op jit(solution)/shard_map/all_to_all | solution.py:491
  9.6 9.0 %collective-permute-start.4 = (bf16[4,2,96,128]{3,2,1,0:T(8,128)(2,1)}, bf16[4,2,96,128]{3,2,1,0:T(8,128)(2,1)S(1)}, u32[]{:S(2)}, u32[]{:S(2)}) collective-permute-start(bf16[4,2,96,128]{3,2,1,0:T(8,128)(2,1)} %get-tuple-element.46), channel_id=1, source_target_pairs={{0,4},{4,0},{8,12},{12,8},{16,20},{20,16},{24,28},{28,24},{1,5},{5... | collective-permute-start | bytes 589832 | tf_op jit(solution)/shard_map/ppermute | solution.py:488
  9.7 9.0 %collective-permute-start.5 = (bf16[4,2,96,128]{3,2,1,0:T(8,128)(2,1)}, bf16[4,2,96,128]{3,2,1,0:T(8,128)(2,1)S(1)}, u32[]{:S(2)}, u32[]{:S(2)}) collective-permute-start(bf16[4,2,96,128]{3,2,1,0:T(8,128)(2,1)} %get-tuple-element.47), channel_id=1, source_target_pairs={{0,28},{4,8},{8,4},{12,16},{16,12},{20,24},{24,20},{28,0},{1,29},{... | collective-permute-start | bytes 589832 | tf_op jit(solution)/shard_map/ppermute | solution.py:488
  13.4 11.4 %collective-permute-start.1 = (bf16[768,128]{1,0:T(8,128)(2,1)}, bf16[768,128]{1,0:T(8,128)(2,1)S(1)}, u32[]{:S(2)}, u32[]{:S(2)}) collective-permute-start(bf16[768,128]{1,0:T(8,128)(2,1)} %get-tuple-element.49), channel_id=1, source_target_pairs={{0,1},{1,2},{2,3},{3,0},{4,5},{5,6},{6,7},{7,4},{8,9},{9,10},{10,1... | collective-permute-start | bytes 589832 | tf_op jit(solution)/shard_map/ppermute | solution.py:529
  15.4 9.4 %collective-permute-start.2 = (bf16[768,128]{1,0:T(8,128)(2,1)}, bf16[768,128]{1,0:T(8,128)(2,1)S(1)}, u32[]{:S(2)}, u32[]{:S(2)}) collective-permute-start(bf16[768,128]{1,0:T(8,128)(2,1)} %get-tuple-element.50), channel_id=1, source_target_pairs={{0,2},{1,3},{2,0},{3,1},{4,6},{5,7},{6,4},{7,5},{8,10},{9,11},{10,... | collective-permute-start | bytes 589832 | tf_op jit(solution)/shard_map/ppermute | solution.py:529
  16.9 7.9 %collective-permute-start.3 = (bf16[768,128]{1,0:T(8,128)(2,1)}, bf16[768,128]{1,0:T(8,128)(2,1)S(1)}, u32[]{:S(2)}, u32[]{:S(2)}) collective-permute-start(bf16[768,128]{1,0:T(8,128)(2,1)} %get-tuple-element.51), channel_id=1, source_target_pairs={{0,3},{1,0},{2,1},{3,2},{4,7},{5,4},{6,5},{7,6},{8,11},{9,8},{10,9... | collective-permute-start | bytes 589832 | tf_op jit(solution)/shard_map/ppermute | solution.py:529
  18.7 6.2 %collective-permute-start = (bf16[192,256]{1,0:T(8,128)(2,1)S(1)}, bf16[192,256]{1,0:T(8,128)(2,1)S(1)}, u32[]{:S(2)}, u32[]{:S(2)}) collective-permute-start(bf16[192,256]{1,0:T(8,128)(2,1)S(1)} %get-tuple-element.53), channel_id=1, source_target_pairs={{0,4},{4,0},{8,12},{12,8},{16,20},{20,16},{24,28},{28,24},{1,5},{5... | collective-permute-start | bytes 294920 | tf_op jit(solution)/shard_map/ppermute | solution.py:488
  18.8 6.4 %collective-permute-start.6 = (bf16[192,256]{1,0:T(8,128)(2,1)S(1)}, bf16[192,256]{1,0:T(8,128)(2,1)S(1)}, u32[]{:S(2)}, u32[]{:S(2)}) collective-permute-start(bf16[192,256]{1,0:T(8,128)(2,1)S(1)} %get-tuple-element.59), channel_id=1, source_target_pairs={{0,28},{4,8},{8,4},{12,16},{16,12},{20,24},{24,20},{28,0},{1,29},{... | collective-permute-start | bytes 294920 | tf_op jit(solution)/shard_map/ppermute | solution.py:488
  24.8 8.0 %copy-start.10 = (bf16[640,128]{1,0:T(8,128)(2,1)S(1)}, bf16[640,128]{1,0:T(8,128)(2,1)}, u32[]{:S(2)}) copy-start(bf16[640,128]{1,0:T(8,128)(2,1)} %get-tuple-element.75) | copy-start | bytes 491524
  24.8 9.9 %copy-start.9 = (bf16[640,128]{1,0:T(8,128)(2,1)S(1)}, bf16[640,128]{1,0:T(8,128)(2,1)}, u32[]{:S(2)}) copy-start(bf16[640,128]{1,0:T(8,128)(2,1)} %get-tuple-element.76) | copy-start | bytes 491524
  24.8 11.3 %copy-start.8 = (bf16[640,128]{1,0:T(8,128)(2,1)S(1)}, bf16[640,128]{1,0:T(8,128)(2,1)}, u32[]{:S(2)}) copy-start(bf16[640,128]{1,0:T(8,128)(2,1)} %get-tuple-element.77) | copy-start | bytes 491524
  24.8 13.9 %copy-start.2 = (bf16[768,128]{1,0:T(8,128)(2,1)S(1)}, bf16[768,128]{1,0:T(8,128)(2,1)}, u32[]{:S(2)}) copy-start(bf16[768,128]{1,0:T(8,128)(2,1)} %get-tuple-element.69.rest_0_) | copy-start | bytes 589828
  24.8 4.0 %copy-start.3 = (bf16[768,128]{1,0:T(8,128)(2,1)}, bf16[768,128]{1,0:T(8,128)(2,1)S(1)}, u32[]{:S(2)}) copy-start(bf16[768,128]{1,0:T(8,128)(2,1)S(1)} %collective-permute-done.3.rest_3_) | copy-start | bytes 589828
  28.8 23.7 %copy-start.5 = (bf16[640,128]{1,0:T(8,128)(2,1)S(1)}, bf16[640,128]{1,0:T(8,128)(2,1)}, u32[]{:S(2)}) copy-start(bf16[640,128]{1,0:T(8,128)(2,1)} %get-tuple-element.74.rest_0_) | copy-start | bytes 491524
  28.8 30.4 %all-to-all-start.2 = ((bf16[32,4,32,128]{3,2,1,0:T(8,128)(2,1)}), bf16[32,4,32,128]{3,2,1,0:T(8,128)(2,1)S(1)}, u32[]{:S(2)}, u32[]{:S(2)}) async-start(bf16[32,4,32,128]{3,2,1,0:T(8,128)(2,1)} %get-tuple-element.78), calls=%async_computation.2 | async-start | bytes 2097152 | tf_op jit(solution)/shard_map/all_to_all | solution.py:494
  32.8 19.7 %copy-start.1 = (f32[8,256,128]{2,1,0:T(8,128)S(1)}, f32[8,256,128]{2,1,0:T(8,128)}, u32[]{:S(2)}) copy-start(f32[8,256,128]{2,1,0:T(8,128)} %get-tuple-element.63.psi_ref) | copy-start | bytes 3145732
  32.8 16.5 %collective-permute-start.7 = (bf16[640,128]{1,0:T(8,128)(2,1)S(1)}, bf16[640,128]{1,0:T(8,128)(2,1)S(1)}, u32[]{:S(2)}, u32[]{:S(2)}) collective-permute-start(bf16[640,128]{1,0:T(8,128)(2,1)S(1)} %copy-done.10), channel_id=1, source_target_pairs={{0,1},{1,2},{2,3},{3,0},{4,5},{5,6},{6,7},{7,4},{8,9},{9,10},{10,1... | collective-permute-start | bytes 491528 | tf_op jit(solution)/shard_map/ppermute | solution.py:529
  34.6 17.9 %collective-permute-start.8 = (bf16[640,128]{1,0:T(8,128)(2,1)S(1)}, bf16[640,128]{1,0:T(8,128)(2,1)S(1)}, u32[]{:S(2)}, u32[]{:S(2)}) collective-permute-start(bf16[640,128]{1,0:T(8,128)(2,1)S(1)} %copy-done.9), channel_id=1, source_target_pairs={{0,2},{1,3},{2,0},{3,1},{4,6},{5,7},{6,4},{7,5},{8,10},{9,11},{10,... | collective-permute-start | bytes 491528 | tf_op jit(solution)/shard_map/ppermute | solution.py:529
  36.1 16.4 %collective-permute-start.9 = (bf16[640,128]{1,0:T(8,128)(2,1)S(1)}, bf16[640,128]{1,0:T(8,128)(2,1)S(1)}, u32[]{:S(2)}, u32[]{:S(2)}) collective-permute-start(bf16[640,128]{1,0:T(8,128)(2,1)S(1)} %copy-done.8), channel_id=1, source_target_pairs={{0,3},{1,0},{2,1},{3,2},{4,7},{5,4},{6,5},{7,6},{8,11},{9,8},{10,9... | collective-permute-start | bytes 491528 | tf_op jit(solution)/shard_map/ppermute | solution.py:529
  38.7 0.9 copy-start.4
  59.2 52.5 %all-to-all-start.1 = ((bf16[32,4,32,256]{3,2,1,0:T(8,128)(2,1)}), bf16[32,4,32,256]{3,2,1,0:T(8,128)(2,1)S(1)}, u32[]{:S(2)}, u32[]{:S(2)}) async-start(bf16[32,4,32,256]{3,2,1,0:T(8,128)(2,1)} %filter_rest.1), calls=%async_computation.1 | async-start | bytes 4194304 | tf_op jit(solution)/shard_map/all_to_all | solution.py:494

commit v7 on v6

--- a/solution.py
+++ b/solution.py
@@ -136,8 +136,8 @@
     for step, out_ref in enumerate(out_refs):
         to = lax.rem(me + step, walls)
         left = out_ref.shape[0] - 2 * some * height
-        source = pl.multiple_of(to * block + block - left, math.gcd(block, left))
-        parts = [(noise_ref.at[0, pl.ds(source, left)], 0, left)]
+        source = pl.multiple_of(to * block + block - left, math.gcd(block, left) or block)
+        parts = [(noise_ref.at[0, pl.ds(source, left)], 0, left)] if left else []
         for side, ref in enumerate((near_ref, far_ref)):
             for c in range(some):
                 parts.append((ref.at[to, c], left + (side * some + c) * height, height))
@@ -463,11 +463,11 @@
     slots = max(8, 2 * elements // devices)
     count = elements // cols
     rest = trio - 1
-    ahead = rest * planes - planes // 2
+    ahead = rest * planes
     struct = jax.ShapeDtypeStruct
     hbm = pltpu.MemorySpace.HBM
 
-    def call(kernel, ins, outs, name, limit, scratch=(), grid=(), out_specs=None):
+    def call(kernel, ins, outs, name, limit, scratch=(), grid=(), out_specs=None, us=1):
         specs = out_specs or [VMEM] * len(outs)
         return pl.pallas_call(
             kernel,
@@ -477,7 +477,7 @@
             out_shape=outs if len(outs) > 1 else outs[0],
             scratch_shapes=scratch,
             compiler_params=pltpu.CompilerParams(vmem_limit_bytes=limit * 1024 * 1024),
-            cost_estimate=pl.CostEstimate(flops=1024, bytes_accessed=1024, transcendentals=0),
+            cost_estimate=pl.CostEstimate(flops=us * 10**9, bytes_accessed=1024, transcendentals=0),
             name=name,
         )
 
@@ -557,7 +557,9 @@
         functools.partial(edges_kernel, planes), [VMEM], [edge, edge], "edges_first", 16
     )(packed)
     near, far = exchange(near, far)
+    early, rest_near = lax.optimization_barrier((early, rest_near))
     early = spread(early)
+    (rest_near, rest_far), _ = lax.optimization_barrier(((rest_near, rest_far), (near, far)))
     late = call(
         pack_late_kernel,
         [pl.BlockSpec((1, all_planes * rows, cols), lambda i: (trio - 1, 0, 0)), VMEM, VMEM],
@@ -568,7 +570,7 @@
         grid=(1,),
         out_specs=[ANYWHERE] * n_wall,
     )(noise, rest_near, rest_far)
-    near, early, late = lax.optimization_barrier((near, early, late))
+    near, late = lax.optimization_barrier((near, late))
 
     psi = struct((planes, full, cols), F32)
     psi_main = call(
@@ -597,7 +599,7 @@
         [pltpu.VMEM(psi.shape, F32), cells, *more, dma((1,))],
         out_specs=[ANYWHERE, ANYWHERE],
     )(psi_main, near, far, factor, target, wall_first, halo_first)
-    (wall_scale, span_scale), sent = lax.optimization_barrier(((wall_scale, span_scale), sent))
+    (wall_scale, span_scale, late), sent = lax.optimization_barrier(((wall_scale, span_scale, late), sent))
     got_first = send(sent)
     late = spread(late)
     wall_rest, main_rest, halo_rest = taps(1, rest, struct, "taps_rest")
@@ -616,6 +618,7 @@
         32,
         scratch(rest),
         out_specs=[ANYWHERE],
+        us=100,
     )(psi, psi_next, factor, target, wall_rest, main_rest, halo_rest, *late)
     got_rest = send(sent)
 

time: 113 us -> 112 us (level)
  starting transfers between devices: 29.2 us -> 25.3 us
  waiting for transfers between devices: 61.1 us -> 64.1 us
    all_to_all x2, waiting for transfers between devices: 49.1 us -> 53.3 us  [send(): lax.all_to_all(x, ('span', 'wall'), 0, 0, tiled=True)]
    ppermute x6, waiting for transfers between devices: 11.7 us -> 8.44 us  [spread(): lax.ppermute(x, 'wall', [(i, (i + step) % n_wall) for i in range(n_wall)])]
    ppermute x2, waiting for transfers between devices: 0.28 us -> 2.39 us  [exchange(): lax.ppermute(far, 'span', chip_pairs)]
    ppermute x2, starting transfers between devices: 6.46 us -> 4.43 us  [exchange(): lax.ppermute(far, 'span', chip_pairs)]
    all_to_all x2, starting transfers between devices: 7.7 us -> 5.99 us  [send(): lax.all_to_all(x, ('span', 'wall'), 0, 0, tiled=True)]
  transfers between devices with their start and end apart: 13 -> 13, of which waited for: 5 -> 6; matrix products, arithmetic and copies ran while one was open for 0% -> 0% of each run, Pallas kernels for 13% -> 16%
where the time goes in v7:
time: 112 us
  waiting for transfers between devices  64.1 us (57%)
  starting transfers between devices  25.3 us (23%)
  Pallas kernels  21.7 us (19%)
    all_to_all x2, waiting for transfers between devices, send(): lax.all_to_all(x, ('span', 'wall'), 0, 0, tiled=True)  53.3 us
    ppermute x6, starting transfers between devices, spread(): lax.ppermute(x, 'wall', [(i, (i + step) % n_wall) for i in range(n_wall)])  9.58 us
    ppermute x6, waiting for transfers between devices, spread(): lax.ppermute(x, 'wall', [(i, (i + step) % n_wall) for i in range(n_wall)])  8.44 us
    all_to_all x2, starting transfers between devices, send(): lax.all_to_all(x, ('span', 'wall'), 0, 0, tiled=True)  5.99 us
    all_to_all x1, starting transfers between devices, swap(): return lax.all_to_all(x, 'wall', 0, 0, tiled=True)  5.17 us
    pallas_call x1, Pallas kernels, per_device(): call(functools.partial(rest_kernel, planes), [VMEM] * (7 + n_wall), [out(...  5.15 us
    ppermute x2, starting transfers between devices, exchange(): lax.ppermute(far, 'span', chip_pairs)  4.43 us
    pallas_call x1, Pallas kernels, per_device(): call(functools.partial(first_kernel, planes), [VMEM] * 7, [out(1), hbm(ps...  3.68 us
  transfers between devices with their start and end apart: 13, of which 6 were waited for; matrix products, arithmetic and copies ran while one was open for 0% of the time, Pallas kernels for 16%

profile of v7, /device:TPU:0, one launch (start us, length us, event | category | flops | bytes accessed | tf_op | source)
XLA Modules:
  0.0 112.1 jit_solution(14065623237748735371)
XLA Ops:
  0.0 2.1 %pack.1 = bf16[4,544,128]{2,1,0:T(8,128)(2,1)} custom-call(bf16[3,2048,128]{2,1,0:T(8,128)(2,1)} %bitcast.8, f32[6,64]{1,0:T(8,128)} %lund_ref.1, f32[1,64]{1,0:T(1,128)} %bitcast.12, s32[1,512]{1,0:T(1,128)} %bitcast.11), custom_call_target="tpu_custom_call" | custom-call | flops 1000000000 | bytes 1024 | tf_op jit(solution)/shard_map/pack/pallas_call | solution.py:498
  2.1 5.2 %all-to-all-start = ((bf16[4,544,128]{2,1,0:T(8,128)(2,1)}), bf16[4,544,128]{2,1,0:T(8,128)(2,1)S(1)}, u32[]{:S(2)}, u32[]{:S(2)}) async-start(bf16[4,544,128]{2,1,0:T(8,128)(2,1)} %pack.1), calls=%async_computation | async-start | bytes 1114112 | tf_op jit(solution)/shard_map/all_to_all | solution.py:491
  7.3 0.0 copy-done.1
  7.3 2.5 %prepare_rest.1 = (bf16[4,2,96,128]{3,2,1,0:T(8,128)(2,1)}, bf16[4,2,96,128]{3,2,1,0:T(8,128)(2,1)}, bf16[1024,128]{1,0:T(8,128)(2,1)}, bf16[1024,128]{1,0:T(8,1...) custom-call(bf16[3,2048,128]{2,1,0:T(8,128)(2,1)S(1)} %bitcast.9), custom_call_target="tpu_custom_call" | custom-call | flops 1000000000 | bytes 1024 | tf_op jit(solution)/shard_map/prepare_rest/pallas_call | solution.py:514
  9.7 0.1 collective-permute-start.1
  9.8 3.7 %collective-permute-start.2 = (bf16[4,2,96,128]{3,2,1,0:T(8,128)(2,1)}, bf16[4,2,96,128]{3,2,1,0:T(8,128)(2,1)S(1)}, u32[]{:S(2)}, u32[]{:S(2)}) collective-permute-start(bf16[4,2,96,128]{3,2,1,0:T(8,128)(2,1)} %get-tuple-element.54), channel_id=1, source_target_pairs={{0,28},{4,8},{8,4},{12,16},{16,12},{20,24},{24,20},{28,0},{1,29},{... | collective-permute-start | bytes 589832 | tf_op jit(solution)/shard_map/ppermute | solution.py:488
  13.5 0.0 copy-done.2
  13.5 0.0 copy-done.3
  13.5 0.9 taps_first.1
  14.4 0.0 copy-start.5
  14.5 0.7 copy-done.5
  15.1 0.0 collective-permute-done.1.near_ref
  15.1 2.0 %collective-permute-start.4 = (bf16[1024,128]{1,0:T(8,128)(2,1)}, bf16[1024,128]{1,0:T(8,128)(2,1)S(1)}, u32[]{:S(2)}, u32[]{:S(2)}) collective-permute-start(bf16[1024,128]{1,0:T(8,128)(2,1)} %get-tuple-element.84), channel_id=1, source_target_pairs={{0,1},{1,2},{2,3},{3,0},{4,5},{5,6},{6,7},{7,4},{8,9},{9,10},{10,1... | collective-permute-start | bytes 786440 | tf_op jit(solution)/shard_map/ppermute | solution.py:529
  17.1 1.5 %collective-permute-start.5 = (bf16[1024,128]{1,0:T(8,128)(2,1)}, bf16[1024,128]{1,0:T(8,128)(2,1)S(1)}, u32[]{:S(2)}, u32[]{:S(2)}) collective-permute-start(bf16[1024,128]{1,0:T(8,128)(2,1)} %get-tuple-element.85), channel_id=1, source_target_pairs={{0,2},{1,3},{2,0},{3,1},{4,6},{5,7},{6,4},{7,5},{8,10},{9,11},{10,... | collective-permute-start | bytes 786440 | tf_op jit(solution)/shard_map/ppermute | solution.py:529
  18.6 0.0 all-to-all-done.noise_ref.in_ref
  18.6 0.3 edges_first.1
  18.9 0.1 collective-permute-start
  19.0 0.7 collective-permute-start.3
  19.7 0.4 small.1
  20.1 0.9 main_first.1.psi_in
  21.0 0.0 copy-start.6
  21.0 0.0 collective-permute-done.2.far_ref
  21.0 1.5 %collective-permute-start.6 = (bf16[1024,128]{1,0:T(8,128)(2,1)}, bf16[1024,128]{1,0:T(8,128)(2,1)S(1)}, u32[]{:S(2)}, u32[]{:S(2)}) collective-permute-start(bf16[1024,128]{1,0:T(8,128)(2,1)} %get-tuple-element.86), channel_id=1, source_target_pairs={{0,3},{1,0},{2,1},{3,2},{4,7},{5,4},{6,5},{7,6},{8,11},{9,8},{10,9... | collective-permute-start | bytes 786440 | tf_op jit(solution)/shard_map/ppermute | solution.py:529
  22.5 0.0 collective-permute-done.near_ref
  22.5 2.4 %collective-permute-done.3.far_ref = bf16[192,256]{1,0:T(8,128)(2,1)S(1)} collective-permute-done((bf16[192,256]{1,0:T(8,128)(2,1)S(1)}, bf16[192,256]{1,0:T(8,128)(2,1)S(1)}, u32[]{:S(2)}, u32[]{:S(2)}) %collective-permute-start.3) | collective-permute-done | bytes 98336 | tf_op jit(solution)/shard_map/ppermute | solution.py:488
  24.9 0.9 pack_late.1
  25.9 0.0 copy-done.7
  25.9 0.0 copy-done.6
  25.9 3.7 %filter_first.1 = (bf16[32,4,32,128]{3,2,1,0:T(8,128)(2,1)}, f32[8,256,128]{2,1,0:T(8,128)}) custom-call(f32[8,256,128]{2,1,0:T(8,128)S(1)} %main_first.1.psi_in, bf16[192,256]{1,0:T(8,128)(2,1)S(1)} %collective-permute-done.near_ref, bf16[192,256]{1,0:T(8,128)(2,1)S(1)} %collective-permute-done.3.far_ref, f32[256,128]{1,0:T(8,128)S(1)} %get-tuple-element.70.factor_ref, ...), custom_call_target="tpu_custom_call" | custom-call | flops 1000000000 | bytes 1024 | tf_op jit(solution)/shard_map/filter_first/pallas_call | solution.py:593
  29.6 2.7 %all-to-all-start.2 = ((bf16[32,4,32,128]{3,2,1,0:T(8,128)(2,1)}), bf16[32,4,32,128]{3,2,1,0:T(8,128)(2,1)S(1)}, u32[]{:S(2)}, u32[]{:S(2)}) async-start(bf16[32,4,32,128]{3,2,1,0:T(8,128)(2,1)} %get-tuple-element.92), calls=%async_computation.2 | async-start | bytes 2097152 | tf_op jit(solution)/shard_map/all_to_all | solution.py:494
  32.3 1.7 %collective-permute-start.7 = (bf16[384,128]{1,0:T(8,128)(2,1)S(1)}, bf16[384,128]{1,0:T(8,128)(2,1)S(1)}, u32[]{:S(2)}, u32[]{:S(2)}) collective-permute-start(bf16[384,128]{1,0:T(8,128)(2,1)S(1)} %copy-done.12), channel_id=1, source_target_pairs={{0,1},{1,2},{2,3},{3,0},{4,5},{5,6},{6,7},{7,4},{8,9},{9,10},{10,1... | collective-permute-start | bytes 294920 | tf_op jit(solution)/shard_map/ppermute | solution.py:529
  34.0 0.0 copy-done.11
  34.0 1.5 %collective-permute-start.8 = (bf16[384,128]{1,0:T(8,128)(2,1)S(1)}, bf16[384,128]{1,0:T(8,128)(2,1)S(1)}, u32[]{:S(2)}, u32[]{:S(2)}) collective-permute-start(bf16[384,128]{1,0:T(8,128)(2,1)S(1)} %copy-done.11), channel_id=1, source_target_pairs={{0,2},{1,3},{2,0},{3,1},{4,6},{5,7},{6,4},{7,5},{8,10},{9,11},{10,... | collective-permute-start | bytes 294920 | tf_op jit(solution)/shard_map/ppermute | solution.py:529
  35.5 0.0 collective-permute-done.4.rest_1_
  35.5 1.4 %collective-permute-start.9 = (bf16[384,128]{1,0:T(8,128)(2,1)S(1)}, bf16[384,128]{1,0:T(8,128)(2,1)S(1)}, u32[]{:S(2)}, u32[]{:S(2)}) collective-permute-start(bf16[384,128]{1,0:T(8,128)(2,1)S(1)} %copy-done.10), channel_id=1, source_target_pairs={{0,3},{1,0},{2,1},{3,2},{4,7},{5,4},{6,5},{7,6},{8,11},{9,8},{10,9... | collective-permute-start | bytes 294920 | tf_op jit(solution)/shard_map/ppermute | solution.py:529
  36.9 1.1 taps_rest.1
  38.1 0.0 collective-permute-done.5.rest_2_
  38.1 0.0 collective-permute-done.6.rest_3_
  38.1 1.4 %main_next.1.next_ref = f32[16,256,128]{2,1,0:T(8,128)S(1)} custom-call(bf16[2,256,512]{2,1,0:T(8,128)(2,1)S(1)} %get-tuple-element.81.wall_ref, bf16[2,256,256]{2,1,0:T(8,128)(2,1)S(1)} %get-tuple-element.82.main_ref, bf16[1024,128]{1,0:T(8,128)(2,1)S(1)} %copy-done, bf16[1024,128]{1,0:T(8,128)(2,1)S(1)} %collective-permute-done.4.rest_1_, ...), custom_call_target="tpu_custom_call" | custom-call | flops 1000000000 | bytes 1024 | tf_op jit(solution)/shard_map/main_next/pallas_call | solution.py:606
  39.5 6.5 %collective-permute-done.7.rest_1_ = bf16[384,128]{1,0:T(8,128)(2,1)S(1)} collective-permute-done((bf16[384,128]{1,0:T(8,128)(2,1)S(1)}, bf16[384,128]{1,0:T(8,128)(2,1)S(1)}, u32[]{:S(2)}, u32[]{:S(2)}) %collective-permute-start.7) | collective-permute-done | bytes 98336 | tf_op jit(solution)/shard_map/ppermute | solution.py:529
  46.0 1.7 %collective-permute-done.8.rest_2_ = bf16[384,128]{1,0:T(8,128)(2,1)S(1)} collective-permute-done((bf16[384,128]{1,0:T(8,128)(2,1)S(1)}, bf16[384,128]{1,0:T(8,128)(2,1)S(1)}, u32[]{:S(2)}, u32[]{:S(2)}) %collective-permute-start.8) | collective-permute-done | bytes 98336 | tf_op jit(solution)/shard_map/ppermute | solution.py:529
  47.7 0.2 collective-permute-done.9.rest_3_
  48.0 5.1 %filter_rest.1 = bf16[32,4,32,256]{3,2,1,0:T(8,128)(2,1)} custom-call(f32[8,256,128]{2,1,0:T(8,128)S(1)} %copy-done.4, f32[16,256,128]{2,1,0:T(8,128)S(1)} %main_next.1.next_ref, f32[256,128]{1,0:T(8,128)S(1)} %copy-done.8, s32[4,4,128]{2,1,0:T(4,128)S(1)} %get-tuple-element.71.target_ref, bf16[2,256,512]{2,1,0:T(8,128)(2,1)S(1)} %get-tuple-element.81.wall_ref, ...), custom_call_target="tpu_custom_call" | custom-call | flops 99999997952 | bytes 1024 | tf_op jit(solution)/shard_map/filter_rest/pallas_call | solution.py:613
  53.1 5.6 %all-to-all-done.2 = bf16[32,4,32,128]{3,2,1,0:T(8,128)(2,1)S(1)} async-done(((bf16[32,4,32,128]{3,2,1,0:T(8,128)(2,1)}), bf16[32,4,32,128]{3,2,1,0:T(8,128)(2,1)S(1)}, u32[]{:S(2)}, u32[]{:S(2)}) %all-to-all-start.2) | async-done | bytes 1048608 | tf_op jit(solution)/shard_map/all_to_all | solution.py:494
  58.7 3.3 %all-to-all-start.1 = ((bf16[32,4,32,256]{3,2,1,0:T(8,128)(2,1)}), bf16[32,4,32,256]{3,2,1,0:T(8,128)(2,1)S(1)}, u32[]{:S(2)}, u32[]{:S(2)}) async-start(bf16[32,4,32,256]{3,2,1,0:T(8,128)(2,1)} %filter_rest.1), calls=%async_computation.1 | async-start | bytes 4194304 | tf_op jit(solution)/shard_map/all_to_all | solution.py:494
  62.0 1.0 join.2.rest_0_
  63.0 47.7 %all-to-all-done.1 = bf16[32,4,32,256]{3,2,1,0:T(8,128)(2,1)S(1)} async-done(((bf16[32,4,32,256]{3,2,1,0:T(8,128)(2,1)}), bf16[32,4,32,256]{3,2,1,0:T(8,128)(2,1)S(1)}, u32[]{:S(2)}, u32[]{:S(2)}) %all-to-all-start.1) | async-done | bytes 2097184 | tf_op jit(solution)/shard_map/all_to_all | solution.py:494
  110.7 1.4 %join.3 = bf16[8,128,1536]{2,1,0:T(8,128)(2,1)} custom-call(bf16[8,4,128,256]{3,2,1,0:T(8,128)(2,1)S(1)} %bitcast.6, bf16[8,128,1536]{2,1,0:T(8,128)(2,1)} %join.2.rest_0_), custom_call_target="tpu_custom_call", output_to_operand_aliasing={{}: (1, {})} | custom-call | tf_op jit(solution)/shard_map/join/pallas_call | solution.py:631
  (17 shorter events, 0.0 us)
Async XLA Ops:
  0.0 7.3 %copy-start.1 = (bf16[3,32,64,128]{3,2,1,0:T(8,128)(2,1)S(1)}, bf16[3,32,64,128]{3,2,1,0:T(8,128)(2,1)}, u32[]{:S(2)}) copy-start(bf16[3,32,64,128]{3,2,1,0:T(8,128)(2,1)} %param.6) | copy-start | bytes 4718596
  2.1 16.5 %all-to-all-start = ((bf16[4,544,128]{2,1,0:T(8,128)(2,1)}), bf16[4,544,128]{2,1,0:T(8,128)(2,1)S(1)}, u32[]{:S(2)}, u32[]{:S(2)}) async-start(bf16[4,544,128]{2,1,0:T(8,128)(2,1)} %pack.1), calls=%async_computation | async-start | bytes 1114112 | tf_op jit(solution)/shard_map/all_to_all | solution.py:491
  7.3 6.3 %copy-start.2 = (f32[3]{0:T(128)S(1)}, f32[3]{0:T(128)}, u32[]{:S(2)}) copy-start(f32[3]{0:T(128)} %wall_scale.2) | copy-start | bytes 40
  7.3 6.3 %copy-start.3 = (f32[3]{0:T(128)S(1)}, f32[3]{0:T(128)}, u32[]{:S(2)}) copy-start(f32[3]{0:T(128)} %span_scale.2) | copy-start | bytes 40
  9.7 5.4 %collective-permute-start.1 = (bf16[4,2,96,128]{3,2,1,0:T(8,128)(2,1)}, bf16[4,2,96,128]{3,2,1,0:T(8,128)(2,1)S(1)}, u32[]{:S(2)}, u32[]{:S(2)}) collective-permute-start(bf16[4,2,96,128]{3,2,1,0:T(8,128)(2,1)} %get-tuple-element.53), channel_id=1, source_target_pairs={{0,4},{4,0},{8,12},{12,8},{16,20},{20,16},{24,28},{28,24},{1,5},{5... | collective-permute-start | bytes 589832 | tf_op jit(solution)/shard_map/ppermute | solution.py:488
  9.8 11.2 %collective-permute-start.2 = (bf16[4,2,96,128]{3,2,1,0:T(8,128)(2,1)}, bf16[4,2,96,128]{3,2,1,0:T(8,128)(2,1)S(1)}, u32[]{:S(2)}, u32[]{:S(2)}) collective-permute-start(bf16[4,2,96,128]{3,2,1,0:T(8,128)(2,1)} %get-tuple-element.54), channel_id=1, source_target_pairs={{0,28},{4,8},{8,4},{12,16},{16,12},{20,24},{24,20},{28,0},{1,29},{... | collective-permute-start | bytes 589832 | tf_op jit(solution)/shard_map/ppermute | solution.py:488
  14.4 0.7 copy-start.5
  15.1 20.3 %collective-permute-start.4 = (bf16[1024,128]{1,0:T(8,128)(2,1)}, bf16[1024,128]{1,0:T(8,128)(2,1)S(1)}, u32[]{:S(2)}, u32[]{:S(2)}) collective-permute-start(bf16[1024,128]{1,0:T(8,128)(2,1)} %get-tuple-element.84), channel_id=1, source_target_pairs={{0,1},{1,2},{2,3},{3,0},{4,5},{5,6},{6,7},{7,4},{8,9},{9,10},{10,1... | collective-permute-start | bytes 786440 | tf_op jit(solution)/shard_map/ppermute | solution.py:529
  17.1 20.9 %collective-permute-start.5 = (bf16[1024,128]{1,0:T(8,128)(2,1)}, bf16[1024,128]{1,0:T(8,128)(2,1)S(1)}, u32[]{:S(2)}, u32[]{:S(2)}) collective-permute-start(bf16[1024,128]{1,0:T(8,128)(2,1)} %get-tuple-element.85), channel_id=1, source_target_pairs={{0,2},{1,3},{2,0},{3,1},{4,6},{5,7},{6,4},{7,5},{8,10},{9,11},{10,... | collective-permute-start | bytes 786440 | tf_op jit(solution)/shard_map/ppermute | solution.py:529
  18.9 3.6 %collective-permute-start = (bf16[192,256]{1,0:T(8,128)(2,1)S(1)}, bf16[192,256]{1,0:T(8,128)(2,1)S(1)}, u32[]{:S(2)}, u32[]{:S(2)}) collective-permute-start(bf16[192,256]{1,0:T(8,128)(2,1)S(1)} %get-tuple-element.60), channel_id=1, source_target_pairs={{0,4},{4,0},{8,12},{12,8},{16,20},{20,16},{24,28},{28,24},{1,5},{5... | collective-permute-start | bytes 294920 | tf_op jit(solution)/shard_map/ppermute | solution.py:488
  19.0 5.9 %collective-permute-start.3 = (bf16[192,256]{1,0:T(8,128)(2,1)S(1)}, bf16[192,256]{1,0:T(8,128)(2,1)S(1)}, u32[]{:S(2)}, u32[]{:S(2)}) collective-permute-start(bf16[192,256]{1,0:T(8,128)(2,1)S(1)} %get-tuple-element.62), channel_id=1, source_target_pairs={{0,28},{4,8},{8,4},{12,16},{16,12},{20,24},{24,20},{28,0},{1,29},{... | collective-permute-start | bytes 294920 | tf_op jit(solution)/shard_map/ppermute | solution.py:488
  20.1 5.7 %copy-start.7 = (f32[256,128]{1,0:T(8,128)}, f32[256,128]{1,0:T(8,128)S(1)}, u32[]{:S(2)}) copy-start(f32[256,128]{1,0:T(8,128)S(1)} %get-tuple-element.70.factor_ref) | copy-start | bytes 393220
  21.0 4.8 %copy-start.6 = (bf16[1,2,256,256]{3,2,1,0:T(8,128)(2,1)S(1)}, bf16[1,2,256,256]{3,2,1,0:T(8,128)(2,1)}, u32[]{:S(2)}) copy-start(bf16[1,2,256,256]{3,2,1,0:T(8,128)(2,1)} %copy-done.5) | copy-start | bytes 786436
  21.0 17.0 %collective-permute-start.6 = (bf16[1024,128]{1,0:T(8,128)(2,1)}, bf16[1024,128]{1,0:T(8,128)(2,1)S(1)}, u32[]{:S(2)}, u32[]{:S(2)}) collective-permute-start(bf16[1024,128]{1,0:T(8,128)(2,1)} %get-tuple-element.86), channel_id=1, source_target_pairs={{0,3},{1,0},{2,1},{3,2},{4,7},{5,4},{6,5},{7,6},{8,11},{9,8},{10,9... | collective-permute-start | bytes 786440 | tf_op jit(solution)/shard_map/ppermute | solution.py:529
  25.9 6.4 %copy-start.12 = (bf16[384,128]{1,0:T(8,128)(2,1)S(1)}, bf16[384,128]{1,0:T(8,128)(2,1)}, u32[]{:S(2)}) copy-start(bf16[384,128]{1,0:T(8,128)(2,1)} %get-tuple-element.89) | copy-start | bytes 294916
  25.9 8.1 %copy-start.11 = (bf16[384,128]{1,0:T(8,128)(2,1)S(1)}, bf16[384,128]{1,0:T(8,128)(2,1)}, u32[]{:S(2)}) copy-start(bf16[384,128]{1,0:T(8,128)(2,1)} %get-tuple-element.90) | copy-start | bytes 294916
  25.9 9.6 %copy-start.10 = (bf16[384,128]{1,0:T(8,128)(2,1)S(1)}, bf16[384,128]{1,0:T(8,128)(2,1)}, u32[]{:S(2)}) copy-start(bf16[384,128]{1,0:T(8,128)(2,1)} %get-tuple-element.91) | copy-start | bytes 294916
  29.6 29.1 %all-to-all-start.2 = ((bf16[32,4,32,128]{3,2,1,0:T(8,128)(2,1)}), bf16[32,4,32,128]{3,2,1,0:T(8,128)(2,1)S(1)}, u32[]{:S(2)}, u32[]{:S(2)}) async-start(bf16[32,4,32,128]{3,2,1,0:T(8,128)(2,1)} %get-tuple-element.92), calls=%async_computation.2 | async-start | bytes 2097152 | tf_op jit(solution)/shard_map/all_to_all | solution.py:494
  32.3 5.8 %copy-start = (bf16[1024,128]{1,0:T(8,128)(2,1)S(1)}, bf16[1024,128]{1,0:T(8,128)(2,1)}, u32[]{:S(2)}) copy-start(bf16[1024,128]{1,0:T(8,128)(2,1)} %get-tuple-element.83.rest_0_) | copy-start | bytes 786436
  32.3 13.7 %collective-permute-start.7 = (bf16[384,128]{1,0:T(8,128)(2,1)S(1)}, bf16[384,128]{1,0:T(8,128)(2,1)S(1)}, u32[]{:S(2)}, u32[]{:S(2)}) collective-permute-start(bf16[384,128]{1,0:T(8,128)(2,1)S(1)} %copy-done.12), channel_id=1, source_target_pairs={{0,1},{1,2},{2,3},{3,0},{4,5},{5,6},{6,7},{7,4},{8,9},{9,10},{10,1... | collective-permute-start | bytes 294920 | tf_op jit(solution)/shard_map/ppermute | solution.py:529
  34.0 13.8 %collective-permute-start.8 = (bf16[384,128]{1,0:T(8,128)(2,1)S(1)}, bf16[384,128]{1,0:T(8,128)(2,1)S(1)}, u32[]{:S(2)}, u32[]{:S(2)}) collective-permute-start(bf16[384,128]{1,0:T(8,128)(2,1)S(1)} %copy-done.11), channel_id=1, source_target_pairs={{0,2},{1,3},{2,0},{3,1},{4,6},{5,7},{6,4},{7,5},{8,10},{9,11},{10,... | collective-permute-start | bytes 294920 | tf_op jit(solution)/shard_map/ppermute | solution.py:529
  35.5 12.5 %collective-permute-start.9 = (bf16[384,128]{1,0:T(8,128)(2,1)S(1)}, bf16[384,128]{1,0:T(8,128)(2,1)S(1)}, u32[]{:S(2)}, u32[]{:S(2)}) collective-permute-start(bf16[384,128]{1,0:T(8,128)(2,1)S(1)} %copy-done.10), channel_id=1, source_target_pairs={{0,3},{1,0},{2,1},{3,2},{4,7},{5,4},{6,5},{7,6},{8,11},{9,8},{10,9... | collective-permute-start | bytes 294920 | tf_op jit(solution)/shard_map/ppermute | solution.py:529
  38.0 9.9 %copy-start.4 = (f32[8,256,128]{2,1,0:T(8,128)S(1)}, f32[8,256,128]{2,1,0:T(8,128)}, u32[]{:S(2)}) copy-start(f32[8,256,128]{2,1,0:T(8,128)} %get-tuple-element.73.psi_ref) | copy-start | bytes 3145732
  38.0 9.9 %copy-start.8 = (f32[256,128]{1,0:T(8,128)S(1)}, f32[256,128]{1,0:T(8,128)}, u32[]{:S(2)}) copy-start(f32[256,128]{1,0:T(8,128)} %copy-done.7) | copy-start | bytes 393220
  38.0 9.9 %copy-start.9 = (bf16[384,128]{1,0:T(8,128)(2,1)S(1)}, bf16[384,128]{1,0:T(8,128)(2,1)}, u32[]{:S(2)}) copy-start(bf16[384,128]{1,0:T(8,128)(2,1)} %get-tuple-element.88.rest_0_) | copy-start | bytes 294916
  58.7 52.0 %all-to-all-start.1 = ((bf16[32,4,32,256]{3,2,1,0:T(8,128)(2,1)}), bf16[32,4,32,256]{3,2,1,0:T(8,128)(2,1)S(1)}, u32[]{:S(2)}, u32[]{:S(2)}) async-start(bf16[32,4,32,256]{3,2,1,0:T(8,128)(2,1)} %filter_rest.1), calls=%async_computation.1 | async-start | bytes 4194304 | tf_op jit(solution)/shard_map/all_to_all | solution.py:494

commit v8 on v7

--- a/solution.py
+++ b/solution.py
@@ -57,7 +57,7 @@
     i, j = iota((full, full), 0), iota((full, full), 1)
     y = cell_row(i, full // (EDGE * EDGE))
     source = lax.rem(lax.axis_index("wall") + walls - j // rows, walls)
-    column = source * rows + j % rows if first else j
+    column = source * rows + j % rows
     n = iota((cols, cols), 1)
     target = (n % (cols // EDGE)) * EDGE + n // (cols // EDGE)
     k = iota((cols, cols), 0)
@@ -88,17 +88,21 @@
         copy.wait()
 
 
-def pack_kernel(devices, noise_ref, lund_ref, mean_ref, owner_ref, out_ref, small_ref, noise_sems, small_sems):
-    walls, height, cols = out_ref.shape
-    tail = small_ref.shape[0]
-    block = height - tail
+def pack_kernel(devices, noise_ref, lund_ref, mean_ref, owner_ref, *rest):
+    *out_refs, small_ref, noise_sems, small_sems = rest
+    walls = len(out_refs)
+    tail, cols = small_ref.shape
+    block = out_refs[0].shape[0] - tail
     rows = mean_ref.shape[1]
-    copies = [
-        pltpu.make_async_copy(
-            noise_ref.at[0, pl.ds(w * block, block)], out_ref.at[w, pl.ds(0, block)], noise_sems.at[w]
+    me = lax.axis_index("wall")
+    copies = []
+    for step, out_ref in enumerate(out_refs):
+        start = pl.multiple_of(lax.rem(me + step, walls) * block, block)
+        copies.append(
+            pltpu.make_async_copy(
+                noise_ref.at[0, pl.ds(start, block)], out_ref.at[pl.ds(0, block)], noise_sems.at[step]
+            )
         )
-        for w in range(walls)
-    ]
     for copy in copies:
         copy.start()
     owner = owner_ref[...]
@@ -119,8 +123,8 @@
     small_ref[...] = jnp.concatenate(pieces, axis=0).astype(BF16)
     run(
         [
-            pltpu.make_async_copy(small_ref, out_ref.at[w, pl.ds(block, tail)], small_sems.at[w])
-            for w in range(walls)
+            pltpu.make_async_copy(small_ref, out_ref.at[pl.ds(block, tail)], small_sems.at[step])
+            for step, out_ref in enumerate(out_refs)
         ]
     )
     for copy in copies:
@@ -148,22 +152,26 @@
     run(copies)
 
 
-def small_kernel(slots, in_ref, factor_ref, target_ref):
-    walls, height, cols = in_ref.shape
+def small_kernel(slots, *rest):
+    *in_refs, factor_ref, target_ref = rest
+    walls = len(in_refs)
+    height, cols = in_refs[0].shape
     full = factor_ref.shape[0]
     rows = full // walls
     count = target_ref.shape[1]
     tail = tail_rows(count)
+    me = lax.axis_index("wall")
     columns = jnp.zeros((full, tail), F32)
     y = cell_row(iota((full, cols), 0), full // (EDGE * EDGE))
-    for w in range(walls):
-        small = in_ref[w, height - tail :]
+    for step, in_ref in enumerate(in_refs):
+        w = lax.rem(me + walls - step, walls)
+        small = in_ref[height - tail :]
         pick = jnp.where(y == iota((full, cols), 1) + w * rows, 1.0, 0.0)
         pick = jnp.where(iota((full, cols), 1) < rows, pick, 0.0).astype(BF16)
         columns = columns + lax.dot_general(pick, small, ROWS_BY_ROWS, preferred_element_type=F32)
         numbers = small.astype(F32)
         target = numbers[:count] * slots + numbers[count : 2 * count]
-        target_ref[w] = target.astype(jnp.int32)
+        target_ref[pl.ds(w, 1)] = target.astype(jnp.int32)[None]
     at = 2 * count
     factor = sum(columns[:, at + p * FACTORS : at + (p + 1) * FACTORS] for p in range(3))
     factor_ref[...] = jnp.concatenate([factor, jnp.zeros((full, cols - FACTORS), F32)], axis=1)
@@ -176,15 +184,16 @@
     return jnp.where(col == start + row % HALO, 1.0, 0.0).astype(BF16)
 
 
-def edges_kernel(planes, noise_ref, near_ref, far_ref):
-    walls, _, cols = noise_ref.shape
-    rows = near_ref.shape[1] // walls
+def edges_kernel(planes, *rest):
+    *noise_refs, near_ref, far_ref = rest
+    cols = noise_refs[0].shape[1]
+    rows = near_ref.shape[1] // len(noise_refs)
     wide = 2 * HALO
     pick = edge_picker(cols)
     for pair in range(planes // 2):
         edges = []
         for t in (2 * pair, 2 * pair + 1):
-            plane = [noise_ref[w, t * rows : (t + 1) * rows] for w in range(walls)]
+            plane = [ref[t * rows : (t + 1) * rows] for ref in noise_refs]
             plane = jnp.concatenate(plane, axis=0)
             edges.append(lax.dot_general(pick, plane, ROWS_BY_ROWS, preferred_element_type=F32))
         at = pl.ds(pair * wide, wide)
@@ -297,14 +306,7 @@
     ]
 
 
-def main_first_kernel(planes, wall_ref, main_ref, noise_ref, psi_ref):
-    refs = [noise_ref.at[w] for w in range(noise_ref.shape[0])]
-    rows = psi_ref.shape[1] // len(refs)
-    for t in range(0, planes, 2):
-        psi_ref[t], psi_ref[t + 1] = main_part(planes_of(refs, t, rows), wall_ref[0], main_ref[0])
-
-
-def main_next_kernel(planes, wall_ref, main_ref, *rest):
+def main_kernel(planes, wall_ref, main_ref, *rest):
     *refs, psi_ref = rest
     rows = psi_ref.shape[1] // len(refs)
     for t in range(0, psi_ref.shape[0], 2):
@@ -487,8 +489,11 @@
     def exchange(near, far):
         return lax.ppermute(near, "span", core_pairs), lax.ppermute(far, "span", chip_pairs)
 
-    def swap(x):
-        return lax.all_to_all(x, "wall", 0, 0, tiled=True)
+    def spread(blocks):
+        return [blocks[0]] + [
+            lax.ppermute(x, "wall", [(i, (i + step) % n_wall) for i in range(n_wall)])
+            for step, x in enumerate(blocks[1:], 1)
+        ]
 
     def send(x):
         return lax.all_to_all(x, ("span", "wall"), 0, 0, tiled=True).reshape(devices, n_wall * slots, -1)
@@ -498,15 +503,15 @@
     packed = call(
         functools.partial(pack_kernel, devices),
         [pl.BlockSpec((1, all_planes * rows, cols), lambda i: (0, 0, 0)), VMEM, VMEM, VMEM],
-        [hbm((n_wall, planes * rows + tail_rows(count), cols), BF16)],
+        [hbm((planes * rows + tail_rows(count), cols), BF16)] * n_wall,
         "pack",
         56,
         [pltpu.VMEM((tail_rows(count), cols), BF16), dma((n_wall,)), dma((n_wall,))],
         grid=(1,),
-        out_specs=[ANYWHERE],
+        out_specs=[ANYWHERE] * n_wall,
     )(noise, lund_factor, mean_velocity.reshape(1, rows), owners)
     noise, packed = lax.optimization_barrier((noise, packed))
-    packed = swap(packed)
+    packed = spread(packed)
 
     height = pairs * HALO
     edge = hbm((n_wall, rest, height, cols), BF16)
@@ -524,12 +529,6 @@
     rest_near, rest_far = exchange(near, far)
     packed, _ = lax.optimization_barrier((packed, (near, far, early)))
 
-    def spread(blocks):
-        return [blocks[0]] + [
-            lax.ppermute(x, "wall", [(i, (i + step) % n_wall) for i in range(n_wall)])
-            for step, x in enumerate(blocks[1:], 1)
-        ]
-
     def taps(first, some, make, name):
         return call(
             functools.partial(taps_kernel, first),
@@ -546,16 +545,16 @@
     wall_first, main_first, halo_first = taps(0, 1, struct, "taps_first")
     factor, target = call(
         functools.partial(small_kernel, slots),
-        [VMEM],
+        [VMEM] * n_wall,
         [struct((full, cols), F32), struct((n_wall, count, cols), jnp.int32)],
         "small",
         16,
-    )(packed)
+    )(*packed)
 
     edge = struct((planes * HALO, full), BF16)
     near, far = call(
-        functools.partial(edges_kernel, planes), [VMEM], [edge, edge], "edges_first", 16
-    )(packed)
+        functools.partial(edges_kernel, planes), [VMEM] * n_wall, [edge, edge], "edges_first", 16
+    )(*packed)
     near, far = exchange(near, far)
     early, rest_near = lax.optimization_barrier((early, rest_near))
     early = spread(early)
@@ -574,8 +573,8 @@
 
     psi = struct((planes, full, cols), F32)
     psi_main = call(
-        functools.partial(main_first_kernel, planes), [VMEM] * 3, [psi], "main_first", 16
-    )(wall_first, main_first, packed)
+        functools.partial(main_kernel, planes), [VMEM] * (2 + n_wall), [psi], "main_first", 16
+    )(wall_first, main_first, *packed)
 
     def scratch(some):
         return [
@@ -604,7 +603,7 @@
     late = spread(late)
     wall_rest, main_rest, halo_rest = taps(1, rest, struct, "taps_rest")
     psi_next = call(
-        functools.partial(main_next_kernel, planes),
+        functools.partial(main_kernel, planes),
         [VMEM] * (2 + n_wall),
         [struct((ahead, full, cols), F32)],
         "main_next",

time: 112 us -> 111 us (level)
  waiting for transfers between devices: 64.1 us -> 61.7 us
  starting transfers between devices: 25.3 us -> 26.6 us
    ppermute x6 -> x9, starting transfers between devices: 9.58 us -> 15.1 us  [spread(): lax.ppermute(x, 'wall', [(i, (i + step) % n_wall) for i in range(n_wall)])]
    all_to_all x1 -> x0, starting transfers between devices: 5.17 us -> none  [swap(): return lax.all_to_all(x, 'wall', 0, 0, tiled=True)]
    ppermute x2, waiting for transfers between devices: 2.39 us -> 0.01 us  [exchange(): lax.ppermute(far, 'span', chip_pairs)]
    ppermute x6 -> x9, waiting for transfers between devices: 8.44 us -> 8.46 us  [spread(): lax.ppermute(x, 'wall', [(i, (i + step) % n_wall) for i in range(n_wall)])]
  transfers between devices with their start and end apart: 13 -> 15, of which waited for: 6 -> 5; matrix products, arithmetic and copies ran while one was open for 0% -> 0% of each run, Pallas kernels for 16% -> 16%
where the time goes in v8:
time: 111 us; the launch traced here: 110 us
  waiting for transfers between devices  61.7 us (56%)
  starting transfers between devices  26.6 us (24%)
  Pallas kernels  21.6 us (19%)
    all_to_all x2, waiting for transfers between devices, send(): lax.all_to_all(x, ('span', 'wall'), 0, 0, tiled=True)  53.3 us
    ppermute x9, starting transfers between devices, spread(): lax.ppermute(x, 'wall', [(i, (i + step) % n_wall) for i in range(n_wall)])  15.1 us
    ppermute x9, waiting for transfers between devices, spread(): lax.ppermute(x, 'wall', [(i, (i + step) % n_wall) for i in range(n_wall)])  8.46 us
    all_to_all x2, starting transfers between devices, send(): lax.all_to_all(x, ('span', 'wall'), 0, 0, tiled=True)  5.99 us
    ppermute x2, starting transfers between devices, exchange(): lax.ppermute(far, 'span', chip_pairs)  5.4 us
    pallas_call x1, Pallas kernels, per_device(): call(functools.partial(rest_kernel, planes), [VMEM] * (7 + n_wall), [out(...  5.13 us
    pallas_call x1, Pallas kernels, per_device(): call(functools.partial(first_kernel, planes), [VMEM] * 7, [out(1), hbm(ps...  3.68 us
    pallas_call x2, Pallas kernels, join(): pl.pallas_call(functools.partial(join_narrow_kernel, some) if narrow else...  2.37 us
  transfers between devices with their start and end apart: 15, of which 5 were waited for; matrix products, arithmetic and copies ran while one was open for 0% of the time, Pallas kernels for 16%

profile of v8, /device:TPU:0, one launch (start us, length us, event | category | flops | bytes accessed | tf_op | source)
XLA Modules:
  0.0 110.3 jit_solution(10889536408741978684)
XLA Ops:
  0.0 2.1 %pack.1 = (bf16[544,128]{1,0:T(8,128)(2,1)}, bf16[544,128]{1,0:T(8,128)(2,1)}, bf16[544,128]{1,0:T(8,128)(2,1)}, bf16[544,128]{1,0:T(8,128)(2,1)}) custom-call(bf16[3,2048,128]{2,1,0:T(8,128)(2,1)} %bitcast.8, f32[6,64]{1,0:T(8,128)} %lund_ref.1, f32[1,64]{1,0:T(1,128)} %bitcast.12, s32[1,512]{1,0:T(1,128)} %bitcast.11), custom_call_target="tpu_custom_call" | custom-call | flops 1000000000 | bytes 1024 | tf_op jit(solution)/shard_map/pack/pallas_call | solution.py:503
  2.1 0.0 copy-start.2
  2.1 0.0 copy-start.3
  2.1 3.0 %collective-permute-start = (bf16[544,128]{1,0:T(8,128)(2,1)}, bf16[544,128]{1,0:T(8,128)(2,1)S(1)}, u32[]{:S(2)}, u32[]{:S(2)}) collective-permute-start(bf16[544,128]{1,0:T(8,128)(2,1)} %get-tuple-element.66), channel_id=1, source_target_pairs={{0,1},{1,2},{2,3},{3,0},{4,5},{5,6},{6,7},{7,4},{8,9},{9,10},{10,1... | collective-permute-start | bytes 417800 | tf_op jit(solution)/shard_map/ppermute | solution.py:494
  5.1 1.5 %collective-permute-start.1 = (bf16[544,128]{1,0:T(8,128)(2,1)}, bf16[544,128]{1,0:T(8,128)(2,1)S(1)}, u32[]{:S(2)}, u32[]{:S(2)}) collective-permute-start(bf16[544,128]{1,0:T(8,128)(2,1)} %get-tuple-element.67), channel_id=1, source_target_pairs={{0,2},{1,3},{2,0},{3,1},{4,6},{5,7},{6,4},{7,5},{8,10},{9,11},{10,... | collective-permute-start | bytes 417800 | tf_op jit(solution)/shard_map/ppermute | solution.py:494
  6.6 1.4 %collective-permute-start.2 = (bf16[544,128]{1,0:T(8,128)(2,1)}, bf16[544,128]{1,0:T(8,128)(2,1)S(1)}, u32[]{:S(2)}, u32[]{:S(2)}) collective-permute-start(bf16[544,128]{1,0:T(8,128)(2,1)} %get-tuple-element.68), channel_id=1, source_target_pairs={{0,3},{1,0},{2,1},{3,2},{4,7},{5,4},{6,5},{7,6},{8,11},{9,8},{10,9... | collective-permute-start | bytes 417800 | tf_op jit(solution)/shard_map/ppermute | solution.py:494
  8.1 2.4 %prepare_rest.1 = (bf16[4,2,96,128]{3,2,1,0:T(8,128)(2,1)}, bf16[4,2,96,128]{3,2,1,0:T(8,128)(2,1)}, bf16[1024,128]{1,0:T(8,128)(2,1)}, bf16[1024,128]{1,0:T(8,1...) custom-call(bf16[3,2048,128]{2,1,0:T(8,128)(2,1)S(1)} %bitcast.9), custom_call_target="tpu_custom_call" | custom-call | flops 1000000000 | bytes 1024 | tf_op jit(solution)/shard_map/prepare_rest/pallas_call | solution.py:519
  10.5 0.1 collective-permute-start.4
  10.5 3.7 %collective-permute-start.5 = (bf16[4,2,96,128]{3,2,1,0:T(8,128)(2,1)}, bf16[4,2,96,128]{3,2,1,0:T(8,128)(2,1)S(1)}, u32[]{:S(2)}, u32[]{:S(2)}) collective-permute-start(bf16[4,2,96,128]{3,2,1,0:T(8,128)(2,1)} %get-tuple-element.71), channel_id=1, source_target_pairs={{0,28},{4,8},{8,4},{12,16},{16,12},{20,24},{24,20},{28,0},{1,29},{... | collective-permute-start | bytes 589832 | tf_op jit(solution)/shard_map/ppermute | solution.py:490
  14.2 0.0 copy-done.2
  14.2 0.9 taps_first.1
  15.2 0.0 collective-permute-done.rest_1_
  15.2 0.0 collective-permute-done.1.rest_2_
  15.2 0.0 collective-permute-done.2.rest_3_
  15.2 0.3 edges_first.1
  15.5 0.0 copy-start.9
  15.5 0.1 collective-permute-start.3
  15.6 1.7 %collective-permute-start.6 = (bf16[192,256]{1,0:T(8,128)(2,1)S(1)}, bf16[192,256]{1,0:T(8,128)(2,1)S(1)}, u32[]{:S(2)}, u32[]{:S(2)}) collective-permute-start(bf16[192,256]{1,0:T(8,128)(2,1)S(1)} %get-tuple-element.82), channel_id=1, source_target_pairs={{0,28},{4,8},{8,4},{12,16},{16,12},{20,24},{24,20},{28,0},{1,29},{... | collective-permute-start | bytes 294920 | tf_op jit(solution)/shard_map/ppermute | solution.py:490
  17.3 0.4 small.1
  17.7 0.0 collective-permute-done.4.near_ref
  17.7 1.8 %collective-permute-start.7 = (bf16[1024,128]{1,0:T(8,128)(2,1)S(1)}, bf16[1024,128]{1,0:T(8,128)(2,1)S(1)}, u32[]{:S(2)}, u32[]{:S(2)}) collective-permute-start(bf16[1024,128]{1,0:T(8,128)(2,1)S(1)} %copy-done.9), channel_id=1, source_target_pairs={{0,1},{1,2},{2,3},{3,0},{4,5},{5,6},{6,7},{7,4},{8,9},{9,10},{10,1... | collective-permute-start | bytes 786440 | tf_op jit(solution)/shard_map/ppermute | solution.py:494
  19.5 0.9 main_first.1.psi_in
  20.4 0.6 collective-permute-start.8
  21.0 0.0 collective-permute-done.5.far_ref
  21.0 0.0 copy-done.7
  21.0 2.1 %collective-permute-start.9 = (bf16[1024,128]{1,0:T(8,128)(2,1)S(1)}, bf16[1024,128]{1,0:T(8,128)(2,1)S(1)}, u32[]{:S(2)}, u32[]{:S(2)}) collective-permute-start(bf16[1024,128]{1,0:T(8,128)(2,1)S(1)} %copy-done.7), channel_id=1, source_target_pairs={{0,3},{1,0},{2,1},{3,2},{4,7},{5,4},{6,5},{7,6},{8,11},{9,8},{10,9... | collective-permute-start | bytes 786440 | tf_op jit(solution)/shard_map/ppermute | solution.py:494
  23.1 0.0 collective-permute-done.3.near_ref
  23.1 0.0 collective-permute-done.6.far_ref
  23.2 0.9 pack_late.1
  24.1 3.7 %filter_first.1 = (bf16[32,4,32,128]{3,2,1,0:T(8,128)(2,1)}, f32[8,256,128]{2,1,0:T(8,128)}) custom-call(f32[8,256,128]{2,1,0:T(8,128)S(1)} %main_first.1.psi_in, bf16[192,256]{1,0:T(8,128)(2,1)S(1)} %collective-permute-done.3.near_ref, bf16[192,256]{1,0:T(8,128)(2,1)S(1)} %collective-permute-done.6.far_ref, f32[256,128]{1,0:T(8,128)S(1)} %get-tuple-element.90.factor_ref, ...), custom_call_target="tpu_custom_call" | custom-call | flops 1000000000 | bytes 1024 | tf_op jit(solution)/shard_map/filter_first/pallas_call | solution.py:592
  27.8 2.7 %all-to-all-start.1 = ((bf16[32,4,32,128]{3,2,1,0:T(8,128)(2,1)}), bf16[32,4,32,128]{3,2,1,0:T(8,128)(2,1)S(1)}, u32[]{:S(2)}, u32[]{:S(2)}) async-start(bf16[32,4,32,128]{3,2,1,0:T(8,128)(2,1)} %get-tuple-element.112), calls=%async_computation.1 | async-start | bytes 2097152 | tf_op jit(solution)/shard_map/all_to_all | solution.py:499
  30.5 1.7 %collective-permute-start.10 = (bf16[384,128]{1,0:T(8,128)(2,1)S(1)}, bf16[384,128]{1,0:T(8,128)(2,1)S(1)}, u32[]{:S(2)}, u32[]{:S(2)}) collective-permute-start(bf16[384,128]{1,0:T(8,128)(2,1)S(1)} %copy-done.12), channel_id=1, source_target_pairs={{0,1},{1,2},{2,3},{3,0},{4,5},{5,6},{6,7},{7,4},{8,9},{9,10},{10,1... | collective-permute-start | bytes 294920 | tf_op jit(solution)/shard_map/ppermute | solution.py:494
  32.2 1.5 %collective-permute-start.11 = (bf16[384,128]{1,0:T(8,128)(2,1)S(1)}, bf16[384,128]{1,0:T(8,128)(2,1)S(1)}, u32[]{:S(2)}, u32[]{:S(2)}) collective-permute-start(bf16[384,128]{1,0:T(8,128)(2,1)S(1)} %copy-done.11), channel_id=1, source_target_pairs={{0,2},{1,3},{2,0},{3,1},{4,6},{5,7},{6,4},{7,5},{8,10},{9,11},{10,... | collective-permute-start | bytes 294920 | tf_op jit(solution)/shard_map/ppermute | solution.py:494
  33.7 0.0 collective-permute-done.7.rest_1_
  33.7 1.4 %collective-permute-start.12 = (bf16[384,128]{1,0:T(8,128)(2,1)S(1)}, bf16[384,128]{1,0:T(8,128)(2,1)S(1)}, u32[]{:S(2)}, u32[]{:S(2)}) collective-permute-start(bf16[384,128]{1,0:T(8,128)(2,1)S(1)} %copy-done.10), channel_id=1, source_target_pairs={{0,3},{1,0},{2,1},{3,2},{4,7},{5,4},{6,5},{7,6},{8,11},{9,8},{10,9... | collective-permute-start | bytes 294920 | tf_op jit(solution)/shard_map/ppermute | solution.py:494
  35.2 1.1 taps_rest.1
  36.3 0.0 collective-permute-done.8.rest_2_
  36.3 0.0 collective-permute-done.9.rest_3_
  36.3 1.4 %main_next.1.next_ref = f32[16,256,128]{2,1,0:T(8,128)S(1)} custom-call(bf16[2,256,512]{2,1,0:T(8,128)(2,1)S(1)} %get-tuple-element.101.wall_ref, bf16[2,256,256]{2,1,0:T(8,128)(2,1)S(1)} %get-tuple-element.102.main_ref, bf16[1024,128]{1,0:T(8,128)(2,1)S(1)} %copy-done, bf16[1024,128]{1,0:T(8,128)(2,1)S(1)} %collective-permute-done.7.rest_1_, ...), custom_call_target="tpu_custom_call" | custom-call | flops 1000000000 | bytes 1024 | tf_op jit(solution)/shard_map/main_next/pallas_call | solution.py:605
  37.8 6.5 %collective-permute-done.10.rest_1_ = bf16[384,128]{1,0:T(8,128)(2,1)S(1)} collective-permute-done((bf16[384,128]{1,0:T(8,128)(2,1)S(1)}, bf16[384,128]{1,0:T(8,128)(2,1)S(1)}, u32[]{:S(2)}, u32[]{:S(2)}) %collective-permute-start.10) | collective-permute-done | bytes 98336 | tf_op jit(solution)/shard_map/ppermute | solution.py:494
  44.2 1.7 %collective-permute-done.11.rest_2_ = bf16[384,128]{1,0:T(8,128)(2,1)S(1)} collective-permute-done((bf16[384,128]{1,0:T(8,128)(2,1)S(1)}, bf16[384,128]{1,0:T(8,128)(2,1)S(1)}, u32[]{:S(2)}, u32[]{:S(2)}) %collective-permute-start.11) | collective-permute-done | bytes 98336 | tf_op jit(solution)/shard_map/ppermute | solution.py:494
  46.0 0.2 collective-permute-done.12.rest_3_
  46.2 5.1 %filter_rest.1 = bf16[32,4,32,256]{3,2,1,0:T(8,128)(2,1)} custom-call(f32[8,256,128]{2,1,0:T(8,128)S(1)} %copy-done.4, f32[16,256,128]{2,1,0:T(8,128)S(1)} %main_next.1.next_ref, f32[256,128]{1,0:T(8,128)S(1)} %get-tuple-element.90.factor_ref, s32[4,4,128]{2,1,0:T(4,128)S(1)} %get-tuple-element.91.target_ref, ...), custom_call_target="tpu_custom_call" | custom-call | flops 99999997952 | bytes 1024 | tf_op jit(solution)/shard_map/filter_rest/pallas_call | solution.py:612
  51.3 5.6 %all-to-all-done.1 = bf16[32,4,32,128]{3,2,1,0:T(8,128)(2,1)S(1)} async-done(((bf16[32,4,32,128]{3,2,1,0:T(8,128)(2,1)}), bf16[32,4,32,128]{3,2,1,0:T(8,128)(2,1)S(1)}, u32[]{:S(2)}, u32[]{:S(2)}) %all-to-all-start.1) | async-done | bytes 1048608 | tf_op jit(solution)/shard_map/all_to_all | solution.py:499
  56.9 3.3 %all-to-all-start = ((bf16[32,4,32,256]{3,2,1,0:T(8,128)(2,1)}), bf16[32,4,32,256]{3,2,1,0:T(8,128)(2,1)S(1)}, u32[]{:S(2)}, u32[]{:S(2)}) async-start(bf16[32,4,32,256]{3,2,1,0:T(8,128)(2,1)} %filter_rest.1), calls=%async_computation | async-start | bytes 4194304 | tf_op jit(solution)/shard_map/all_to_all | solution.py:499
  60.3 1.0 join.2.rest_0_
  61.3 47.7 %all-to-all-done = bf16[32,4,32,256]{3,2,1,0:T(8,128)(2,1)S(1)} async-done(((bf16[32,4,32,256]{3,2,1,0:T(8,128)(2,1)}), bf16[32,4,32,256]{3,2,1,0:T(8,128)(2,1)S(1)}, u32[]{:S(2)}, u32[]{:S(2)}) %all-to-all-start) | async-done | bytes 2097184 | tf_op jit(solution)/shard_map/all_to_all | solution.py:499
  109.0 1.4 %join.3 = bf16[8,128,1536]{2,1,0:T(8,128)(2,1)} custom-call(bf16[8,4,128,256]{3,2,1,0:T(8,128)(2,1)S(1)} %bitcast.6, bf16[8,128,1536]{2,1,0:T(8,128)(2,1)} %join.2.rest_0_), custom_call_target="tpu_custom_call", output_to_operand_aliasing={{}: (1, {})} | custom-call | tf_op jit(solution)/shard_map/join/pallas_call | solution.py:630
  (21 shorter events, 0.0 us)
Async XLA Ops:
  0.0 8.1 %copy-start.1 = (bf16[3,32,64,128]{3,2,1,0:T(8,128)(2,1)S(1)}, bf16[3,32,64,128]{3,2,1,0:T(8,128)(2,1)}, u32[]{:S(2)}) copy-start(bf16[3,32,64,128]{3,2,1,0:T(8,128)(2,1)} %param.6) | copy-start | bytes 4718596
  2.1 12.1 %copy-start.2 = (f32[3]{0:T(128)S(1)}, f32[3]{0:T(128)}, u32[]{:S(2)}) copy-start(f32[3]{0:T(128)} %wall_scale.2) | copy-start | bytes 40
  2.1 12.1 %copy-start.3 = (f32[3]{0:T(128)S(1)}, f32[3]{0:T(128)}, u32[]{:S(2)}) copy-start(f32[3]{0:T(128)} %span_scale.2) | copy-start | bytes 40
  2.1 13.0 %collective-permute-start = (bf16[544,128]{1,0:T(8,128)(2,1)}, bf16[544,128]{1,0:T(8,128)(2,1)S(1)}, u32[]{:S(2)}, u32[]{:S(2)}) collective-permute-start(bf16[544,128]{1,0:T(8,128)(2,1)} %get-tuple-element.66), channel_id=1, source_target_pairs={{0,1},{1,2},{2,3},{3,0},{4,5},{5,6},{6,7},{7,4},{8,9},{9,10},{10,1... | collective-permute-start | bytes 417800 | tf_op jit(solution)/shard_map/ppermute | solution.py:494
  5.1 10.1 %collective-permute-start.1 = (bf16[544,128]{1,0:T(8,128)(2,1)}, bf16[544,128]{1,0:T(8,128)(2,1)S(1)}, u32[]{:S(2)}, u32[]{:S(2)}) collective-permute-start(bf16[544,128]{1,0:T(8,128)(2,1)} %get-tuple-element.67), channel_id=1, source_target_pairs={{0,2},{1,3},{2,0},{3,1},{4,6},{5,7},{6,4},{7,5},{8,10},{9,11},{10,... | collective-permute-start | bytes 417800 | tf_op jit(solution)/shard_map/ppermute | solution.py:494
  6.6 8.6 %collective-permute-start.2 = (bf16[544,128]{1,0:T(8,128)(2,1)}, bf16[544,128]{1,0:T(8,128)(2,1)S(1)}, u32[]{:S(2)}, u32[]{:S(2)}) collective-permute-start(bf16[544,128]{1,0:T(8,128)(2,1)} %get-tuple-element.68), channel_id=1, source_target_pairs={{0,3},{1,0},{2,1},{3,2},{4,7},{5,4},{6,5},{7,6},{8,11},{9,8},{10,9... | collective-permute-start | bytes 417800 | tf_op jit(solution)/shard_map/ppermute | solution.py:494
  10.4 4.8 %copy-start.5 = (bf16[544,128]{1,0:T(8,128)(2,1)S(1)}, bf16[544,128]{1,0:T(8,128)(2,1)}, u32[]{:S(2)}) copy-start(bf16[544,128]{1,0:T(8,128)(2,1)} %get-tuple-element.76.rest_0_) | copy-start | bytes 417796
  10.5 7.2 %collective-permute-start.4 = (bf16[4,2,96,128]{3,2,1,0:T(8,128)(2,1)}, bf16[4,2,96,128]{3,2,1,0:T(8,128)(2,1)S(1)}, u32[]{:S(2)}, u32[]{:S(2)}) collective-permute-start(bf16[4,2,96,128]{3,2,1,0:T(8,128)(2,1)} %get-tuple-element.70), channel_id=1, source_target_pairs={{0,4},{4,0},{8,12},{12,8},{16,20},{20,16},{24,28},{28,24},{1,5},{5... | collective-permute-start | bytes 589832 | tf_op jit(solution)/shard_map/ppermute | solution.py:490
  10.5 10.5 %collective-permute-start.5 = (bf16[4,2,96,128]{3,2,1,0:T(8,128)(2,1)}, bf16[4,2,96,128]{3,2,1,0:T(8,128)(2,1)S(1)}, u32[]{:S(2)}, u32[]{:S(2)}) collective-permute-start(bf16[4,2,96,128]{3,2,1,0:T(8,128)(2,1)} %get-tuple-element.71), channel_id=1, source_target_pairs={{0,28},{4,8},{8,4},{12,16},{16,12},{20,24},{24,20},{28,0},{1,29},{... | collective-permute-start | bytes 589832 | tf_op jit(solution)/shard_map/ppermute | solution.py:490
  15.5 2.2 %copy-start.9 = (bf16[1024,128]{1,0:T(8,128)(2,1)S(1)}, bf16[1024,128]{1,0:T(8,128)(2,1)}, u32[]{:S(2)}) copy-start(bf16[1024,128]{1,0:T(8,128)(2,1)} %get-tuple-element.104) | copy-start | bytes 786436
  15.5 7.6 %collective-permute-start.3 = (bf16[192,256]{1,0:T(8,128)(2,1)S(1)}, bf16[192,256]{1,0:T(8,128)(2,1)S(1)}, u32[]{:S(2)}, u32[]{:S(2)}) collective-permute-start(bf16[192,256]{1,0:T(8,128)(2,1)S(1)} %get-tuple-element.80), channel_id=1, source_target_pairs={{0,4},{4,0},{8,12},{12,8},{16,20},{20,16},{24,28},{28,24},{1,5},{5... | collective-permute-start | bytes 294920 | tf_op jit(solution)/shard_map/ppermute | solution.py:490
  15.6 7.6 %collective-permute-start.6 = (bf16[192,256]{1,0:T(8,128)(2,1)S(1)}, bf16[192,256]{1,0:T(8,128)(2,1)S(1)}, u32[]{:S(2)}, u32[]{:S(2)}) collective-permute-start(bf16[192,256]{1,0:T(8,128)(2,1)S(1)} %get-tuple-element.82), channel_id=1, source_target_pairs={{0,28},{4,8},{8,4},{12,16},{16,12},{20,24},{24,20},{28,0},{1,29},{... | collective-permute-start | bytes 294920 | tf_op jit(solution)/shard_map/ppermute | solution.py:490
  17.7 2.7 %copy-start.8 = (bf16[1024,128]{1,0:T(8,128)(2,1)S(1)}, bf16[1024,128]{1,0:T(8,128)(2,1)}, u32[]{:S(2)}) copy-start(bf16[1024,128]{1,0:T(8,128)(2,1)} %get-tuple-element.105) | copy-start | bytes 786436
  17.7 3.3 %copy-start.7 = (bf16[1024,128]{1,0:T(8,128)(2,1)S(1)}, bf16[1024,128]{1,0:T(8,128)(2,1)}, u32[]{:S(2)}) copy-start(bf16[1024,128]{1,0:T(8,128)(2,1)} %get-tuple-element.106) | copy-start | bytes 786436
  17.7 16.0 %collective-permute-start.7 = (bf16[1024,128]{1,0:T(8,128)(2,1)S(1)}, bf16[1024,128]{1,0:T(8,128)(2,1)S(1)}, u32[]{:S(2)}, u32[]{:S(2)}) collective-permute-start(bf16[1024,128]{1,0:T(8,128)(2,1)S(1)} %copy-done.9), channel_id=1, source_target_pairs={{0,1},{1,2},{2,3},{3,0},{4,5},{5,6},{6,7},{7,4},{8,9},{9,10},{10,1... | collective-permute-start | bytes 786440 | tf_op jit(solution)/shard_map/ppermute | solution.py:494
  20.4 15.8 %collective-permute-start.8 = (bf16[1024,128]{1,0:T(8,128)(2,1)S(1)}, bf16[1024,128]{1,0:T(8,128)(2,1)S(1)}, u32[]{:S(2)}, u32[]{:S(2)}) collective-permute-start(bf16[1024,128]{1,0:T(8,128)(2,1)S(1)} %copy-done.8), channel_id=1, source_target_pairs={{0,2},{1,3},{2,0},{3,1},{4,6},{5,7},{6,4},{7,5},{8,10},{9,11},{10,... | collective-permute-start | bytes 786440 | tf_op jit(solution)/shard_map/ppermute | solution.py:494
  21.0 15.3 %collective-permute-start.9 = (bf16[1024,128]{1,0:T(8,128)(2,1)S(1)}, bf16[1024,128]{1,0:T(8,128)(2,1)S(1)}, u32[]{:S(2)}, u32[]{:S(2)}) collective-permute-start(bf16[1024,128]{1,0:T(8,128)(2,1)S(1)} %copy-done.7), channel_id=1, source_target_pairs={{0,3},{1,0},{2,1},{3,2},{4,7},{5,4},{6,5},{7,6},{8,11},{9,8},{10,9... | collective-permute-start | bytes 786440 | tf_op jit(solution)/shard_map/ppermute | solution.py:494
  24.1 6.4 %copy-start.12 = (bf16[384,128]{1,0:T(8,128)(2,1)S(1)}, bf16[384,128]{1,0:T(8,128)(2,1)}, u32[]{:S(2)}) copy-start(bf16[384,128]{1,0:T(8,128)(2,1)} %get-tuple-element.109) | copy-start | bytes 294916
  24.1 8.1 %copy-start.11 = (bf16[384,128]{1,0:T(8,128)(2,1)S(1)}, bf16[384,128]{1,0:T(8,128)(2,1)}, u32[]{:S(2)}) copy-start(bf16[384,128]{1,0:T(8,128)(2,1)} %get-tuple-element.110) | copy-start | bytes 294916
  24.1 9.6 %copy-start.10 = (bf16[384,128]{1,0:T(8,128)(2,1)S(1)}, bf16[384,128]{1,0:T(8,128)(2,1)}, u32[]{:S(2)}) copy-start(bf16[384,128]{1,0:T(8,128)(2,1)} %get-tuple-element.111) | copy-start | bytes 294916
  27.8 29.1 %all-to-all-start.1 = ((bf16[32,4,32,128]{3,2,1,0:T(8,128)(2,1)}), bf16[32,4,32,128]{3,2,1,0:T(8,128)(2,1)S(1)}, u32[]{:S(2)}, u32[]{:S(2)}) async-start(bf16[32,4,32,128]{3,2,1,0:T(8,128)(2,1)} %get-tuple-element.112), calls=%async_computation.1 | async-start | bytes 2097152 | tf_op jit(solution)/shard_map/all_to_all | solution.py:499
  30.5 5.8 %copy-start = (bf16[1024,128]{1,0:T(8,128)(2,1)S(1)}, bf16[1024,128]{1,0:T(8,128)(2,1)}, u32[]{:S(2)}) copy-start(bf16[1024,128]{1,0:T(8,128)(2,1)} %get-tuple-element.103.rest_0_) | copy-start | bytes 786436
  30.5 13.7 %collective-permute-start.10 = (bf16[384,128]{1,0:T(8,128)(2,1)S(1)}, bf16[384,128]{1,0:T(8,128)(2,1)S(1)}, u32[]{:S(2)}, u32[]{:S(2)}) collective-permute-start(bf16[384,128]{1,0:T(8,128)(2,1)S(1)} %copy-done.12), channel_id=1, source_target_pairs={{0,1},{1,2},{2,3},{3,0},{4,5},{5,6},{6,7},{7,4},{8,9},{9,10},{10,1... | collective-permute-start | bytes 294920 | tf_op jit(solution)/shard_map/ppermute | solution.py:494
  32.2 13.8 %collective-permute-start.11 = (bf16[384,128]{1,0:T(8,128)(2,1)S(1)}, bf16[384,128]{1,0:T(8,128)(2,1)S(1)}, u32[]{:S(2)}, u32[]{:S(2)}) collective-permute-start(bf16[384,128]{1,0:T(8,128)(2,1)S(1)} %copy-done.11), channel_id=1, source_target_pairs={{0,2},{1,3},{2,0},{3,1},{4,6},{5,7},{6,4},{7,5},{8,10},{9,11},{10,... | collective-permute-start | bytes 294920 | tf_op jit(solution)/shard_map/ppermute | solution.py:494
  33.7 12.5 %collective-permute-start.12 = (bf16[384,128]{1,0:T(8,128)(2,1)S(1)}, bf16[384,128]{1,0:T(8,128)(2,1)S(1)}, u32[]{:S(2)}, u32[]{:S(2)}) collective-permute-start(bf16[384,128]{1,0:T(8,128)(2,1)S(1)} %copy-done.10), channel_id=1, source_target_pairs={{0,3},{1,0},{2,1},{3,2},{4,7},{5,4},{6,5},{7,6},{8,11},{9,8},{10,9... | collective-permute-start | bytes 294920 | tf_op jit(solution)/shard_map/ppermute | solution.py:494
  36.3 9.9 %copy-start.4 = (f32[8,256,128]{2,1,0:T(8,128)S(1)}, f32[8,256,128]{2,1,0:T(8,128)}, u32[]{:S(2)}) copy-start(f32[8,256,128]{2,1,0:T(8,128)} %get-tuple-element.93.psi_ref) | copy-start | bytes 3145732
  36.3 9.9 %copy-start.6 = (bf16[384,128]{1,0:T(8,128)(2,1)S(1)}, bf16[384,128]{1,0:T(8,128)(2,1)}, u32[]{:S(2)}) copy-start(bf16[384,128]{1,0:T(8,128)(2,1)} %get-tuple-element.108.rest_0_) | copy-start | bytes 294916
  56.9 52.0 %all-to-all-start = ((bf16[32,4,32,256]{3,2,1,0:T(8,128)(2,1)}), bf16[32,4,32,256]{3,2,1,0:T(8,128)(2,1)S(1)}, u32[]{:S(2)}, u32[]{:S(2)}) async-start(bf16[32,4,32,256]{3,2,1,0:T(8,128)(2,1)} %filter_rest.1), calls=%async_computation | async-start | bytes 4194304 | tf_op jit(solution)/shard_map/all_to_all | solution.py:499

commit v9 on v8

--- a/solution.py
+++ b/solution.py
@@ -88,23 +88,18 @@
         copy.wait()
 
 
-def pack_kernel(devices, noise_ref, lund_ref, mean_ref, owner_ref, *rest):
-    *out_refs, small_ref, noise_sems, small_sems = rest
+def pack_kernel(devices, noise_in, lund_in, mean_in, owner_in, *rest):
+    *out_refs, noise_ref, lund_ref, mean_ref, owner_ref, sems = rest
     walls = len(out_refs)
-    tail, cols = small_ref.shape
-    block = out_refs[0].shape[0] - tail
+    cols = noise_ref.shape[1]
+    block = noise_ref.shape[0] // walls
+    tail = out_refs[0].shape[0] - block
     rows = mean_ref.shape[1]
     me = lax.axis_index("wall")
-    copies = []
-    for step, out_ref in enumerate(out_refs):
-        start = pl.multiple_of(lax.rem(me + step, walls) * block, block)
-        copies.append(
-            pltpu.make_async_copy(
-                noise_ref.at[0, pl.ds(start, block)], out_ref.at[pl.ds(0, block)], noise_sems.at[step]
-            )
-        )
-    for copy in copies:
-        copy.start()
+    pairs = ((lund_in, lund_ref), (mean_in, mean_ref), (owner_in, owner_ref), (noise_in.at[0], noise_ref))
+    *small, noise = [pltpu.make_async_copy(a, b, sems.at[i]) for i, (a, b) in enumerate(pairs)]
+    noise.start()
+    run(small)
     owner = owner_ref[...]
     elements = owner.shape[1]
     mine = jnp.where(iota((devices, elements), 0) == owner, 1.0, 0.0)
@@ -120,35 +115,29 @@
         pieces.append(part)
         factor = factor - part
     pieces.append(jnp.zeros((tail - sum(p.shape[0] for p in pieces), cols), F32))
-    small_ref[...] = jnp.concatenate(pieces, axis=0).astype(BF16)
-    run(
-        [
-            pltpu.make_async_copy(small_ref, out_ref.at[pl.ds(block, tail)], small_sems.at[step])
-            for step, out_ref in enumerate(out_refs)
-        ]
-    )
-    for copy in copies:
-        copy.wait()
-
-
-def pack_late_kernel(noise_ref, near_ref, far_ref, *rest):
+    small = jnp.concatenate(pieces, axis=0).astype(BF16)
+    noise.wait()
+    for step, out_ref in enumerate(out_refs):
+        start = pl.multiple_of(lax.rem(me + step, walls) * block, block)
+        out_ref[:block] = noise_ref[pl.ds(start, block)]
+        out_ref[block:] = small
+
+
+def pack_late_kernel(near_ref, far_ref, *rest):
     out_refs, sems = rest[:-1], rest[-1]
     walls, some, height, _ = near_ref.shape
-    block = noise_ref.shape[1] // walls
     me = lax.axis_index("wall")
     copies = []
     for step, out_ref in enumerate(out_refs):
         to = lax.rem(me + step, walls)
-        left = out_ref.shape[0] - 2 * some * height
-        source = pl.multiple_of(to * block + block - left, math.gcd(block, left) or block)
-        parts = [(noise_ref.at[0, pl.ds(source, left)], 0, left)] if left else []
         for side, ref in enumerate((near_ref, far_ref)):
             for c in range(some):
-                parts.append((ref.at[to, c], left + (side * some + c) * height, height))
-        for part, (ref, start, size) in enumerate(parts):
-            copies.append(
-                pltpu.make_async_copy(ref, out_ref.at[pl.ds(start, size)], sems.at[step, part])
-            )
+                at = side * some + c
+                copies.append(
+                    pltpu.make_async_copy(
+                        ref.at[to, c], out_ref.at[pl.ds(at * height, height)], sems.at[step, at]
+                    )
+                )
     run(copies)
 
 
@@ -201,38 +190,15 @@
         far_ref[at] = jnp.concatenate([e[HALO:] for e in edges], axis=0).astype(BF16)
 
 
-def prepare_rest_kernel(noise_ref, near_ref, far_ref, *rest):
-    out_refs, sems = rest[:-1], rest[-1]
+def prepare_rest_kernel(noise_ref, near_ref, far_ref, *out_refs):
     walls, _, height, cols = near_ref.shape
     block = noise_ref.shape[1] // walls
     me = lax.axis_index("wall")
     c = pl.program_id(0)
-    last = pl.num_programs(0) - 1
-
-    def copies(size):
-        out = []
-        for step, out_ref in enumerate(out_refs):
-            source = pl.multiple_of(lax.rem(me + step, walls) * block, block)
-            target = pl.multiple_of(c * block, block)
-            out.append(
-                pltpu.make_async_copy(
-                    noise_ref.at[0, pl.ds(source, size)], out_ref.at[pl.ds(target, size)], sems.at[step]
-                )
-            )
-        return out
-
-    def each(do):
-        @pl.when(c < last)
-        def _():
-            for copy in copies(block):
-                do(copy)
-
-        @pl.when(c == last)
-        def _():
-            for copy in copies(out_refs[0].shape[0] - last * block):
-                do(copy)
-
-    each(lambda copy: copy.start())
+    target = pl.ds(pl.multiple_of(c * block, block), block)
+    for step, out_ref in enumerate(out_refs):
+        source = pl.multiple_of(lax.rem(me + step, walls) * block, block)
+        out_ref[target] = noise_ref[0, pl.ds(source, block)]
     pairs = height // HALO
     pick = edge_picker(cols)
     for w in range(walls):
@@ -240,10 +206,8 @@
         for pair in range(pairs):
             plane = noise_ref[0, (w * pairs + pair) * cols : (w * pairs + pair + 1) * cols]
             edges.append(lax.dot_general(pick, plane, ROWS_BY_ROWS, preferred_element_type=F32))
-        near_ref[w, 0] = jnp.concatenate([e[:HALO] for e in edges], axis=0).astype(BF16)
-        far_ref[w, 0] = jnp.concatenate([e[HALO:] for e in edges], axis=0).astype(BF16)
-
-    each(lambda copy: copy.wait())
+        near_ref[w, c] = jnp.concatenate([e[:HALO] for e in edges], axis=0).astype(BF16)
+        far_ref[w, c] = jnp.concatenate([e[HALO:] for e in edges], axis=0).astype(BF16)
 
 
 def swap_blocks(blocks, cols):
@@ -391,13 +355,11 @@
     *late_refs, out_ref, cells_ref, tile_ref, wide_ref, sent_ref, sems = rest
     full, cols = psi_ref.shape[1:]
     some = wall_ref.shape[0]
-    rows = full // len(late_refs)
     pairs = planes // 2
     height = pairs * HALO
     widen(factor_ref, wide_ref, range(1, 6))
     for c in range(some):
-        left = (some * planes - next_ref.shape[0]) * rows
-        starts = [left + (side * some + c) * height for side in range(2)]
+        starts = [(side * some + c) * height for side in range(2)]
         parts = [[ref[pl.ds(at, height)].astype(F32) for ref in late_refs] for at in starts]
         for pair, tile in enumerate(halo_tiles(parts, cols)):
             tile_ref[c * pairs + pair] = tile
@@ -405,12 +367,7 @@
     for pair in range(pairs):
         psi = []
         for c in range(some):
-            at = c * planes + 2 * pair
-            if at < next_ref.shape[0]:
-                main = [next_ref[at], next_ref[at + 1]]
-            else:
-                at = at - next_ref.shape[0]
-                main = main_part(planes_of(late_refs, at, rows), wall_ref[c], main_ref[c])
+            main = [next_ref[c * planes + 2 * pair + odd] for odd in range(2)]
             beside = halo_part(tile_ref[c * pairs + pair], wall_ref[c], halo_ref.at[c])
             psi.append([m + b for m, b in zip(main, beside)])
         for odd in range(2):
@@ -465,7 +422,6 @@
     slots = max(8, 2 * elements // devices)
     count = elements // cols
     rest = trio - 1
-    ahead = rest * planes
     struct = jax.ShapeDtypeStruct
     hbm = pltpu.MemorySpace.HBM
 
@@ -502,29 +458,30 @@
     noise = noise.reshape(trio, all_planes * rows, cols)
     packed = call(
         functools.partial(pack_kernel, devices),
-        [pl.BlockSpec((1, all_planes * rows, cols), lambda i: (0, 0, 0)), VMEM, VMEM, VMEM],
-        [hbm((planes * rows + tail_rows(count), cols), BF16)] * n_wall,
+        [pl.BlockSpec(memory_space=hbm)] * 4,
+        [pltpu.MemorySpace.VMEM((planes * rows + tail_rows(count), cols), BF16)] * n_wall,
         "pack",
         56,
-        [pltpu.VMEM((tail_rows(count), cols), BF16), dma((n_wall,)), dma((n_wall,))],
-        grid=(1,),
-        out_specs=[ANYWHERE] * n_wall,
+        [
+            pltpu.VMEM((all_planes * rows, cols), BF16),
+            pltpu.VMEM(lund_factor.shape, F32),
+            pltpu.VMEM((1, rows), F32),
+            pltpu.VMEM(owners.shape, jnp.int32),
+            dma((4,)),
+        ],
     )(noise, lund_factor, mean_velocity.reshape(1, rows), owners)
     noise, packed = lax.optimization_barrier((noise, packed))
     packed = spread(packed)
 
     height = pairs * HALO
-    edge = hbm((n_wall, rest, height, cols), BF16)
-    spec = pl.BlockSpec((n_wall, 1, height, cols), lambda c: (0, c, 0, 0))
+    edge = struct((n_wall, rest, height, cols), BF16)
     near, far, *early = call(
         prepare_rest_kernel,
         [pl.BlockSpec((1, all_planes * rows, cols), lambda c: (c + 1, 0, 0))],
-        [edge, edge] + [hbm((ahead * rows, cols), BF16)] * n_wall,
+        [edge, edge] + [struct((rest * planes * rows, cols), BF16)] * n_wall,
         "prepare_rest",
         16,
-        [dma((n_wall,))],
         grid=(rest,),
-        out_specs=[spec, spec] + [ANYWHERE] * n_wall,
     )(noise)
     rest_near, rest_far = exchange(near, far)
     packed, _ = lax.optimization_barrier((packed, (near, far, early)))
@@ -561,14 +518,13 @@
     (rest_near, rest_far), _ = lax.optimization_barrier(((rest_near, rest_far), (near, far)))
     late = call(
         pack_late_kernel,
-        [pl.BlockSpec((1, all_planes * rows, cols), lambda i: (trio - 1, 0, 0)), VMEM, VMEM],
-        [hbm(((rest * planes - ahead) * rows + 2 * rest * height, cols), BF16)] * n_wall,
+        [VMEM] * 2,
+        [hbm((2 * rest * height, cols), BF16)] * n_wall,
         "pack_late",
         16,
-        [dma((n_wall, 1 + 2 * rest))],
-        grid=(1,),
+        [dma((n_wall, 2 * rest))],
         out_specs=[ANYWHERE] * n_wall,
-    )(noise, rest_near, rest_far)
+    )(rest_near, rest_far)
     near, late = lax.optimization_barrier((near, late))
 
     psi = struct((planes, full, cols), F32)
@@ -605,7 +561,7 @@
     psi_next = call(
         functools.partial(main_kernel, planes),
         [VMEM] * (2 + n_wall),
-        [struct((ahead, full, cols), F32)],
+        [struct((rest * planes, full, cols), F32)],
         "main_next",
         16,
     )(wall_rest, main_rest, *early)

time: 111 us -> 109 us (0.982)
  Pallas kernels: 21.6 us -> 19.3 us
  starting transfers between devices: 26.6 us -> 27.9 us
    pallas_call x1, Pallas kernels: 2.37 us -> 0.94 us  [per_device(): call(prepare_rest_kernel, [pl.BlockSpec((1, all_planes * rows, cols), lam...]
    ppermute x2, starting transfers between devices: 5.4 us -> 6.65 us  [exchange(): lax.ppermute(far, 'span', chip_pairs)]
  transfers between devices with their start and end apart: 15 -> 15, of which waited for: 5 -> 5; matrix products, arithmetic and copies ran while one was open for 0% -> 0% of each run, Pallas kernels for 16% -> 15%
where the time goes in v9:
time: 109 us
  waiting for transfers between devices  61.7 us (57%)
  starting transfers between devices  27.9 us (26%)
  Pallas kernels  19.3 us (18%)
    all_to_all x2, waiting for transfers between devices, send(): lax.all_to_all(x, ('span', 'wall'), 0, 0, tiled=True)  53.2 us
    ppermute x9, starting transfers between devices, spread(): lax.ppermute(x, 'wall', [(i, (i + step) % n_wall) for i in range(n_wall)])  15.1 us
    ppermute x9, waiting for transfers between devices, spread(): lax.ppermute(x, 'wall', [(i, (i + step) % n_wall) for i in range(n_wall)])  8.48 us
    ppermute x2, starting transfers between devices, exchange(): lax.ppermute(far, 'span', chip_pairs)  6.65 us
    all_to_all x2, starting transfers between devices, send(): lax.all_to_all(x, ('span', 'wall'), 0, 0, tiled=True)  5.99 us
    pallas_call x1, Pallas kernels, per_device(): call(functools.partial(rest_kernel, planes), [VMEM] * (7 + n_wall), [out(...  5.19 us
    pallas_call x1, Pallas kernels, per_device(): call(functools.partial(first_kernel, planes), [VMEM] * 7, [out(1), hbm(ps...  3.66 us
    pallas_call x2, Pallas kernels, join(): pl.pallas_call(functools.partial(join_narrow_kernel, some) if narrow else...  2.37 us
  transfers between devices with their start and end apart: 15, of which 5 were waited for; matrix products, arithmetic and copies ran while one was open for 0% of the time, Pallas kernels for 15%

profile of v9, /device:TPU:0, one launch (start us, length us, event | category | flops | bytes accessed | tf_op | source)
XLA Modules:
  0.0 109.2 jit_solution(1318675222226767410)
XLA Ops:
  0.0 1.3 %pack.1 = (bf16[544,128]{1,0:T(8,128)(2,1)S(1)}, bf16[544,128]{1,0:T(8,128)(2,1)S(1)}, bf16[544,128]{1,0:T(8,128)(2,1)S(1)}, bf16[544,128]{1,0:T(8,128)(2,1)S(1)}) custom-call(bf16[3,2048,128]{2,1,0:T(8,128)(2,1)} %bitcast.8, f32[6,64]{1,0:T(8,128)} %lund_in.1, f32[1,64]{1,0:T(1,128)} %bitcast.11, s32[1,512]{1,0:T(1,128)} %bitcast.10), custom_call_target="tpu_custom_call" | custom-call | flops 1000000000 | bytes 1024 | tf_op jit(solution)/shard_map/pack/pallas_call | solution.py:459
  1.3 0.0 copy-start.1
  1.3 0.0 copy-start.2
  1.3 3.0 %collective-permute-start = (bf16[544,128]{1,0:T(8,128)(2,1)S(1)}, bf16[544,128]{1,0:T(8,128)(2,1)S(1)}, u32[]{:S(2)}, u32[]{:S(2)}) collective-permute-start(bf16[544,128]{1,0:T(8,128)(2,1)S(1)} %get-tuple-element.66), channel_id=1, source_target_pairs={{0,1},{1,2},{2,3},{3,0},{4,5},{5,6},{6,7},{7,4},{8,9},{9,10},{10,1... | collective-permute-start | bytes 417800 | tf_op jit(solution)/shard_map/ppermute | solution.py:450
  4.3 1.5 %collective-permute-start.1 = (bf16[544,128]{1,0:T(8,128)(2,1)S(1)}, bf16[544,128]{1,0:T(8,128)(2,1)S(1)}, u32[]{:S(2)}, u32[]{:S(2)}) collective-permute-start(bf16[544,128]{1,0:T(8,128)(2,1)S(1)} %get-tuple-element.67), channel_id=1, source_target_pairs={{0,2},{1,3},{2,0},{3,1},{4,6},{5,7},{6,4},{7,5},{8,10},{9,11},{10,... | collective-permute-start | bytes 417800 | tf_op jit(solution)/shard_map/ppermute | solution.py:450
  5.8 1.4 %collective-permute-start.2 = (bf16[544,128]{1,0:T(8,128)(2,1)S(1)}, bf16[544,128]{1,0:T(8,128)(2,1)S(1)}, u32[]{:S(2)}, u32[]{:S(2)}) collective-permute-start(bf16[544,128]{1,0:T(8,128)(2,1)S(1)} %get-tuple-element.68), channel_id=1, source_target_pairs={{0,3},{1,0},{2,1},{3,2},{4,7},{5,4},{6,5},{7,6},{8,11},{9,8},{10,9... | collective-permute-start | bytes 417800 | tf_op jit(solution)/shard_map/ppermute | solution.py:450
  7.2 0.9 prepare_rest.1
  8.2 0.1 collective-permute-start.4
  8.3 3.7 %collective-permute-start.5 = (bf16[4,2,96,128]{3,2,1,0:T(8,128)(2,1)S(1)}, bf16[4,2,96,128]{3,2,1,0:T(8,128)(2,1)S(1)}, u32[]{:S(2)}, u32[]{:S(2)}) collective-permute-start(bf16[4,2,96,128]{3,2,1,0:T(8,128)(2,1)S(1)} %get-tuple-element.71), channel_id=1, source_target_pairs={{0,28},{4,8},{8,4},{12,16},{16,12},{20,24},{24,20},{28,0},{1,29},{... | collective-permute-start | bytes 589832 | tf_op jit(solution)/shard_map/ppermute | solution.py:446
  12.0 0.0 copy-done.2
  12.0 0.9 taps_first.1
  12.9 0.0 collective-permute-done.rest_1_
  12.9 0.0 collective-permute-done.1.rest_2_
  12.9 0.0 collective-permute-done.2.rest_3_
  12.9 0.3 edges_first.1
  13.2 0.1 collective-permute-start.3
  13.3 2.9 %collective-permute-start.6 = (bf16[192,256]{1,0:T(8,128)(2,1)S(1)}, bf16[192,256]{1,0:T(8,128)(2,1)S(1)}, u32[]{:S(2)}, u32[]{:S(2)}) collective-permute-start(bf16[192,256]{1,0:T(8,128)(2,1)S(1)} %get-tuple-element.82), channel_id=1, source_target_pairs={{0,28},{4,8},{8,4},{12,16},{16,12},{20,24},{24,20},{28,0},{1,29},{... | collective-permute-start | bytes 294920 | tf_op jit(solution)/shard_map/ppermute | solution.py:446
  16.2 0.4 small.1
  16.6 0.0 collective-permute-done.4.near_ref
  16.6 1.8 %collective-permute-start.7 = (bf16[1024,128]{1,0:T(8,128)(2,1)S(1)}, bf16[1024,128]{1,0:T(8,128)(2,1)S(1)}, u32[]{:S(2)}, u32[]{:S(2)}) collective-permute-start(bf16[1024,128]{1,0:T(8,128)(2,1)S(1)} %get-tuple-element.104), channel_id=1, source_target_pairs={{0,1},{1,2},{2,3},{3,0},{4,5},{5,6},{6,7},{7,4},{8,9},{9,10},{10,1... | collective-permute-start | bytes 786440 | tf_op jit(solution)/shard_map/ppermute | solution.py:450
  18.4 0.9 main_first.1.psi_in
  19.3 0.6 collective-permute-start.8
  19.9 0.0 collective-permute-done.5.far_ref
  19.9 2.1 %collective-permute-start.9 = (bf16[1024,128]{1,0:T(8,128)(2,1)S(1)}, bf16[1024,128]{1,0:T(8,128)(2,1)S(1)}, u32[]{:S(2)}, u32[]{:S(2)}) collective-permute-start(bf16[1024,128]{1,0:T(8,128)(2,1)S(1)} %get-tuple-element.106), channel_id=1, source_target_pairs={{0,3},{1,0},{2,1},{3,2},{4,7},{5,4},{6,5},{7,6},{8,11},{9,8},{10,9... | collective-permute-start | bytes 786440 | tf_op jit(solution)/shard_map/ppermute | solution.py:450
  22.0 0.0 collective-permute-done.3.near_ref
  22.0 0.0 collective-permute-done.6.far_ref
  22.1 0.9 pack_late.1
  23.0 3.7 %filter_first.1 = (bf16[32,4,32,128]{3,2,1,0:T(8,128)(2,1)}, f32[8,256,128]{2,1,0:T(8,128)}) custom-call(f32[8,256,128]{2,1,0:T(8,128)S(1)} %main_first.1.psi_in, bf16[192,256]{1,0:T(8,128)(2,1)S(1)} %collective-permute-done.3.near_ref, bf16[192,256]{1,0:T(8,128)(2,1)S(1)} %collective-permute-done.6.far_ref, f32[256,128]{1,0:T(8,128)S(1)} %get-tuple-element.90.factor_ref, ...), custom_call_target="tpu_custom_call" | custom-call | flops 1000000000 | bytes 1024 | tf_op jit(solution)/shard_map/filter_first/pallas_call | solution.py:548
  26.6 2.7 %all-to-all-start.1 = ((bf16[32,4,32,128]{3,2,1,0:T(8,128)(2,1)}), bf16[32,4,32,128]{3,2,1,0:T(8,128)(2,1)S(1)}, u32[]{:S(2)}, u32[]{:S(2)}) async-start(bf16[32,4,32,128]{3,2,1,0:T(8,128)(2,1)} %get-tuple-element.112), calls=%async_computation.1 | async-start | bytes 2097152 | tf_op jit(solution)/shard_map/all_to_all | solution.py:455
  29.3 1.7 %collective-permute-start.10 = (bf16[384,128]{1,0:T(8,128)(2,1)S(1)}, bf16[384,128]{1,0:T(8,128)(2,1)S(1)}, u32[]{:S(2)}, u32[]{:S(2)}) collective-permute-start(bf16[384,128]{1,0:T(8,128)(2,1)S(1)} %copy-done.7), channel_id=1, source_target_pairs={{0,1},{1,2},{2,3},{3,0},{4,5},{5,6},{6,7},{7,4},{8,9},{9,10},{10,1... | collective-permute-start | bytes 294920 | tf_op jit(solution)/shard_map/ppermute | solution.py:450
  31.0 0.0 copy-done.6
  31.0 1.5 %collective-permute-start.11 = (bf16[384,128]{1,0:T(8,128)(2,1)S(1)}, bf16[384,128]{1,0:T(8,128)(2,1)S(1)}, u32[]{:S(2)}, u32[]{:S(2)}) collective-permute-start(bf16[384,128]{1,0:T(8,128)(2,1)S(1)} %copy-done.6), channel_id=1, source_target_pairs={{0,2},{1,3},{2,0},{3,1},{4,6},{5,7},{6,4},{7,5},{8,10},{9,11},{10,... | collective-permute-start | bytes 294920 | tf_op jit(solution)/shard_map/ppermute | solution.py:450
  32.5 0.0 collective-permute-done.7.rest_1_
  32.5 1.4 %collective-permute-start.12 = (bf16[384,128]{1,0:T(8,128)(2,1)S(1)}, bf16[384,128]{1,0:T(8,128)(2,1)S(1)}, u32[]{:S(2)}, u32[]{:S(2)}) collective-permute-start(bf16[384,128]{1,0:T(8,128)(2,1)S(1)} %copy-done.5), channel_id=1, source_target_pairs={{0,3},{1,0},{2,1},{3,2},{4,7},{5,4},{6,5},{7,6},{8,11},{9,8},{10,9... | collective-permute-start | bytes 294920 | tf_op jit(solution)/shard_map/ppermute | solution.py:450
  34.0 1.1 %taps_rest.1 = (bf16[2,256,512]{2,1,0:T(8,128)(2,1)S(1)}, bf16[2,256,256]{2,1,0:T(8,128)(2,1)S(1)}, bf16[2,2,256,256]{3,2,1,0:T(8,128)(2,1)S(1)}) custom-call(f32[3]{0:T(128)S(1)} %copy-done.1, f32[3]{0:T(128)S(1)} %copy-done.2), custom_call_target="tpu_custom_call" | custom-call | flops 1000000000 | bytes 1024 | tf_op jit(solution)/shard_map/taps_rest/pallas_call | solution.py:490
  35.1 0.0 collective-permute-done.8.rest_2_
  35.1 0.0 collective-permute-done.9.rest_3_
  35.1 1.4 %main_next.1.next_ref = f32[16,256,128]{2,1,0:T(8,128)S(1)} custom-call(bf16[2,256,512]{2,1,0:T(8,128)(2,1)S(1)} %get-tuple-element.101.wall_ref, bf16[2,256,256]{2,1,0:T(8,128)(2,1)S(1)} %get-tuple-element.102.main_ref, bf16[1024,128]{1,0:T(8,128)(2,1)S(1)} %get-tuple-element.103.rest_0_, bf16[1024,128]{1,0:T(8,128)(2,1)S(1)} %collective-permute-done.7.rest_1_, ...), custom_call_target="tpu_custom_call" | custom-call | flops 1000000000 | bytes 1024 | tf_op jit(solution)/shard_map/main_next/pallas_call | solution.py:561
  36.6 6.5 %collective-permute-done.10.rest_1_ = bf16[384,128]{1,0:T(8,128)(2,1)S(1)} collective-permute-done((bf16[384,128]{1,0:T(8,128)(2,1)S(1)}, bf16[384,128]{1,0:T(8,128)(2,1)S(1)}, u32[]{:S(2)}, u32[]{:S(2)}) %collective-permute-start.10) | collective-permute-done | bytes 98336 | tf_op jit(solution)/shard_map/ppermute | solution.py:450
  43.1 1.7 %collective-permute-done.11.rest_2_ = bf16[384,128]{1,0:T(8,128)(2,1)S(1)} collective-permute-done((bf16[384,128]{1,0:T(8,128)(2,1)S(1)}, bf16[384,128]{1,0:T(8,128)(2,1)S(1)}, u32[]{:S(2)}, u32[]{:S(2)}) %collective-permute-start.11) | collective-permute-done | bytes 98336 | tf_op jit(solution)/shard_map/ppermute | solution.py:450
  44.8 0.2 collective-permute-done.12.rest_3_
  45.0 0.0 copy-done.3
  45.0 5.2 %filter_rest.1 = bf16[32,4,32,256]{3,2,1,0:T(8,128)(2,1)} custom-call(f32[8,256,128]{2,1,0:T(8,128)S(1)} %copy-done.3, f32[16,256,128]{2,1,0:T(8,128)S(1)} %main_next.1.next_ref, f32[256,128]{1,0:T(8,128)S(1)} %get-tuple-element.90.factor_ref, s32[4,4,128]{2,1,0:T(4,128)S(1)} %get-tuple-element.91.target_ref, ...), custom_call_target="tpu_custom_call" | custom-call | flops 99999997952 | bytes 1024 | tf_op jit(solution)/shard_map/filter_rest/pallas_call | solution.py:568
  50.2 5.5 %all-to-all-done.1 = bf16[32,4,32,128]{3,2,1,0:T(8,128)(2,1)S(1)} async-done(((bf16[32,4,32,128]{3,2,1,0:T(8,128)(2,1)}), bf16[32,4,32,128]{3,2,1,0:T(8,128)(2,1)S(1)}, u32[]{:S(2)}, u32[]{:S(2)}) %all-to-all-start.1) | async-done | bytes 1048608 | tf_op jit(solution)/shard_map/all_to_all | solution.py:455
  55.7 3.3 %all-to-all-start = ((bf16[32,4,32,256]{3,2,1,0:T(8,128)(2,1)}), bf16[32,4,32,256]{3,2,1,0:T(8,128)(2,1)S(1)}, u32[]{:S(2)}, u32[]{:S(2)}) async-start(bf16[32,4,32,256]{3,2,1,0:T(8,128)(2,1)} %filter_rest.1), calls=%async_computation | async-start | bytes 4194304 | tf_op jit(solution)/shard_map/all_to_all | solution.py:455
  59.1 1.0 join.2.rest_0_
  60.1 47.7 %all-to-all-done = bf16[32,4,32,256]{3,2,1,0:T(8,128)(2,1)S(1)} async-done(((bf16[32,4,32,256]{3,2,1,0:T(8,128)(2,1)}), bf16[32,4,32,256]{3,2,1,0:T(8,128)(2,1)S(1)}, u32[]{:S(2)}, u32[]{:S(2)}) %all-to-all-start) | async-done | bytes 2097184 | tf_op jit(solution)/shard_map/all_to_all | solution.py:455
  107.8 1.4 %join.3 = bf16[8,128,1536]{2,1,0:T(8,128)(2,1)} custom-call(bf16[8,4,128,256]{3,2,1,0:T(8,128)(2,1)S(1)} %bitcast.6, bf16[8,128,1536]{2,1,0:T(8,128)(2,1)} %join.2.rest_0_), custom_call_target="tpu_custom_call", output_to_operand_aliasing={{}: (1, {})} | custom-call | tf_op jit(solution)/shard_map/join/pallas_call | solution.py:586
  (11 shorter events, 0.0 us)
Async XLA Ops:
  0.0 7.2 %copy-start = (bf16[3,32,64,128]{3,2,1,0:T(8,128)(2,1)S(1)}, bf16[3,32,64,128]{3,2,1,0:T(8,128)(2,1)}, u32[]{:S(2)}) copy-start(bf16[3,32,64,128]{3,2,1,0:T(8,128)(2,1)} %param.6) | copy-start | bytes 4718596
  1.3 10.7 %copy-start.1 = (f32[3]{0:T(128)S(1)}, f32[3]{0:T(128)}, u32[]{:S(2)}) copy-start(f32[3]{0:T(128)} %wall_scale.2) | copy-start | bytes 40
  1.3 10.7 %copy-start.2 = (f32[3]{0:T(128)S(1)}, f32[3]{0:T(128)}, u32[]{:S(2)}) copy-start(f32[3]{0:T(128)} %span_scale.2) | copy-start | bytes 40
  1.3 11.6 %collective-permute-start = (bf16[544,128]{1,0:T(8,128)(2,1)S(1)}, bf16[544,128]{1,0:T(8,128)(2,1)S(1)}, u32[]{:S(2)}, u32[]{:S(2)}) collective-permute-start(bf16[544,128]{1,0:T(8,128)(2,1)S(1)} %get-tuple-element.66), channel_id=1, source_target_pairs={{0,1},{1,2},{2,3},{3,0},{4,5},{5,6},{6,7},{7,4},{8,9},{9,10},{10,1... | collective-permute-start | bytes 417800 | tf_op jit(solution)/shard_map/ppermute | solution.py:450
  4.3 8.6 %collective-permute-start.1 = (bf16[544,128]{1,0:T(8,128)(2,1)S(1)}, bf16[544,128]{1,0:T(8,128)(2,1)S(1)}, u32[]{:S(2)}, u32[]{:S(2)}) collective-permute-start(bf16[544,128]{1,0:T(8,128)(2,1)S(1)} %get-tuple-element.67), channel_id=1, source_target_pairs={{0,2},{1,3},{2,0},{3,1},{4,6},{5,7},{6,4},{7,5},{8,10},{9,11},{10,... | collective-permute-start | bytes 417800 | tf_op jit(solution)/shard_map/ppermute | solution.py:450
  5.8 7.1 %collective-permute-start.2 = (bf16[544,128]{1,0:T(8,128)(2,1)S(1)}, bf16[544,128]{1,0:T(8,128)(2,1)S(1)}, u32[]{:S(2)}, u32[]{:S(2)}) collective-permute-start(bf16[544,128]{1,0:T(8,128)(2,1)S(1)} %get-tuple-element.68), channel_id=1, source_target_pairs={{0,3},{1,0},{2,1},{3,2},{4,7},{5,4},{6,5},{7,6},{8,11},{9,8},{10,9... | collective-permute-start | bytes 417800 | tf_op jit(solution)/shard_map/ppermute | solution.py:450
  8.2 8.5 %collective-permute-start.4 = (bf16[4,2,96,128]{3,2,1,0:T(8,128)(2,1)S(1)}, bf16[4,2,96,128]{3,2,1,0:T(8,128)(2,1)S(1)}, u32[]{:S(2)}, u32[]{:S(2)}) collective-permute-start(bf16[4,2,96,128]{3,2,1,0:T(8,128)(2,1)S(1)} %get-tuple-element.70), channel_id=1, source_target_pairs={{0,4},{4,0},{8,12},{12,8},{16,20},{20,16},{24,28},{28,24},{1,5},{5... | collective-permute-start | bytes 589832 | tf_op jit(solution)/shard_map/ppermute | solution.py:446
  8.3 11.6 %collective-permute-start.5 = (bf16[4,2,96,128]{3,2,1,0:T(8,128)(2,1)S(1)}, bf16[4,2,96,128]{3,2,1,0:T(8,128)(2,1)S(1)}, u32[]{:S(2)}, u32[]{:S(2)}) collective-permute-start(bf16[4,2,96,128]{3,2,1,0:T(8,128)(2,1)S(1)} %get-tuple-element.71), channel_id=1, source_target_pairs={{0,28},{4,8},{8,4},{12,16},{16,12},{20,24},{24,20},{28,0},{1,29},{... | collective-permute-start | bytes 589832 | tf_op jit(solution)/shard_map/ppermute | solution.py:446
  13.2 8.8 %collective-permute-start.3 = (bf16[192,256]{1,0:T(8,128)(2,1)S(1)}, bf16[192,256]{1,0:T(8,128)(2,1)S(1)}, u32[]{:S(2)}, u32[]{:S(2)}) collective-permute-start(bf16[192,256]{1,0:T(8,128)(2,1)S(1)} %get-tuple-element.80), channel_id=1, source_target_pairs={{0,4},{4,0},{8,12},{12,8},{16,20},{20,16},{24,28},{28,24},{1,5},{5... | collective-permute-start | bytes 294920 | tf_op jit(solution)/shard_map/ppermute | solution.py:446
  13.3 8.8 %collective-permute-start.6 = (bf16[192,256]{1,0:T(8,128)(2,1)S(1)}, bf16[192,256]{1,0:T(8,128)(2,1)S(1)}, u32[]{:S(2)}, u32[]{:S(2)}) collective-permute-start(bf16[192,256]{1,0:T(8,128)(2,1)S(1)} %get-tuple-element.82), channel_id=1, source_target_pairs={{0,28},{4,8},{8,4},{12,16},{16,12},{20,24},{24,20},{28,0},{1,29},{... | collective-permute-start | bytes 294920 | tf_op jit(solution)/shard_map/ppermute | solution.py:446
  16.6 15.9 %collective-permute-start.7 = (bf16[1024,128]{1,0:T(8,128)(2,1)S(1)}, bf16[1024,128]{1,0:T(8,128)(2,1)S(1)}, u32[]{:S(2)}, u32[]{:S(2)}) collective-permute-start(bf16[1024,128]{1,0:T(8,128)(2,1)S(1)} %get-tuple-element.104), channel_id=1, source_target_pairs={{0,1},{1,2},{2,3},{3,0},{4,5},{5,6},{6,7},{7,4},{8,9},{9,10},{10,1... | collective-permute-start | bytes 786440 | tf_op jit(solution)/shard_map/ppermute | solution.py:450
  19.3 15.8 %collective-permute-start.8 = (bf16[1024,128]{1,0:T(8,128)(2,1)S(1)}, bf16[1024,128]{1,0:T(8,128)(2,1)S(1)}, u32[]{:S(2)}, u32[]{:S(2)}) collective-permute-start(bf16[1024,128]{1,0:T(8,128)(2,1)S(1)} %get-tuple-element.105), channel_id=1, source_target_pairs={{0,2},{1,3},{2,0},{3,1},{4,6},{5,7},{6,4},{7,5},{8,10},{9,11},{10,... | collective-permute-start | bytes 786440 | tf_op jit(solution)/shard_map/ppermute | solution.py:450
  19.9 15.2 %collective-permute-start.9 = (bf16[1024,128]{1,0:T(8,128)(2,1)S(1)}, bf16[1024,128]{1,0:T(8,128)(2,1)S(1)}, u32[]{:S(2)}, u32[]{:S(2)}) collective-permute-start(bf16[1024,128]{1,0:T(8,128)(2,1)S(1)} %get-tuple-element.106), channel_id=1, source_target_pairs={{0,3},{1,0},{2,1},{3,2},{4,7},{5,4},{6,5},{7,6},{8,11},{9,8},{10,9... | collective-permute-start | bytes 786440 | tf_op jit(solution)/shard_map/ppermute | solution.py:450
  22.9 6.4 %copy-start.7 = (bf16[384,128]{1,0:T(8,128)(2,1)S(1)}, bf16[384,128]{1,0:T(8,128)(2,1)}, u32[]{:S(2)}) copy-start(bf16[384,128]{1,0:T(8,128)(2,1)} %get-tuple-element.109) | copy-start | bytes 294916
  23.0 8.1 %copy-start.6 = (bf16[384,128]{1,0:T(8,128)(2,1)S(1)}, bf16[384,128]{1,0:T(8,128)(2,1)}, u32[]{:S(2)}) copy-start(bf16[384,128]{1,0:T(8,128)(2,1)} %get-tuple-element.110) | copy-start | bytes 294916
  23.0 9.6 %copy-start.5 = (bf16[384,128]{1,0:T(8,128)(2,1)S(1)}, bf16[384,128]{1,0:T(8,128)(2,1)}, u32[]{:S(2)}) copy-start(bf16[384,128]{1,0:T(8,128)(2,1)} %get-tuple-element.111) | copy-start | bytes 294916
  26.6 29.1 %all-to-all-start.1 = ((bf16[32,4,32,128]{3,2,1,0:T(8,128)(2,1)}), bf16[32,4,32,128]{3,2,1,0:T(8,128)(2,1)S(1)}, u32[]{:S(2)}, u32[]{:S(2)}) async-start(bf16[32,4,32,128]{3,2,1,0:T(8,128)(2,1)} %get-tuple-element.112), calls=%async_computation.1 | async-start | bytes 2097152 | tf_op jit(solution)/shard_map/all_to_all | solution.py:455
  29.3 13.7 %collective-permute-start.10 = (bf16[384,128]{1,0:T(8,128)(2,1)S(1)}, bf16[384,128]{1,0:T(8,128)(2,1)S(1)}, u32[]{:S(2)}, u32[]{:S(2)}) collective-permute-start(bf16[384,128]{1,0:T(8,128)(2,1)S(1)} %copy-done.7), channel_id=1, source_target_pairs={{0,1},{1,2},{2,3},{3,0},{4,5},{5,6},{6,7},{7,4},{8,9},{9,10},{10,1... | collective-permute-start | bytes 294920 | tf_op jit(solution)/shard_map/ppermute | solution.py:450
  31.0 13.8 %collective-permute-start.11 = (bf16[384,128]{1,0:T(8,128)(2,1)S(1)}, bf16[384,128]{1,0:T(8,128)(2,1)S(1)}, u32[]{:S(2)}, u32[]{:S(2)}) collective-permute-start(bf16[384,128]{1,0:T(8,128)(2,1)S(1)} %copy-done.6), channel_id=1, source_target_pairs={{0,2},{1,3},{2,0},{3,1},{4,6},{5,7},{6,4},{7,5},{8,10},{9,11},{10,... | collective-permute-start | bytes 294920 | tf_op jit(solution)/shard_map/ppermute | solution.py:450
  32.5 12.5 %collective-permute-start.12 = (bf16[384,128]{1,0:T(8,128)(2,1)S(1)}, bf16[384,128]{1,0:T(8,128)(2,1)S(1)}, u32[]{:S(2)}, u32[]{:S(2)}) collective-permute-start(bf16[384,128]{1,0:T(8,128)(2,1)S(1)} %copy-done.5), channel_id=1, source_target_pairs={{0,3},{1,0},{2,1},{3,2},{4,7},{5,4},{6,5},{7,6},{8,11},{9,8},{10,9... | collective-permute-start | bytes 294920 | tf_op jit(solution)/shard_map/ppermute | solution.py:450
  35.1 10.0 %copy-start.3 = (f32[8,256,128]{2,1,0:T(8,128)S(1)}, f32[8,256,128]{2,1,0:T(8,128)}, u32[]{:S(2)}) copy-start(f32[8,256,128]{2,1,0:T(8,128)} %get-tuple-element.93.psi_ref) | copy-start | bytes 3145732
  35.1 9.9 %copy-start.4 = (bf16[384,128]{1,0:T(8,128)(2,1)S(1)}, bf16[384,128]{1,0:T(8,128)(2,1)}, u32[]{:S(2)}) copy-start(bf16[384,128]{1,0:T(8,128)(2,1)} %get-tuple-element.108.rest_0_) | copy-start | bytes 294916
  55.7 52.0 %all-to-all-start = ((bf16[32,4,32,256]{3,2,1,0:T(8,128)(2,1)}), bf16[32,4,32,256]{3,2,1,0:T(8,128)(2,1)S(1)}, u32[]{:S(2)}, u32[]{:S(2)}) async-start(bf16[32,4,32,256]{3,2,1,0:T(8,128)(2,1)} %filter_rest.1), calls=%async_computation | async-start | bytes 4194304 | tf_op jit(solution)/shard_map/all_to_all | solution.py:455

commit v10 on v9

--- a/solution.py
+++ b/solution.py
@@ -516,16 +516,7 @@
     early, rest_near = lax.optimization_barrier((early, rest_near))
     early = spread(early)
     (rest_near, rest_far), _ = lax.optimization_barrier(((rest_near, rest_far), (near, far)))
-    late = call(
-        pack_late_kernel,
-        [VMEM] * 2,
-        [hbm((2 * rest * height, cols), BF16)] * n_wall,
-        "pack_late",
-        16,
-        [dma((n_wall, 2 * rest))],
-        out_specs=[ANYWHERE] * n_wall,
-    )(rest_near, rest_far)
-    near, late = lax.optimization_barrier((near, late))
+    near, rest_near, rest_far = lax.optimization_barrier((near, rest_near, rest_far))
 
     psi = struct((planes, full, cols), F32)
     psi_main = call(
@@ -554,8 +545,19 @@
         [pltpu.VMEM(psi.shape, F32), cells, *more, dma((1,))],
         out_specs=[ANYWHERE, ANYWHERE],
     )(psi_main, near, far, factor, target, wall_first, halo_first)
-    (wall_scale, span_scale, late), sent = lax.optimization_barrier(((wall_scale, span_scale, late), sent))
+    (wall_scale, span_scale, rest_near, rest_far), sent = lax.optimization_barrier(
+        ((wall_scale, span_scale, rest_near, rest_far), sent)
+    )
     got_first = send(sent)
+    late = call(
+        pack_late_kernel,
+        [VMEM] * 2,
+        [hbm((2 * rest * height, cols), BF16)] * n_wall,
+        "pack_late",
+        16,
+        [dma((n_wall, 2 * rest))],
+        out_specs=[ANYWHERE] * n_wall,
+    )(rest_near, rest_far)
     late = spread(late)
     wall_rest, main_rest, halo_rest = taps(1, rest, struct, "taps_rest")
     psi_next = call(

time: 109 us -> 109 us (level)
  no operation moved by 1% of the time
where the time goes in v10:
time: 109 us; the launch traced here: 108 us
  waiting for transfers between devices  60.9 us (56%)
  starting transfers between devices  27.8 us (26%)
  Pallas kernels  19.3 us (18%)
    all_to_all x2, waiting for transfers between devices, send(): lax.all_to_all(x, ('span', 'wall'), 0, 0, tiled=True)  53.3 us
    ppermute x9, starting transfers between devices, spread(): lax.ppermute(x, 'wall', [(i, (i + step) % n_wall) for i in range(n_wall)])  15.1 us
    ppermute x9, waiting for transfers between devices, spread(): lax.ppermute(x, 'wall', [(i, (i + step) % n_wall) for i in range(n_wall)])  7.6 us
    ppermute x2, starting transfers between devices, exchange(): lax.ppermute(far, 'span', chip_pairs)  6.65 us
    all_to_all x2, starting transfers between devices, send(): lax.all_to_all(x, ('span', 'wall'), 0, 0, tiled=True)  5.99 us
    pallas_call x1, Pallas kernels, per_device(): call(functools.partial(rest_kernel, planes), [VMEM] * (7 + n_wall), [out(...  5.12 us
    pallas_call x1, Pallas kernels, per_device(): call(functools.partial(first_kernel, planes), [VMEM] * 7, [out(1), hbm(ps...  3.67 us
    pallas_call x2, Pallas kernels, join(): pl.pallas_call(functools.partial(join_narrow_kernel, some) if narrow else...  2.37 us
  transfers between devices with their start and end apart: 15, of which 5 were waited for; matrix products, arithmetic and copies ran while one was open for 0% of the time, Pallas kernels for 15%

profile of v10, /device:TPU:0, one launch (start us, length us, event | category | flops | bytes accessed | tf_op | source)
XLA Modules:
  0.0 108.2 jit_solution(17841416460259686749)
XLA Ops:
  0.0 1.3 %pack.1 = (bf16[544,128]{1,0:T(8,128)(2,1)S(1)}, bf16[544,128]{1,0:T(8,128)(2,1)S(1)}, bf16[544,128]{1,0:T(8,128)(2,1)S(1)}, bf16[544,128]{1,0:T(8,128)(2,1)S(1)}) custom-call(bf16[3,2048,128]{2,1,0:T(8,128)(2,1)} %bitcast.8, f32[6,64]{1,0:T(8,128)} %lund_in.1, f32[1,64]{1,0:T(1,128)} %bitcast.11, s32[1,512]{1,0:T(1,128)} %bitcast.10), custom_call_target="tpu_custom_call" | custom-call | flops 1000000000 | bytes 1024 | tf_op jit(solution)/shard_map/pack/pallas_call | solution.py:459
  1.3 0.0 copy-start.1
  1.3 0.0 copy-start.2
  1.3 3.0 %collective-permute-start = (bf16[544,128]{1,0:T(8,128)(2,1)S(1)}, bf16[544,128]{1,0:T(8,128)(2,1)S(1)}, u32[]{:S(2)}, u32[]{:S(2)}) collective-permute-start(bf16[544,128]{1,0:T(8,128)(2,1)S(1)} %get-tuple-element.62), channel_id=1, source_target_pairs={{0,1},{1,2},{2,3},{3,0},{4,5},{5,6},{6,7},{7,4},{8,9},{9,10},{10,1... | collective-permute-start | bytes 417800 | tf_op jit(solution)/shard_map/ppermute | solution.py:450
  4.3 1.5 %collective-permute-start.1 = (bf16[544,128]{1,0:T(8,128)(2,1)S(1)}, bf16[544,128]{1,0:T(8,128)(2,1)S(1)}, u32[]{:S(2)}, u32[]{:S(2)}) collective-permute-start(bf16[544,128]{1,0:T(8,128)(2,1)S(1)} %get-tuple-element.63), channel_id=1, source_target_pairs={{0,2},{1,3},{2,0},{3,1},{4,6},{5,7},{6,4},{7,5},{8,10},{9,11},{10,... | collective-permute-start | bytes 417800 | tf_op jit(solution)/shard_map/ppermute | solution.py:450
  5.8 1.4 %collective-permute-start.2 = (bf16[544,128]{1,0:T(8,128)(2,1)S(1)}, bf16[544,128]{1,0:T(8,128)(2,1)S(1)}, u32[]{:S(2)}, u32[]{:S(2)}) collective-permute-start(bf16[544,128]{1,0:T(8,128)(2,1)S(1)} %get-tuple-element.64), channel_id=1, source_target_pairs={{0,3},{1,0},{2,1},{3,2},{4,7},{5,4},{6,5},{7,6},{8,11},{9,8},{10,9... | collective-permute-start | bytes 417800 | tf_op jit(solution)/shard_map/ppermute | solution.py:450
  7.2 0.9 prepare_rest.1
  8.2 0.1 collective-permute-start.4
  8.3 3.7 %collective-permute-start.5 = (bf16[4,2,96,128]{3,2,1,0:T(8,128)(2,1)S(1)}, bf16[4,2,96,128]{3,2,1,0:T(8,128)(2,1)S(1)}, u32[]{:S(2)}, u32[]{:S(2)}) collective-permute-start(bf16[4,2,96,128]{3,2,1,0:T(8,128)(2,1)S(1)} %get-tuple-element.67), channel_id=1, source_target_pairs={{0,28},{4,8},{8,4},{12,16},{16,12},{20,24},{24,20},{28,0},{1,29},{... | collective-permute-start | bytes 589832 | tf_op jit(solution)/shard_map/ppermute | solution.py:446
  12.0 0.0 copy-done.2
  12.0 0.9 taps_first.1
  12.9 0.0 collective-permute-done.rest_1_
  12.9 0.0 collective-permute-done.1.rest_2_
  12.9 0.0 collective-permute-done.2.rest_3_
  12.9 0.3 edges_first.1
  13.2 0.1 collective-permute-start.3
  13.3 2.9 %collective-permute-start.6 = (bf16[192,256]{1,0:T(8,128)(2,1)S(1)}, bf16[192,256]{1,0:T(8,128)(2,1)S(1)}, u32[]{:S(2)}, u32[]{:S(2)}) collective-permute-start(bf16[192,256]{1,0:T(8,128)(2,1)S(1)} %get-tuple-element.78), channel_id=1, source_target_pairs={{0,28},{4,8},{8,4},{12,16},{16,12},{20,24},{24,20},{28,0},{1,29},{... | collective-permute-start | bytes 294920 | tf_op jit(solution)/shard_map/ppermute | solution.py:446
  16.2 0.4 small.1
  16.6 0.0 collective-permute-done.4.near_ref
  16.6 1.8 %collective-permute-start.7 = (bf16[1024,128]{1,0:T(8,128)(2,1)S(1)}, bf16[1024,128]{1,0:T(8,128)(2,1)S(1)}, u32[]{:S(2)}, u32[]{:S(2)}) collective-permute-start(bf16[1024,128]{1,0:T(8,128)(2,1)S(1)} %get-tuple-element.94), channel_id=1, source_target_pairs={{0,1},{1,2},{2,3},{3,0},{4,5},{5,6},{6,7},{7,4},{8,9},{9,10},{10,1... | collective-permute-start | bytes 786440 | tf_op jit(solution)/shard_map/ppermute | solution.py:450
  18.4 0.9 main_first.1.psi_in
  19.3 0.6 collective-permute-start.8
  19.9 0.0 collective-permute-done.5.far_ref
  19.9 2.1 %collective-permute-start.9 = (bf16[1024,128]{1,0:T(8,128)(2,1)S(1)}, bf16[1024,128]{1,0:T(8,128)(2,1)S(1)}, u32[]{:S(2)}, u32[]{:S(2)}) collective-permute-start(bf16[1024,128]{1,0:T(8,128)(2,1)S(1)} %get-tuple-element.96), channel_id=1, source_target_pairs={{0,3},{1,0},{2,1},{3,2},{4,7},{5,4},{6,5},{7,6},{8,11},{9,8},{10,9... | collective-permute-start | bytes 786440 | tf_op jit(solution)/shard_map/ppermute | solution.py:450
  22.0 0.0 collective-permute-done.3.near_ref
  22.0 0.0 collective-permute-done.6.far_ref
  22.1 3.7 %filter_first.1 = (bf16[32,4,32,128]{3,2,1,0:T(8,128)(2,1)}, f32[8,256,128]{2,1,0:T(8,128)}) custom-call(f32[8,256,128]{2,1,0:T(8,128)S(1)} %main_first.1.psi_in, bf16[192,256]{1,0:T(8,128)(2,1)S(1)} %collective-permute-done.3.near_ref, bf16[192,256]{1,0:T(8,128)(2,1)S(1)} %collective-permute-done.6.far_ref, f32[256,128]{1,0:T(8,128)S(1)} %get-tuple-element.82.factor_ref, ...), custom_call_target="tpu_custom_call" | custom-call | flops 1000000000 | bytes 1024 | tf_op jit(solution)/shard_map/filter_first/pallas_call | solution.py:539
  25.7 2.7 %all-to-all-start.1 = ((bf16[32,4,32,128]{3,2,1,0:T(8,128)(2,1)}), bf16[32,4,32,128]{3,2,1,0:T(8,128)(2,1)S(1)}, u32[]{:S(2)}, u32[]{:S(2)}) async-start(bf16[32,4,32,128]{3,2,1,0:T(8,128)(2,1)} %get-tuple-element.104), calls=%async_computation.1 | async-start | bytes 2097152 | tf_op jit(solution)/shard_map/all_to_all | solution.py:455
  28.4 0.9 pack_late.1
  29.3 1.7 %collective-permute-start.10 = (bf16[384,128]{1,0:T(8,128)(2,1)}, bf16[384,128]{1,0:T(8,128)(2,1)S(1)}, u32[]{:S(2)}, u32[]{:S(2)}) collective-permute-start(bf16[384,128]{1,0:T(8,128)(2,1)} %get-tuple-element.101), channel_id=1, source_target_pairs={{0,1},{1,2},{2,3},{3,0},{4,5},{5,6},{6,7},{7,4},{8,9},{9,10},{10,1... | collective-permute-start | bytes 294920 | tf_op jit(solution)/shard_map/ppermute | solution.py:450
  31.0 1.5 %collective-permute-start.11 = (bf16[384,128]{1,0:T(8,128)(2,1)}, bf16[384,128]{1,0:T(8,128)(2,1)S(1)}, u32[]{:S(2)}, u32[]{:S(2)}) collective-permute-start(bf16[384,128]{1,0:T(8,128)(2,1)} %get-tuple-element.102), channel_id=1, source_target_pairs={{0,2},{1,3},{2,0},{3,1},{4,6},{5,7},{6,4},{7,5},{8,10},{9,11},{10,... | collective-permute-start | bytes 294920 | tf_op jit(solution)/shard_map/ppermute | solution.py:450
  32.5 0.0 collective-permute-done.7.rest_1_
  32.5 1.4 %collective-permute-start.12 = (bf16[384,128]{1,0:T(8,128)(2,1)}, bf16[384,128]{1,0:T(8,128)(2,1)S(1)}, u32[]{:S(2)}, u32[]{:S(2)}) collective-permute-start(bf16[384,128]{1,0:T(8,128)(2,1)} %get-tuple-element.103), channel_id=1, source_target_pairs={{0,3},{1,0},{2,1},{3,2},{4,7},{5,4},{6,5},{7,6},{8,11},{9,8},{10,9... | collective-permute-start | bytes 294920 | tf_op jit(solution)/shard_map/ppermute | solution.py:450
  33.9 1.1 %taps_rest.1 = (bf16[2,256,512]{2,1,0:T(8,128)(2,1)S(1)}, bf16[2,256,256]{2,1,0:T(8,128)(2,1)S(1)}, bf16[2,2,256,256]{3,2,1,0:T(8,128)(2,1)S(1)}) custom-call(f32[3]{0:T(128)S(1)} %copy-done.1, f32[3]{0:T(128)S(1)} %copy-done.2), custom_call_target="tpu_custom_call" | custom-call | flops 1000000000 | bytes 1024 | tf_op jit(solution)/shard_map/taps_rest/pallas_call | solution.py:490
  35.0 0.0 copy-start.3
  35.0 0.0 copy-start.4
  35.1 0.0 collective-permute-done.8.rest_2_
  35.1 0.0 collective-permute-done.9.rest_3_
  35.1 1.4 %main_next.1.next_ref = f32[16,256,128]{2,1,0:T(8,128)S(1)} custom-call(bf16[2,256,512]{2,1,0:T(8,128)(2,1)S(1)} %get-tuple-element.91.wall_ref, bf16[2,256,256]{2,1,0:T(8,128)(2,1)S(1)} %get-tuple-element.92.main_ref, bf16[1024,128]{1,0:T(8,128)(2,1)S(1)} %get-tuple-element.93.rest_0_, bf16[1024,128]{1,0:T(8,128)(2,1)S(1)} %collective-permute-done.7.rest_1_, ...), custom_call_target="tpu_custom_call" | custom-call | flops 1000000000 | bytes 1024 | tf_op jit(solution)/shard_map/main_next/pallas_call | solution.py:563
  36.5 5.6 %collective-permute-done.10.rest_1_ = bf16[384,128]{1,0:T(8,128)(2,1)S(1)} collective-permute-done((bf16[384,128]{1,0:T(8,128)(2,1)}, bf16[384,128]{1,0:T(8,128)(2,1)S(1)}, u32[]{:S(2)}, u32[]{:S(2)}) %collective-permute-start.10) | collective-permute-done | bytes 98336 | tf_op jit(solution)/shard_map/ppermute | solution.py:450
  42.2 1.7 %collective-permute-done.11.rest_2_ = bf16[384,128]{1,0:T(8,128)(2,1)S(1)} collective-permute-done((bf16[384,128]{1,0:T(8,128)(2,1)}, bf16[384,128]{1,0:T(8,128)(2,1)S(1)}, u32[]{:S(2)}, u32[]{:S(2)}) %collective-permute-start.11) | collective-permute-done | bytes 98336 | tf_op jit(solution)/shard_map/ppermute | solution.py:450
  43.9 0.2 collective-permute-done.12.rest_3_
  44.1 5.1 %filter_rest.1 = bf16[32,4,32,256]{3,2,1,0:T(8,128)(2,1)} custom-call(f32[8,256,128]{2,1,0:T(8,128)S(1)} %copy-done.3, f32[16,256,128]{2,1,0:T(8,128)S(1)} %main_next.1.next_ref, f32[256,128]{1,0:T(8,128)S(1)} %get-tuple-element.82.factor_ref, s32[4,4,128]{2,1,0:T(4,128)S(1)} %get-tuple-element.83.target_ref, ...), custom_call_target="tpu_custom_call" | custom-call | flops 99999997952 | bytes 1024 | tf_op jit(solution)/shard_map/filter_rest/pallas_call | solution.py:570
  49.2 5.6 %all-to-all-done.1 = bf16[32,4,32,128]{3,2,1,0:T(8,128)(2,1)S(1)} async-done(((bf16[32,4,32,128]{3,2,1,0:T(8,128)(2,1)}), bf16[32,4,32,128]{3,2,1,0:T(8,128)(2,1)S(1)}, u32[]{:S(2)}, u32[]{:S(2)}) %all-to-all-start.1) | async-done | bytes 1048608 | tf_op jit(solution)/shard_map/all_to_all | solution.py:455
  54.8 3.3 %all-to-all-start = ((bf16[32,4,32,256]{3,2,1,0:T(8,128)(2,1)}), bf16[32,4,32,256]{3,2,1,0:T(8,128)(2,1)S(1)}, u32[]{:S(2)}, u32[]{:S(2)}) async-start(bf16[32,4,32,256]{3,2,1,0:T(8,128)(2,1)} %filter_rest.1), calls=%async_computation | async-start | bytes 4194304 | tf_op jit(solution)/shard_map/all_to_all | solution.py:455
  58.2 1.0 join.2.rest_0_
  59.2 47.7 %all-to-all-done = bf16[32,4,32,256]{3,2,1,0:T(8,128)(2,1)S(1)} async-done(((bf16[32,4,32,256]{3,2,1,0:T(8,128)(2,1)}), bf16[32,4,32,256]{3,2,1,0:T(8,128)(2,1)S(1)}, u32[]{:S(2)}, u32[]{:S(2)}) %all-to-all-start) | async-done | bytes 2097184 | tf_op jit(solution)/shard_map/all_to_all | solution.py:455
  106.9 1.4 %join.3 = bf16[8,128,1536]{2,1,0:T(8,128)(2,1)} custom-call(bf16[8,4,128,256]{3,2,1,0:T(8,128)(2,1)S(1)} %bitcast.6, bf16[8,128,1536]{2,1,0:T(8,128)(2,1)} %join.2.rest_0_), custom_call_target="tpu_custom_call", output_to_operand_aliasing={{}: (1, {})} | custom-call | tf_op jit(solution)/shard_map/join/pallas_call | solution.py:588
  (5 shorter events, 0.0 us)
Async XLA Ops:
  0.0 7.2 %copy-start = (bf16[3,32,64,128]{3,2,1,0:T(8,128)(2,1)S(1)}, bf16[3,32,64,128]{3,2,1,0:T(8,128)(2,1)}, u32[]{:S(2)}) copy-start(bf16[3,32,64,128]{3,2,1,0:T(8,128)(2,1)} %param.6) | copy-start | bytes 4718596
  1.3 10.7 %copy-start.1 = (f32[3]{0:T(128)S(1)}, f32[3]{0:T(128)}, u32[]{:S(2)}) copy-start(f32[3]{0:T(128)} %wall_scale.2) | copy-start | bytes 40
  1.3 10.7 %copy-start.2 = (f32[3]{0:T(128)S(1)}, f32[3]{0:T(128)}, u32[]{:S(2)}) copy-start(f32[3]{0:T(128)} %span_scale.2) | copy-start | bytes 40
  1.3 11.6 %collective-permute-start = (bf16[544,128]{1,0:T(8,128)(2,1)S(1)}, bf16[544,128]{1,0:T(8,128)(2,1)S(1)}, u32[]{:S(2)}, u32[]{:S(2)}) collective-permute-start(bf16[544,128]{1,0:T(8,128)(2,1)S(1)} %get-tuple-element.62), channel_id=1, source_target_pairs={{0,1},{1,2},{2,3},{3,0},{4,5},{5,6},{6,7},{7,4},{8,9},{9,10},{10,1... | collective-permute-start | bytes 417800 | tf_op jit(solution)/shard_map/ppermute | solution.py:450
  4.3 8.6 %collective-permute-start.1 = (bf16[544,128]{1,0:T(8,128)(2,1)S(1)}, bf16[544,128]{1,0:T(8,128)(2,1)S(1)}, u32[]{:S(2)}, u32[]{:S(2)}) collective-permute-start(bf16[544,128]{1,0:T(8,128)(2,1)S(1)} %get-tuple-element.63), channel_id=1, source_target_pairs={{0,2},{1,3},{2,0},{3,1},{4,6},{5,7},{6,4},{7,5},{8,10},{9,11},{10,... | collective-permute-start | bytes 417800 | tf_op jit(solution)/shard_map/ppermute | solution.py:450
  5.8 7.1 %collective-permute-start.2 = (bf16[544,128]{1,0:T(8,128)(2,1)S(1)}, bf16[544,128]{1,0:T(8,128)(2,1)S(1)}, u32[]{:S(2)}, u32[]{:S(2)}) collective-permute-start(bf16[544,128]{1,0:T(8,128)(2,1)S(1)} %get-tuple-element.64), channel_id=1, source_target_pairs={{0,3},{1,0},{2,1},{3,2},{4,7},{5,4},{6,5},{7,6},{8,11},{9,8},{10,9... | collective-permute-start | bytes 417800 | tf_op jit(solution)/shard_map/ppermute | solution.py:450
  8.2 8.5 %collective-permute-start.4 = (bf16[4,2,96,128]{3,2,1,0:T(8,128)(2,1)S(1)}, bf16[4,2,96,128]{3,2,1,0:T(8,128)(2,1)S(1)}, u32[]{:S(2)}, u32[]{:S(2)}) collective-permute-start(bf16[4,2,96,128]{3,2,1,0:T(8,128)(2,1)S(1)} %get-tuple-element.66), channel_id=1, source_target_pairs={{0,4},{4,0},{8,12},{12,8},{16,20},{20,16},{24,28},{28,24},{1,5},{5... | collective-permute-start | bytes 589832 | tf_op jit(solution)/shard_map/ppermute | solution.py:446
  8.3 11.6 %collective-permute-start.5 = (bf16[4,2,96,128]{3,2,1,0:T(8,128)(2,1)S(1)}, bf16[4,2,96,128]{3,2,1,0:T(8,128)(2,1)S(1)}, u32[]{:S(2)}, u32[]{:S(2)}) collective-permute-start(bf16[4,2,96,128]{3,2,1,0:T(8,128)(2,1)S(1)} %get-tuple-element.67), channel_id=1, source_target_pairs={{0,28},{4,8},{8,4},{12,16},{16,12},{20,24},{24,20},{28,0},{1,29},{... | collective-permute-start | bytes 589832 | tf_op jit(solution)/shard_map/ppermute | solution.py:446
  13.2 8.8 %collective-permute-start.3 = (bf16[192,256]{1,0:T(8,128)(2,1)S(1)}, bf16[192,256]{1,0:T(8,128)(2,1)S(1)}, u32[]{:S(2)}, u32[]{:S(2)}) collective-permute-start(bf16[192,256]{1,0:T(8,128)(2,1)S(1)} %get-tuple-element.76), channel_id=1, source_target_pairs={{0,4},{4,0},{8,12},{12,8},{16,20},{20,16},{24,28},{28,24},{1,5},{5... | collective-permute-start | bytes 294920 | tf_op jit(solution)/shard_map/ppermute | solution.py:446
  13.3 8.8 %collective-permute-start.6 = (bf16[192,256]{1,0:T(8,128)(2,1)S(1)}, bf16[192,256]{1,0:T(8,128)(2,1)S(1)}, u32[]{:S(2)}, u32[]{:S(2)}) collective-permute-start(bf16[192,256]{1,0:T(8,128)(2,1)S(1)} %get-tuple-element.78), channel_id=1, source_target_pairs={{0,28},{4,8},{8,4},{12,16},{16,12},{20,24},{24,20},{28,0},{1,29},{... | collective-permute-start | bytes 294920 | tf_op jit(solution)/shard_map/ppermute | solution.py:446
  16.6 15.8 %collective-permute-start.7 = (bf16[1024,128]{1,0:T(8,128)(2,1)S(1)}, bf16[1024,128]{1,0:T(8,128)(2,1)S(1)}, u32[]{:S(2)}, u32[]{:S(2)}) collective-permute-start(bf16[1024,128]{1,0:T(8,128)(2,1)S(1)} %get-tuple-element.94), channel_id=1, source_target_pairs={{0,1},{1,2},{2,3},{3,0},{4,5},{5,6},{6,7},{7,4},{8,9},{9,10},{10,1... | collective-permute-start | bytes 786440 | tf_op jit(solution)/shard_map/ppermute | solution.py:450
  19.3 15.7 %collective-permute-start.8 = (bf16[1024,128]{1,0:T(8,128)(2,1)S(1)}, bf16[1024,128]{1,0:T(8,128)(2,1)S(1)}, u32[]{:S(2)}, u32[]{:S(2)}) collective-permute-start(bf16[1024,128]{1,0:T(8,128)(2,1)S(1)} %get-tuple-element.95), channel_id=1, source_target_pairs={{0,2},{1,3},{2,0},{3,1},{4,6},{5,7},{6,4},{7,5},{8,10},{9,11},{10,... | collective-permute-start | bytes 786440 | tf_op jit(solution)/shard_map/ppermute | solution.py:450
  19.9 15.2 %collective-permute-start.9 = (bf16[1024,128]{1,0:T(8,128)(2,1)S(1)}, bf16[1024,128]{1,0:T(8,128)(2,1)S(1)}, u32[]{:S(2)}, u32[]{:S(2)}) collective-permute-start(bf16[1024,128]{1,0:T(8,128)(2,1)S(1)} %get-tuple-element.96), channel_id=1, source_target_pairs={{0,3},{1,0},{2,1},{3,2},{4,7},{5,4},{6,5},{7,6},{8,11},{9,8},{10,9... | collective-permute-start | bytes 786440 | tf_op jit(solution)/shard_map/ppermute | solution.py:450
  25.7 29.1 %all-to-all-start.1 = ((bf16[32,4,32,128]{3,2,1,0:T(8,128)(2,1)}), bf16[32,4,32,128]{3,2,1,0:T(8,128)(2,1)S(1)}, u32[]{:S(2)}, u32[]{:S(2)}) async-start(bf16[32,4,32,128]{3,2,1,0:T(8,128)(2,1)} %get-tuple-element.104), calls=%async_computation.1 | async-start | bytes 2097152 | tf_op jit(solution)/shard_map/all_to_all | solution.py:455
  29.3 12.9 %collective-permute-start.10 = (bf16[384,128]{1,0:T(8,128)(2,1)}, bf16[384,128]{1,0:T(8,128)(2,1)S(1)}, u32[]{:S(2)}, u32[]{:S(2)}) collective-permute-start(bf16[384,128]{1,0:T(8,128)(2,1)} %get-tuple-element.101), channel_id=1, source_target_pairs={{0,1},{1,2},{2,3},{3,0},{4,5},{5,6},{6,7},{7,4},{8,9},{9,10},{10,1... | collective-permute-start | bytes 294920 | tf_op jit(solution)/shard_map/ppermute | solution.py:450
  31.0 12.9 %collective-permute-start.11 = (bf16[384,128]{1,0:T(8,128)(2,1)}, bf16[384,128]{1,0:T(8,128)(2,1)S(1)}, u32[]{:S(2)}, u32[]{:S(2)}) collective-permute-start(bf16[384,128]{1,0:T(8,128)(2,1)} %get-tuple-element.102), channel_id=1, source_target_pairs={{0,2},{1,3},{2,0},{3,1},{4,6},{5,7},{6,4},{7,5},{8,10},{9,11},{10,... | collective-permute-start | bytes 294920 | tf_op jit(solution)/shard_map/ppermute | solution.py:450
  32.5 11.6 %collective-permute-start.12 = (bf16[384,128]{1,0:T(8,128)(2,1)}, bf16[384,128]{1,0:T(8,128)(2,1)S(1)}, u32[]{:S(2)}, u32[]{:S(2)}) collective-permute-start(bf16[384,128]{1,0:T(8,128)(2,1)} %get-tuple-element.103), channel_id=1, source_target_pairs={{0,3},{1,0},{2,1},{3,2},{4,7},{5,4},{6,5},{7,6},{8,11},{9,8},{10,9... | collective-permute-start | bytes 294920 | tf_op jit(solution)/shard_map/ppermute | solution.py:450
  35.0 9.1 %copy-start.3 = (f32[8,256,128]{2,1,0:T(8,128)S(1)}, f32[8,256,128]{2,1,0:T(8,128)}, u32[]{:S(2)}) copy-start(f32[8,256,128]{2,1,0:T(8,128)} %get-tuple-element.85.psi_ref) | copy-start | bytes 3145732
  35.0 9.1 %copy-start.4 = (bf16[384,128]{1,0:T(8,128)(2,1)S(1)}, bf16[384,128]{1,0:T(8,128)(2,1)}, u32[]{:S(2)}) copy-start(bf16[384,128]{1,0:T(8,128)(2,1)} %get-tuple-element.100.rest_0_) | copy-start | bytes 294916
  54.8 52.0 %all-to-all-start = ((bf16[32,4,32,256]{3,2,1,0:T(8,128)(2,1)}), bf16[32,4,32,256]{3,2,1,0:T(8,128)(2,1)S(1)}, u32[]{:S(2)}, u32[]{:S(2)}) async-start(bf16[32,4,32,256]{3,2,1,0:T(8,128)(2,1)} %filter_rest.1), calls=%async_computation | async-start | bytes 4194304 | tf_op jit(solution)/shard_map/all_to_all | solution.py:455

commit v11 on v10

--- a/solution.py
+++ b/solution.py
@@ -56,7 +56,7 @@
     rows = full // walls
     i, j = iota((full, full), 0), iota((full, full), 1)
     y = cell_row(i, full // (EDGE * EDGE))
-    source = lax.rem(lax.axis_index("wall") + walls - j // rows, walls)
+    source = lax.axis_index("wall") ^ (j // rows)
     column = source * rows + j % rows
     n = iota((cols, cols), 1)
     target = (n % (cols // EDGE)) * EDGE + n // (cols // EDGE)
@@ -118,7 +118,7 @@
     small = jnp.concatenate(pieces, axis=0).astype(BF16)
     noise.wait()
     for step, out_ref in enumerate(out_refs):
-        start = pl.multiple_of(lax.rem(me + step, walls) * block, block)
+        start = pl.multiple_of((me ^ step) * block, block)
         out_ref[:block] = noise_ref[pl.ds(start, block)]
         out_ref[block:] = small
 
@@ -129,7 +129,7 @@
     me = lax.axis_index("wall")
     copies = []
     for step, out_ref in enumerate(out_refs):
-        to = lax.rem(me + step, walls)
+        to = (me ^ step)
         for side, ref in enumerate((near_ref, far_ref)):
             for c in range(some):
                 at = side * some + c
@@ -153,7 +153,7 @@
     columns = jnp.zeros((full, tail), F32)
     y = cell_row(iota((full, cols), 0), full // (EDGE * EDGE))
     for step, in_ref in enumerate(in_refs):
-        w = lax.rem(me + walls - step, walls)
+        w = me ^ step
         small = in_ref[height - tail :]
         pick = jnp.where(y == iota((full, cols), 1) + w * rows, 1.0, 0.0)
         pick = jnp.where(iota((full, cols), 1) < rows, pick, 0.0).astype(BF16)
@@ -197,7 +197,7 @@
     c = pl.program_id(0)
     target = pl.ds(pl.multiple_of(c * block, block), block)
     for step, out_ref in enumerate(out_refs):
-        source = pl.multiple_of(lax.rem(me + step, walls) * block, block)
+        source = pl.multiple_of((me ^ step) * block, block)
         out_ref[target] = noise_ref[0, pl.ds(source, block)]
     pairs = height // HALO
     pick = edge_picker(cols)
@@ -447,7 +447,7 @@
 
     def spread(blocks):
         return [blocks[0]] + [
-            lax.ppermute(x, "wall", [(i, (i + step) % n_wall) for i in range(n_wall)])
+            lax.ppermute(x, "wall", [(i, i ^ step) for i in range(n_wall)])
             for step, x in enumerate(blocks[1:], 1)
         ]
 

time: 109 us -> 108 us (level)
  starting transfers between devices: 27.8 us -> 25.7 us
  waiting for transfers between devices: 60.9 us -> 62.4 us
    ppermute x9, starting transfers between devices: 15.1 us -> 11.7 us  [spread(): lax.ppermute(x, 'wall', [(i, i ^ step) for i in range(n_wall)])]
    ppermute x9, waiting for transfers between devices: 7.6 us -> 9.82 us  [spread(): lax.ppermute(x, 'wall', [(i, i ^ step) for i in range(n_wall)])]
    ppermute x2, starting transfers between devices: 6.65 us -> 7.86 us  [exchange(): lax.ppermute(far, 'span', chip_pairs)]
where the time goes in v11:
time: 108 us
  waiting for transfers between devices  62.4 us (58%)
  starting transfers between devices  25.7 us (24%)
  Pallas kernels  19.3 us (18%)
    all_to_all x2, waiting for transfers between devices, send(): lax.all_to_all(x, ('span', 'wall'), 0, 0, tiled=True)  52.6 us
    ppermute x9, starting transfers between devices, spread(): lax.ppermute(x, 'wall', [(i, i ^ step) for i in range(n_wall)])  11.7 us
    ppermute x9, waiting for transfers between devices, spread(): lax.ppermute(x, 'wall', [(i, i ^ step) for i in range(n_wall)])  9.82 us
    ppermute x2, starting transfers between devices, exchange(): lax.ppermute(far, 'span', chip_pairs)  7.86 us
    all_to_all x2, starting transfers between devices, send(): lax.all_to_all(x, ('span', 'wall'), 0, 0, tiled=True)  5.99 us
    pallas_call x1, Pallas kernels, per_device(): call(functools.partial(rest_kernel, planes), [VMEM] * (7 + n_wall), [out(...  5.13 us
    pallas_call x1, Pallas kernels, per_device(): call(functools.partial(first_kernel, planes), [VMEM] * 7, [out(1), hbm(ps...  3.67 us
    pallas_call x2, Pallas kernels, join(): pl.pallas_call(functools.partial(join_narrow_kernel, some) if narrow else...  2.37 us
  transfers between devices with their start and end apart: 15, of which 5 were waited for; matrix products, arithmetic and copies ran while one was open for 0% of the time, Pallas kernels for 15%

profile of v11, /device:TPU:0, one launch (start us, length us, event | category | flops | bytes accessed | tf_op | source)
XLA Modules:
  0.0 107.6 jit_solution(8576556081679117740)
XLA Ops:
  0.0 1.3 %pack.1 = (bf16[544,128]{1,0:T(8,128)(2,1)S(1)}, bf16[544,128]{1,0:T(8,128)(2,1)S(1)}, bf16[544,128]{1,0:T(8,128)(2,1)S(1)}, bf16[544,128]{1,0:T(8,128)(2,1)S(1)}) custom-call(bf16[3,2048,128]{2,1,0:T(8,128)(2,1)} %bitcast.8, f32[6,64]{1,0:T(8,128)} %lund_in.1, f32[1,64]{1,0:T(1,128)} %bitcast.11, s32[1,512]{1,0:T(1,128)} %bitcast.10), custom_call_target="tpu_custom_call" | custom-call | flops 1000000000 | bytes 1024 | tf_op jit(solution)/shard_map/pack/pallas_call | solution.py:459
  1.3 0.0 copy-start.1
  1.3 0.0 copy-start.2
  1.3 3.0 %collective-permute-start = (bf16[544,128]{1,0:T(8,128)(2,1)S(1)}, bf16[544,128]{1,0:T(8,128)(2,1)S(1)}, u32[]{:S(2)}, u32[]{:S(2)}) collective-permute-start(bf16[544,128]{1,0:T(8,128)(2,1)S(1)} %get-tuple-element.62), channel_id=1, source_target_pairs={{0,1},{1,0},{2,3},{3,2},{4,5},{5,4},{6,7},{7,6},{8,9},{9,8},{10,11... | collective-permute-start | bytes 417800 | tf_op jit(solution)/shard_map/ppermute | solution.py:450
  4.3 1.5 %collective-permute-start.1 = (bf16[544,128]{1,0:T(8,128)(2,1)S(1)}, bf16[544,128]{1,0:T(8,128)(2,1)S(1)}, u32[]{:S(2)}, u32[]{:S(2)}) collective-permute-start(bf16[544,128]{1,0:T(8,128)(2,1)S(1)} %get-tuple-element.63), channel_id=1, source_target_pairs={{0,2},{1,3},{2,0},{3,1},{4,6},{5,7},{6,4},{7,5},{8,10},{9,11},{10,... | collective-permute-start | bytes 417800 | tf_op jit(solution)/shard_map/ppermute | solution.py:450
  5.8 0.0 collective-permute-start.2
  5.8 0.0 copy-done
  5.8 0.9 prepare_rest.1
  6.8 0.1 collective-permute-start.4
  6.9 4.2 %collective-permute-start.5 = (bf16[4,2,96,128]{3,2,1,0:T(8,128)(2,1)S(1)}, bf16[4,2,96,128]{3,2,1,0:T(8,128)(2,1)S(1)}, u32[]{:S(2)}, u32[]{:S(2)}) collective-permute-start(bf16[4,2,96,128]{3,2,1,0:T(8,128)(2,1)S(1)} %get-tuple-element.67), channel_id=1, source_target_pairs={{0,28},{4,8},{8,4},{12,16},{16,12},{20,24},{24,20},{28,0},{1,29},{... | collective-permute-start | bytes 589832 | tf_op jit(solution)/shard_map/ppermute | solution.py:446
  11.0 0.0 copy-done.1
  11.0 0.9 taps_first.1
  11.9 0.0 collective-permute-done.rest_1_
  11.9 0.5 collective-permute-done.1.rest_2_
  12.4 0.0 collective-permute-done.2.rest_3_
  12.4 0.3 edges_first.1
  12.7 0.1 collective-permute-start.3
  12.8 3.7 %collective-permute-start.6 = (bf16[192,256]{1,0:T(8,128)(2,1)S(1)}, bf16[192,256]{1,0:T(8,128)(2,1)S(1)}, u32[]{:S(2)}, u32[]{:S(2)}) collective-permute-start(bf16[192,256]{1,0:T(8,128)(2,1)S(1)} %get-tuple-element.78), channel_id=1, source_target_pairs={{0,28},{4,8},{8,4},{12,16},{16,12},{20,24},{24,20},{28,0},{1,29},{... | collective-permute-start | bytes 294920 | tf_op jit(solution)/shard_map/ppermute | solution.py:446
  16.5 0.4 small.1
  16.9 0.0 collective-permute-done.4.near_ref
  16.9 1.3 %collective-permute-start.7 = (bf16[1024,128]{1,0:T(8,128)(2,1)S(1)}, bf16[1024,128]{1,0:T(8,128)(2,1)S(1)}, u32[]{:S(2)}, u32[]{:S(2)}) collective-permute-start(bf16[1024,128]{1,0:T(8,128)(2,1)S(1)} %get-tuple-element.94), channel_id=1, source_target_pairs={{0,1},{1,0},{2,3},{3,2},{4,5},{5,4},{6,7},{7,6},{8,9},{9,8},{10,11... | collective-permute-start | bytes 786440 | tf_op jit(solution)/shard_map/ppermute | solution.py:450
  18.2 0.9 main_first.1.psi_in
  19.1 0.9 collective-permute-start.8
  20.0 0.0 collective-permute-done.5.far_ref
  20.0 1.4 %collective-permute-start.9 = (bf16[1024,128]{1,0:T(8,128)(2,1)S(1)}, bf16[1024,128]{1,0:T(8,128)(2,1)S(1)}, u32[]{:S(2)}, u32[]{:S(2)}) collective-permute-start(bf16[1024,128]{1,0:T(8,128)(2,1)S(1)} %get-tuple-element.96), channel_id=1, source_target_pairs={{0,3},{1,2},{2,1},{3,0},{4,7},{5,6},{6,5},{7,4},{8,11},{9,10},{10,... | collective-permute-start | bytes 786440 | tf_op jit(solution)/shard_map/ppermute | solution.py:450
  21.4 0.0 collective-permute-done.3.near_ref
  21.4 0.0 collective-permute-done.6.far_ref
  21.4 3.7 %filter_first.1 = (bf16[32,4,32,128]{3,2,1,0:T(8,128)(2,1)}, f32[8,256,128]{2,1,0:T(8,128)}) custom-call(f32[8,256,128]{2,1,0:T(8,128)S(1)} %main_first.1.psi_in, bf16[192,256]{1,0:T(8,128)(2,1)S(1)} %collective-permute-done.3.near_ref, bf16[192,256]{1,0:T(8,128)(2,1)S(1)} %collective-permute-done.6.far_ref, f32[256,128]{1,0:T(8,128)S(1)} %get-tuple-element.82.factor_ref, ...), custom_call_target="tpu_custom_call" | custom-call | flops 1000000000 | bytes 1024 | tf_op jit(solution)/shard_map/filter_first/pallas_call | solution.py:539
  25.1 2.7 %all-to-all-start.1 = ((bf16[32,4,32,128]{3,2,1,0:T(8,128)(2,1)}), bf16[32,4,32,128]{3,2,1,0:T(8,128)(2,1)S(1)}, u32[]{:S(2)}, u32[]{:S(2)}) async-start(bf16[32,4,32,128]{3,2,1,0:T(8,128)(2,1)} %get-tuple-element.104), calls=%async_computation.1 | async-start | bytes 2097152 | tf_op jit(solution)/shard_map/all_to_all | solution.py:455
  27.8 0.9 pack_late.1
  28.7 1.7 %collective-permute-start.10 = (bf16[384,128]{1,0:T(8,128)(2,1)}, bf16[384,128]{1,0:T(8,128)(2,1)S(1)}, u32[]{:S(2)}, u32[]{:S(2)}) collective-permute-start(bf16[384,128]{1,0:T(8,128)(2,1)} %get-tuple-element.101), channel_id=1, source_target_pairs={{0,1},{1,0},{2,3},{3,2},{4,5},{5,4},{6,7},{7,6},{8,9},{9,8},{10,11... | collective-permute-start | bytes 294920 | tf_op jit(solution)/shard_map/ppermute | solution.py:450
  30.4 1.5 %collective-permute-start.11 = (bf16[384,128]{1,0:T(8,128)(2,1)}, bf16[384,128]{1,0:T(8,128)(2,1)S(1)}, u32[]{:S(2)}, u32[]{:S(2)}) collective-permute-start(bf16[384,128]{1,0:T(8,128)(2,1)} %get-tuple-element.102), channel_id=1, source_target_pairs={{0,2},{1,3},{2,0},{3,1},{4,6},{5,7},{6,4},{7,5},{8,10},{9,11},{10,... | collective-permute-start | bytes 294920 | tf_op jit(solution)/shard_map/ppermute | solution.py:450
  31.9 0.0 collective-permute-done.7.rest_1_
  31.9 0.4 collective-permute-start.12
  32.2 1.1 %taps_rest.1 = (bf16[2,256,512]{2,1,0:T(8,128)(2,1)S(1)}, bf16[2,256,256]{2,1,0:T(8,128)(2,1)S(1)}, bf16[2,2,256,256]{3,2,1,0:T(8,128)(2,1)S(1)}) custom-call(f32[3]{0:T(128)S(1)} %copy-done.1, f32[3]{0:T(128)S(1)} %copy-done.2), custom_call_target="tpu_custom_call" | custom-call | flops 1000000000 | bytes 1024 | tf_op jit(solution)/shard_map/taps_rest/pallas_call | solution.py:490
  33.4 0.0 collective-permute-done.8.rest_2_
  33.4 0.0 collective-permute-done.9.rest_3_
  33.4 1.4 %main_next.1.next_ref = f32[16,256,128]{2,1,0:T(8,128)S(1)} custom-call(bf16[2,256,512]{2,1,0:T(8,128)(2,1)S(1)} %get-tuple-element.91.wall_ref, bf16[2,256,256]{2,1,0:T(8,128)(2,1)S(1)} %get-tuple-element.92.main_ref, bf16[1024,128]{1,0:T(8,128)(2,1)S(1)} %get-tuple-element.93.rest_0_, bf16[1024,128]{1,0:T(8,128)(2,1)S(1)} %collective-permute-done.7.rest_1_, ...), custom_call_target="tpu_custom_call" | custom-call | flops 1000000000 | bytes 1024 | tf_op jit(solution)/shard_map/main_next/pallas_call | solution.py:563
  34.8 6.0 %collective-permute-done.10.rest_1_ = bf16[384,128]{1,0:T(8,128)(2,1)S(1)} collective-permute-done((bf16[384,128]{1,0:T(8,128)(2,1)}, bf16[384,128]{1,0:T(8,128)(2,1)S(1)}, u32[]{:S(2)}, u32[]{:S(2)}) %collective-permute-start.10) | collective-permute-done | bytes 98336 | tf_op jit(solution)/shard_map/ppermute | solution.py:450
  40.8 0.0 collective-permute-done.11.rest_2_
  40.8 3.3 %collective-permute-done.12.rest_3_ = bf16[384,128]{1,0:T(8,128)(2,1)S(1)} collective-permute-done((bf16[384,128]{1,0:T(8,128)(2,1)}, bf16[384,128]{1,0:T(8,128)(2,1)S(1)}, u32[]{:S(2)}, u32[]{:S(2)}) %collective-permute-start.12) | collective-permute-done | bytes 98336 | tf_op jit(solution)/shard_map/ppermute | solution.py:450
  44.2 0.0 copy-done.4
  44.2 5.1 %filter_rest.1 = bf16[32,4,32,256]{3,2,1,0:T(8,128)(2,1)} custom-call(f32[8,256,128]{2,1,0:T(8,128)S(1)} %copy-done.3, f32[16,256,128]{2,1,0:T(8,128)S(1)} %main_next.1.next_ref, f32[256,128]{1,0:T(8,128)S(1)} %get-tuple-element.82.factor_ref, s32[4,4,128]{2,1,0:T(4,128)S(1)} %get-tuple-element.83.target_ref, ...), custom_call_target="tpu_custom_call" | custom-call | flops 99999997952 | bytes 1024 | tf_op jit(solution)/shard_map/filter_rest/pallas_call | solution.py:570
  49.3 4.9 %all-to-all-done.1 = bf16[32,4,32,128]{3,2,1,0:T(8,128)(2,1)S(1)} async-done(((bf16[32,4,32,128]{3,2,1,0:T(8,128)(2,1)}), bf16[32,4,32,128]{3,2,1,0:T(8,128)(2,1)S(1)}, u32[]{:S(2)}, u32[]{:S(2)}) %all-to-all-start.1) | async-done | bytes 1048608 | tf_op jit(solution)/shard_map/all_to_all | solution.py:455
  54.2 3.3 %all-to-all-start = ((bf16[32,4,32,256]{3,2,1,0:T(8,128)(2,1)}), bf16[32,4,32,256]{3,2,1,0:T(8,128)(2,1)S(1)}, u32[]{:S(2)}, u32[]{:S(2)}) async-start(bf16[32,4,32,256]{3,2,1,0:T(8,128)(2,1)} %filter_rest.1), calls=%async_computation | async-start | bytes 4194304 | tf_op jit(solution)/shard_map/all_to_all | solution.py:455
  57.6 1.0 join.2.rest_0_
  58.6 47.7 %all-to-all-done = bf16[32,4,32,256]{3,2,1,0:T(8,128)(2,1)S(1)} async-done(((bf16[32,4,32,256]{3,2,1,0:T(8,128)(2,1)}), bf16[32,4,32,256]{3,2,1,0:T(8,128)(2,1)S(1)}, u32[]{:S(2)}, u32[]{:S(2)}) %all-to-all-start) | async-done | bytes 2097184 | tf_op jit(solution)/shard_map/all_to_all | solution.py:455
  106.3 1.4 %join.3 = bf16[8,128,1536]{2,1,0:T(8,128)(2,1)} custom-call(bf16[8,4,128,256]{3,2,1,0:T(8,128)(2,1)S(1)} %bitcast.6, bf16[8,128,1536]{2,1,0:T(8,128)(2,1)} %join.2.rest_0_), custom_call_target="tpu_custom_call", output_to_operand_aliasing={{}: (1, {})} | custom-call | tf_op jit(solution)/shard_map/join/pallas_call | solution.py:588
  (5 shorter events, 0.0 us)
Async XLA Ops:
  0.0 5.8 %copy-start = (bf16[3,32,64,128]{3,2,1,0:T(8,128)(2,1)S(1)}, bf16[3,32,64,128]{3,2,1,0:T(8,128)(2,1)}, u32[]{:S(2)}) copy-start(bf16[3,32,64,128]{3,2,1,0:T(8,128)(2,1)} %param.6) | copy-start | bytes 4718596
  1.3 9.7 %copy-start.1 = (f32[3]{0:T(128)S(1)}, f32[3]{0:T(128)}, u32[]{:S(2)}) copy-start(f32[3]{0:T(128)} %wall_scale.2) | copy-start | bytes 40
  1.3 9.7 %copy-start.2 = (f32[3]{0:T(128)S(1)}, f32[3]{0:T(128)}, u32[]{:S(2)}) copy-start(f32[3]{0:T(128)} %span_scale.2) | copy-start | bytes 40
  1.3 10.6 %collective-permute-start = (bf16[544,128]{1,0:T(8,128)(2,1)S(1)}, bf16[544,128]{1,0:T(8,128)(2,1)S(1)}, u32[]{:S(2)}, u32[]{:S(2)}) collective-permute-start(bf16[544,128]{1,0:T(8,128)(2,1)S(1)} %get-tuple-element.62), channel_id=1, source_target_pairs={{0,1},{1,0},{2,3},{3,2},{4,5},{5,4},{6,7},{7,6},{8,9},{9,8},{10,11... | collective-permute-start | bytes 417800 | tf_op jit(solution)/shard_map/ppermute | solution.py:450
  4.3 8.1 %collective-permute-start.1 = (bf16[544,128]{1,0:T(8,128)(2,1)S(1)}, bf16[544,128]{1,0:T(8,128)(2,1)S(1)}, u32[]{:S(2)}, u32[]{:S(2)}) collective-permute-start(bf16[544,128]{1,0:T(8,128)(2,1)S(1)} %get-tuple-element.63), channel_id=1, source_target_pairs={{0,2},{1,3},{2,0},{3,1},{4,6},{5,7},{6,4},{7,5},{8,10},{9,11},{10,... | collective-permute-start | bytes 417800 | tf_op jit(solution)/shard_map/ppermute | solution.py:450
  5.8 6.6 %collective-permute-start.2 = (bf16[544,128]{1,0:T(8,128)(2,1)S(1)}, bf16[544,128]{1,0:T(8,128)(2,1)S(1)}, u32[]{:S(2)}, u32[]{:S(2)}) collective-permute-start(bf16[544,128]{1,0:T(8,128)(2,1)S(1)} %get-tuple-element.64), channel_id=1, source_target_pairs={{0,3},{1,2},{2,1},{3,0},{4,7},{5,6},{6,5},{7,4},{8,11},{9,10},{10,... | collective-permute-start | bytes 417800 | tf_op jit(solution)/shard_map/ppermute | solution.py:450
  6.8 10.1 %collective-permute-start.4 = (bf16[4,2,96,128]{3,2,1,0:T(8,128)(2,1)S(1)}, bf16[4,2,96,128]{3,2,1,0:T(8,128)(2,1)S(1)}, u32[]{:S(2)}, u32[]{:S(2)}) collective-permute-start(bf16[4,2,96,128]{3,2,1,0:T(8,128)(2,1)S(1)} %get-tuple-element.66), channel_id=1, source_target_pairs={{0,4},{4,0},{8,12},{12,8},{16,20},{20,16},{24,28},{28,24},{1,5},{5... | collective-permute-start | bytes 589832 | tf_op jit(solution)/shard_map/ppermute | solution.py:446
  6.9 13.1 %collective-permute-start.5 = (bf16[4,2,96,128]{3,2,1,0:T(8,128)(2,1)S(1)}, bf16[4,2,96,128]{3,2,1,0:T(8,128)(2,1)S(1)}, u32[]{:S(2)}, u32[]{:S(2)}) collective-permute-start(bf16[4,2,96,128]{3,2,1,0:T(8,128)(2,1)S(1)} %get-tuple-element.67), channel_id=1, source_target_pairs={{0,28},{4,8},{8,4},{12,16},{16,12},{20,24},{24,20},{28,0},{1,29},{... | collective-permute-start | bytes 589832 | tf_op jit(solution)/shard_map/ppermute | solution.py:446
  12.7 8.7 %collective-permute-start.3 = (bf16[192,256]{1,0:T(8,128)(2,1)S(1)}, bf16[192,256]{1,0:T(8,128)(2,1)S(1)}, u32[]{:S(2)}, u32[]{:S(2)}) collective-permute-start(bf16[192,256]{1,0:T(8,128)(2,1)S(1)} %get-tuple-element.76), channel_id=1, source_target_pairs={{0,4},{4,0},{8,12},{12,8},{16,20},{20,16},{24,28},{28,24},{1,5},{5... | collective-permute-start | bytes 294920 | tf_op jit(solution)/shard_map/ppermute | solution.py:446
  12.8 8.6 %collective-permute-start.6 = (bf16[192,256]{1,0:T(8,128)(2,1)S(1)}, bf16[192,256]{1,0:T(8,128)(2,1)S(1)}, u32[]{:S(2)}, u32[]{:S(2)}) collective-permute-start(bf16[192,256]{1,0:T(8,128)(2,1)S(1)} %get-tuple-element.78), channel_id=1, source_target_pairs={{0,28},{4,8},{8,4},{12,16},{16,12},{20,24},{24,20},{28,0},{1,29},{... | collective-permute-start | bytes 294920 | tf_op jit(solution)/shard_map/ppermute | solution.py:446
  16.9 15.0 %collective-permute-start.7 = (bf16[1024,128]{1,0:T(8,128)(2,1)S(1)}, bf16[1024,128]{1,0:T(8,128)(2,1)S(1)}, u32[]{:S(2)}, u32[]{:S(2)}) collective-permute-start(bf16[1024,128]{1,0:T(8,128)(2,1)S(1)} %get-tuple-element.94), channel_id=1, source_target_pairs={{0,1},{1,0},{2,3},{3,2},{4,5},{5,4},{6,7},{7,6},{8,9},{9,8},{10,11... | collective-permute-start | bytes 786440 | tf_op jit(solution)/shard_map/ppermute | solution.py:450
  19.1 14.3 %collective-permute-start.8 = (bf16[1024,128]{1,0:T(8,128)(2,1)S(1)}, bf16[1024,128]{1,0:T(8,128)(2,1)S(1)}, u32[]{:S(2)}, u32[]{:S(2)}) collective-permute-start(bf16[1024,128]{1,0:T(8,128)(2,1)S(1)} %get-tuple-element.95), channel_id=1, source_target_pairs={{0,2},{1,3},{2,0},{3,1},{4,6},{5,7},{6,4},{7,5},{8,10},{9,11},{10,... | collective-permute-start | bytes 786440 | tf_op jit(solution)/shard_map/ppermute | solution.py:450
  20.0 13.4 %collective-permute-start.9 = (bf16[1024,128]{1,0:T(8,128)(2,1)S(1)}, bf16[1024,128]{1,0:T(8,128)(2,1)S(1)}, u32[]{:S(2)}, u32[]{:S(2)}) collective-permute-start(bf16[1024,128]{1,0:T(8,128)(2,1)S(1)} %get-tuple-element.96), channel_id=1, source_target_pairs={{0,3},{1,2},{2,1},{3,0},{4,7},{5,6},{6,5},{7,4},{8,11},{9,10},{10,... | collective-permute-start | bytes 786440 | tf_op jit(solution)/shard_map/ppermute | solution.py:450
  25.1 29.1 %all-to-all-start.1 = ((bf16[32,4,32,128]{3,2,1,0:T(8,128)(2,1)}), bf16[32,4,32,128]{3,2,1,0:T(8,128)(2,1)S(1)}, u32[]{:S(2)}, u32[]{:S(2)}) async-start(bf16[32,4,32,128]{3,2,1,0:T(8,128)(2,1)} %get-tuple-element.104), calls=%async_computation.1 | async-start | bytes 2097152 | tf_op jit(solution)/shard_map/all_to_all | solution.py:455
  28.7 12.1 %collective-permute-start.10 = (bf16[384,128]{1,0:T(8,128)(2,1)}, bf16[384,128]{1,0:T(8,128)(2,1)S(1)}, u32[]{:S(2)}, u32[]{:S(2)}) collective-permute-start(bf16[384,128]{1,0:T(8,128)(2,1)} %get-tuple-element.101), channel_id=1, source_target_pairs={{0,1},{1,0},{2,3},{3,2},{4,5},{5,4},{6,7},{7,6},{8,9},{9,8},{10,11... | collective-permute-start | bytes 294920 | tf_op jit(solution)/shard_map/ppermute | solution.py:450
  30.4 10.4 %collective-permute-start.11 = (bf16[384,128]{1,0:T(8,128)(2,1)}, bf16[384,128]{1,0:T(8,128)(2,1)S(1)}, u32[]{:S(2)}, u32[]{:S(2)}) collective-permute-start(bf16[384,128]{1,0:T(8,128)(2,1)} %get-tuple-element.102), channel_id=1, source_target_pairs={{0,2},{1,3},{2,0},{3,1},{4,6},{5,7},{6,4},{7,5},{8,10},{9,11},{10,... | collective-permute-start | bytes 294920 | tf_op jit(solution)/shard_map/ppermute | solution.py:450
  31.9 12.3 %collective-permute-start.12 = (bf16[384,128]{1,0:T(8,128)(2,1)}, bf16[384,128]{1,0:T(8,128)(2,1)S(1)}, u32[]{:S(2)}, u32[]{:S(2)}) collective-permute-start(bf16[384,128]{1,0:T(8,128)(2,1)} %get-tuple-element.103), channel_id=1, source_target_pairs={{0,3},{1,2},{2,1},{3,0},{4,7},{5,6},{6,5},{7,4},{8,11},{9,10},{10,... | collective-permute-start | bytes 294920 | tf_op jit(solution)/shard_map/ppermute | solution.py:450
  33.3 10.8 %copy-start.3 = (f32[8,256,128]{2,1,0:T(8,128)S(1)}, f32[8,256,128]{2,1,0:T(8,128)}, u32[]{:S(2)}) copy-start(f32[8,256,128]{2,1,0:T(8,128)} %get-tuple-element.85.psi_ref) | copy-start | bytes 3145732
  33.4 10.8 %copy-start.4 = (bf16[384,128]{1,0:T(8,128)(2,1)S(1)}, bf16[384,128]{1,0:T(8,128)(2,1)}, u32[]{:S(2)}) copy-start(bf16[384,128]{1,0:T(8,128)(2,1)} %get-tuple-element.100.rest_0_) | copy-start | bytes 294916
  54.2 52.0 %all-to-all-start = ((bf16[32,4,32,256]{3,2,1,0:T(8,128)(2,1)}), bf16[32,4,32,256]{3,2,1,0:T(8,128)(2,1)S(1)}, u32[]{:S(2)}, u32[]{:S(2)}) async-start(bf16[32,4,32,256]{3,2,1,0:T(8,128)(2,1)} %filter_rest.1), calls=%async_computation | async-start | bytes 4194304 | tf_op jit(solution)/shard_map/all_to_all | solution.py:455

commit v12 on v11

--- a/solution.py
+++ b/solution.py
@@ -331,6 +331,10 @@
     wide = 2 * HALO
     widen(factor_ref, wide_ref, (0, 6))
 
+    def psi_copy(pair):
+        at = pl.ds(2 * pair, 2)
+        return pltpu.make_async_copy(psi_ref.at[at], psi_out.at[at], psi_sem.at[pair])
+
     def pair_step(pair, carry):
         at = pl.ds(pl.multiple_of(pair * wide, wide), wide)
         tile = [near_ref[at], far_ref[at], jnp.zeros((cols - 2 * wide, full), BF16)]
@@ -340,13 +344,13 @@
             psi = psi_in[t] + beside[odd]
             psi_ref[t] = psi
             place_cells(wide_ref[6] + wide_ref[0] * psi, t, cells_ref, 0)
+        psi_copy(pair).start()
         return carry
 
     lax.fori_loop(0, planes // 2, pair_step, 0, unroll=True)
-    copy = pltpu.make_async_copy(psi_ref, psi_out, psi_sem.at[0])
-    copy.start()
     scatter_cells(cells_ref, target_ref, sent_ref, out_ref, sems)
-    copy.wait()
+    for pair in range(planes // 2):
+        psi_copy(pair).wait()
 
 
 def rest_kernel(
@@ -542,7 +546,7 @@
         [out(1), hbm(psi.shape, F32)],
         "filter_first",
         24,
-        [pltpu.VMEM(psi.shape, F32), cells, *more, dma((1,))],
+        [pltpu.VMEM(psi.shape, F32), cells, *more, dma((pairs,))],
         out_specs=[ANYWHERE, ANYWHERE],
     )(psi_main, near, far, factor, target, wall_first, halo_first)
     (wall_scale, span_scale, rest_near, rest_far), sent = lax.optimization_barrier(

time: 108 us -> 108 us (level)
  no operation moved by 1% of the time
where the time goes in v12:
time: 108 us; the launch traced here: 107 us
  waiting for transfers between devices  62.5 us (58%)
  starting transfers between devices  25.7 us (24%)
  Pallas kernels  19.1 us (18%)
    all_to_all x2, waiting for transfers between devices, send(): lax.all_to_all(x, ('span', 'wall'), 0, 0, tiled=True)  52.6 us
    ppermute x9, starting transfers between devices, spread(): lax.ppermute(x, 'wall', [(i, i ^ step) for i in range(n_wall)])  11.7 us
    ppermute x9, waiting for transfers between devices, spread(): lax.ppermute(x, 'wall', [(i, i ^ step) for i in range(n_wall)])  9.82 us
    ppermute x2, starting transfers between devices, exchange(): lax.ppermute(far, 'span', chip_pairs)  7.86 us
    all_to_all x2, starting transfers between devices, send(): lax.all_to_all(x, ('span', 'wall'), 0, 0, tiled=True)  5.99 us
    pallas_call x1, Pallas kernels, per_device(): call(functools.partial(rest_kernel, planes), [VMEM] * (7 + n_wall), [out(...  5.11 us
    pallas_call x1, Pallas kernels, per_device(): call(functools.partial(first_kernel, planes), [VMEM] * 7, [out(1), hbm(ps...  3.47 us
    pallas_call x2, Pallas kernels, join(): pl.pallas_call(functools.partial(join_narrow_kernel, some) if narrow else...  2.37 us
  transfers between devices with their start and end apart: 15, of which 5 were waited for; matrix products, arithmetic and copies ran while one was open for 0% of the time, Pallas kernels for 15%

profile of v12, /device:TPU:0, one launch (start us, length us, event | category | flops | bytes accessed | tf_op | source)
XLA Modules:
  0.0 107.4 jit_solution(5730582910418190955)
XLA Ops:
  0.0 1.3 %pack.1 = (bf16[544,128]{1,0:T(8,128)(2,1)S(1)}, bf16[544,128]{1,0:T(8,128)(2,1)S(1)}, bf16[544,128]{1,0:T(8,128)(2,1)S(1)}, bf16[544,128]{1,0:T(8,128)(2,1)S(1)}) custom-call(bf16[3,2048,128]{2,1,0:T(8,128)(2,1)} %bitcast.8, f32[6,64]{1,0:T(8,128)} %lund_in.1, f32[1,64]{1,0:T(1,128)} %bitcast.11, s32[1,512]{1,0:T(1,128)} %bitcast.10), custom_call_target="tpu_custom_call" | custom-call | flops 1000000000 | bytes 1024 | tf_op jit(solution)/shard_map/pack/pallas_call | solution.py:463
  1.3 0.0 copy-start.1
  1.3 0.0 copy-start.2
  1.3 3.0 %collective-permute-start = (bf16[544,128]{1,0:T(8,128)(2,1)S(1)}, bf16[544,128]{1,0:T(8,128)(2,1)S(1)}, u32[]{:S(2)}, u32[]{:S(2)}) collective-permute-start(bf16[544,128]{1,0:T(8,128)(2,1)S(1)} %get-tuple-element.62), channel_id=1, source_target_pairs={{0,1},{1,0},{2,3},{3,2},{4,5},{5,4},{6,7},{7,6},{8,9},{9,8},{10,11... | collective-permute-start | bytes 417800 | tf_op jit(solution)/shard_map/ppermute | solution.py:454
  4.3 1.5 %collective-permute-start.1 = (bf16[544,128]{1,0:T(8,128)(2,1)S(1)}, bf16[544,128]{1,0:T(8,128)(2,1)S(1)}, u32[]{:S(2)}, u32[]{:S(2)}) collective-permute-start(bf16[544,128]{1,0:T(8,128)(2,1)S(1)} %get-tuple-element.63), channel_id=1, source_target_pairs={{0,2},{1,3},{2,0},{3,1},{4,6},{5,7},{6,4},{7,5},{8,10},{9,11},{10,... | collective-permute-start | bytes 417800 | tf_op jit(solution)/shard_map/ppermute | solution.py:454
  5.8 0.0 collective-permute-start.2
  5.8 0.0 copy-done
  5.8 0.9 prepare_rest.1
  6.8 0.1 collective-permute-start.4
  6.9 4.2 %collective-permute-start.5 = (bf16[4,2,96,128]{3,2,1,0:T(8,128)(2,1)S(1)}, bf16[4,2,96,128]{3,2,1,0:T(8,128)(2,1)S(1)}, u32[]{:S(2)}, u32[]{:S(2)}) collective-permute-start(bf16[4,2,96,128]{3,2,1,0:T(8,128)(2,1)S(1)} %get-tuple-element.67), channel_id=1, source_target_pairs={{0,28},{4,8},{8,4},{12,16},{16,12},{20,24},{24,20},{28,0},{1,29},{... | collective-permute-start | bytes 589832 | tf_op jit(solution)/shard_map/ppermute | solution.py:450
  11.0 0.0 copy-done.1
  11.0 0.9 taps_first.1
  11.9 0.0 collective-permute-done.rest_1_
  11.9 0.5 collective-permute-done.1.rest_2_
  12.4 0.0 collective-permute-done.2.rest_3_
  12.4 0.3 edges_first.1
  12.7 0.1 collective-permute-start.3
  12.8 3.7 %collective-permute-start.6 = (bf16[192,256]{1,0:T(8,128)(2,1)S(1)}, bf16[192,256]{1,0:T(8,128)(2,1)S(1)}, u32[]{:S(2)}, u32[]{:S(2)}) collective-permute-start(bf16[192,256]{1,0:T(8,128)(2,1)S(1)} %get-tuple-element.78), channel_id=1, source_target_pairs={{0,28},{4,8},{8,4},{12,16},{16,12},{20,24},{24,20},{28,0},{1,29},{... | collective-permute-start | bytes 294920 | tf_op jit(solution)/shard_map/ppermute | solution.py:450
  16.5 0.4 small.1
  16.9 0.0 collective-permute-done.4.near_ref
  16.9 1.3 %collective-permute-start.7 = (bf16[1024,128]{1,0:T(8,128)(2,1)S(1)}, bf16[1024,128]{1,0:T(8,128)(2,1)S(1)}, u32[]{:S(2)}, u32[]{:S(2)}) collective-permute-start(bf16[1024,128]{1,0:T(8,128)(2,1)S(1)} %get-tuple-element.94), channel_id=1, source_target_pairs={{0,1},{1,0},{2,3},{3,2},{4,5},{5,4},{6,7},{7,6},{8,9},{9,8},{10,11... | collective-permute-start | bytes 786440 | tf_op jit(solution)/shard_map/ppermute | solution.py:454
  18.2 0.9 main_first.1.psi_in
  19.1 0.9 collective-permute-start.8
  20.0 0.0 collective-permute-done.5.far_ref
  20.0 1.4 %collective-permute-start.9 = (bf16[1024,128]{1,0:T(8,128)(2,1)S(1)}, bf16[1024,128]{1,0:T(8,128)(2,1)S(1)}, u32[]{:S(2)}, u32[]{:S(2)}) collective-permute-start(bf16[1024,128]{1,0:T(8,128)(2,1)S(1)} %get-tuple-element.96), channel_id=1, source_target_pairs={{0,3},{1,2},{2,1},{3,0},{4,7},{5,6},{6,5},{7,4},{8,11},{9,10},{10,... | collective-permute-start | bytes 786440 | tf_op jit(solution)/shard_map/ppermute | solution.py:454
  21.4 0.0 collective-permute-done.3.near_ref
  21.4 0.0 collective-permute-done.6.far_ref
  21.4 3.5 %filter_first.1 = (bf16[32,4,32,128]{3,2,1,0:T(8,128)(2,1)}, f32[8,256,128]{2,1,0:T(8,128)}) custom-call(f32[8,256,128]{2,1,0:T(8,128)S(1)} %main_first.1.psi_in, bf16[192,256]{1,0:T(8,128)(2,1)S(1)} %collective-permute-done.3.near_ref, bf16[192,256]{1,0:T(8,128)(2,1)S(1)} %collective-permute-done.6.far_ref, f32[256,128]{1,0:T(8,128)S(1)} %get-tuple-element.82.factor_ref, ...), custom_call_target="tpu_custom_call" | custom-call | flops 1000000000 | bytes 1024 | tf_op jit(solution)/shard_map/filter_first/pallas_call | solution.py:543
  24.9 2.7 %all-to-all-start.1 = ((bf16[32,4,32,128]{3,2,1,0:T(8,128)(2,1)}), bf16[32,4,32,128]{3,2,1,0:T(8,128)(2,1)S(1)}, u32[]{:S(2)}, u32[]{:S(2)}) async-start(bf16[32,4,32,128]{3,2,1,0:T(8,128)(2,1)} %get-tuple-element.104), calls=%async_computation.1 | async-start | bytes 2097152 | tf_op jit(solution)/shard_map/all_to_all | solution.py:459
  27.6 0.9 pack_late.1
  28.5 1.7 %collective-permute-start.10 = (bf16[384,128]{1,0:T(8,128)(2,1)}, bf16[384,128]{1,0:T(8,128)(2,1)S(1)}, u32[]{:S(2)}, u32[]{:S(2)}) collective-permute-start(bf16[384,128]{1,0:T(8,128)(2,1)} %get-tuple-element.101), channel_id=1, source_target_pairs={{0,1},{1,0},{2,3},{3,2},{4,5},{5,4},{6,7},{7,6},{8,9},{9,8},{10,11... | collective-permute-start | bytes 294920 | tf_op jit(solution)/shard_map/ppermute | solution.py:454
  30.2 1.5 %collective-permute-start.11 = (bf16[384,128]{1,0:T(8,128)(2,1)}, bf16[384,128]{1,0:T(8,128)(2,1)S(1)}, u32[]{:S(2)}, u32[]{:S(2)}) collective-permute-start(bf16[384,128]{1,0:T(8,128)(2,1)} %get-tuple-element.102), channel_id=1, source_target_pairs={{0,2},{1,3},{2,0},{3,1},{4,6},{5,7},{6,4},{7,5},{8,10},{9,11},{10,... | collective-permute-start | bytes 294920 | tf_op jit(solution)/shard_map/ppermute | solution.py:454
  31.7 0.0 collective-permute-done.7.rest_1_
  31.7 0.4 collective-permute-start.12
  32.0 1.1 %taps_rest.1 = (bf16[2,256,512]{2,1,0:T(8,128)(2,1)S(1)}, bf16[2,256,256]{2,1,0:T(8,128)(2,1)S(1)}, bf16[2,2,256,256]{3,2,1,0:T(8,128)(2,1)S(1)}) custom-call(f32[3]{0:T(128)S(1)} %copy-done.1, f32[3]{0:T(128)S(1)} %copy-done.2), custom_call_target="tpu_custom_call" | custom-call | flops 1000000000 | bytes 1024 | tf_op jit(solution)/shard_map/taps_rest/pallas_call | solution.py:494
  33.2 0.0 collective-permute-done.8.rest_2_
  33.2 0.0 collective-permute-done.9.rest_3_
  33.2 1.4 %main_next.1.next_ref = f32[16,256,128]{2,1,0:T(8,128)S(1)} custom-call(bf16[2,256,512]{2,1,0:T(8,128)(2,1)S(1)} %get-tuple-element.91.wall_ref, bf16[2,256,256]{2,1,0:T(8,128)(2,1)S(1)} %get-tuple-element.92.main_ref, bf16[1024,128]{1,0:T(8,128)(2,1)S(1)} %get-tuple-element.93.rest_0_, bf16[1024,128]{1,0:T(8,128)(2,1)S(1)} %collective-permute-done.7.rest_1_, ...), custom_call_target="tpu_custom_call" | custom-call | flops 1000000000 | bytes 1024 | tf_op jit(solution)/shard_map/main_next/pallas_call | solution.py:567
  34.6 6.0 %collective-permute-done.10.rest_1_ = bf16[384,128]{1,0:T(8,128)(2,1)S(1)} collective-permute-done((bf16[384,128]{1,0:T(8,128)(2,1)}, bf16[384,128]{1,0:T(8,128)(2,1)S(1)}, u32[]{:S(2)}, u32[]{:S(2)}) %collective-permute-start.10) | collective-permute-done | bytes 98336 | tf_op jit(solution)/shard_map/ppermute | solution.py:454
  40.6 0.0 collective-permute-done.11.rest_2_
  40.6 3.4 %collective-permute-done.12.rest_3_ = bf16[384,128]{1,0:T(8,128)(2,1)S(1)} collective-permute-done((bf16[384,128]{1,0:T(8,128)(2,1)}, bf16[384,128]{1,0:T(8,128)(2,1)S(1)}, u32[]{:S(2)}, u32[]{:S(2)}) %collective-permute-start.12) | collective-permute-done | bytes 98336 | tf_op jit(solution)/shard_map/ppermute | solution.py:454
  44.0 0.0 copy-done.3
  44.0 5.1 %filter_rest.1 = bf16[32,4,32,256]{3,2,1,0:T(8,128)(2,1)} custom-call(f32[8,256,128]{2,1,0:T(8,128)S(1)} %copy-done.3, f32[16,256,128]{2,1,0:T(8,128)S(1)} %main_next.1.next_ref, f32[256,128]{1,0:T(8,128)S(1)} %get-tuple-element.82.factor_ref, s32[4,4,128]{2,1,0:T(4,128)S(1)} %get-tuple-element.83.target_ref, ...), custom_call_target="tpu_custom_call" | custom-call | flops 99999997952 | bytes 1024 | tf_op jit(solution)/shard_map/filter_rest/pallas_call | solution.py:574
  49.1 4.9 %all-to-all-done.1 = bf16[32,4,32,128]{3,2,1,0:T(8,128)(2,1)S(1)} async-done(((bf16[32,4,32,128]{3,2,1,0:T(8,128)(2,1)}), bf16[32,4,32,128]{3,2,1,0:T(8,128)(2,1)S(1)}, u32[]{:S(2)}, u32[]{:S(2)}) %all-to-all-start.1) | async-done | bytes 1048608 | tf_op jit(solution)/shard_map/all_to_all | solution.py:459
  54.0 3.3 %all-to-all-start = ((bf16[32,4,32,256]{3,2,1,0:T(8,128)(2,1)}), bf16[32,4,32,256]{3,2,1,0:T(8,128)(2,1)S(1)}, u32[]{:S(2)}, u32[]{:S(2)}) async-start(bf16[32,4,32,256]{3,2,1,0:T(8,128)(2,1)} %filter_rest.1), calls=%async_computation | async-start | bytes 4194304 | tf_op jit(solution)/shard_map/all_to_all | solution.py:459
  57.4 1.0 join.2.rest_0_
  58.4 47.7 %all-to-all-done = bf16[32,4,32,256]{3,2,1,0:T(8,128)(2,1)S(1)} async-done(((bf16[32,4,32,256]{3,2,1,0:T(8,128)(2,1)}), bf16[32,4,32,256]{3,2,1,0:T(8,128)(2,1)S(1)}, u32[]{:S(2)}, u32[]{:S(2)}) %all-to-all-start) | async-done | bytes 2097184 | tf_op jit(solution)/shard_map/all_to_all | solution.py:459
  106.1 1.4 %join.3 = bf16[8,128,1536]{2,1,0:T(8,128)(2,1)} custom-call(bf16[8,4,128,256]{3,2,1,0:T(8,128)(2,1)S(1)} %bitcast.6, bf16[8,128,1536]{2,1,0:T(8,128)(2,1)} %join.2.rest_0_), custom_call_target="tpu_custom_call", output_to_operand_aliasing={{}: (1, {})} | custom-call | tf_op jit(solution)/shard_map/join/pallas_call | solution.py:592
  (5 shorter events, 0.0 us)
Async XLA Ops:
  0.0 5.8 %copy-start = (bf16[3,32,64,128]{3,2,1,0:T(8,128)(2,1)S(1)}, bf16[3,32,64,128]{3,2,1,0:T(8,128)(2,1)}, u32[]{:S(2)}) copy-start(bf16[3,32,64,128]{3,2,1,0:T(8,128)(2,1)} %param.6) | copy-start | bytes 4718596
  1.3 9.7 %copy-start.1 = (f32[3]{0:T(128)S(1)}, f32[3]{0:T(128)}, u32[]{:S(2)}) copy-start(f32[3]{0:T(128)} %wall_scale.2) | copy-start | bytes 40
  1.3 9.7 %copy-start.2 = (f32[3]{0:T(128)S(1)}, f32[3]{0:T(128)}, u32[]{:S(2)}) copy-start(f32[3]{0:T(128)} %span_scale.2) | copy-start | bytes 40
  1.3 10.6 %collective-permute-start = (bf16[544,128]{1,0:T(8,128)(2,1)S(1)}, bf16[544,128]{1,0:T(8,128)(2,1)S(1)}, u32[]{:S(2)}, u32[]{:S(2)}) collective-permute-start(bf16[544,128]{1,0:T(8,128)(2,1)S(1)} %get-tuple-element.62), channel_id=1, source_target_pairs={{0,1},{1,0},{2,3},{3,2},{4,5},{5,4},{6,7},{7,6},{8,9},{9,8},{10,11... | collective-permute-start | bytes 417800 | tf_op jit(solution)/shard_map/ppermute | solution.py:454
  4.3 8.1 %collective-permute-start.1 = (bf16[544,128]{1,0:T(8,128)(2,1)S(1)}, bf16[544,128]{1,0:T(8,128)(2,1)S(1)}, u32[]{:S(2)}, u32[]{:S(2)}) collective-permute-start(bf16[544,128]{1,0:T(8,128)(2,1)S(1)} %get-tuple-element.63), channel_id=1, source_target_pairs={{0,2},{1,3},{2,0},{3,1},{4,6},{5,7},{6,4},{7,5},{8,10},{9,11},{10,... | collective-permute-start | bytes 417800 | tf_op jit(solution)/shard_map/ppermute | solution.py:454
  5.8 6.6 %collective-permute-start.2 = (bf16[544,128]{1,0:T(8,128)(2,1)S(1)}, bf16[544,128]{1,0:T(8,128)(2,1)S(1)}, u32[]{:S(2)}, u32[]{:S(2)}) collective-permute-start(bf16[544,128]{1,0:T(8,128)(2,1)S(1)} %get-tuple-element.64), channel_id=1, source_target_pairs={{0,3},{1,2},{2,1},{3,0},{4,7},{5,6},{6,5},{7,4},{8,11},{9,10},{10,... | collective-permute-start | bytes 417800 | tf_op jit(solution)/shard_map/ppermute | solution.py:454
  6.8 10.1 %collective-permute-start.4 = (bf16[4,2,96,128]{3,2,1,0:T(8,128)(2,1)S(1)}, bf16[4,2,96,128]{3,2,1,0:T(8,128)(2,1)S(1)}, u32[]{:S(2)}, u32[]{:S(2)}) collective-permute-start(bf16[4,2,96,128]{3,2,1,0:T(8,128)(2,1)S(1)} %get-tuple-element.66), channel_id=1, source_target_pairs={{0,4},{4,0},{8,12},{12,8},{16,20},{20,16},{24,28},{28,24},{1,5},{5... | collective-permute-start | bytes 589832 | tf_op jit(solution)/shard_map/ppermute | solution.py:450
  6.9 13.1 %collective-permute-start.5 = (bf16[4,2,96,128]{3,2,1,0:T(8,128)(2,1)S(1)}, bf16[4,2,96,128]{3,2,1,0:T(8,128)(2,1)S(1)}, u32[]{:S(2)}, u32[]{:S(2)}) collective-permute-start(bf16[4,2,96,128]{3,2,1,0:T(8,128)(2,1)S(1)} %get-tuple-element.67), channel_id=1, source_target_pairs={{0,28},{4,8},{8,4},{12,16},{16,12},{20,24},{24,20},{28,0},{1,29},{... | collective-permute-start | bytes 589832 | tf_op jit(solution)/shard_map/ppermute | solution.py:450
  12.7 8.7 %collective-permute-start.3 = (bf16[192,256]{1,0:T(8,128)(2,1)S(1)}, bf16[192,256]{1,0:T(8,128)(2,1)S(1)}, u32[]{:S(2)}, u32[]{:S(2)}) collective-permute-start(bf16[192,256]{1,0:T(8,128)(2,1)S(1)} %get-tuple-element.76), channel_id=1, source_target_pairs={{0,4},{4,0},{8,12},{12,8},{16,20},{20,16},{24,28},{28,24},{1,5},{5... | collective-permute-start | bytes 294920 | tf_op jit(solution)/shard_map/ppermute | solution.py:450
  12.8 8.6 %collective-permute-start.6 = (bf16[192,256]{1,0:T(8,128)(2,1)S(1)}, bf16[192,256]{1,0:T(8,128)(2,1)S(1)}, u32[]{:S(2)}, u32[]{:S(2)}) collective-permute-start(bf16[192,256]{1,0:T(8,128)(2,1)S(1)} %get-tuple-element.78), channel_id=1, source_target_pairs={{0,28},{4,8},{8,4},{12,16},{16,12},{20,24},{24,20},{28,0},{1,29},{... | collective-permute-start | bytes 294920 | tf_op jit(solution)/shard_map/ppermute | solution.py:450
  16.9 14.8 %collective-permute-start.7 = (bf16[1024,128]{1,0:T(8,128)(2,1)S(1)}, bf16[1024,128]{1,0:T(8,128)(2,1)S(1)}, u32[]{:S(2)}, u32[]{:S(2)}) collective-permute-start(bf16[1024,128]{1,0:T(8,128)(2,1)S(1)} %get-tuple-element.94), channel_id=1, source_target_pairs={{0,1},{1,0},{2,3},{3,2},{4,5},{5,4},{6,7},{7,6},{8,9},{9,8},{10,11... | collective-permute-start | bytes 786440 | tf_op jit(solution)/shard_map/ppermute | solution.py:454
  19.1 14.1 %collective-permute-start.8 = (bf16[1024,128]{1,0:T(8,128)(2,1)S(1)}, bf16[1024,128]{1,0:T(8,128)(2,1)S(1)}, u32[]{:S(2)}, u32[]{:S(2)}) collective-permute-start(bf16[1024,128]{1,0:T(8,128)(2,1)S(1)} %get-tuple-element.95), channel_id=1, source_target_pairs={{0,2},{1,3},{2,0},{3,1},{4,6},{5,7},{6,4},{7,5},{8,10},{9,11},{10,... | collective-permute-start | bytes 786440 | tf_op jit(solution)/shard_map/ppermute | solution.py:454
  20.0 13.2 %collective-permute-start.9 = (bf16[1024,128]{1,0:T(8,128)(2,1)S(1)}, bf16[1024,128]{1,0:T(8,128)(2,1)S(1)}, u32[]{:S(2)}, u32[]{:S(2)}) collective-permute-start(bf16[1024,128]{1,0:T(8,128)(2,1)S(1)} %get-tuple-element.96), channel_id=1, source_target_pairs={{0,3},{1,2},{2,1},{3,0},{4,7},{5,6},{6,5},{7,4},{8,11},{9,10},{10,... | collective-permute-start | bytes 786440 | tf_op jit(solution)/shard_map/ppermute | solution.py:454
  24.9 29.1 %all-to-all-start.1 = ((bf16[32,4,32,128]{3,2,1,0:T(8,128)(2,1)}), bf16[32,4,32,128]{3,2,1,0:T(8,128)(2,1)S(1)}, u32[]{:S(2)}, u32[]{:S(2)}) async-start(bf16[32,4,32,128]{3,2,1,0:T(8,128)(2,1)} %get-tuple-element.104), calls=%async_computation.1 | async-start | bytes 2097152 | tf_op jit(solution)/shard_map/all_to_all | solution.py:459
  28.5 12.1 %collective-permute-start.10 = (bf16[384,128]{1,0:T(8,128)(2,1)}, bf16[384,128]{1,0:T(8,128)(2,1)S(1)}, u32[]{:S(2)}, u32[]{:S(2)}) collective-permute-start(bf16[384,128]{1,0:T(8,128)(2,1)} %get-tuple-element.101), channel_id=1, source_target_pairs={{0,1},{1,0},{2,3},{3,2},{4,5},{5,4},{6,7},{7,6},{8,9},{9,8},{10,11... | collective-permute-start | bytes 294920 | tf_op jit(solution)/shard_map/ppermute | solution.py:454
  30.2 10.4 %collective-permute-start.11 = (bf16[384,128]{1,0:T(8,128)(2,1)}, bf16[384,128]{1,0:T(8,128)(2,1)S(1)}, u32[]{:S(2)}, u32[]{:S(2)}) collective-permute-start(bf16[384,128]{1,0:T(8,128)(2,1)} %get-tuple-element.102), channel_id=1, source_target_pairs={{0,2},{1,3},{2,0},{3,1},{4,6},{5,7},{6,4},{7,5},{8,10},{9,11},{10,... | collective-permute-start | bytes 294920 | tf_op jit(solution)/shard_map/ppermute | solution.py:454
  31.7 12.3 %collective-permute-start.12 = (bf16[384,128]{1,0:T(8,128)(2,1)}, bf16[384,128]{1,0:T(8,128)(2,1)S(1)}, u32[]{:S(2)}, u32[]{:S(2)}) collective-permute-start(bf16[384,128]{1,0:T(8,128)(2,1)} %get-tuple-element.103), channel_id=1, source_target_pairs={{0,3},{1,2},{2,1},{3,0},{4,7},{5,6},{6,5},{7,4},{8,11},{9,10},{10,... | collective-permute-start | bytes 294920 | tf_op jit(solution)/shard_map/ppermute | solution.py:454
  33.1 10.8 %copy-start.3 = (f32[8,256,128]{2,1,0:T(8,128)S(1)}, f32[8,256,128]{2,1,0:T(8,128)}, u32[]{:S(2)}) copy-start(f32[8,256,128]{2,1,0:T(8,128)} %get-tuple-element.85.psi_ref) | copy-start | bytes 3145732
  33.2 10.8 %copy-start.4 = (bf16[384,128]{1,0:T(8,128)(2,1)S(1)}, bf16[384,128]{1,0:T(8,128)(2,1)}, u32[]{:S(2)}) copy-start(bf16[384,128]{1,0:T(8,128)(2,1)} %get-tuple-element.100.rest_0_) | copy-start | bytes 294916
  54.0 52.0 %all-to-all-start = ((bf16[32,4,32,256]{3,2,1,0:T(8,128)(2,1)}), bf16[32,4,32,256]{3,2,1,0:T(8,128)(2,1)S(1)}, u32[]{:S(2)}, u32[]{:S(2)}) async-start(bf16[32,4,32,256]{3,2,1,0:T(8,128)(2,1)} %filter_rest.1), calls=%async_computation | async-start | bytes 4194304 | tf_op jit(solution)/shard_map/all_to_all | solution.py:459

commit v13 on v12

--- a/solution.py
+++ b/solution.py
@@ -278,6 +278,12 @@
         psi_ref[t], psi_ref[t + 1] = main_part(planes_of(refs, t, rows), wall_ref[c], main_ref[c])
 
 
+def main_and_small_kernel(planes, slots, wall_ref, main_ref, *rest):
+    *in_refs, psi_ref, factor_ref, target_ref = rest
+    main_kernel(planes, wall_ref, main_ref, *in_refs, psi_ref)
+    small_kernel(slots, *in_refs, factor_ref, target_ref)
+
+
 def widen(factor_ref, wide_ref, which):
     for f in which:
         wide_ref[f] = jnp.broadcast_to(factor_ref[:, f : f + 1], wide_ref.shape[1:])
@@ -504,13 +510,6 @@
         )(wall_scale, span_scale)
 
     wall_first, main_first, halo_first = taps(0, 1, struct, "taps_first")
-    factor, target = call(
-        functools.partial(small_kernel, slots),
-        [VMEM] * n_wall,
-        [struct((full, cols), F32), struct((n_wall, count, cols), jnp.int32)],
-        "small",
-        16,
-    )(*packed)
 
     edge = struct((planes * HALO, full), BF16)
     near, far = call(
@@ -523,8 +522,12 @@
     near, rest_near, rest_far = lax.optimization_barrier((near, rest_near, rest_far))
 
     psi = struct((planes, full, cols), F32)
-    psi_main = call(
-        functools.partial(main_kernel, planes), [VMEM] * (2 + n_wall), [psi], "main_first", 16
+    psi_main, factor, target = call(
+        functools.partial(main_and_small_kernel, planes, slots),
+        [VMEM] * (2 + n_wall),
+        [psi, struct((full, cols), F32), struct((n_wall, count, cols), jnp.int32)],
+        "main_first",
+        16,
     )(wall_first, main_first, *packed)
 
     def scratch(some):

time: 108 us -> 108 us (level)
  no operation moved by 1% of the time
where the time goes in v13:
time: 108 us
  waiting for transfers between devices  63.4 us (59%)
  starting transfers between devices  25.7 us (24%)
  Pallas kernels  18.7 us (17%)
    all_to_all x2, waiting for transfers between devices, send(): lax.all_to_all(x, ('span', 'wall'), 0, 0, tiled=True)  52.6 us
    ppermute x9, starting transfers between devices, spread(): lax.ppermute(x, 'wall', [(i, i ^ step) for i in range(n_wall)])  11.7 us
    ppermute x9, waiting for transfers between devices, spread(): lax.ppermute(x, 'wall', [(i, i ^ step) for i in range(n_wall)])  10.7 us
    ppermute x2, starting transfers between devices, exchange(): lax.ppermute(far, 'span', chip_pairs)  7.86 us
    all_to_all x2, starting transfers between devices, send(): lax.all_to_all(x, ('span', 'wall'), 0, 0, tiled=True)  5.99 us
    pallas_call x1, Pallas kernels, per_device(): call(functools.partial(rest_kernel, planes), [VMEM] * (7 + n_wall), [out(...  5.11 us
    pallas_call x1, Pallas kernels, per_device(): call(functools.partial(first_kernel, planes), [VMEM] * 7, [out(1), hbm(ps...  3.47 us
    pallas_call x2, Pallas kernels, join(): pl.pallas_call(functools.partial(join_narrow_kernel, some) if narrow else...  2.37 us
  transfers between devices with their start and end apart: 15, of which 5 were waited for; matrix products, arithmetic and copies ran while one was open for 0% of the time, Pallas kernels for 15%

profile of v13, /device:TPU:0, one launch (start us, length us, event | category | flops | bytes accessed | tf_op | source)
XLA Modules:
  0.0 108.0 jit_solution(5910904698929480728)
XLA Ops:
  0.0 1.3 %pack.1 = (bf16[544,128]{1,0:T(8,128)(2,1)S(1)}, bf16[544,128]{1,0:T(8,128)(2,1)S(1)}, bf16[544,128]{1,0:T(8,128)(2,1)S(1)}, bf16[544,128]{1,0:T(8,128)(2,1)S(1)}) custom-call(bf16[3,2048,128]{2,1,0:T(8,128)(2,1)} %bitcast.8, f32[6,64]{1,0:T(8,128)} %lund_in.1, f32[1,64]{1,0:T(1,128)} %bitcast.11, s32[1,512]{1,0:T(1,128)} %bitcast.10), custom_call_target="tpu_custom_call" | custom-call | flops 1000000000 | bytes 1024 | tf_op jit(solution)/shard_map/pack/pallas_call | solution.py:469
  1.3 3.0 %collective-permute-start = (bf16[544,128]{1,0:T(8,128)(2,1)S(1)}, bf16[544,128]{1,0:T(8,128)(2,1)S(1)}, u32[]{:S(2)}, u32[]{:S(2)}) collective-permute-start(bf16[544,128]{1,0:T(8,128)(2,1)S(1)} %get-tuple-element.63), channel_id=1, source_target_pairs={{0,1},{1,0},{2,3},{3,2},{4,5},{5,4},{6,7},{7,6},{8,9},{9,8},{10,11... | collective-permute-start | bytes 417800 | tf_op jit(solution)/shard_map/ppermute | solution.py:460
  4.3 1.5 %collective-permute-start.1 = (bf16[544,128]{1,0:T(8,128)(2,1)S(1)}, bf16[544,128]{1,0:T(8,128)(2,1)S(1)}, u32[]{:S(2)}, u32[]{:S(2)}) collective-permute-start(bf16[544,128]{1,0:T(8,128)(2,1)S(1)} %get-tuple-element.64), channel_id=1, source_target_pairs={{0,2},{1,3},{2,0},{3,1},{4,6},{5,7},{6,4},{7,5},{8,10},{9,11},{10,... | collective-permute-start | bytes 417800 | tf_op jit(solution)/shard_map/ppermute | solution.py:460
  5.8 0.0 collective-permute-start.2
  5.8 0.0 copy-done
  5.8 0.9 prepare_rest.1
  6.8 0.0 copy-start.2
  6.8 0.1 collective-permute-start.4
  6.9 4.2 %collective-permute-start.5 = (bf16[4,2,96,128]{3,2,1,0:T(8,128)(2,1)S(1)}, bf16[4,2,96,128]{3,2,1,0:T(8,128)(2,1)S(1)}, u32[]{:S(2)}, u32[]{:S(2)}) collective-permute-start(bf16[4,2,96,128]{3,2,1,0:T(8,128)(2,1)S(1)} %get-tuple-element.68), channel_id=1, source_target_pairs={{0,28},{4,8},{8,4},{12,16},{16,12},{20,24},{24,20},{28,0},{1,29},{... | collective-permute-start | bytes 589832 | tf_op jit(solution)/shard_map/ppermute | solution.py:456
  11.0 0.0 collective-permute-done.rest_1_
  11.0 1.4 %collective-permute-done.1.rest_2_ = bf16[544,128]{1,0:T(8,128)(2,1)S(1)} collective-permute-done((bf16[544,128]{1,0:T(8,128)(2,1)S(1)}, bf16[544,128]{1,0:T(8,128)(2,1)S(1)}, u32[]{:S(2)}, u32[]{:S(2)}) %collective-permute-start.1) | collective-permute-done | bytes 139296 | tf_op jit(solution)/shard_map/ppermute | solution.py:460
  12.4 0.0 collective-permute-done.2.rest_3_
  12.4 0.3 edges_first.1
  12.7 0.1 collective-permute-start.3
  12.8 3.7 %collective-permute-start.6 = (bf16[192,256]{1,0:T(8,128)(2,1)S(1)}, bf16[192,256]{1,0:T(8,128)(2,1)S(1)}, u32[]{:S(2)}, u32[]{:S(2)}) collective-permute-start(bf16[192,256]{1,0:T(8,128)(2,1)S(1)} %get-tuple-element.80), channel_id=1, source_target_pairs={{0,28},{4,8},{8,4},{12,16},{16,12},{20,24},{24,20},{28,0},{1,29},{... | collective-permute-start | bytes 294920 | tf_op jit(solution)/shard_map/ppermute | solution.py:456
  16.5 0.0 copy-done.1
  16.5 0.0 copy-done.2
  16.5 0.9 taps_first.1
  17.4 0.0 collective-permute-done.4.near_ref
  17.4 1.3 %collective-permute-start.7 = (bf16[1024,128]{1,0:T(8,128)(2,1)S(1)}, bf16[1024,128]{1,0:T(8,128)(2,1)S(1)}, u32[]{:S(2)}, u32[]{:S(2)}) collective-permute-start(bf16[1024,128]{1,0:T(8,128)(2,1)S(1)} %get-tuple-element.96), channel_id=1, source_target_pairs={{0,1},{1,0},{2,3},{3,2},{4,5},{5,4},{6,7},{7,6},{8,9},{9,8},{10,11... | collective-permute-start | bytes 786440 | tf_op jit(solution)/shard_map/ppermute | solution.py:460
  18.7 1.0 main_first.1
  19.7 0.9 collective-permute-start.8
  20.5 0.0 collective-permute-done.5.far_ref
  20.6 1.4 %collective-permute-start.9 = (bf16[1024,128]{1,0:T(8,128)(2,1)S(1)}, bf16[1024,128]{1,0:T(8,128)(2,1)S(1)}, u32[]{:S(2)}, u32[]{:S(2)}) collective-permute-start(bf16[1024,128]{1,0:T(8,128)(2,1)S(1)} %get-tuple-element.98), channel_id=1, source_target_pairs={{0,3},{1,2},{2,1},{3,0},{4,7},{5,6},{6,5},{7,4},{8,11},{9,10},{10,... | collective-permute-start | bytes 786440 | tf_op jit(solution)/shard_map/ppermute | solution.py:460
  22.0 0.0 collective-permute-done.3.near_ref
  22.0 0.0 collective-permute-done.6.far_ref
  22.0 3.5 %filter_first.1 = (bf16[32,4,32,128]{3,2,1,0:T(8,128)(2,1)}, f32[8,256,128]{2,1,0:T(8,128)}) custom-call(f32[8,256,128]{2,1,0:T(8,128)S(1)} %get-tuple-element.77.psi_in, bf16[192,256]{1,0:T(8,128)(2,1)S(1)} %collective-permute-done.3.near_ref, bf16[192,256]{1,0:T(8,128)(2,1)S(1)} %collective-permute-done.6.far_ref, ...), custom_call_target="tpu_custom_call" | custom-call | flops 1000000000 | bytes 1024 | tf_op jit(solution)/shard_map/filter_first/pallas_call | solution.py:546
  25.5 2.7 %all-to-all-start.1 = ((bf16[32,4,32,128]{3,2,1,0:T(8,128)(2,1)}), bf16[32,4,32,128]{3,2,1,0:T(8,128)(2,1)S(1)}, u32[]{:S(2)}, u32[]{:S(2)}) async-start(bf16[32,4,32,128]{3,2,1,0:T(8,128)(2,1)} %get-tuple-element.106), calls=%async_computation.1 | async-start | bytes 2097152 | tf_op jit(solution)/shard_map/all_to_all | solution.py:465
  28.1 0.9 pack_late.1
  29.0 1.7 %collective-permute-start.10 = (bf16[384,128]{1,0:T(8,128)(2,1)}, bf16[384,128]{1,0:T(8,128)(2,1)S(1)}, u32[]{:S(2)}, u32[]{:S(2)}) collective-permute-start(bf16[384,128]{1,0:T(8,128)(2,1)} %get-tuple-element.103), channel_id=1, source_target_pairs={{0,1},{1,0},{2,3},{3,2},{4,5},{5,4},{6,7},{7,6},{8,9},{9,8},{10,11... | collective-permute-start | bytes 294920 | tf_op jit(solution)/shard_map/ppermute | solution.py:460
  30.7 1.5 %collective-permute-start.11 = (bf16[384,128]{1,0:T(8,128)(2,1)}, bf16[384,128]{1,0:T(8,128)(2,1)S(1)}, u32[]{:S(2)}, u32[]{:S(2)}) collective-permute-start(bf16[384,128]{1,0:T(8,128)(2,1)} %get-tuple-element.104), channel_id=1, source_target_pairs={{0,2},{1,3},{2,0},{3,1},{4,6},{5,7},{6,4},{7,5},{8,10},{9,11},{10,... | collective-permute-start | bytes 294920 | tf_op jit(solution)/shard_map/ppermute | solution.py:460
  32.2 0.0 collective-permute-done.7.rest_1_
  32.2 0.4 collective-permute-start.12
  32.6 1.1 %taps_rest.1 = (bf16[2,256,512]{2,1,0:T(8,128)(2,1)S(1)}, bf16[2,256,256]{2,1,0:T(8,128)(2,1)S(1)}, bf16[2,2,256,256]{3,2,1,0:T(8,128)(2,1)S(1)}) custom-call(f32[3]{0:T(128)S(1)} %copy-done.1, f32[3]{0:T(128)S(1)} %copy-done.2), custom_call_target="tpu_custom_call" | custom-call | flops 1000000000 | bytes 1024 | tf_op jit(solution)/shard_map/taps_rest/pallas_call | solution.py:500
  33.7 0.0 copy-start.3
  33.7 0.0 copy-start.4
  33.7 0.0 collective-permute-done.8.rest_2_
  33.7 0.0 collective-permute-done.9.rest_3_
  33.7 1.4 %main_next.1.next_ref = f32[16,256,128]{2,1,0:T(8,128)S(1)} custom-call(bf16[2,256,512]{2,1,0:T(8,128)(2,1)S(1)} %get-tuple-element.93.wall_ref, bf16[2,256,256]{2,1,0:T(8,128)(2,1)S(1)} %get-tuple-element.94.main_ref, bf16[1024,128]{1,0:T(8,128)(2,1)S(1)} %get-tuple-element.95.rest_0_, bf16[1024,128]{1,0:T(8,128)(2,1)S(1)} %collective-permute-done.7.rest_1_, ...), custom_call_target="tpu_custom_call" | custom-call | flops 1000000000 | bytes 1024 | tf_op jit(solution)/shard_map/main_next/pallas_call | solution.py:570
  35.2 6.0 %collective-permute-done.10.rest_1_ = bf16[384,128]{1,0:T(8,128)(2,1)S(1)} collective-permute-done((bf16[384,128]{1,0:T(8,128)(2,1)}, bf16[384,128]{1,0:T(8,128)(2,1)S(1)}, u32[]{:S(2)}, u32[]{:S(2)}) %collective-permute-start.10) | collective-permute-done | bytes 98336 | tf_op jit(solution)/shard_map/ppermute | solution.py:460
  41.2 0.0 collective-permute-done.11.rest_2_
  41.2 3.4 %collective-permute-done.12.rest_3_ = bf16[384,128]{1,0:T(8,128)(2,1)S(1)} collective-permute-done((bf16[384,128]{1,0:T(8,128)(2,1)}, bf16[384,128]{1,0:T(8,128)(2,1)S(1)}, u32[]{:S(2)}, u32[]{:S(2)}) %collective-permute-start.12) | collective-permute-done | bytes 98336 | tf_op jit(solution)/shard_map/ppermute | solution.py:460
  44.5 5.1 %filter_rest.1 = bf16[32,4,32,256]{3,2,1,0:T(8,128)(2,1)} custom-call(f32[8,256,128]{2,1,0:T(8,128)S(1)} %copy-done.3, f32[16,256,128]{2,1,0:T(8,128)S(1)} %main_next.1.next_ref, f32[256,128]{1,0:T(8,128)S(1)} %get-tuple-element.84.factor_ref, s32[4,4,128]{2,1,0:T(4,128)S(1)} %get-tuple-element.85.target_ref, ...), custom_call_target="tpu_custom_call" | custom-call | flops 99999997952 | bytes 1024 | tf_op jit(solution)/shard_map/filter_rest/pallas_call | solution.py:577
  49.6 4.9 %all-to-all-done.1 = bf16[32,4,32,128]{3,2,1,0:T(8,128)(2,1)S(1)} async-done(((bf16[32,4,32,128]{3,2,1,0:T(8,128)(2,1)}), bf16[32,4,32,128]{3,2,1,0:T(8,128)(2,1)S(1)}, u32[]{:S(2)}, u32[]{:S(2)}) %all-to-all-start.1) | async-done | bytes 1048608 | tf_op jit(solution)/shard_map/all_to_all | solution.py:465
  54.6 3.3 %all-to-all-start = ((bf16[32,4,32,256]{3,2,1,0:T(8,128)(2,1)}), bf16[32,4,32,256]{3,2,1,0:T(8,128)(2,1)S(1)}, u32[]{:S(2)}, u32[]{:S(2)}) async-start(bf16[32,4,32,256]{3,2,1,0:T(8,128)(2,1)} %filter_rest.1), calls=%async_computation | async-start | bytes 4194304 | tf_op jit(solution)/shard_map/all_to_all | solution.py:465
  57.9 1.0 join.2.rest_0_
  58.9 47.7 %all-to-all-done = bf16[32,4,32,256]{3,2,1,0:T(8,128)(2,1)S(1)} async-done(((bf16[32,4,32,256]{3,2,1,0:T(8,128)(2,1)}), bf16[32,4,32,256]{3,2,1,0:T(8,128)(2,1)S(1)}, u32[]{:S(2)}, u32[]{:S(2)}) %all-to-all-start) | async-done | bytes 2097184 | tf_op jit(solution)/shard_map/all_to_all | solution.py:465
  106.6 1.4 %join.3 = bf16[8,128,1536]{2,1,0:T(8,128)(2,1)} custom-call(bf16[8,4,128,256]{3,2,1,0:T(8,128)(2,1)S(1)} %bitcast.6, bf16[8,128,1536]{2,1,0:T(8,128)(2,1)} %join.2.rest_0_), custom_call_target="tpu_custom_call", output_to_operand_aliasing={{}: (1, {})} | custom-call | tf_op jit(solution)/shard_map/join/pallas_call | solution.py:595
  (4 shorter events, 0.0 us)
Async XLA Ops:
  0.0 5.8 %copy-start = (bf16[3,32,64,128]{3,2,1,0:T(8,128)(2,1)S(1)}, bf16[3,32,64,128]{3,2,1,0:T(8,128)(2,1)}, u32[]{:S(2)}) copy-start(bf16[3,32,64,128]{3,2,1,0:T(8,128)(2,1)} %param.6) | copy-start | bytes 4718596
  1.3 9.7 %collective-permute-start = (bf16[544,128]{1,0:T(8,128)(2,1)S(1)}, bf16[544,128]{1,0:T(8,128)(2,1)S(1)}, u32[]{:S(2)}, u32[]{:S(2)}) collective-permute-start(bf16[544,128]{1,0:T(8,128)(2,1)S(1)} %get-tuple-element.63), channel_id=1, source_target_pairs={{0,1},{1,0},{2,3},{3,2},{4,5},{5,4},{6,7},{7,6},{8,9},{9,8},{10,11... | collective-permute-start | bytes 417800 | tf_op jit(solution)/shard_map/ppermute | solution.py:460
  4.3 8.1 %collective-permute-start.1 = (bf16[544,128]{1,0:T(8,128)(2,1)S(1)}, bf16[544,128]{1,0:T(8,128)(2,1)S(1)}, u32[]{:S(2)}, u32[]{:S(2)}) collective-permute-start(bf16[544,128]{1,0:T(8,128)(2,1)S(1)} %get-tuple-element.64), channel_id=1, source_target_pairs={{0,2},{1,3},{2,0},{3,1},{4,6},{5,7},{6,4},{7,5},{8,10},{9,11},{10,... | collective-permute-start | bytes 417800 | tf_op jit(solution)/shard_map/ppermute | solution.py:460
  5.8 6.6 %collective-permute-start.2 = (bf16[544,128]{1,0:T(8,128)(2,1)S(1)}, bf16[544,128]{1,0:T(8,128)(2,1)S(1)}, u32[]{:S(2)}, u32[]{:S(2)}) collective-permute-start(bf16[544,128]{1,0:T(8,128)(2,1)S(1)} %get-tuple-element.65), channel_id=1, source_target_pairs={{0,3},{1,2},{2,1},{3,0},{4,7},{5,6},{6,5},{7,4},{8,11},{9,10},{10,... | collective-permute-start | bytes 417800 | tf_op jit(solution)/shard_map/ppermute | solution.py:460
  6.8 9.7 %copy-start.1 = (f32[3]{0:T(128)S(1)}, f32[3]{0:T(128)}, u32[]{:S(2)}) copy-start(f32[3]{0:T(128)} %wall_scale.2) | copy-start | bytes 40
  6.8 9.7 %copy-start.2 = (f32[3]{0:T(128)S(1)}, f32[3]{0:T(128)}, u32[]{:S(2)}) copy-start(f32[3]{0:T(128)} %span_scale.2) | copy-start | bytes 40
  6.8 10.6 %collective-permute-start.4 = (bf16[4,2,96,128]{3,2,1,0:T(8,128)(2,1)S(1)}, bf16[4,2,96,128]{3,2,1,0:T(8,128)(2,1)S(1)}, u32[]{:S(2)}, u32[]{:S(2)}) collective-permute-start(bf16[4,2,96,128]{3,2,1,0:T(8,128)(2,1)S(1)} %get-tuple-element.67), channel_id=1, source_target_pairs={{0,4},{4,0},{8,12},{12,8},{16,20},{20,16},{24,28},{28,24},{1,5},{5... | collective-permute-start | bytes 589832 | tf_op jit(solution)/shard_map/ppermute | solution.py:456
  6.9 13.7 %collective-permute-start.5 = (bf16[4,2,96,128]{3,2,1,0:T(8,128)(2,1)S(1)}, bf16[4,2,96,128]{3,2,1,0:T(8,128)(2,1)S(1)}, u32[]{:S(2)}, u32[]{:S(2)}) collective-permute-start(bf16[4,2,96,128]{3,2,1,0:T(8,128)(2,1)S(1)} %get-tuple-element.68), channel_id=1, source_target_pairs={{0,28},{4,8},{8,4},{12,16},{16,12},{20,24},{24,20},{28,0},{1,29},{... | collective-permute-start | bytes 589832 | tf_op jit(solution)/shard_map/ppermute | solution.py:456
  12.7 9.3 %collective-permute-start.3 = (bf16[192,256]{1,0:T(8,128)(2,1)S(1)}, bf16[192,256]{1,0:T(8,128)(2,1)S(1)}, u32[]{:S(2)}, u32[]{:S(2)}) collective-permute-start(bf16[192,256]{1,0:T(8,128)(2,1)S(1)} %get-tuple-element.78), channel_id=1, source_target_pairs={{0,4},{4,0},{8,12},{12,8},{16,20},{20,16},{24,28},{28,24},{1,5},{5... | collective-permute-start | bytes 294920 | tf_op jit(solution)/shard_map/ppermute | solution.py:456
  12.8 9.2 %collective-permute-start.6 = (bf16[192,256]{1,0:T(8,128)(2,1)S(1)}, bf16[192,256]{1,0:T(8,128)(2,1)S(1)}, u32[]{:S(2)}, u32[]{:S(2)}) collective-permute-start(bf16[192,256]{1,0:T(8,128)(2,1)S(1)} %get-tuple-element.80), channel_id=1, source_target_pairs={{0,28},{4,8},{8,4},{12,16},{16,12},{20,24},{24,20},{28,0},{1,29},{... | collective-permute-start | bytes 294920 | tf_op jit(solution)/shard_map/ppermute | solution.py:456
  17.4 14.8 %collective-permute-start.7 = (bf16[1024,128]{1,0:T(8,128)(2,1)S(1)}, bf16[1024,128]{1,0:T(8,128)(2,1)S(1)}, u32[]{:S(2)}, u32[]{:S(2)}) collective-permute-start(bf16[1024,128]{1,0:T(8,128)(2,1)S(1)} %get-tuple-element.96), channel_id=1, source_target_pairs={{0,1},{1,0},{2,3},{3,2},{4,5},{5,4},{6,7},{7,6},{8,9},{9,8},{10,11... | collective-permute-start | bytes 786440 | tf_op jit(solution)/shard_map/ppermute | solution.py:460
  19.7 14.1 %collective-permute-start.8 = (bf16[1024,128]{1,0:T(8,128)(2,1)S(1)}, bf16[1024,128]{1,0:T(8,128)(2,1)S(1)}, u32[]{:S(2)}, u32[]{:S(2)}) collective-permute-start(bf16[1024,128]{1,0:T(8,128)(2,1)S(1)} %get-tuple-element.97), channel_id=1, source_target_pairs={{0,2},{1,3},{2,0},{3,1},{4,6},{5,7},{6,4},{7,5},{8,10},{9,11},{10,... | collective-permute-start | bytes 786440 | tf_op jit(solution)/shard_map/ppermute | solution.py:460
  20.6 13.2 %collective-permute-start.9 = (bf16[1024,128]{1,0:T(8,128)(2,1)S(1)}, bf16[1024,128]{1,0:T(8,128)(2,1)S(1)}, u32[]{:S(2)}, u32[]{:S(2)}) collective-permute-start(bf16[1024,128]{1,0:T(8,128)(2,1)S(1)} %get-tuple-element.98), channel_id=1, source_target_pairs={{0,3},{1,2},{2,1},{3,0},{4,7},{5,6},{6,5},{7,4},{8,11},{9,10},{10,... | collective-permute-start | bytes 786440 | tf_op jit(solution)/shard_map/ppermute | solution.py:460
  25.5 29.1 %all-to-all-start.1 = ((bf16[32,4,32,128]{3,2,1,0:T(8,128)(2,1)}), bf16[32,4,32,128]{3,2,1,0:T(8,128)(2,1)S(1)}, u32[]{:S(2)}, u32[]{:S(2)}) async-start(bf16[32,4,32,128]{3,2,1,0:T(8,128)(2,1)} %get-tuple-element.106), calls=%async_computation.1 | async-start | bytes 2097152 | tf_op jit(solution)/shard_map/all_to_all | solution.py:465
  29.0 12.1 %collective-permute-start.10 = (bf16[384,128]{1,0:T(8,128)(2,1)}, bf16[384,128]{1,0:T(8,128)(2,1)S(1)}, u32[]{:S(2)}, u32[]{:S(2)}) collective-permute-start(bf16[384,128]{1,0:T(8,128)(2,1)} %get-tuple-element.103), channel_id=1, source_target_pairs={{0,1},{1,0},{2,3},{3,2},{4,5},{5,4},{6,7},{7,6},{8,9},{9,8},{10,11... | collective-permute-start | bytes 294920 | tf_op jit(solution)/shard_map/ppermute | solution.py:460
  30.7 10.4 %collective-permute-start.11 = (bf16[384,128]{1,0:T(8,128)(2,1)}, bf16[384,128]{1,0:T(8,128)(2,1)S(1)}, u32[]{:S(2)}, u32[]{:S(2)}) collective-permute-start(bf16[384,128]{1,0:T(8,128)(2,1)} %get-tuple-element.104), channel_id=1, source_target_pairs={{0,2},{1,3},{2,0},{3,1},{4,6},{5,7},{6,4},{7,5},{8,10},{9,11},{10,... | collective-permute-start | bytes 294920 | tf_op jit(solution)/shard_map/ppermute | solution.py:460
  32.2 12.3 %collective-permute-start.12 = (bf16[384,128]{1,0:T(8,128)(2,1)}, bf16[384,128]{1,0:T(8,128)(2,1)S(1)}, u32[]{:S(2)}, u32[]{:S(2)}) collective-permute-start(bf16[384,128]{1,0:T(8,128)(2,1)} %get-tuple-element.105), channel_id=1, source_target_pairs={{0,3},{1,2},{2,1},{3,0},{4,7},{5,6},{6,5},{7,4},{8,11},{9,10},{10,... | collective-permute-start | bytes 294920 | tf_op jit(solution)/shard_map/ppermute | solution.py:460
  33.7 10.8 %copy-start.3 = (f32[8,256,128]{2,1,0:T(8,128)S(1)}, f32[8,256,128]{2,1,0:T(8,128)}, u32[]{:S(2)}) copy-start(f32[8,256,128]{2,1,0:T(8,128)} %get-tuple-element.87.psi_ref) | copy-start | bytes 3145732
  33.7 10.8 %copy-start.4 = (bf16[384,128]{1,0:T(8,128)(2,1)S(1)}, bf16[384,128]{1,0:T(8,128)(2,1)}, u32[]{:S(2)}) copy-start(bf16[384,128]{1,0:T(8,128)(2,1)} %get-tuple-element.102.rest_0_) | copy-start | bytes 294916
  54.6 52.0 %all-to-all-start = ((bf16[32,4,32,256]{3,2,1,0:T(8,128)(2,1)}), bf16[32,4,32,256]{3,2,1,0:T(8,128)(2,1)S(1)}, u32[]{:S(2)}, u32[]{:S(2)}) async-start(bf16[32,4,32,256]{3,2,1,0:T(8,128)(2,1)} %filter_rest.1), calls=%async_computation | async-start | bytes 4194304 | tf_op jit(solution)/shard_map/all_to_all | solution.py:465
